TPU v7x, 256 devices: a whole 4x4x8 slice. The times are simulated.
256 devices in a mesh: gx: 16 (over z_hi, y, core), gy: 16 (over x, z_lo).
Axes of the slice: x: 4, y: 4, z: 8 (z_hi: 2, z_lo: 4; z = z_hi * 4 + z_lo), core: 2. Of those that a mesh axis runs over, the one named last changes fastest.
Arguments:
- tokens: bfloat16 [768, 16384], P('gy', 'gx'), may hold values from -6 to 6
- gate_weight: bfloat16 [16384, 26624], P('gx', 'gy'), may hold values from -0.046875 to 0.046875
- up_weight: bfloat16 [16384, 26624], P('gx', 'gy'), may hold values from -0.046875 to 0.046875
- down_weight: bfloat16 [26624, 16384], P('gy', 'gx'), may hold values from -0.0390625 to 0.0390625
Outputs:
- mixed: bfloat16 [768, 16384], P('gy', 'gx')
All inputs are finite; a program needn't handle non-finite values.
Results may differ from a plain program's by a relative error of at most 0.035.
Values may be sent and summed in bfloat16 or wider, within the bound.
No kernel may reach another device: no remote copies, remote signals or barrier semaphores. Data moves between devices by JAX's collectives and lax.ppermute only.
A program may use at most 64 MiB of HBM per device.

v0:
```python
import jax
import jax.numpy as jnp
from jax import lax
from jax.sharding import PartitionSpec as P


def shards(tokens, gate_weight, up_weight, down_weight):
    whole = lax.all_gather(tokens, "gy", axis=0, tiled=True)
    hidden_units = gate_weight.shape[1]
    gate_term = jnp.dot(whole, gate_weight, preferred_element_type=jnp.float32)
    up_term = jnp.dot(whole, up_weight, preferred_element_type=jnp.float32)
    summed = lax.psum_scatter(
        jnp.concatenate([gate_term, up_term], axis=1).astype(jnp.bfloat16),
        "gx",
        scatter_dimension=0,
        tiled=True,
    ).astype(jnp.float32)
    gate = summed[:, :hidden_units]
    up = summed[:, hidden_units:]
    hidden = (jax.nn.silu(gate) * up).astype(jnp.bfloat16)
    partial_out = jnp.dot(
        lax.all_gather(hidden, "gx", axis=0, tiled=True),
        down_weight,
        preferred_element_type=jnp.float32,
    )
    mixed = lax.psum_scatter(
        partial_out.astype(jnp.bfloat16), "gy", scatter_dimension=0, tiled=True
    )
    return mixed


def solution(mesh):
    in_specs = (P("gy", "gx"), P("gx", "gy"), P("gx", "gy"), P("gy", "gx"))
    out_specs = P("gy", "gx")
    return jax.shard_map(shards, mesh=mesh, in_specs=in_specs, out_specs=out_specs, check_vma=False)
```

profile of v0, /device:TPU:24, one launch (start us, length us, event | category | flops | bytes accessed | tf_op | source)
XLA Modules:
  0.0 380.6 jit_solution(10926365156780912345)
XLA Ops:
  6.5 0.0 copy-start
  6.5 0.0 all-gather.3.cloned.1.call-start
  6.5 0.7 all-gather.3.cloned.1.call-update
  7.3 0.0 reduce-scatter.3.cloned.1.call-start
  7.3 89.2 %all-gather.3.cloned.1.call-done = bf16[768,1024]{1,0:T(8,128)(2,1)} async-done(((bf16[48,1024]{1,0:T(8,128)(2,1)}), bf16[768,1024]{1,0:T(8,128)(2,1)}) %all-gather.3.cloned.1.call-update) | async-done | bytes 1572880 | tf_op jit(solution)/shard_map/all_gather | solution.py:8
  96.5 0.0 copy-done
  96.5 0.0 copy-start.1
  96.5 0.0 copy-start.2
  96.5 4.6 %convolution_convert_fusion = bf16[768,1664]{1,0:T(8,128)(2,1)S(1)} fusion(bf16[768,1024]{1,0:T(8,128)(2,1)} %all-gather.3.cloned.1.call-done, bf16[1024,1664]{1,0:T(8,128)(2,1)S(1)} %copy-done), kind=kOutput, calls=%fused_computation.1 | convolution fusion | flops 2618523648 | bytes 7536640 | tf_op jit(solution)/shard_map/dot_general | solution.py:11
  101.1 0.0 copy-done.1
  101.1 0.0 copy-done.2
  101.1 3.2 convolution_convert_fusion.1
  104.3 2.6 pad_maximum_fusion
  106.9 0.0 reduce-scatter.3.cloned.1.call-update
  107.0 0.0 all-gather.5.cloned.1.call-start
  107.0 110.1 %reduce-scatter.3.cloned.1.call-done = bf16[48,3328]{1,0:T(8,128)(2,1)} async-done(((bf16[768,3328]{1,0:T(8,128)(2,1)}), bf16[48,3328]{1,0:T(8,128)(2,1)}) %reduce-scatter.3.cloned.1.call-update) | async-done | bytes 319504 | tf_op jit(solution)/shard_map/reduce_scatter | solution.py:12
  217.1 1.0 convert_element_type.10
  218.1 0.8 fusion
  218.9 0.0 all-gather.5.cloned.1.call-update
  218.9 0.0 reduce-scatter.5.cloned.1.call-start
  218.9 63.5 %all-gather.5.cloned.1.call-done = bf16[768,1664]{1,0:T(8,128)(2,1)} async-done(((bf16[48,1664]{1,0:T(8,128)(2,1)}), bf16[768,1664]{1,0:T(8,128)(2,1)}) %all-gather.5.cloned.1.call-update) | async-done | bytes 2555920 | tf_op jit(solution)/shard_map/all_gather | solution.py:22
  282.4 6.9 %convolution_convert_fusion.2 = bf16[768,1024]{1,0:T(8,128)(2,1)} fusion(bf16[768,1664]{1,0:T(8,128)(2,1)} %all-gather.5.cloned.1.call-done, bf16[1664,1024]{1,0:T(8,128)(2,1)} %param.7), kind=kOutput, calls=%fused_computation.3 | convolution fusion | flops 2618032128 | bytes 7536640 | tf_op jit(solution)/shard_map/dot_general | solution.py:21
  289.3 0.0 reduce-scatter.5.cloned.1.call-update
  289.3 84.8 %reduce-scatter.5.cloned.1.call-done = bf16[48,1024]{1,0:T(8,128)(2,1)} async-done(((bf16[768,1024]{1,0:T(8,128)(2,1)}), bf16[48,1024]{1,0:T(8,128)(2,1)}) %reduce-scatter.5.cloned.1.call-update) | async-done | bytes 98320 | tf_op jit(solution)/shard_map/reduce_scatter | solution.py:26
Async XLA Ops:
  6.5 90.0 %copy-start = (bf16[1024,1664]{1,0:T(8,128)(2,1)S(1)}, bf16[1024,1664]{1,0:T(8,128)(2,1)}, u32[]{:S(2)}) copy-start(bf16[1024,1664]{1,0:T(8,128)(2,1)} %param.6) | copy-start | bytes 10223620
  6.5 90.0 %all-gather.3.cloned.1.call-start = ((), (), s32[]{:S(2)}) async-start(), calls=%async_computation.2 | async-start | bytes 1671168 | tf_op jit(solution)/shard_map/all_gather | solution.py:8
  7.3 209.8 %reduce-scatter.3.cloned.1.call-start = ((), (), s32[]{:S(2)}) async-start(), calls=%async_computation.3 | async-start | bytes 5431296 | tf_op jit(solution)/shard_map/reduce_scatter | solution.py:12
  96.5 4.6 %copy-start.1 = (bf16[1024,1664]{1,0:T(8,128)(2,1)S(1)}, bf16[1024,1664]{1,0:T(8,128)(2,1)}, u32[]{:S(2)}) copy-start(bf16[1024,1664]{1,0:T(8,128)(2,1)} %param.5) | copy-start | bytes 10223620
  96.5 4.6 %copy-start.2 = (bf16[768,1024]{1,0:T(8,128)(2,1)S(1)}, bf16[768,1024]{1,0:T(8,128)(2,1)}, u32[]{:S(2)}) copy-start(bf16[768,1024]{1,0:T(8,128)(2,1)} %all-gather.3.cloned.1.call-done) | copy-start | bytes 4718596
  107.0 175.4 %all-gather.5.cloned.1.call-start = ((), (), s32[]{:S(2)}) async-start(), calls=%async_computation.4 | async-start | bytes 2715648 | tf_op jit(solution)/shard_map/all_gather | solution.py:22
  218.9 155.2 %reduce-scatter.5.cloned.1.call-start = ((), (), s32[]{:S(2)}) async-start(), calls=%async_computation.5 | async-start | bytes 1671168 | tf_op jit(solution)/shard_map/reduce_scatter | solution.py:26
Sparse Core Ops, SparseCore 0:
  9.1 87.3 all-gather.2
  107.1 109.9 reduce-scatter.2
  220.1 62.2 all-gather.4
  289.4 84.6 reduce-scatter.4
where the time goes:
time: 381 us
  waiting for transfers between devices  348 us (91%)
  matrix products  14.7 us (4%)
  between operations  13.2 us (3%)
  other arithmetic  4.38 us (1%)
    reduce_scatter x1, waiting for transfers between devices, shards(): lax.psum_scatter(jnp.concatenate([gate_term, up_term], axis=1).astype(jnp...  110 us
    all_gather x1, waiting for transfers between devices, shards(): whole = lax.all_gather(tokens, 'gy', axis=0, tiled=True)  89.2 us
    reduce_scatter x1, waiting for transfers between devices, shards(): lax.psum_scatter(partial_out.astype(jnp.bfloat16), 'gy', scatter_dimensio...  84.8 us
    all_gather x1, waiting for transfers between devices, shards(): lax.all_gather(hidden, 'gx', axis=0, tiled=True)  63.5 us
  transfers between devices with their start and end apart: 4, of which 4 were waited for; matrix products, arithmetic and copies ran while one was open for 0% of the time, Pallas kernels for 0%

commit v1 on v0

v1 whole, which is shorter than its diff:
```python
import functools

import jax
import jax.numpy as jnp
from jax import lax
from jax.experimental import pallas as pl
from jax.experimental.pallas import tpu as pltpu
from jax.sharding import PartitionSpec as P

BF = jnp.bfloat16
F32 = jnp.float32
N = 16
FIRST = (1, 3)
SECOND = (3, 1)


def exchange(value, masks_x=(0, 0), z=0, masks_y=(0, 0), zhi=0, core=0):
    pairs = []
    for gx in range(N):
        for gy in range(N):
            other = (gx ^ (2 * masks_y[gx & 1]) ^ (8 * zhi) ^ core) * N + (gy ^ (4 * masks_x[gx & 1]) ^ z)
            pairs.append((gx * N + gy, other))
    return lax.ppermute(value, ("gx", "gy"), pairs)


def gray(v):
    return v ^ (v >> 1)


def kept(gx):
    odd = (gx & 1) == 1
    ys = [lax.select(odd, jnp.int32(gray(i)), jnp.int32(3 * gray(i) & 3)) for i in range(4)]
    return [gx ^ (2 * y) ^ (8 * z) for y in ys for z in (0, 1)]


def gathered_slot(block):
    x, z = block >> 2, block & 3
    return 8 * (z >> 1) + 2 * gray(lax.select(z < 2, x, (3 * x) & 3)) + (z & 1)


def scattered_slot(gx, block):
    x, z = block >> 2, block & 3
    return 4 * gray(lax.select((gx & 1) == 0, x, (3 * x) & 3)) + z


def pick_kernel(rows, *refs):
    *pieces, a_ref, b_ref, whole = refs
    first = 0
    for piece in pieces:
        whole[pl.ds(first, piece.shape[0]), :] = piece[...].astype(F32)
        first += piece.shape[0]
    me = lax.axis_index("gx")
    slots = [gathered_slot(block) for block in kept(me ^ 1) + kept(me)]
    for chunk, out in enumerate((a_ref, b_ref)):
        for pair in range(N // 2):
            blocks = []
            for s in slots[2 * pair : 2 * pair + 2]:
                source = pl.multiple_of(s * (2 * rows) + chunk * rows, 8)
                blocks.append(whole[pl.ds(source, rows), :])
            out[pl.ds(2 * pair * rows, 2 * rows), :] = jnp.concatenate(blocks).astype(BF)


def place_kernel(rows, *refs):
    *pieces, out_ref, whole = refs
    me = lax.axis_index("gx")
    blocks = iter(kept(me) + kept(me ^ 1))
    for piece in pieces:
        value = piece[...].astype(F32)
        for part in range(piece.shape[0] // rows):
            target = pl.multiple_of(scattered_slot(me, next(blocks)) * rows, 8)
            whole[pl.ds(target, rows), :] = value[part * rows : (part + 1) * rows]
    out_ref[...] = whole[...].astype(BF)


def pack_kernel(gate_ref, up_ref, out_ref, sems):
    copies = []
    for j in range(gate_ref.shape[1] // 128):
        for k, ref in enumerate((gate_ref, up_ref)):
            copies.append(
                pltpu.make_async_copy(
                    ref.at[:, pl.ds(128 * j, 128)], out_ref.at[:, pl.ds(256 * j + 128 * k, 128)], sems.at[2 * j + k]
                )
            )
    for copy in copies:
        copy.start()
    for copy in copies:
        copy.wait()


def pack(gate_weight, up_weight):
    width, units = gate_weight.shape
    return pl.pallas_call(
        pack_kernel,
        out_shape=jax.ShapeDtypeStruct((width, 2 * units), BF),
        in_specs=[pl.BlockSpec(memory_space=pl.ANY)] * 2,
        out_specs=pl.BlockSpec(memory_space=pltpu.VMEM),
        scratch_shapes=[pltpu.SemaphoreType.DMA((2 * units // 128,))],
        compiler_params=pltpu.CompilerParams(vmem_limit_bytes=16 * 2**20),
        cost_estimate=pl.CostEstimate(flops=0, bytes_accessed=8 * width * units, transcendentals=0),
        name="pack",
    )(gate_weight, up_weight)


def in_vmem(kernel, shapes, name, *values, scratch=(), limit=8):
    spec = pl.BlockSpec(memory_space=pltpu.VMEM)
    out = tuple(jax.ShapeDtypeStruct(shape, BF) for shape in shapes)
    result = pl.pallas_call(
        kernel,
        out_shape=out,
        in_specs=[spec] * len(values),
        out_specs=(spec,) * len(out),
        scratch_shapes=scratch,
        compiler_params=pltpu.CompilerParams(vmem_limit_bytes=limit * 2**20),
        name=name,
    )(*values)
    return result if len(out) > 1 else result[0]


def pick(pieces, rows):
    width = pieces[0].shape[1]
    return in_vmem(
        functools.partial(pick_kernel, rows),
        [(N * rows, width)] * 2,
        "pick",
        *pieces,
        scratch=[pltpu.VMEM((2 * N * rows, width), F32)],
        limit=16,
    )


def place(pieces, rows):
    shape = (N * rows, pieces[0].shape[1])
    return in_vmem(
        functools.partial(place_kernel, rows), [shape], "place", *pieces, scratch=[pltpu.VMEM(shape, F32)], limit=16
    )


def silu_kernel(a_ref, b_ref, out_ref):
    for j in range(out_ref.shape[1] // 128):
        gate = pl.ds(256 * j, 128)
        up = pl.ds(256 * j + 128, 128)
        g = a_ref[:, gate].astype(F32) + b_ref[:, gate].astype(F32)
        u = a_ref[:, up].astype(F32) + b_ref[:, up].astype(F32)
        out_ref[:, pl.ds(128 * j, 128)] = (g / (1.0 + jnp.exp(-g)) * u).astype(BF)


def silu(a, b):
    return in_vmem(silu_kernel, [(a.shape[0], a.shape[1] // 2)], "silu", a, b)


def join_kernel(*refs):
    first = 0
    for ref in refs[:-1]:
        refs[-1][pl.ds(first, ref.shape[0]), :] = ref[...]
        first += ref.shape[0]


def join(*values):
    return in_vmem(join_kernel, [(sum(v.shape[0] for v in values), values[0].shape[1])], "join", *values)


def add(a, b):
    return (a.astype(F32) + b.astype(F32)).astype(BF)


def dot(a, b):
    return jnp.dot(a, b, preferred_element_type=F32).astype(BF)


def tie(*values):
    return lax.optimization_barrier(values)


def gather_tokens(t, weight):
    t1, t2, t3 = (exchange(t, z=m) for m in (1, 2, 3))
    t1, t2, t3, weight = tie(t1, t2, t3, weight)
    h0, h1 = join(t, t1), join(t2, t3)
    p0, p1 = exchange(h0, masks_x=(1, 1)), exchange(h1, masks_x=(3, 3))
    q0, q1 = exchange(join(h0, p0), masks_x=(3, 3)), exchange(join(h1, p1), masks_x=(1, 1))
    return [h0, p0, q0, h1, p1, q1], weight


def chain(rows, down_weight):
    def halve(size, **how):
        def step(stays, got):
            v = add(stays, got)
            return v[: size * rows], v[size * rows :], how

        return step

    def first_hidden(stays, got):
        h = silu(stays, got)
        return h, h, dict(zhi=1)

    def double(**how):
        def step(stays, got):
            h = join(stays, got)
            return h, h, how

        return step

    def product(stays, got):
        s = dot(place([stays, got], rows), down_weight)
        return s[: 8 * rows], s[8 * rows :], dict(masks_x=SECOND)

    return [
        halve(4, masks_y=FIRST),
        halve(2, masks_y=SECOND),
        halve(1, zhi=1),
        first_hidden,
        double(masks_y=SECOND),
        double(masks_y=FIRST),
        double(core=1),
        product,
        halve(4, masks_x=FIRST),
    ]


def shards(tokens, gate_weight, up_weight, down_weight):
    rows = tokens.shape[0] // 2
    pieces, weight = gather_tokens(tokens, pack(gate_weight, up_weight))
    stays, got, sent = [None, None], [None, None], None
    for c, picked in enumerate(pick(pieces, rows)):
        s = dot(picked, weight)
        stays[c], sent = s[8 * rows :], s[: 8 * rows]
        got[c] = exchange(sent, core=1)
    for step in chain(rows, down_weight):
        for c in range(2):
            got[c], _ = tie(got[c], sent)
            stays[c], sent, how = step(stays[c], got[c])
            got[c] = exchange(sent, **how)
    mixed = []
    for c in range(2):
        v = add(stays[c], got[c])
        parts = [v[:rows]] + [exchange(v[m * rows : (m + 1) * rows], z=m) for m in (1, 2, 3)]
        mixed.append(functools.reduce(jnp.add, [p.astype(F32) for p in parts]).astype(BF))
    return jnp.concatenate(mixed)


def solution(mesh):
    in_specs = (P("gy", "gx"), P("gx", "gy"), P("gx", "gy"), P("gy", "gx"))
    out_specs = P("gy", "gx")
    return jax.shard_map(shards, mesh=mesh, in_specs=in_specs, out_specs=out_specs, check_vma=False)
```

time: 381 us -> 147 us (0.39)
  waiting for transfers between devices: 348 us -> 70.2 us
  starting transfers between devices: 0.12 us -> 57.8 us
  between operations: 13.2 us -> 0.41 us
  matrix products: 14.7 us -> 9.24 us
  local copies, waits for them, and re-layouts: 0.01 us -> 4.39 us
    reduce_scatter x2 -> x0, waiting for transfers between devices: 195 us -> none  [the longest x1 110 us: shards(): lax.psum_scatter(jnp.concatenate([gate_term, up_term], axis=1).astype(jnp...]
    all_gather x2 -> x0, waiting for transfers between devices: 153 us -> none  [the longest x1 89.2 us: shards(): whole = lax.all_gather(tokens, 'gy', axis=0, tiled=True)]
    ppermute x0 -> x33, waiting for transfers between devices: none -> 70.2 us  [exchange(): return lax.ppermute(value, ('gx', 'gy'), pairs)]
    ppermute x0 -> x33, starting transfers between devices: none -> 57.8 us  [exchange(): return lax.ppermute(value, ('gx', 'gy'), pairs)]
    dot_general x3 -> x4, matrix products: 14.7 us -> 9.24 us  [dot(): return jnp.dot(a, b, preferred_element_type=F32).astype(BF)]
    unnamed x6 -> x8, local copies, waits for them, and re-layouts: 0.01 us -> 3.93 us
  transfers between devices with their start and end apart: 4 -> 33, of which waited for: 4 -> 21; matrix products, arithmetic and copies ran while one was open for 0% -> 5% of each run, Pallas kernels for 0% -> 2%
where the time goes in v1:
time: 147 us
  waiting for transfers between devices  70.2 us (48%)
  starting transfers between devices  57.8 us (39%)
  matrix products  9.24 us (6%)
  local copies, waits for them, and re-layouts  4.39 us (3%)
  Pallas kernels  2.88 us (2%)
  other arithmetic  2.12 us (1%)
    ppermute x33, waiting for transfers between devices, exchange(): return lax.ppermute(value, ('gx', 'gy'), pairs)  70.2 us
    ppermute x33, starting transfers between devices, exchange(): return lax.ppermute(value, ('gx', 'gy'), pairs)  57.8 us
    dot_general x4, matrix products, dot(): return jnp.dot(a, b, preferred_element_type=F32).astype(BF)  9.24 us
    unnamed x8, local copies, waits for them, and re-layouts  3.93 us
  transfers between devices with their start and end apart: 33, of which 21 were waited for; matrix products, arithmetic and copies ran while one was open for 5% of the time, Pallas kernels for 2%

profile of v1, /device:TPU:24, one launch (start us, length us, event | category | flops | bytes accessed | tf_op | source)
XLA Modules:
  0.0 147.0 jit_solution(4717010978924613476)
XLA Ops:
  0.0 3.3 %collective-permute-start.1 = (bf16[48,1024]{1,0:T(8,128)(2,1)}, bf16[48,1024]{1,0:T(8,128)(2,1)S(1)}, u32[]{:S(2)}, u32[]{:S(2)}) collective-permute-start(bf16[48,1024]{1,0:T(8,128)(2,1)} %refs_0_.1), channel_id=1, source_target_pairs={{0,2},{1,3},{2,0},{3,1},{4,6},{5,7},{6,4},{7,5},{8,10},{9,11},{10,... | collective-permute-start | bytes 294920 | tf_op jit(solution)/shard_map/ppermute | solution.py:23
  3.3 1.9 %collective-permute-start = (bf16[48,1024]{1,0:T(8,128)(2,1)}, bf16[48,1024]{1,0:T(8,128)(2,1)S(1)}, u32[]{:S(2)}, u32[]{:S(2)}) collective-permute-start(bf16[48,1024]{1,0:T(8,128)(2,1)} %refs_0_.1), channel_id=1, source_target_pairs={{0,1},{1,0},{2,3},{3,2},{4,5},{5,4},{6,7},{7,6},{8,9},{9,8},{10,11... | collective-permute-start | bytes 294920 | tf_op jit(solution)/shard_map/ppermute | solution.py:23
  5.2 2.0 %copy-done.1 = bf16[1024,1664]{1,0:T(8,128)(2,1)S(1)} copy-done((bf16[1024,1664]{1,0:T(8,128)(2,1)S(1)}, bf16[1024,1664]{1,0:T(8,128)(2,1)}, u32[]{:S(2)}) %copy-start.1) | copy-done | bytes 3407896
  7.2 2.0 %copy-done.2 = bf16[1024,1664]{1,0:T(8,128)(2,1)S(1)} copy-done((bf16[1024,1664]{1,0:T(8,128)(2,1)S(1)}, bf16[1024,1664]{1,0:T(8,128)(2,1)}, u32[]{:S(2)}) %copy-start.2) | copy-done | bytes 3407896
  9.1 1.5 pack.1
  10.6 1.4 collective-permute-done.2.refs_1_
  12.0 2.8 %collective-permute-start.5 = (bf16[96,1024]{1,0:T(8,128)(2,1)S(1)}, bf16[96,1024]{1,0:T(8,128)(2,1)S(1)}, u32[]{:S(2)}, u32[]{:S(2)}) collective-permute-start(bf16[96,1024]{1,0:T(8,128)(2,1)S(1)} %join.12.refs_0_.refs_3_), channel_id=1, source_target_pairs={{0,12},{1,13},{2,14},{3,15},{4,8},{5,9},{6,10},{7,11},{8,4},{9,5},... | collective-permute-start | bytes 589832 | tf_op jit(solution)/shard_map/ppermute | solution.py:23
  15.2 3.8 %collective-permute-done.5.refs_1_.refs_4_ = bf16[96,1024]{1,0:T(8,128)(2,1)S(1)} collective-permute-done((bf16[96,1024]{1,0:T(8,128)(2,1)S(1)}, bf16[96,1024]{1,0:T(8,128)(2,1)S(1)}, u32[]{:S(2)}, u32[]{:S(2)}) %collective-permute-start.5) | collective-permute-done | bytes 196640 | tf_op jit(solution)/shard_map/ppermute | solution.py:23
  19.4 2.6 %collective-permute-done.3.refs_1_ = bf16[96,1024]{1,0:T(8,128)(2,1)S(1)} collective-permute-done((bf16[96,1024]{1,0:T(8,128)(2,1)S(1)}, bf16[96,1024]{1,0:T(8,128)(2,1)S(1)}, u32[]{:S(2)}, u32[]{:S(2)}) %collective-permute-start.3) | collective-permute-done | bytes 196640 | tf_op jit(solution)/shard_map/ppermute | solution.py:23
  22.1 6.9 %collective-permute-done.6.refs_5_ = bf16[192,1024]{1,0:T(8,128)(2,1)S(1)} collective-permute-done((bf16[192,1024]{1,0:T(8,128)(2,1)S(1)}, bf16[192,1024]{1,0:T(8,128)(2,1)S(1)}, u32[]{:S(2)}, u32[]{:S(2)}) %collective-permute-start.6) | collective-permute-done | bytes 393248 | tf_op jit(solution)/shard_map/ppermute | solution.py:23
  29.1 2.0 %collective-permute-done.4.refs_2_ = bf16[192,1024]{1,0:T(8,128)(2,1)S(1)} collective-permute-done((bf16[192,1024]{1,0:T(8,128)(2,1)S(1)}, bf16[192,1024]{1,0:T(8,128)(2,1)S(1)}, u32[]{:S(2)}, u32[]{:S(2)}) %collective-permute-start.4) | collective-permute-done | bytes 393248 | tf_op jit(solution)/shard_map/ppermute | solution.py:23
  31.5 3.0 %convolution_convert_fusion.1 = bf16[384,3328]{1,0:T(8,128)(2,1)S(1)} fusion(bf16[384,1024]{1,0:T(8,128)(2,1)S(1)} %get-tuple-element.32, bf16[1024,3328]{1,0:T(8,128)(2,1)S(1)} %pack.1), kind=kOutput, calls=%fused_computation.1 | convolution fusion | flops 2618523648 | bytes 10158080 | tf_op jit(solution)/shard_map/dot_general | solution.py:167
  34.7 3.0 %convolution_convert_fusion = bf16[384,3328]{1,0:T(8,128)(2,1)S(1)} fusion(bf16[384,1024]{1,0:T(8,128)(2,1)S(1)} %get-tuple-element.34, bf16[1024,3328]{1,0:T(8,128)(2,1)S(1)} %pack.1), kind=kOutput, calls=%fused_computation | convolution fusion | flops 2618523648 | bytes 10158080 | tf_op jit(solution)/shard_map/dot_general | solution.py:167
  37.8 0.6 collective-permute-start.9
  38.7 0.8 collective-permute-start.8
  39.6 1.4 collective-permute-done.9
  41.4 0.8 collective-permute-start.11
  42.2 7.0 %collective-permute-done.8 = bf16[96,3328]{1,0:T(8,128)(2,1)S(1)} collective-permute-done((bf16[96,3328]{1,0:T(8,128)(2,1)S(1)}, bf16[96,3328]{1,0:T(8,128)(2,1)S(1)}, u32[]{:S(2)}, u32[]{:S(2)}) %collective-permute-start.8) | collective-permute-done | bytes 639008 | tf_op jit(solution)/shard_map/ppermute | solution.py:23
  49.4 0.5 collective-permute-start.10
  50.0 9.5 %collective-permute-done.11 = bf16[96,3328]{1,0:T(8,128)(2,1)S(1)} collective-permute-done((bf16[96,3328]{1,0:T(8,128)(2,1)S(1)}, bf16[96,3328]{1,0:T(8,128)(2,1)S(1)}, u32[]{:S(2)}, u32[]{:S(2)}) %collective-permute-start.11) | collective-permute-done | bytes 639008 | tf_op jit(solution)/shard_map/ppermute | solution.py:23
  60.2 5.8 %collective-permute-start.12 = (bf16[24,3328]{1,0:T(8,128)(2,1)S(1)}, bf16[24,3328]{1,0:T(8,128)(2,1)S(1)}, u32[]{:S(2)}, u32[]{:S(2)}) collective-permute-start(bf16[24,3328]{1,0:T(8,128)(2,1)S(1)} %get-tuple-element.54), channel_id=1, source_target_pairs={{0,128},{1,129},{2,130},{3,131},{4,132},{5,133},{6,134},{7,135},{8... | collective-permute-start | bytes 479240 | tf_op jit(solution)/shard_map/ppermute | solution.py:23
  66.0 2.0 %collective-permute-done.13 = bf16[48,3328]{1,0:T(8,128)(2,1)S(1)} collective-permute-done((bf16[48,3328]{1,0:T(8,128)(2,1)S(1)}, bf16[48,3328]{1,0:T(8,128)(2,1)S(1)}, u32[]{:S(2)}, u32[]{:S(2)}) %collective-permute-start.13) | collective-permute-done | bytes 319520 | tf_op jit(solution)/shard_map/ppermute | solution.py:23
  68.1 5.9 %collective-permute-start.15 = (bf16[24,3328]{1,0:T(8,128)(2,1)S(1)}, bf16[24,3328]{1,0:T(8,128)(2,1)S(1)}, u32[]{:S(2)}, u32[]{:S(2)}) collective-permute-start(bf16[24,3328]{1,0:T(8,128)(2,1)S(1)} %get-tuple-element.55), channel_id=1, source_target_pairs={{0,128},{1,129},{2,130},{3,131},{4,132},{5,133},{6,134},{7,135},{8... | collective-permute-start | bytes 479240 | tf_op jit(solution)/shard_map/ppermute | solution.py:23
  74.0 3.9 %collective-permute-start.14 = (bf16[24,1664]{1,0:T(8,128)(2,1)S(1)}, bf16[24,1664]{1,0:T(8,128)(2,1)S(1)}, u32[]{:S(2)}, u32[]{:S(2)}) collective-permute-start(bf16[24,1664]{1,0:T(8,128)(2,1)S(1)} %silu.2.refs_0_), channel_id=1, source_target_pairs={{0,128},{1,129},{2,130},{3,131},{4,132},{5,133},{6,134},{7,135},{8... | collective-permute-start | bytes 239624 | tf_op jit(solution)/shard_map/ppermute | solution.py:23
  77.9 4.4 %collective-permute-done.15.b_ref = bf16[24,3328]{1,0:T(8,128)(2,1)S(1)} collective-permute-done((bf16[24,3328]{1,0:T(8,128)(2,1)S(1)}, bf16[24,3328]{1,0:T(8,128)(2,1)S(1)}, u32[]{:S(2)}, u32[]{:S(2)}) %collective-permute-start.15) | collective-permute-done | bytes 159776 | tf_op jit(solution)/shard_map/ppermute | solution.py:23
  82.4 0.8 collective-permute-done.14.refs_1_
  83.3 6.1 %collective-permute-start.17 = (bf16[24,1664]{1,0:T(8,128)(2,1)S(1)}, bf16[24,1664]{1,0:T(8,128)(2,1)S(1)}, u32[]{:S(2)}, u32[]{:S(2)}) collective-permute-start(bf16[24,1664]{1,0:T(8,128)(2,1)S(1)} %silu.3.refs_0_), channel_id=1, source_target_pairs={{0,128},{1,129},{2,130},{3,131},{4,132},{5,133},{6,134},{7,135},{8... | collective-permute-start | bytes 239624 | tf_op jit(solution)/shard_map/ppermute | solution.py:23
  89.4 2.8 %collective-permute-done.17.refs_1_ = bf16[24,1664]{1,0:T(8,128)(2,1)S(1)} collective-permute-done((bf16[24,1664]{1,0:T(8,128)(2,1)S(1)}, bf16[24,1664]{1,0:T(8,128)(2,1)S(1)}, u32[]{:S(2)}, u32[]{:S(2)}) %collective-permute-start.17) | collective-permute-done | bytes 79904 | tf_op jit(solution)/shard_map/ppermute | solution.py:23
  92.4 3.6 %collective-permute-start.19 = (bf16[48,1664]{1,0:T(8,128)(2,1)S(1)}, bf16[48,1664]{1,0:T(8,128)(2,1)S(1)}, u32[]{:S(2)}, u32[]{:S(2)}) collective-permute-start(bf16[48,1664]{1,0:T(8,128)(2,1)S(1)} %join.15.refs_0_), channel_id=1, source_target_pairs={{0,96},{1,97},{2,98},{3,99},{4,100},{5,101},{6,102},{7,103},{8,104... | collective-permute-start | bytes 479240 | tf_op jit(solution)/shard_map/ppermute | solution.py:23
  96.0 3.3 %collective-permute-done.19.refs_1_ = bf16[48,1664]{1,0:T(8,128)(2,1)S(1)} collective-permute-done((bf16[48,1664]{1,0:T(8,128)(2,1)S(1)}, bf16[48,1664]{1,0:T(8,128)(2,1)S(1)}, u32[]{:S(2)}, u32[]{:S(2)}) %collective-permute-start.19) | collective-permute-done | bytes 159776 | tf_op jit(solution)/shard_map/ppermute | solution.py:23
  99.5 1.3 collective-permute-start.21
  100.8 5.8 %collective-permute-done.21.refs_1_ = bf16[96,1664]{1,0:T(8,128)(2,1)S(1)} collective-permute-done((bf16[96,1664]{1,0:T(8,128)(2,1)S(1)}, bf16[96,1664]{1,0:T(8,128)(2,1)S(1)}, u32[]{:S(2)}, u32[]{:S(2)}) %collective-permute-start.21) | collective-permute-done | bytes 319520 | tf_op jit(solution)/shard_map/ppermute | solution.py:23
  106.6 1.1 collective-permute-start.23
  108.1 1.6 %convolution_convert_fusion.3 = bf16[384,1024]{1,0:T(8,128)(2,1)S(1)} fusion(bf16[384,1664]{1,0:T(8,128)(2,1)S(1)} %place.2, bf16[1664,1024]{1,0:T(8,128)(2,1)S(1)} %copy-done), kind=kOutput, calls=%fused_computation.5 | convolution fusion | flops 1309016064 | bytes 5472256 | tf_op jit(solution)/shard_map/dot_general | solution.py:167
  110.2 1.6 %convolution_convert_fusion.2 = bf16[384,1024]{1,0:T(8,128)(2,1)S(1)} fusion(bf16[384,1664]{1,0:T(8,128)(2,1)S(1)} %place.3, bf16[1664,1024]{1,0:T(8,128)(2,1)S(1)} %copy-done), kind=kOutput, calls=%fused_computation.4 | convolution fusion | flops 1309016064 | bytes 5472256 | tf_op jit(solution)/shard_map/dot_general | solution.py:167
  111.8 3.3 %collective-permute-start.28 = (bf16[192,1024]{1,0:T(8,128)(2,1)S(1)}, bf16[192,1024]{1,0:T(8,128)(2,1)S(1)}, u32[]{:S(2)}, u32[]{:S(2)}) collective-permute-start(bf16[192,1024]{1,0:T(8,128)(2,1)S(1)} %slice.146), channel_id=1, source_target_pairs={{0,12},{1,13},{2,14},{3,15},{4,8},{5,9},{6,10},{7,11},{8,4},{9,5},... | collective-permute-start | bytes 1179656 | tf_op jit(solution)/shard_map/ppermute | solution.py:23
  115.1 3.7 %collective-permute-done.22 = bf16[192,1024]{1,0:T(8,128)(2,1)S(1)} collective-permute-done((bf16[192,1024]{1,0:T(8,128)(2,1)S(1)}, bf16[192,1024]{1,0:T(8,128)(2,1)S(1)}, u32[]{:S(2)}, u32[]{:S(2)}) %collective-permute-start.22) | collective-permute-done | bytes 393248 | tf_op jit(solution)/shard_map/ppermute | solution.py:23
  119.0 4.1 %collective-permute-done.28 = bf16[192,1024]{1,0:T(8,128)(2,1)S(1)} collective-permute-done((bf16[192,1024]{1,0:T(8,128)(2,1)S(1)}, bf16[192,1024]{1,0:T(8,128)(2,1)S(1)}, u32[]{:S(2)}, u32[]{:S(2)}) %collective-permute-start.28) | collective-permute-done | bytes 393248 | tf_op jit(solution)/shard_map/ppermute | solution.py:23
  123.3 2.0 %collective-permute-start.24 = (bf16[96,1024]{1,0:T(8,128)(2,1)S(1)}, bf16[96,1024]{1,0:T(8,128)(2,1)S(1)}, u32[]{:S(2)}, u32[]{:S(2)}) collective-permute-start(bf16[96,1024]{1,0:T(8,128)(2,1)S(1)} %slice.148), channel_id=1, source_target_pairs={{0,4},{1,5},{2,6},{3,7},{4,0},{5,1},{6,2},{7,3},{8,12},{9,13},{10,... | collective-permute-start | bytes 589832 | tf_op jit(solution)/shard_map/ppermute | solution.py:23
  125.3 3.6 %collective-permute-done.29 = bf16[96,1024]{1,0:T(8,128)(2,1)S(1)} collective-permute-done((bf16[96,1024]{1,0:T(8,128)(2,1)S(1)}, bf16[96,1024]{1,0:T(8,128)(2,1)S(1)}, u32[]{:S(2)}, u32[]{:S(2)}) %collective-permute-start.29) | collective-permute-done | bytes 196640 | tf_op jit(solution)/shard_map/ppermute | solution.py:23
  129.0 5.4 %collective-permute-start.30 = (bf16[24,1024]{1,0:T(8,128)(2,1)S(1)}, bf16[24,1024]{1,0:T(8,128)(2,1)S(1)}, u32[]{:S(2)}, u32[]{:S(2)}) collective-permute-start(bf16[24,1024]{1,0:T(8,128)(2,1)S(1)} %get-tuple-element.60), channel_id=1, source_target_pairs={{0,1},{1,0},{2,3},{3,2},{4,5},{5,4},{6,7},{7,6},{8,9},{9,8},{10,11... | collective-permute-start | bytes 147464 | tf_op jit(solution)/shard_map/ppermute | solution.py:23
  134.4 2.4 %collective-permute-start.32 = (bf16[24,1024]{1,0:T(8,128)(2,1)S(1)}, bf16[24,1024]{1,0:T(8,128)(2,1)S(1)}, u32[]{:S(2)}, u32[]{:S(2)}) collective-permute-start(bf16[24,1024]{1,0:T(8,128)(2,1)S(1)} %get-tuple-element.61), channel_id=1, source_target_pairs={{0,3},{1,2},{2,1},{3,0},{4,7},{5,6},{6,5},{7,4},{8,11},{9,10},{10,... | collective-permute-start | bytes 147464 | tf_op jit(solution)/shard_map/ppermute | solution.py:23
  136.9 2.1 %collective-permute-start.25 = (bf16[24,1024]{1,0:T(8,128)(2,1)S(1)}, bf16[24,1024]{1,0:T(8,128)(2,1)S(1)}, u32[]{:S(2)}, u32[]{:S(2)}) collective-permute-start(bf16[24,1024]{1,0:T(8,128)(2,1)S(1)} %get-tuple-element.57), channel_id=1, source_target_pairs={{0,1},{1,0},{2,3},{3,2},{4,5},{5,4},{6,7},{7,6},{8,9},{9,8},{10,11... | collective-permute-start | bytes 147464 | tf_op jit(solution)/shard_map/ppermute | solution.py:23
  139.0 2.4 %collective-permute-start.27 = (bf16[24,1024]{1,0:T(8,128)(2,1)S(1)}, bf16[24,1024]{1,0:T(8,128)(2,1)S(1)}, u32[]{:S(2)}, u32[]{:S(2)}) collective-permute-start(bf16[24,1024]{1,0:T(8,128)(2,1)S(1)} %get-tuple-element.58), channel_id=1, source_target_pairs={{0,3},{1,2},{2,1},{3,0},{4,7},{5,6},{6,5},{7,4},{8,11},{9,10},{10,... | collective-permute-start | bytes 147464 | tf_op jit(solution)/shard_map/ppermute | solution.py:23
  141.4 1.6 %collective-permute-done.31 = bf16[24,1024]{1,0:T(8,128)(2,1)S(1)} collective-permute-done((bf16[24,1024]{1,0:T(8,128)(2,1)S(1)}, bf16[24,1024]{1,0:T(8,128)(2,1)S(1)}, u32[]{:S(2)}, u32[]{:S(2)}) %collective-permute-start.31) | collective-permute-done | bytes 49184 | tf_op jit(solution)/shard_map/ppermute | solution.py:23
  143.0 1.9 %collective-permute-done.27 = bf16[24,1024]{1,0:T(8,128)(2,1)S(1)} collective-permute-done((bf16[24,1024]{1,0:T(8,128)(2,1)S(1)}, bf16[24,1024]{1,0:T(8,128)(2,1)S(1)}, u32[]{:S(2)}, u32[]{:S(2)}) %collective-permute-start.27) | collective-permute-done | bytes 49184 | tf_op jit(solution)/shard_map/ppermute | solution.py:23
  144.9 1.5 %collective-permute-done.26 = bf16[24,1024]{1,0:T(8,128)(2,1)S(1)} collective-permute-done((bf16[24,1024]{1,0:T(8,128)(2,1)S(1)}, bf16[24,1024]{1,0:T(8,128)(2,1)S(1)}, u32[]{:S(2)}, u32[]{:S(2)}) %collective-permute-start.26) | collective-permute-done | bytes 49184 | tf_op jit(solution)/shard_map/ppermute | solution.py:23
  146.4 0.6 pad_maximum_fusion
  (73 shorter events, 5.2 us)
Async XLA Ops:
  0.0 108.1 %copy-start = (bf16[1664,1024]{1,0:T(8,128)(2,1)S(1)}, bf16[1664,1024]{1,0:T(8,128)(2,1)}, u32[]{:S(2)}) copy-start(bf16[1664,1024]{1,0:T(8,128)(2,1)} %param.7) | copy-start | bytes 10223620
  0.0 10.6 %collective-permute-start.1 = (bf16[48,1024]{1,0:T(8,128)(2,1)}, bf16[48,1024]{1,0:T(8,128)(2,1)S(1)}, u32[]{:S(2)}, u32[]{:S(2)}) collective-permute-start(bf16[48,1024]{1,0:T(8,128)(2,1)} %refs_0_.1), channel_id=1, source_target_pairs={{0,2},{1,3},{2,0},{3,1},{4,6},{5,7},{6,4},{7,5},{8,10},{9,11},{10,... | collective-permute-start | bytes 294920 | tf_op jit(solution)/shard_map/ppermute | solution.py:23
  3.3 7.3 %collective-permute-start = (bf16[48,1024]{1,0:T(8,128)(2,1)}, bf16[48,1024]{1,0:T(8,128)(2,1)S(1)}, u32[]{:S(2)}, u32[]{:S(2)}) collective-permute-start(bf16[48,1024]{1,0:T(8,128)(2,1)} %refs_0_.1), channel_id=1, source_target_pairs={{0,1},{1,0},{2,3},{3,2},{4,5},{5,4},{6,7},{7,6},{8,9},{9,8},{10,11... | collective-permute-start | bytes 294920 | tf_op jit(solution)/shard_map/ppermute | solution.py:23
  5.2 6.8 %collective-permute-start.2 = (bf16[48,1024]{1,0:T(8,128)(2,1)}, bf16[48,1024]{1,0:T(8,128)(2,1)S(1)}, u32[]{:S(2)}, u32[]{:S(2)}) collective-permute-start(bf16[48,1024]{1,0:T(8,128)(2,1)} %refs_0_.1), channel_id=1, source_target_pairs={{0,3},{1,2},{2,1},{3,0},{4,7},{5,6},{6,5},{7,4},{8,11},{9,10},{10,... | collective-permute-start | bytes 294920 | tf_op jit(solution)/shard_map/ppermute | solution.py:23
  5.2 2.0 %copy-start.1 = (bf16[1024,1664]{1,0:T(8,128)(2,1)S(1)}, bf16[1024,1664]{1,0:T(8,128)(2,1)}, u32[]{:S(2)}) copy-start(bf16[1024,1664]{1,0:T(8,128)(2,1)} %gate_ref.1) | copy-start | bytes 10223620
  7.2 2.0 %copy-start.2 = (bf16[1024,1664]{1,0:T(8,128)(2,1)S(1)}, bf16[1024,1664]{1,0:T(8,128)(2,1)}, u32[]{:S(2)}) copy-start(bf16[1024,1664]{1,0:T(8,128)(2,1)} %up_ref.1) | copy-start | bytes 10223620
  9.1 5.7 %copy-start.3 = (bf16[48,1024]{1,0:T(8,128)(2,1)S(1)}, bf16[48,1024]{1,0:T(8,128)(2,1)}, u32[]{:S(2)}) copy-start(bf16[48,1024]{1,0:T(8,128)(2,1)} %refs_0_.1) | copy-start | bytes 294916
  12.0 7.0 %collective-permute-start.5 = (bf16[96,1024]{1,0:T(8,128)(2,1)S(1)}, bf16[96,1024]{1,0:T(8,128)(2,1)S(1)}, u32[]{:S(2)}, u32[]{:S(2)}) collective-permute-start(bf16[96,1024]{1,0:T(8,128)(2,1)S(1)} %join.12.refs_0_.refs_3_), channel_id=1, source_target_pairs={{0,12},{1,13},{2,14},{3,15},{4,8},{5,9},{6,10},{7,11},{8,4},{9,5},... | collective-permute-start | bytes 589832 | tf_op jit(solution)/shard_map/ppermute | solution.py:23
  14.9 7.1 %collective-permute-start.3 = (bf16[96,1024]{1,0:T(8,128)(2,1)S(1)}, bf16[96,1024]{1,0:T(8,128)(2,1)S(1)}, u32[]{:S(2)}, u32[]{:S(2)}) collective-permute-start(bf16[96,1024]{1,0:T(8,128)(2,1)S(1)} %join.10.refs_0_), channel_id=1, source_target_pairs={{0,4},{1,5},{2,6},{3,7},{4,0},{5,1},{6,2},{7,3},{8,12},{9,13},{10,... | collective-permute-start | bytes 589832 | tf_op jit(solution)/shard_map/ppermute | solution.py:23
  19.0 10.1 %collective-permute-start.6 = (bf16[192,1024]{1,0:T(8,128)(2,1)S(1)}, bf16[192,1024]{1,0:T(8,128)(2,1)S(1)}, u32[]{:S(2)}, u32[]{:S(2)}) collective-permute-start(bf16[192,1024]{1,0:T(8,128)(2,1)S(1)} %join.13), channel_id=1, source_target_pairs={{0,4},{1,5},{2,6},{3,7},{4,0},{5,1},{6,2},{7,3},{8,12},{9,13},{10,... | collective-permute-start | bytes 1179656 | tf_op jit(solution)/shard_map/ppermute | solution.py:23
  22.0 9.1 %collective-permute-start.4 = (bf16[192,1024]{1,0:T(8,128)(2,1)S(1)}, bf16[192,1024]{1,0:T(8,128)(2,1)S(1)}, u32[]{:S(2)}, u32[]{:S(2)}) collective-permute-start(bf16[192,1024]{1,0:T(8,128)(2,1)S(1)} %join.11), channel_id=1, source_target_pairs={{0,12},{1,13},{2,14},{3,15},{4,8},{5,9},{6,10},{7,11},{8,4},{9,5},... | collective-permute-start | bytes 1179656 | tf_op jit(solution)/shard_map/ppermute | solution.py:23
  34.6 3.8 %collective-permute-start.7 = (bf16[192,3328]{1,0:T(8,128)(2,1)S(1)}, bf16[192,3328]{1,0:T(8,128)(2,1)S(1)}, u32[]{:S(2)}, u32[]{:S(2)}) collective-permute-start(bf16[192,3328]{1,0:T(8,128)(2,1)S(1)} %slice.129), channel_id=1, source_target_pairs={{0,16},{1,17},{2,18},{3,19},{4,20},{5,21},{6,22},{7,23},{8,24},{9,... | collective-permute-start | bytes 3833864 | tf_op jit(solution)/shard_map/ppermute | solution.py:23
  37.8 3.2 %collective-permute-start.9 = (bf16[192,3328]{1,0:T(8,128)(2,1)S(1)}, bf16[192,3328]{1,0:T(8,128)(2,1)S(1)}, u32[]{:S(2)}, u32[]{:S(2)}) collective-permute-start(bf16[192,3328]{1,0:T(8,128)(2,1)S(1)} %slice.130), channel_id=1, source_target_pairs={{0,16},{1,17},{2,18},{3,19},{4,20},{5,21},{6,22},{7,23},{8,24},{9,... | collective-permute-start | bytes 3833864 | tf_op jit(solution)/shard_map/ppermute | solution.py:23
  38.7 10.5 %collective-permute-start.8 = (bf16[96,3328]{1,0:T(8,128)(2,1)S(1)}, bf16[96,3328]{1,0:T(8,128)(2,1)S(1)}, u32[]{:S(2)}, u32[]{:S(2)}) collective-permute-start(bf16[96,3328]{1,0:T(8,128)(2,1)S(1)} %slice.132), channel_id=1, source_target_pairs={{0,32},{1,33},{2,34},{3,35},{4,36},{5,37},{6,38},{7,39},{8,40},{9,... | collective-permute-start | bytes 1916936 | tf_op jit(solution)/shard_map/ppermute | solution.py:23
  41.4 18.1 %collective-permute-start.11 = (bf16[96,3328]{1,0:T(8,128)(2,1)S(1)}, bf16[96,3328]{1,0:T(8,128)(2,1)S(1)}, u32[]{:S(2)}, u32[]{:S(2)}) collective-permute-start(bf16[96,3328]{1,0:T(8,128)(2,1)S(1)} %slice.134), channel_id=1, source_target_pairs={{0,32},{1,33},{2,34},{3,35},{4,36},{5,37},{6,38},{7,39},{8,40},{9,... | collective-permute-start | bytes 1916936 | tf_op jit(solution)/shard_map/ppermute | solution.py:23
  49.4 10.6 %collective-permute-start.10 = (bf16[48,3328]{1,0:T(8,128)(2,1)S(1)}, bf16[48,3328]{1,0:T(8,128)(2,1)S(1)}, u32[]{:S(2)}, u32[]{:S(2)}) collective-permute-start(bf16[48,3328]{1,0:T(8,128)(2,1)S(1)} %slice.136), channel_id=1, source_target_pairs={{0,96},{1,97},{2,98},{3,99},{4,100},{5,101},{6,102},{7,103},{8,104... | collective-permute-start | bytes 958472 | tf_op jit(solution)/shard_map/ppermute | solution.py:23
  59.7 8.3 %collective-permute-start.13 = (bf16[48,3328]{1,0:T(8,128)(2,1)S(1)}, bf16[48,3328]{1,0:T(8,128)(2,1)S(1)}, u32[]{:S(2)}, u32[]{:S(2)}) collective-permute-start(bf16[48,3328]{1,0:T(8,128)(2,1)S(1)} %slice.138), channel_id=1, source_target_pairs={{0,96},{1,97},{2,98},{3,99},{4,100},{5,101},{6,102},{7,103},{8,104... | collective-permute-start | bytes 958472 | tf_op jit(solution)/shard_map/ppermute | solution.py:23
  60.2 13.8 %collective-permute-start.12 = (bf16[24,3328]{1,0:T(8,128)(2,1)S(1)}, bf16[24,3328]{1,0:T(8,128)(2,1)S(1)}, u32[]{:S(2)}, u32[]{:S(2)}) collective-permute-start(bf16[24,3328]{1,0:T(8,128)(2,1)S(1)} %get-tuple-element.54), channel_id=1, source_target_pairs={{0,128},{1,129},{2,130},{3,131},{4,132},{5,133},{6,134},{7,135},{8... | collective-permute-start | bytes 479240 | tf_op jit(solution)/shard_map/ppermute | solution.py:23
  68.1 14.3 %collective-permute-start.15 = (bf16[24,3328]{1,0:T(8,128)(2,1)S(1)}, bf16[24,3328]{1,0:T(8,128)(2,1)S(1)}, u32[]{:S(2)}, u32[]{:S(2)}) collective-permute-start(bf16[24,3328]{1,0:T(8,128)(2,1)S(1)} %get-tuple-element.55), channel_id=1, source_target_pairs={{0,128},{1,129},{2,130},{3,131},{4,132},{5,133},{6,134},{7,135},{8... | collective-permute-start | bytes 479240 | tf_op jit(solution)/shard_map/ppermute | solution.py:23
  74.0 9.2 %collective-permute-start.14 = (bf16[24,1664]{1,0:T(8,128)(2,1)S(1)}, bf16[24,1664]{1,0:T(8,128)(2,1)S(1)}, u32[]{:S(2)}, u32[]{:S(2)}) collective-permute-start(bf16[24,1664]{1,0:T(8,128)(2,1)S(1)} %silu.2.refs_0_), channel_id=1, source_target_pairs={{0,128},{1,129},{2,130},{3,131},{4,132},{5,133},{6,134},{7,135},{8... | collective-permute-start | bytes 239624 | tf_op jit(solution)/shard_map/ppermute | solution.py:23
  83.2 9.0 %collective-permute-start.16 = (bf16[48,1664]{1,0:T(8,128)(2,1)S(1)}, bf16[48,1664]{1,0:T(8,128)(2,1)S(1)}, u32[]{:S(2)}, u32[]{:S(2)}) collective-permute-start(bf16[48,1664]{1,0:T(8,128)(2,1)S(1)} %join.14.refs_0_), channel_id=1, source_target_pairs={{0,96},{1,97},{2,98},{3,99},{4,100},{5,101},{6,102},{7,103},{8,104... | collective-permute-start | bytes 479240 | tf_op jit(solution)/shard_map/ppermute | solution.py:23
  83.3 8.9 %collective-permute-start.17 = (bf16[24,1664]{1,0:T(8,128)(2,1)S(1)}, bf16[24,1664]{1,0:T(8,128)(2,1)S(1)}, u32[]{:S(2)}, u32[]{:S(2)}) collective-permute-start(bf16[24,1664]{1,0:T(8,128)(2,1)S(1)} %silu.3.refs_0_), channel_id=1, source_target_pairs={{0,128},{1,129},{2,130},{3,131},{4,132},{5,133},{6,134},{7,135},{8... | collective-permute-start | bytes 239624 | tf_op jit(solution)/shard_map/ppermute | solution.py:23
  92.3 7.1 %collective-permute-start.18 = (bf16[96,1664]{1,0:T(8,128)(2,1)S(1)}, bf16[96,1664]{1,0:T(8,128)(2,1)S(1)}, u32[]{:S(2)}, u32[]{:S(2)}) collective-permute-start(bf16[96,1664]{1,0:T(8,128)(2,1)S(1)} %join.16.refs_0_), channel_id=1, source_target_pairs={{0,32},{1,33},{2,34},{3,35},{4,36},{5,37},{6,38},{7,39},{8,40},{9,... | collective-permute-start | bytes 958472 | tf_op jit(solution)/shard_map/ppermute | solution.py:23
  92.4 6.8 %collective-permute-start.19 = (bf16[48,1664]{1,0:T(8,128)(2,1)S(1)}, bf16[48,1664]{1,0:T(8,128)(2,1)S(1)}, u32[]{:S(2)}, u32[]{:S(2)}) collective-permute-start(bf16[48,1664]{1,0:T(8,128)(2,1)S(1)} %join.15.refs_0_), channel_id=1, source_target_pairs={{0,96},{1,97},{2,98},{3,99},{4,100},{5,101},{6,102},{7,103},{8,104... | collective-permute-start | bytes 479240 | tf_op jit(solution)/shard_map/ppermute | solution.py:23
  99.4 8.3 %collective-permute-start.20 = (bf16[192,1664]{1,0:T(8,128)(2,1)S(1)}, bf16[192,1664]{1,0:T(8,128)(2,1)S(1)}, u32[]{:S(2)}, u32[]{:S(2)}) collective-permute-start(bf16[192,1664]{1,0:T(8,128)(2,1)S(1)} %join.18.refs_0_), channel_id=1, source_target_pairs={{0,16},{1,17},{2,18},{3,19},{4,20},{5,21},{6,22},{7,23},{8,24},{9,... | collective-permute-start | bytes 1916936 | tf_op jit(solution)/shard_map/ppermute | solution.py:23
  99.5 7.1 %collective-permute-start.21 = (bf16[96,1664]{1,0:T(8,128)(2,1)S(1)}, bf16[96,1664]{1,0:T(8,128)(2,1)S(1)}, u32[]{:S(2)}, u32[]{:S(2)}) collective-permute-start(bf16[96,1664]{1,0:T(8,128)(2,1)S(1)} %join.17.refs_0_), channel_id=1, source_target_pairs={{0,32},{1,33},{2,34},{3,35},{4,36},{5,37},{6,38},{7,39},{8,40},{9,... | collective-permute-start | bytes 958472 | tf_op jit(solution)/shard_map/ppermute | solution.py:23
  106.6 3.2 %collective-permute-start.23 = (bf16[192,1664]{1,0:T(8,128)(2,1)S(1)}, bf16[192,1664]{1,0:T(8,128)(2,1)S(1)}, u32[]{:S(2)}, u32[]{:S(2)}) collective-permute-start(bf16[192,1664]{1,0:T(8,128)(2,1)S(1)} %join.19.refs_0_), channel_id=1, source_target_pairs={{0,16},{1,17},{2,18},{3,19},{4,20},{5,21},{6,22},{7,23},{8,24},{9,... | collective-permute-start | bytes 1916936 | tf_op jit(solution)/shard_map/ppermute | solution.py:23
  109.7 9.1 %collective-permute-start.22 = (bf16[192,1024]{1,0:T(8,128)(2,1)S(1)}, bf16[192,1024]{1,0:T(8,128)(2,1)S(1)}, u32[]{:S(2)}, u32[]{:S(2)}) collective-permute-start(bf16[192,1024]{1,0:T(8,128)(2,1)S(1)} %slice.145), channel_id=1, source_target_pairs={{0,12},{1,13},{2,14},{3,15},{4,8},{5,9},{6,10},{7,11},{8,4},{9,5},... | collective-permute-start | bytes 1179656 | tf_op jit(solution)/shard_map/ppermute | solution.py:23
  111.8 11.2 %collective-permute-start.28 = (bf16[192,1024]{1,0:T(8,128)(2,1)S(1)}, bf16[192,1024]{1,0:T(8,128)(2,1)S(1)}, u32[]{:S(2)}, u32[]{:S(2)}) collective-permute-start(bf16[192,1024]{1,0:T(8,128)(2,1)S(1)} %slice.146), channel_id=1, source_target_pairs={{0,12},{1,13},{2,14},{3,15},{4,8},{5,9},{6,10},{7,11},{8,4},{9,5},... | collective-permute-start | bytes 1179656 | tf_op jit(solution)/shard_map/ppermute | solution.py:23
  123.2 5.8 %collective-permute-start.29 = (bf16[96,1024]{1,0:T(8,128)(2,1)S(1)}, bf16[96,1024]{1,0:T(8,128)(2,1)S(1)}, u32[]{:S(2)}, u32[]{:S(2)}) collective-permute-start(bf16[96,1024]{1,0:T(8,128)(2,1)S(1)} %slice.155), channel_id=1, source_target_pairs={{0,4},{1,5},{2,6},{3,7},{4,0},{5,1},{6,2},{7,3},{8,12},{9,13},{10,... | collective-permute-start | bytes 589832 | tf_op jit(solution)/shard_map/ppermute | solution.py:23
  123.3 13.6 %collective-permute-start.24 = (bf16[96,1024]{1,0:T(8,128)(2,1)S(1)}, bf16[96,1024]{1,0:T(8,128)(2,1)S(1)}, u32[]{:S(2)}, u32[]{:S(2)}) collective-permute-start(bf16[96,1024]{1,0:T(8,128)(2,1)S(1)} %slice.148), channel_id=1, source_target_pairs={{0,4},{1,5},{2,6},{3,7},{4,0},{5,1},{6,2},{7,3},{8,12},{9,13},{10,... | collective-permute-start | bytes 589832 | tf_op jit(solution)/shard_map/ppermute | solution.py:23
  129.0 12.4 %collective-permute-start.30 = (bf16[24,1024]{1,0:T(8,128)(2,1)S(1)}, bf16[24,1024]{1,0:T(8,128)(2,1)S(1)}, u32[]{:S(2)}, u32[]{:S(2)}) collective-permute-start(bf16[24,1024]{1,0:T(8,128)(2,1)S(1)} %get-tuple-element.60), channel_id=1, source_target_pairs={{0,1},{1,0},{2,3},{3,2},{4,5},{5,4},{6,7},{7,6},{8,9},{9,8},{10,11... | collective-permute-start | bytes 147464 | tf_op jit(solution)/shard_map/ppermute | solution.py:23
  134.4 6.9 %collective-permute-start.32 = (bf16[24,1024]{1,0:T(8,128)(2,1)S(1)}, bf16[24,1024]{1,0:T(8,128)(2,1)S(1)}, u32[]{:S(2)}, u32[]{:S(2)}) collective-permute-start(bf16[24,1024]{1,0:T(8,128)(2,1)S(1)} %get-tuple-element.61), channel_id=1, source_target_pairs={{0,3},{1,2},{2,1},{3,0},{4,7},{5,6},{6,5},{7,4},{8,11},{9,10},{10,... | collective-permute-start | bytes 147464 | tf_op jit(solution)/shard_map/ppermute | solution.py:23
  136.8 6.1 %collective-permute-start.31 = (bf16[24,1024]{1,0:T(8,128)(2,1)S(1)}, bf16[24,1024]{1,0:T(8,128)(2,1)S(1)}, u32[]{:S(2)}, u32[]{:S(2)}) collective-permute-start(bf16[24,1024]{1,0:T(8,128)(2,1)S(1)} %get-tuple-element.62), channel_id=1, source_target_pairs={{0,2},{1,3},{2,0},{3,1},{4,6},{5,7},{6,4},{7,5},{8,10},{9,11},{10,... | collective-permute-start | bytes 147464 | tf_op jit(solution)/shard_map/ppermute | solution.py:23
  136.9 6.1 %collective-permute-start.25 = (bf16[24,1024]{1,0:T(8,128)(2,1)S(1)}, bf16[24,1024]{1,0:T(8,128)(2,1)S(1)}, u32[]{:S(2)}, u32[]{:S(2)}) collective-permute-start(bf16[24,1024]{1,0:T(8,128)(2,1)S(1)} %get-tuple-element.57), channel_id=1, source_target_pairs={{0,1},{1,0},{2,3},{3,2},{4,5},{5,4},{6,7},{7,6},{8,9},{9,8},{10,11... | collective-permute-start | bytes 147464 | tf_op jit(solution)/shard_map/ppermute | solution.py:23
  139.0 5.9 %collective-permute-start.27 = (bf16[24,1024]{1,0:T(8,128)(2,1)S(1)}, bf16[24,1024]{1,0:T(8,128)(2,1)S(1)}, u32[]{:S(2)}, u32[]{:S(2)}) collective-permute-start(bf16[24,1024]{1,0:T(8,128)(2,1)S(1)} %get-tuple-element.58), channel_id=1, source_target_pairs={{0,3},{1,2},{2,1},{3,0},{4,7},{5,6},{6,5},{7,4},{8,11},{9,10},{10,... | collective-permute-start | bytes 147464 | tf_op jit(solution)/shard_map/ppermute | solution.py:23
  141.4 5.0 %collective-permute-start.26 = (bf16[24,1024]{1,0:T(8,128)(2,1)S(1)}, bf16[24,1024]{1,0:T(8,128)(2,1)S(1)}, u32[]{:S(2)}, u32[]{:S(2)}) collective-permute-start(bf16[24,1024]{1,0:T(8,128)(2,1)S(1)} %get-tuple-element.59), channel_id=1, source_target_pairs={{0,2},{1,3},{2,0},{3,1},{4,6},{5,7},{6,4},{7,5},{8,10},{9,11},{10,... | collective-permute-start | bytes 147464 | tf_op jit(solution)/shard_map/ppermute | solution.py:23

commit v2 on v1

v2 whole, which is shorter than its diff:
```python
import functools

import jax
import jax.numpy as jnp
from jax import lax
from jax.experimental import pallas as pl
from jax.experimental.pallas import tpu as pltpu
from jax.sharding import PartitionSpec as P

BF = jnp.bfloat16
F32 = jnp.float32
N = 16
CHUNKS = 3
FIRST = (1, 3)
SECOND = (3, 1)


def exchange(value, masks_x=(0, 0), z=0, masks_y=(0, 0), zhi=0, core=0):
    pairs = []
    for gx in range(N):
        for gy in range(N):
            other = (gx ^ (2 * masks_y[gx & 1]) ^ (8 * zhi) ^ core) * N + (gy ^ (4 * masks_x[gx & 1]) ^ z)
            pairs.append((gx * N + gy, other))
    return lax.ppermute(value, ("gx", "gy"), pairs)


def gray(v):
    return v ^ (v >> 1)


def kept(gx):
    odd = (gx & 1) == 1
    ys = [lax.select(odd, jnp.int32(gray(i)), jnp.int32(3 * gray(i) & 3)) for i in range(4)]
    return [[gx ^ (2 * y) ^ (8 * z) for z in (0, 1)] for y in ys]


def x_place(gx, block):
    return gray(lax.select((gx & 1) == 0, block >> 2, (3 * (block >> 2)) & 3))


def gathered_slot(gx, block):
    return 8 * ((block >> 1) & 1) + 2 * x_place(gx, block) + (block & 1)


def scattered_slot(gx, block):
    return 4 * x_place(gx, block) + (block & 3)


def pick_kernel(rows, n, *refs):
    pieces, outs, whole = refs[: -n - 1], refs[-n - 1 : -1], refs[-1]
    first = 0
    for piece in pieces:
        whole[pl.ds(first, piece.shape[0]), :] = piece[...]
        first += piece.shape[0]
    me = lax.axis_index("gx")
    slots = [gathered_slot(me, block) for gx in (me ^ 1, me) for blocks in kept(gx) for block in blocks]
    for chunk, out in enumerate(outs):
        for k, slot in enumerate(slots):
            source = pl.multiple_of((slot * n + chunk) * rows, 16)
            out[pl.ds(k * rows, rows), :] = whole[pl.ds(source, rows), :]


def place_kernel(rows, *refs):
    *pieces, out_ref = refs
    me = lax.axis_index("gx")
    for piece, (gx, z) in zip(pieces, [(me, 0), (me, 1), (me ^ 1, 0), (me ^ 1, 1)]):
        for part, blocks in enumerate(kept(gx)):
            target = pl.multiple_of(scattered_slot(me, blocks[z]) * rows, 16)
            out_ref[pl.ds(target, rows), :] = piece[pl.ds(part * rows, rows), :]


def pack_kernel(gate_ref, up_ref, out_ref, sems):
    copies = []
    for j in range(gate_ref.shape[1] // 128):
        for k, ref in enumerate((gate_ref, up_ref)):
            copies.append(
                pltpu.make_async_copy(
                    ref.at[:, pl.ds(128 * j, 128)], out_ref.at[:, pl.ds(256 * j + 128 * k, 128)], sems.at[2 * j + k]
                )
            )
    for copy in copies:
        copy.start()
    for copy in copies:
        copy.wait()


def pack(gate_weight, up_weight):
    width, units = gate_weight.shape
    return pl.pallas_call(
        pack_kernel,
        out_shape=jax.ShapeDtypeStruct((width, 2 * units), BF),
        in_specs=[pl.BlockSpec(memory_space=pl.ANY)] * 2,
        out_specs=pl.BlockSpec(memory_space=pltpu.VMEM),
        scratch_shapes=[pltpu.SemaphoreType.DMA((2 * units // 128,))],
        compiler_params=pltpu.CompilerParams(vmem_limit_bytes=16 * 2**20),
        cost_estimate=pl.CostEstimate(flops=0, bytes_accessed=8 * width * units, transcendentals=0),
        name="pack",
    )(gate_weight, up_weight)


def in_vmem(kernel, shapes, name, *values, scratch=(), limit=8):
    spec = pl.BlockSpec(memory_space=pltpu.VMEM)
    out = tuple(jax.ShapeDtypeStruct(shape, BF) for shape in shapes)
    result = pl.pallas_call(
        kernel,
        out_shape=out,
        in_specs=[spec] * len(values),
        out_specs=(spec,) * len(out),
        scratch_shapes=scratch,
        compiler_params=pltpu.CompilerParams(vmem_limit_bytes=limit * 2**20),
        name=name,
    )(*values)
    return result if len(out) > 1 else result[0]


def pick(pieces, rows):
    width = pieces[0].shape[1]
    return in_vmem(
        functools.partial(pick_kernel, rows, CHUNKS),
        [(N * rows, width)] * CHUNKS,
        "pick",
        *pieces,
        scratch=[pltpu.VMEM((CHUNKS * N * rows, width), BF)],
        limit=16,
    )


def place(pieces, rows):
    shape = (N * rows, pieces[0].shape[1])
    return in_vmem(functools.partial(place_kernel, rows), [shape], "place", *pieces)


def silu_kernel(a_ref, b_ref, out_ref):
    for j in range(out_ref.shape[1] // 128):
        gate = pl.ds(256 * j, 128)
        up = pl.ds(256 * j + 128, 128)
        g = a_ref[:, gate].astype(F32) + b_ref[:, gate].astype(F32)
        u = a_ref[:, up].astype(F32) + b_ref[:, up].astype(F32)
        out_ref[:, pl.ds(128 * j, 128)] = (g / (1.0 + jnp.exp(-g)) * u).astype(BF)


def silu(a, b):
    return in_vmem(silu_kernel, [(a.shape[0], a.shape[1] // 2)], "silu", a, b)


def join_kernel(*refs):
    first = 0
    for ref in refs[:-1]:
        refs[-1][pl.ds(first, ref.shape[0]), :] = ref[...]
        first += ref.shape[0]


def join(*values):
    return in_vmem(join_kernel, [(sum(v.shape[0] for v in values), values[0].shape[1])], "join", *values)


def add(a, b):
    return (a.astype(F32) + b.astype(F32)).astype(BF)


def dot(a, b):
    return jnp.dot(a, b, preferred_element_type=F32).astype(BF)


def tie(*values):
    return lax.optimization_barrier(values)


def gather_tokens(t, gate_weight, up_weight):
    t1, t2, t3 = (exchange(t, z=m) for m in (1, 2, 3))
    first = join(t, t1)
    gate_weight, _ = tie(gate_weight, first)
    weight = pack(gate_weight, up_weight)
    t3, weight = tie(t3, weight)
    pieces = []
    for h in first, join(t2, t3):
        p = exchange(h, masks_x=FIRST)
        pieces += [h, p, exchange(join(h, p), masks_x=SECOND)]
    return pieces, weight


def halve(stays, got, size):
    v = add(stays, got)
    return v[:size], v[size:]


def scatter_hidden(chunks, weight, rows):
    stays, got, sent = [None] * CHUNKS, [None] * CHUNKS, None
    for c, picked in enumerate(chunks):
        s = dot(picked, weight)
        stays[c], sent = s[8 * rows :], s[: 8 * rows]
        got[c] = exchange(sent, core=1)
    for size, how in (4, dict(masks_y=FIRST)), (2, dict(masks_y=SECOND)), (1, dict(zhi=1)):
        for c in range(CHUNKS):
            got[c], _ = tie(got[c], sent)
            stays[c], sent = halve(stays[c], got[c], size * rows)
            got[c] = exchange(sent, **how)
    hidden = [silu(stays[0], got[0])]
    for c in range(1, CHUNKS):
        got[c], _ = tie(got[c], hidden[-1])
        hidden.append(silu(stays[c], got[c]))
    return hidden


def gather_hidden(hidden):
    half = [exchange(h, zhi=1) for h in hidden]
    halves = []
    for h in join(*hidden), None:
        if h is None:
            h = join(*half)
        h = join(h, exchange(h, masks_y=SECOND))
        halves.append(join(h, exchange(h, masks_y=FIRST)))
    return halves + [exchange(h, core=1) for h in halves]


def scatter_out(hidden, weight, rows):
    width = weight.shape[1] // 2
    stays, got = [None, None], [None, None]
    for c in range(2):
        s = dot(hidden, weight[:, c * width : (c + 1) * width])
        stays[c], sent = s[: 8 * rows], s[8 * rows :]
        got[c] = exchange(sent, masks_x=SECOND)
    got[0], _ = tie(got[0], sent)
    for c in range(2):
        if c == 1:
            got[1], got[0] = tie(got[1], got[0])
        stays[c], sent = halve(stays[c], got[c], 4 * rows)
        got[c] = exchange(sent, masks_x=FIRST)
    columns = []
    for c in range(2):
        v = add(stays[c], got[c])
        parts = [v[:rows]] + [exchange(v[m * rows : (m + 1) * rows], z=m) for m in (1, 2, 3)]
        columns.append(functools.reduce(jnp.add, [p.astype(F32) for p in parts]).astype(BF))
    return jnp.concatenate(columns, axis=1)


def shards(tokens, gate_weight, up_weight, down_weight):
    rows = tokens.shape[0]
    pieces, weight = gather_tokens(tokens, gate_weight, up_weight)
    hidden = scatter_hidden(pick(pieces, rows // CHUNKS), weight, rows // CHUNKS)
    return scatter_out(place(gather_hidden(hidden), rows), down_weight, rows)


def solution(mesh):
    in_specs = (P("gy", "gx"), P("gx", "gy"), P("gx", "gy"), P("gy", "gx"))
    out_specs = P("gy", "gx")
    return jax.shard_map(shards, mesh=mesh, in_specs=in_specs, out_specs=out_specs, check_vma=False)
```

time: 147 us -> 147 us (level)
  waiting for transfers between devices: 70.2 us -> 64.3 us
  starting transfers between devices: 57.8 us -> 62.1 us
    ppermute x33 -> x38, waiting for transfers between devices: 70.2 us -> 64.3 us  [exchange(): return lax.ppermute(value, ('gx', 'gy'), pairs)]
    ppermute x33 -> x38, starting transfers between devices: 57.8 us -> 62.1 us  [exchange(): return lax.ppermute(value, ('gx', 'gy'), pairs)]
    dot_general x4 -> x5, matrix products: 9.24 us -> 9 us  [dot(): return jnp.dot(a, b, preferred_element_type=F32).astype(BF)]
  transfers between devices with their start and end apart: 33 -> 38, of which waited for: 21 -> 20; matrix products, arithmetic and copies ran while one was open for 5% -> 5% of each run, Pallas kernels for 2% -> 1%
where the time goes in v2:
time: 147 us; the launch traced here: 146 us
  waiting for transfers between devices  64.3 us (44%)
  starting transfers between devices  62.1 us (42%)
  matrix products  9 us (6%)
  local copies, waits for them, and re-layouts  5.32 us (4%)
  Pallas kernels  2.36 us (2%)
  other arithmetic  2.07 us (1%)
    ppermute x38, waiting for transfers between devices, exchange(): return lax.ppermute(value, ('gx', 'gy'), pairs)  64.3 us
    ppermute x38, starting transfers between devices, exchange(): return lax.ppermute(value, ('gx', 'gy'), pairs)  62.1 us
    dot_general x5, matrix products, dot(): return jnp.dot(a, b, preferred_element_type=F32).astype(BF)  9 us
    unnamed x8, local copies, waits for them, and re-layouts  4.86 us
  transfers between devices with their start and end apart: 38, of which 20 were waited for; matrix products, arithmetic and copies ran while one was open for 5% of the time, Pallas kernels for 1%

profile of v2, /device:TPU:24, one launch (start us, length us, event | category | flops | bytes accessed | tf_op | source)
XLA Modules:
  0.0 145.6 jit_solution(781554334934474663)
XLA Ops:
  0.0 1.9 %collective-permute-start = (bf16[48,1024]{1,0:T(8,128)(2,1)}, bf16[48,1024]{1,0:T(8,128)(2,1)S(1)}, u32[]{:S(2)}, u32[]{:S(2)}) collective-permute-start(bf16[48,1024]{1,0:T(8,128)(2,1)} %refs_0_.1), channel_id=1, source_target_pairs={{0,1},{1,0},{2,3},{3,2},{4,5},{5,4},{6,7},{7,6},{8,9},{9,8},{10,11... | collective-permute-start | bytes 294920 | tf_op jit(solution)/shard_map/ppermute | solution.py:24
  1.9 2.8 %collective-permute-start.4 = (bf16[48,1024]{1,0:T(8,128)(2,1)}, bf16[48,1024]{1,0:T(8,128)(2,1)S(1)}, u32[]{:S(2)}, u32[]{:S(2)}) collective-permute-start(bf16[48,1024]{1,0:T(8,128)(2,1)} %refs_0_.1), channel_id=1, source_target_pairs={{0,3},{1,2},{2,1},{3,0},{4,7},{5,6},{6,5},{7,4},{8,11},{9,10},{10,... | collective-permute-start | bytes 294920 | tf_op jit(solution)/shard_map/ppermute | solution.py:24
  5.2 0.9 copy-done.2
  6.1 1.6 %collective-permute-start.1 = (bf16[96,1024]{1,0:T(8,128)(2,1)S(1)}, bf16[96,1024]{1,0:T(8,128)(2,1)S(1)}, u32[]{:S(2)}, u32[]{:S(2)}) collective-permute-start(bf16[96,1024]{1,0:T(8,128)(2,1)S(1)} %join.10.refs_0_), channel_id=1, source_target_pairs={{0,4},{1,5},{2,6},{3,7},{4,0},{5,1},{6,2},{7,3},{8,12},{9,13},{10,... | collective-permute-start | bytes 589832 | tf_op jit(solution)/shard_map/ppermute | solution.py:24
  7.7 2.0 %copy-done = bf16[1024,1664]{1,0:T(8,128)(2,1)S(1)} copy-done((bf16[1024,1664]{1,0:T(8,128)(2,1)S(1)}, bf16[1024,1664]{1,0:T(8,128)(2,1)}, u32[]{:S(2)}) %copy-start) | copy-done | bytes 3407896
  9.7 2.0 %copy-done.1 = bf16[1024,1664]{1,0:T(8,128)(2,1)S(1)} copy-done((bf16[1024,1664]{1,0:T(8,128)(2,1)S(1)}, bf16[1024,1664]{1,0:T(8,128)(2,1)}, u32[]{:S(2)}) %copy-start.1) | copy-done | bytes 3407896
  11.6 1.5 pack.1
  13.1 1.2 collective-permute-done.3.refs_0_
  14.3 1.6 %collective-permute-start.5 = (bf16[96,1024]{1,0:T(8,128)(2,1)S(1)}, bf16[96,1024]{1,0:T(8,128)(2,1)S(1)}, u32[]{:S(2)}, u32[]{:S(2)}) collective-permute-start(bf16[96,1024]{1,0:T(8,128)(2,1)S(1)} %join.12.refs_0_.refs_3_), channel_id=1, source_target_pairs={{0,4},{1,5},{2,6},{3,7},{4,0},{5,1},{6,2},{7,3},{8,12},{9,13},{10,... | collective-permute-start | bytes 589832 | tf_op jit(solution)/shard_map/ppermute | solution.py:24
  15.9 2.2 %collective-permute-start.2 = (bf16[192,1024]{1,0:T(8,128)(2,1)S(1)}, bf16[192,1024]{1,0:T(8,128)(2,1)S(1)}, u32[]{:S(2)}, u32[]{:S(2)}) collective-permute-start(bf16[192,1024]{1,0:T(8,128)(2,1)S(1)} %join.11), channel_id=1, source_target_pairs={{0,12},{1,13},{2,14},{3,15},{4,8},{5,9},{6,10},{7,11},{8,4},{9,5},... | collective-permute-start | bytes 1179656 | tf_op jit(solution)/shard_map/ppermute | solution.py:24
  18.1 3.1 %collective-permute-done.5.refs_1_.refs_4_ = bf16[96,1024]{1,0:T(8,128)(2,1)S(1)} collective-permute-done((bf16[96,1024]{1,0:T(8,128)(2,1)S(1)}, bf16[96,1024]{1,0:T(8,128)(2,1)S(1)}, u32[]{:S(2)}, u32[]{:S(2)}) %collective-permute-start.5) | collective-permute-done | bytes 196640 | tf_op jit(solution)/shard_map/ppermute | solution.py:24
  21.2 3.9 %collective-permute-start.6 = (bf16[192,1024]{1,0:T(8,128)(2,1)S(1)}, bf16[192,1024]{1,0:T(8,128)(2,1)S(1)}, u32[]{:S(2)}, u32[]{:S(2)}) collective-permute-start(bf16[192,1024]{1,0:T(8,128)(2,1)S(1)} %join.13), channel_id=1, source_target_pairs={{0,12},{1,13},{2,14},{3,15},{4,8},{5,9},{6,10},{7,11},{8,4},{9,5},... | collective-permute-start | bytes 1179656 | tf_op jit(solution)/shard_map/ppermute | solution.py:24
  25.0 5.8 %collective-permute-done.6.refs_5_ = bf16[192,1024]{1,0:T(8,128)(2,1)S(1)} collective-permute-done((bf16[192,1024]{1,0:T(8,128)(2,1)S(1)}, bf16[192,1024]{1,0:T(8,128)(2,1)S(1)}, u32[]{:S(2)}, u32[]{:S(2)}) %collective-permute-start.6) | collective-permute-done | bytes 393248 | tf_op jit(solution)/shard_map/ppermute | solution.py:24
  31.0 1.9 %convolution_convert_fusion.2 = bf16[256,3328]{1,0:T(8,128)(2,1)S(1)} fusion(bf16[256,1024]{1,0:T(8,128)(2,1)S(1)} %get-tuple-element.27, bf16[1024,3328]{1,0:T(8,128)(2,1)S(1)} %pack.1), kind=kOutput, calls=%fused_computation.2 | convolution fusion | flops 1745682432 | bytes 9043968 | tf_op jit(solution)/shard_map/dot_general | solution.py:162
  33.1 1.9 %convolution_convert_fusion.1 = bf16[256,3328]{1,0:T(8,128)(2,1)S(1)} fusion(bf16[256,1024]{1,0:T(8,128)(2,1)S(1)} %get-tuple-element.29, bf16[1024,3328]{1,0:T(8,128)(2,1)S(1)} %pack.1), kind=kOutput, calls=%fused_computation.1 | convolution fusion | flops 1745682432 | bytes 9043968 | tf_op jit(solution)/shard_map/dot_general | solution.py:162
  35.1 1.9 %convolution_convert_fusion = bf16[256,3328]{1,0:T(8,128)(2,1)S(1)} fusion(bf16[256,1024]{1,0:T(8,128)(2,1)S(1)} %get-tuple-element.31, bf16[1024,3328]{1,0:T(8,128)(2,1)S(1)} %pack.1), kind=kOutput, calls=%fused_computation | convolution fusion | flops 1745682432 | bytes 9043968 | tf_op jit(solution)/shard_map/dot_general | solution.py:162
  38.3 0.8 collective-permute-start.8
  39.1 0.7 collective-permute-done.10
  40.0 0.8 collective-permute-start.13
  41.2 1.2 collective-permute-start.12
  42.4 4.0 %collective-permute-done.8 = bf16[64,3328]{1,0:T(8,128)(2,1)S(1)} collective-permute-done((bf16[64,3328]{1,0:T(8,128)(2,1)S(1)}, bf16[64,3328]{1,0:T(8,128)(2,1)S(1)}, u32[]{:S(2)}, u32[]{:S(2)}) %collective-permute-start.8) | collective-permute-done | bytes 426016 | tf_op jit(solution)/shard_map/ppermute | solution.py:24
  46.9 5.5 %collective-permute-done.13 = bf16[64,3328]{1,0:T(8,128)(2,1)S(1)} collective-permute-done((bf16[64,3328]{1,0:T(8,128)(2,1)S(1)}, bf16[64,3328]{1,0:T(8,128)(2,1)S(1)}, u32[]{:S(2)}, u32[]{:S(2)}) %collective-permute-start.13) | collective-permute-done | bytes 426016 | tf_op jit(solution)/shard_map/ppermute | solution.py:24
  52.9 7.3 %collective-permute-done.12 = bf16[64,3328]{1,0:T(8,128)(2,1)S(1)} collective-permute-done((bf16[64,3328]{1,0:T(8,128)(2,1)S(1)}, bf16[64,3328]{1,0:T(8,128)(2,1)S(1)}, u32[]{:S(2)}, u32[]{:S(2)}) %collective-permute-start.12) | collective-permute-done | bytes 426016 | tf_op jit(solution)/shard_map/ppermute | solution.py:24
  60.7 5.5 %collective-permute-start.14 = (bf16[16,3328]{1,0:T(8,128)(2,1)S(1)}, bf16[16,3328]{1,0:T(8,128)(2,1)S(1)}, u32[]{:S(2)}, u32[]{:S(2)}) collective-permute-start(bf16[16,3328]{1,0:T(8,128)(2,1)S(1)} %get-tuple-element.49), channel_id=1, source_target_pairs={{0,128},{1,129},{2,130},{3,131},{4,132},{5,133},{6,134},{7,135},{8... | collective-permute-start | bytes 319496 | tf_op jit(solution)/shard_map/ppermute | solution.py:24
  67.5 5.5 %collective-permute-start.18 = (bf16[16,3328]{1,0:T(8,128)(2,1)S(1)}, bf16[16,3328]{1,0:T(8,128)(2,1)S(1)}, u32[]{:S(2)}, u32[]{:S(2)}) collective-permute-start(bf16[16,3328]{1,0:T(8,128)(2,1)S(1)} %get-tuple-element.45), channel_id=1, source_target_pairs={{0,128},{1,129},{2,130},{3,131},{4,132},{5,133},{6,134},{7,135},{8... | collective-permute-start | bytes 319496 | tf_op jit(solution)/shard_map/ppermute | solution.py:24
  73.1 4.6 %collective-permute-start.21 = (bf16[16,1664]{1,0:T(8,128)(2,1)S(1)}, bf16[16,1664]{1,0:T(8,128)(2,1)S(1)}, u32[]{:S(2)}, u32[]{:S(2)}) collective-permute-start(bf16[16,1664]{1,0:T(8,128)(2,1)S(1)} %silu.3.refs_0_), channel_id=1, source_target_pairs={{0,128},{1,129},{2,130},{3,131},{4,132},{5,133},{6,134},{7,135},{8... | collective-permute-start | bytes 159752 | tf_op jit(solution)/shard_map/ppermute | solution.py:24
  77.7 4.7 %collective-permute-start.22 = (bf16[16,1664]{1,0:T(8,128)(2,1)S(1)}, bf16[16,1664]{1,0:T(8,128)(2,1)S(1)}, u32[]{:S(2)}, u32[]{:S(2)}) collective-permute-start(bf16[16,1664]{1,0:T(8,128)(2,1)S(1)} %silu.4.refs_1_), channel_id=1, source_target_pairs={{0,128},{1,129},{2,130},{3,131},{4,132},{5,133},{6,134},{7,135},{8... | collective-permute-start | bytes 159752 | tf_op jit(solution)/shard_map/ppermute | solution.py:24
  82.5 5.0 %collective-permute-start.23 = (bf16[16,1664]{1,0:T(8,128)(2,1)S(1)}, bf16[16,1664]{1,0:T(8,128)(2,1)S(1)}, u32[]{:S(2)}, u32[]{:S(2)}) collective-permute-start(bf16[16,1664]{1,0:T(8,128)(2,1)S(1)} %silu.5.refs_2_), channel_id=1, source_target_pairs={{0,128},{1,129},{2,130},{3,131},{4,132},{5,133},{6,134},{7,135},{8... | collective-permute-start | bytes 159752 | tf_op jit(solution)/shard_map/ppermute | solution.py:24
  87.7 4.1 %collective-permute-done.23.refs_2_ = bf16[16,1664]{1,0:T(8,128)(2,1)S(1)} collective-permute-done((bf16[16,1664]{1,0:T(8,128)(2,1)S(1)}, bf16[16,1664]{1,0:T(8,128)(2,1)S(1)}, u32[]{:S(2)}, u32[]{:S(2)}) %collective-permute-start.23) | collective-permute-done | bytes 53280 | tf_op jit(solution)/shard_map/ppermute | solution.py:24
  91.8 0.8 collective-permute-start.24
  92.6 3.2 %collective-permute-done.19.refs_1_ = bf16[48,1664]{1,0:T(8,128)(2,1)S(1)} collective-permute-done((bf16[48,1664]{1,0:T(8,128)(2,1)S(1)}, bf16[48,1664]{1,0:T(8,128)(2,1)S(1)}, u32[]{:S(2)}, u32[]{:S(2)}) %collective-permute-start.19) | collective-permute-done | bytes 159776 | tf_op jit(solution)/shard_map/ppermute | solution.py:24
  95.9 4.3 %collective-permute-done.24.refs_1_ = bf16[48,1664]{1,0:T(8,128)(2,1)S(1)} collective-permute-done((bf16[48,1664]{1,0:T(8,128)(2,1)S(1)}, bf16[48,1664]{1,0:T(8,128)(2,1)S(1)}, u32[]{:S(2)}, u32[]{:S(2)}) %collective-permute-start.24) | collective-permute-done | bytes 159776 | tf_op jit(solution)/shard_map/ppermute | solution.py:24
  100.3 2.6 %collective-permute-done.20.refs_1_ = bf16[96,1664]{1,0:T(8,128)(2,1)S(1)} collective-permute-done((bf16[96,1664]{1,0:T(8,128)(2,1)S(1)}, bf16[96,1664]{1,0:T(8,128)(2,1)S(1)}, u32[]{:S(2)}, u32[]{:S(2)}) %collective-permute-start.20) | collective-permute-done | bytes 319520 | tf_op jit(solution)/shard_map/ppermute | solution.py:24
  103.0 4.3 %collective-permute-done.25.refs_1_ = bf16[96,1664]{1,0:T(8,128)(2,1)S(1)} collective-permute-done((bf16[96,1664]{1,0:T(8,128)(2,1)S(1)}, bf16[96,1664]{1,0:T(8,128)(2,1)S(1)}, u32[]{:S(2)}, u32[]{:S(2)}) %collective-permute-start.25) | collective-permute-done | bytes 319520 | tf_op jit(solution)/shard_map/ppermute | solution.py:24
  107.7 2.1 %collective-permute-done.27.refs_3_ = bf16[192,1664]{1,0:T(8,128)(2,1)S(1)} collective-permute-done((bf16[192,1664]{1,0:T(8,128)(2,1)S(1)}, bf16[192,1664]{1,0:T(8,128)(2,1)S(1)}, u32[]{:S(2)}, u32[]{:S(2)}) %collective-permute-start.27) | collective-permute-done | bytes 639008 | tf_op jit(solution)/shard_map/ppermute | solution.py:24
  110.0 1.6 %fusion.4 = bf16[768,512]{1,0:T(8,128)(2,1)S(1)} fusion(bf16[768,1664]{1,0:T(8,128)(2,1)S(1)} %place.1, bf16[1664,1024]{1,0:T(8,128)(2,1)S(1)} %copy-done.3), kind=kOutput, calls=%fused_computation.10 | convolution fusion | flops 1309016064 | bytes 5046272 | tf_op jit(solution)/shard_map/dot_general | solution.py:162
  111.6 3.0 %collective-permute-start.28 = (bf16[384,512]{1,0:T(8,128)(2,1)S(1)}, bf16[384,512]{1,0:T(8,128)(2,1)S(1)}, u32[]{:S(2)}, u32[]{:S(2)}) collective-permute-start(bf16[384,512]{1,0:T(8,128)(2,1)S(1)} %slice.193), channel_id=1, source_target_pairs={{0,12},{1,13},{2,14},{3,15},{4,8},{5,9},{6,10},{7,11},{8,4},{9,5},... | collective-permute-start | bytes 1179656 | tf_op jit(solution)/shard_map/ppermute | solution.py:24
  114.7 1.6 %fusion.7 = bf16[768,512]{1,0:T(8,128)(2,1)S(1)} fusion(bf16[768,1664]{1,0:T(8,128)(2,1)S(1)} %place.1, bf16[1664,1024]{1,0:T(8,128)(2,1)S(1)} %copy-done.3), kind=kOutput, calls=%fused_computation.11 | convolution fusion | flops 1309016064 | bytes 5046272 | tf_op jit(solution)/shard_map/dot_general | solution.py:162
  116.7 4.0 %collective-permute-done.28 = bf16[384,512]{1,0:T(8,128)(2,1)S(1)} collective-permute-done((bf16[384,512]{1,0:T(8,128)(2,1)S(1)}, bf16[384,512]{1,0:T(8,128)(2,1)S(1)}, u32[]{:S(2)}, u32[]{:S(2)}) %collective-permute-start.28) | collective-permute-done | bytes 393248 | tf_op jit(solution)/shard_map/ppermute | solution.py:24
  121.3 6.2 %collective-permute-done.29 = bf16[384,512]{1,0:T(8,128)(2,1)S(1)} collective-permute-done((bf16[384,512]{1,0:T(8,128)(2,1)S(1)}, bf16[384,512]{1,0:T(8,128)(2,1)S(1)}, u32[]{:S(2)}, u32[]{:S(2)}) %collective-permute-start.29) | collective-permute-done | bytes 393248 | tf_op jit(solution)/shard_map/ppermute | solution.py:24
  127.8 4.5 %collective-permute-start.31 = (bf16[48,512]{1,0:T(8,128)(2,1)S(1)}, bf16[48,512]{1,0:T(8,128)(2,1)S(1)}, u32[]{:S(2)}, u32[]{:S(2)}) collective-permute-start(bf16[48,512]{1,0:T(8,128)(2,1)S(1)} %get-tuple-element.51), channel_id=1, source_target_pairs={{0,1},{1,0},{2,3},{3,2},{4,5},{5,4},{6,7},{7,6},{8,9},{9,8},{10,11... | collective-permute-start | bytes 147464 | tf_op jit(solution)/shard_map/ppermute | solution.py:24
  132.3 1.6 %collective-permute-start.32 = (bf16[48,512]{1,0:T(8,128)(2,1)S(1)}, bf16[48,512]{1,0:T(8,128)(2,1)S(1)}, u32[]{:S(2)}, u32[]{:S(2)}) collective-permute-start(bf16[48,512]{1,0:T(8,128)(2,1)S(1)} %get-tuple-element.53), channel_id=1, source_target_pairs={{0,2},{1,3},{2,0},{3,1},{4,6},{5,7},{6,4},{7,5},{8,10},{9,11},{10,... | collective-permute-start | bytes 147464 | tf_op jit(solution)/shard_map/ppermute | solution.py:24
  133.9 4.1 %collective-permute-start.35 = (bf16[48,512]{1,0:T(8,128)(2,1)S(1)}, bf16[48,512]{1,0:T(8,128)(2,1)S(1)}, u32[]{:S(2)}, u32[]{:S(2)}) collective-permute-start(bf16[48,512]{1,0:T(8,128)(2,1)S(1)} %get-tuple-element.54), channel_id=1, source_target_pairs={{0,1},{1,0},{2,3},{3,2},{4,5},{5,4},{6,7},{7,6},{8,9},{9,8},{10,11... | collective-permute-start | bytes 147464 | tf_op jit(solution)/shard_map/ppermute | solution.py:24
  138.0 1.6 %collective-permute-start.36 = (bf16[48,512]{1,0:T(8,128)(2,1)S(1)}, bf16[48,512]{1,0:T(8,128)(2,1)S(1)}, u32[]{:S(2)}, u32[]{:S(2)}) collective-permute-start(bf16[48,512]{1,0:T(8,128)(2,1)S(1)} %get-tuple-element.56), channel_id=1, source_target_pairs={{0,2},{1,3},{2,0},{3,1},{4,6},{5,7},{6,4},{7,5},{8,10},{9,11},{10,... | collective-permute-start | bytes 147464 | tf_op jit(solution)/shard_map/ppermute | solution.py:24
  139.6 1.2 collective-permute-done.35
  140.8 3.2 %collective-permute-done.37 = bf16[48,512]{1,0:T(8,128)(2,1)S(1)} collective-permute-done((bf16[48,512]{1,0:T(8,128)(2,1)S(1)}, bf16[48,512]{1,0:T(8,128)(2,1)S(1)}, u32[]{:S(2)}, u32[]{:S(2)}) %collective-permute-start.37) | collective-permute-done | bytes 49184 | tf_op jit(solution)/shard_map/ppermute | solution.py:24
  144.0 1.0 collective-permute-done.36
  145.0 0.6 pad_maximum_fusion
  (91 shorter events, 8.1 us)
Async XLA Ops:
  0.0 5.2 %collective-permute-start = (bf16[48,1024]{1,0:T(8,128)(2,1)}, bf16[48,1024]{1,0:T(8,128)(2,1)S(1)}, u32[]{:S(2)}, u32[]{:S(2)}) collective-permute-start(bf16[48,1024]{1,0:T(8,128)(2,1)} %refs_0_.1), channel_id=1, source_target_pairs={{0,1},{1,0},{2,3},{3,2},{4,5},{5,4},{6,7},{7,6},{8,9},{9,8},{10,11... | collective-permute-start | bytes 294920 | tf_op jit(solution)/shard_map/ppermute | solution.py:24
  1.9 11.2 %collective-permute-start.4 = (bf16[48,1024]{1,0:T(8,128)(2,1)}, bf16[48,1024]{1,0:T(8,128)(2,1)S(1)}, u32[]{:S(2)}, u32[]{:S(2)}) collective-permute-start(bf16[48,1024]{1,0:T(8,128)(2,1)} %refs_0_.1), channel_id=1, source_target_pairs={{0,3},{1,2},{2,1},{3,0},{4,7},{5,6},{6,5},{7,4},{8,11},{9,10},{10,... | collective-permute-start | bytes 294920 | tf_op jit(solution)/shard_map/ppermute | solution.py:24
  4.7 9.5 %collective-permute-start.3 = (bf16[48,1024]{1,0:T(8,128)(2,1)}, bf16[48,1024]{1,0:T(8,128)(2,1)S(1)}, u32[]{:S(2)}, u32[]{:S(2)}) collective-permute-start(bf16[48,1024]{1,0:T(8,128)(2,1)} %refs_0_.1), channel_id=1, source_target_pairs={{0,2},{1,3},{2,0},{3,1},{4,6},{5,7},{6,4},{7,5},{8,10},{9,11},{10,... | collective-permute-start | bytes 294920 | tf_op jit(solution)/shard_map/ppermute | solution.py:24
  5.2 0.9 copy-start.2
  6.1 9.7 %collective-permute-start.1 = (bf16[96,1024]{1,0:T(8,128)(2,1)S(1)}, bf16[96,1024]{1,0:T(8,128)(2,1)S(1)}, u32[]{:S(2)}, u32[]{:S(2)}) collective-permute-start(bf16[96,1024]{1,0:T(8,128)(2,1)S(1)} %join.10.refs_0_), channel_id=1, source_target_pairs={{0,4},{1,5},{2,6},{3,7},{4,0},{5,1},{6,2},{7,3},{8,12},{9,13},{10,... | collective-permute-start | bytes 589832 | tf_op jit(solution)/shard_map/ppermute | solution.py:24
  7.7 2.0 %copy-start = (bf16[1024,1664]{1,0:T(8,128)(2,1)S(1)}, bf16[1024,1664]{1,0:T(8,128)(2,1)}, u32[]{:S(2)}) copy-start(bf16[1024,1664]{1,0:T(8,128)(2,1)} %gate_ref) | copy-start | bytes 10223620
  9.7 2.0 %copy-start.1 = (bf16[1024,1664]{1,0:T(8,128)(2,1)S(1)}, bf16[1024,1664]{1,0:T(8,128)(2,1)}, u32[]{:S(2)}) copy-start(bf16[1024,1664]{1,0:T(8,128)(2,1)} %up_ref.1) | copy-start | bytes 10223620
  14.3 6.9 %collective-permute-start.5 = (bf16[96,1024]{1,0:T(8,128)(2,1)S(1)}, bf16[96,1024]{1,0:T(8,128)(2,1)S(1)}, u32[]{:S(2)}, u32[]{:S(2)}) collective-permute-start(bf16[96,1024]{1,0:T(8,128)(2,1)S(1)} %join.12.refs_0_.refs_3_), channel_id=1, source_target_pairs={{0,4},{1,5},{2,6},{3,7},{4,0},{5,1},{6,2},{7,3},{8,12},{9,13},{10,... | collective-permute-start | bytes 589832 | tf_op jit(solution)/shard_map/ppermute | solution.py:24
  15.9 9.2 %collective-permute-start.2 = (bf16[192,1024]{1,0:T(8,128)(2,1)S(1)}, bf16[192,1024]{1,0:T(8,128)(2,1)S(1)}, u32[]{:S(2)}, u32[]{:S(2)}) collective-permute-start(bf16[192,1024]{1,0:T(8,128)(2,1)S(1)} %join.11), channel_id=1, source_target_pairs={{0,12},{1,13},{2,14},{3,15},{4,8},{5,9},{6,10},{7,11},{8,4},{9,5},... | collective-permute-start | bytes 1179656 | tf_op jit(solution)/shard_map/ppermute | solution.py:24
  21.2 9.6 %collective-permute-start.6 = (bf16[192,1024]{1,0:T(8,128)(2,1)S(1)}, bf16[192,1024]{1,0:T(8,128)(2,1)S(1)}, u32[]{:S(2)}, u32[]{:S(2)}) collective-permute-start(bf16[192,1024]{1,0:T(8,128)(2,1)S(1)} %join.13), channel_id=1, source_target_pairs={{0,12},{1,13},{2,14},{3,15},{4,8},{5,9},{6,10},{7,11},{8,4},{9,5},... | collective-permute-start | bytes 1179656 | tf_op jit(solution)/shard_map/ppermute | solution.py:24
  33.0 5.0 %collective-permute-start.7 = (bf16[128,3328]{1,0:T(8,128)(2,1)S(1)}, bf16[128,3328]{1,0:T(8,128)(2,1)S(1)}, u32[]{:S(2)}, u32[]{:S(2)}) collective-permute-start(bf16[128,3328]{1,0:T(8,128)(2,1)S(1)} %slice.169), channel_id=1, source_target_pairs={{0,16},{1,17},{2,18},{3,19},{4,20},{5,21},{6,22},{7,23},{8,24},{9,... | collective-permute-start | bytes 2555912 | tf_op jit(solution)/shard_map/ppermute | solution.py:24
  37.2 2.6 %collective-permute-start.10 = (bf16[128,3328]{1,0:T(8,128)(2,1)S(1)}, bf16[128,3328]{1,0:T(8,128)(2,1)S(1)}, u32[]{:S(2)}, u32[]{:S(2)}) collective-permute-start(bf16[128,3328]{1,0:T(8,128)(2,1)S(1)} %slice.175), channel_id=1, source_target_pairs={{0,16},{1,17},{2,18},{3,19},{4,20},{5,21},{6,22},{7,23},{8,24},{9,... | collective-permute-start | bytes 2555912 | tf_op jit(solution)/shard_map/ppermute | solution.py:24
  37.7 3.2 %collective-permute-start.9 = (bf16[128,3328]{1,0:T(8,128)(2,1)S(1)}, bf16[128,3328]{1,0:T(8,128)(2,1)S(1)}, u32[]{:S(2)}, u32[]{:S(2)}) collective-permute-start(bf16[128,3328]{1,0:T(8,128)(2,1)S(1)} %slice.170), channel_id=1, source_target_pairs={{0,16},{1,17},{2,18},{3,19},{4,20},{5,21},{6,22},{7,23},{8,24},{9,... | collective-permute-start | bytes 2555912 | tf_op jit(solution)/shard_map/ppermute | solution.py:24
  38.3 8.2 %collective-permute-start.8 = (bf16[64,3328]{1,0:T(8,128)(2,1)S(1)}, bf16[64,3328]{1,0:T(8,128)(2,1)S(1)}, u32[]{:S(2)}, u32[]{:S(2)}) collective-permute-start(bf16[64,3328]{1,0:T(8,128)(2,1)S(1)} %slice.172), channel_id=1, source_target_pairs={{0,32},{1,33},{2,34},{3,35},{4,36},{5,37},{6,38},{7,39},{8,40},{9,... | collective-permute-start | bytes 1277960 | tf_op jit(solution)/shard_map/ppermute | solution.py:24
  40.0 12.4 %collective-permute-start.13 = (bf16[64,3328]{1,0:T(8,128)(2,1)S(1)}, bf16[64,3328]{1,0:T(8,128)(2,1)S(1)}, u32[]{:S(2)}, u32[]{:S(2)}) collective-permute-start(bf16[64,3328]{1,0:T(8,128)(2,1)S(1)} %slice.176), channel_id=1, source_target_pairs={{0,32},{1,33},{2,34},{3,35},{4,36},{5,37},{6,38},{7,39},{8,40},{9,... | collective-permute-start | bytes 1277960 | tf_op jit(solution)/shard_map/ppermute | solution.py:24
  41.2 19.0 %collective-permute-start.12 = (bf16[64,3328]{1,0:T(8,128)(2,1)S(1)}, bf16[64,3328]{1,0:T(8,128)(2,1)S(1)}, u32[]{:S(2)}, u32[]{:S(2)}) collective-permute-start(bf16[64,3328]{1,0:T(8,128)(2,1)S(1)} %slice.177), channel_id=1, source_target_pairs={{0,32},{1,33},{2,34},{3,35},{4,36},{5,37},{6,38},{7,39},{8,40},{9,... | collective-permute-start | bytes 1277960 | tf_op jit(solution)/shard_map/ppermute | solution.py:24
  46.6 14.0 %collective-permute-start.11 = (bf16[32,3328]{1,0:T(8,128)(2,1)S(1)}, bf16[32,3328]{1,0:T(8,128)(2,1)S(1)}, u32[]{:S(2)}, u32[]{:S(2)}) collective-permute-start(bf16[32,3328]{1,0:T(8,128)(2,1)S(1)} %slice.179), channel_id=1, source_target_pairs={{0,96},{1,97},{2,98},{3,99},{4,100},{5,101},{6,102},{7,103},{8,104... | collective-permute-start | bytes 638984 | tf_op jit(solution)/shard_map/ppermute | solution.py:24
  52.6 13.6 %collective-permute-start.15 = (bf16[32,3328]{1,0:T(8,128)(2,1)S(1)}, bf16[32,3328]{1,0:T(8,128)(2,1)S(1)}, u32[]{:S(2)}, u32[]{:S(2)}) collective-permute-start(bf16[32,3328]{1,0:T(8,128)(2,1)S(1)} %slice.182), channel_id=1, source_target_pairs={{0,96},{1,97},{2,98},{3,99},{4,100},{5,101},{6,102},{7,103},{8,104... | collective-permute-start | bytes 638984 | tf_op jit(solution)/shard_map/ppermute | solution.py:24
  60.3 7.1 %collective-permute-start.17 = (bf16[32,3328]{1,0:T(8,128)(2,1)S(1)}, bf16[32,3328]{1,0:T(8,128)(2,1)S(1)}, u32[]{:S(2)}, u32[]{:S(2)}) collective-permute-start(bf16[32,3328]{1,0:T(8,128)(2,1)S(1)} %slice.183), channel_id=1, source_target_pairs={{0,96},{1,97},{2,98},{3,99},{4,100},{5,101},{6,102},{7,103},{8,104... | collective-permute-start | bytes 638984 | tf_op jit(solution)/shard_map/ppermute | solution.py:24
  60.7 12.3 %collective-permute-start.14 = (bf16[16,3328]{1,0:T(8,128)(2,1)S(1)}, bf16[16,3328]{1,0:T(8,128)(2,1)S(1)}, u32[]{:S(2)}, u32[]{:S(2)}) collective-permute-start(bf16[16,3328]{1,0:T(8,128)(2,1)S(1)} %get-tuple-element.49), channel_id=1, source_target_pairs={{0,128},{1,129},{2,130},{3,131},{4,132},{5,133},{6,134},{7,135},{8... | collective-permute-start | bytes 319496 | tf_op jit(solution)/shard_map/ppermute | solution.py:24
  66.3 11.4 %collective-permute-start.16 = (bf16[16,3328]{1,0:T(8,128)(2,1)S(1)}, bf16[16,3328]{1,0:T(8,128)(2,1)S(1)}, u32[]{:S(2)}, u32[]{:S(2)}) collective-permute-start(bf16[16,3328]{1,0:T(8,128)(2,1)S(1)} %get-tuple-element.47), channel_id=1, source_target_pairs={{0,128},{1,129},{2,130},{3,131},{4,132},{5,133},{6,134},{7,135},{8... | collective-permute-start | bytes 319496 | tf_op jit(solution)/shard_map/ppermute | solution.py:24
  67.5 15.0 %collective-permute-start.18 = (bf16[16,3328]{1,0:T(8,128)(2,1)S(1)}, bf16[16,3328]{1,0:T(8,128)(2,1)S(1)}, u32[]{:S(2)}, u32[]{:S(2)}) collective-permute-start(bf16[16,3328]{1,0:T(8,128)(2,1)S(1)} %get-tuple-element.45), channel_id=1, source_target_pairs={{0,128},{1,129},{2,130},{3,131},{4,132},{5,133},{6,134},{7,135},{8... | collective-permute-start | bytes 319496 | tf_op jit(solution)/shard_map/ppermute | solution.py:24
  73.1 14.6 %collective-permute-start.21 = (bf16[16,1664]{1,0:T(8,128)(2,1)S(1)}, bf16[16,1664]{1,0:T(8,128)(2,1)S(1)}, u32[]{:S(2)}, u32[]{:S(2)}) collective-permute-start(bf16[16,1664]{1,0:T(8,128)(2,1)S(1)} %silu.3.refs_0_), channel_id=1, source_target_pairs={{0,128},{1,129},{2,130},{3,131},{4,132},{5,133},{6,134},{7,135},{8... | collective-permute-start | bytes 159752 | tf_op jit(solution)/shard_map/ppermute | solution.py:24
  77.7 9.9 %collective-permute-start.22 = (bf16[16,1664]{1,0:T(8,128)(2,1)S(1)}, bf16[16,1664]{1,0:T(8,128)(2,1)S(1)}, u32[]{:S(2)}, u32[]{:S(2)}) collective-permute-start(bf16[16,1664]{1,0:T(8,128)(2,1)S(1)} %silu.4.refs_1_), channel_id=1, source_target_pairs={{0,128},{1,129},{2,130},{3,131},{4,132},{5,133},{6,134},{7,135},{8... | collective-permute-start | bytes 159752 | tf_op jit(solution)/shard_map/ppermute | solution.py:24
  82.5 9.3 %collective-permute-start.23 = (bf16[16,1664]{1,0:T(8,128)(2,1)S(1)}, bf16[16,1664]{1,0:T(8,128)(2,1)S(1)}, u32[]{:S(2)}, u32[]{:S(2)}) collective-permute-start(bf16[16,1664]{1,0:T(8,128)(2,1)S(1)} %silu.5.refs_2_), channel_id=1, source_target_pairs={{0,128},{1,129},{2,130},{3,131},{4,132},{5,133},{6,134},{7,135},{8... | collective-permute-start | bytes 159752 | tf_op jit(solution)/shard_map/ppermute | solution.py:24
  87.6 8.2 %collective-permute-start.19 = (bf16[48,1664]{1,0:T(8,128)(2,1)S(1)}, bf16[48,1664]{1,0:T(8,128)(2,1)S(1)}, u32[]{:S(2)}, u32[]{:S(2)}) collective-permute-start(bf16[48,1664]{1,0:T(8,128)(2,1)S(1)} %join.14.refs_0_), channel_id=1, source_target_pairs={{0,96},{1,97},{2,98},{3,99},{4,100},{5,101},{6,102},{7,103},{8,104... | collective-permute-start | bytes 479240 | tf_op jit(solution)/shard_map/ppermute | solution.py:24
  91.8 8.3 %collective-permute-start.24 = (bf16[48,1664]{1,0:T(8,128)(2,1)S(1)}, bf16[48,1664]{1,0:T(8,128)(2,1)S(1)}, u32[]{:S(2)}, u32[]{:S(2)}) collective-permute-start(bf16[48,1664]{1,0:T(8,128)(2,1)S(1)} %join.17.refs_0_), channel_id=1, source_target_pairs={{0,96},{1,97},{2,98},{3,99},{4,100},{5,101},{6,102},{7,103},{8,104... | collective-permute-start | bytes 479240 | tf_op jit(solution)/shard_map/ppermute | solution.py:24
  95.8 7.1 %collective-permute-start.20 = (bf16[96,1664]{1,0:T(8,128)(2,1)S(1)}, bf16[96,1664]{1,0:T(8,128)(2,1)S(1)}, u32[]{:S(2)}, u32[]{:S(2)}) collective-permute-start(bf16[96,1664]{1,0:T(8,128)(2,1)S(1)} %join.15.refs_0_), channel_id=1, source_target_pairs={{0,32},{1,33},{2,34},{3,35},{4,36},{5,37},{6,38},{7,39},{8,40},{9,... | collective-permute-start | bytes 958472 | tf_op jit(solution)/shard_map/ppermute | solution.py:24
  100.2 7.1 %collective-permute-start.25 = (bf16[96,1664]{1,0:T(8,128)(2,1)S(1)}, bf16[96,1664]{1,0:T(8,128)(2,1)S(1)}, u32[]{:S(2)}, u32[]{:S(2)}) collective-permute-start(bf16[96,1664]{1,0:T(8,128)(2,1)S(1)} %join.18.refs_0_), channel_id=1, source_target_pairs={{0,32},{1,33},{2,34},{3,35},{4,36},{5,37},{6,38},{7,39},{8,40},{9,... | collective-permute-start | bytes 958472 | tf_op jit(solution)/shard_map/ppermute | solution.py:24
  102.9 4.7 %collective-permute-start.26 = (bf16[192,1664]{1,0:T(8,128)(2,1)S(1)}, bf16[192,1664]{1,0:T(8,128)(2,1)S(1)}, u32[]{:S(2)}, u32[]{:S(2)}) collective-permute-start(bf16[192,1664]{1,0:T(8,128)(2,1)S(1)} %join.16.refs_0_), channel_id=1, source_target_pairs={{0,16},{1,17},{2,18},{3,19},{4,20},{5,21},{6,22},{7,23},{8,24},{9,... | collective-permute-start | bytes 1916936 | tf_op jit(solution)/shard_map/ppermute | solution.py:24
  107.3 2.7 %copy-start.3 = (bf16[1664,1024]{1,0:T(8,128)(2,1)S(1)}, bf16[1664,1024]{1,0:T(8,128)(2,1)}, u32[]{:S(2)}) copy-start(bf16[1664,1024]{1,0:T(8,128)(2,1)} %param.7) | copy-start | bytes 10223620
  107.3 2.4 %collective-permute-start.27 = (bf16[192,1664]{1,0:T(8,128)(2,1)S(1)}, bf16[192,1664]{1,0:T(8,128)(2,1)S(1)}, u32[]{:S(2)}, u32[]{:S(2)}) collective-permute-start(bf16[192,1664]{1,0:T(8,128)(2,1)S(1)} %join.19.refs_1_), channel_id=1, source_target_pairs={{0,16},{1,17},{2,18},{3,19},{4,20},{5,21},{6,22},{7,23},{8,24},{9,... | collective-permute-start | bytes 1916936 | tf_op jit(solution)/shard_map/ppermute | solution.py:24
  111.6 9.1 %collective-permute-start.28 = (bf16[384,512]{1,0:T(8,128)(2,1)S(1)}, bf16[384,512]{1,0:T(8,128)(2,1)S(1)}, u32[]{:S(2)}, u32[]{:S(2)}) collective-permute-start(bf16[384,512]{1,0:T(8,128)(2,1)S(1)} %slice.193), channel_id=1, source_target_pairs={{0,12},{1,13},{2,14},{3,15},{4,8},{5,9},{6,10},{7,11},{8,4},{9,5},... | collective-permute-start | bytes 1179656 | tf_op jit(solution)/shard_map/ppermute | solution.py:24
  116.3 11.2 %collective-permute-start.29 = (bf16[384,512]{1,0:T(8,128)(2,1)S(1)}, bf16[384,512]{1,0:T(8,128)(2,1)S(1)}, u32[]{:S(2)}, u32[]{:S(2)}) collective-permute-start(bf16[384,512]{1,0:T(8,128)(2,1)S(1)} %slice.194), channel_id=1, source_target_pairs={{0,12},{1,13},{2,14},{3,15},{4,8},{5,9},{6,10},{7,11},{8,4},{9,5},... | collective-permute-start | bytes 1179656 | tf_op jit(solution)/shard_map/ppermute | solution.py:24
  120.8 6.7 %collective-permute-start.30 = (bf16[192,512]{1,0:T(8,128)(2,1)S(1)}, bf16[192,512]{1,0:T(8,128)(2,1)S(1)}, u32[]{:S(2)}, u32[]{:S(2)}) collective-permute-start(bf16[192,512]{1,0:T(8,128)(2,1)S(1)} %slice.196), channel_id=1, source_target_pairs={{0,4},{1,5},{2,6},{3,7},{4,0},{5,1},{6,2},{7,3},{8,12},{9,13},{10,... | collective-permute-start | bytes 589832 | tf_op jit(solution)/shard_map/ppermute | solution.py:24
  127.7 6.2 %collective-permute-start.34 = (bf16[192,512]{1,0:T(8,128)(2,1)S(1)}, bf16[192,512]{1,0:T(8,128)(2,1)S(1)}, u32[]{:S(2)}, u32[]{:S(2)}) collective-permute-start(bf16[192,512]{1,0:T(8,128)(2,1)S(1)} %slice.203), channel_id=1, source_target_pairs={{0,4},{1,5},{2,6},{3,7},{4,0},{5,1},{6,2},{7,3},{8,12},{9,13},{10,... | collective-permute-start | bytes 589832 | tf_op jit(solution)/shard_map/ppermute | solution.py:24
  127.8 10.2 %collective-permute-start.31 = (bf16[48,512]{1,0:T(8,128)(2,1)S(1)}, bf16[48,512]{1,0:T(8,128)(2,1)S(1)}, u32[]{:S(2)}, u32[]{:S(2)}) collective-permute-start(bf16[48,512]{1,0:T(8,128)(2,1)S(1)} %get-tuple-element.51), channel_id=1, source_target_pairs={{0,1},{1,0},{2,3},{3,2},{4,5},{5,4},{6,7},{7,6},{8,9},{9,8},{10,11... | collective-permute-start | bytes 147464 | tf_op jit(solution)/shard_map/ppermute | solution.py:24
  132.3 7.3 %collective-permute-start.33 = (bf16[48,512]{1,0:T(8,128)(2,1)S(1)}, bf16[48,512]{1,0:T(8,128)(2,1)S(1)}, u32[]{:S(2)}, u32[]{:S(2)}) collective-permute-start(bf16[48,512]{1,0:T(8,128)(2,1)S(1)} %get-tuple-element.52), channel_id=1, source_target_pairs={{0,3},{1,2},{2,1},{3,0},{4,7},{5,6},{6,5},{7,4},{8,11},{9,10},{10,... | collective-permute-start | bytes 147464 | tf_op jit(solution)/shard_map/ppermute | solution.py:24
  132.3 7.3 %collective-permute-start.32 = (bf16[48,512]{1,0:T(8,128)(2,1)S(1)}, bf16[48,512]{1,0:T(8,128)(2,1)S(1)}, u32[]{:S(2)}, u32[]{:S(2)}) collective-permute-start(bf16[48,512]{1,0:T(8,128)(2,1)S(1)} %get-tuple-element.53), channel_id=1, source_target_pairs={{0,2},{1,3},{2,0},{3,1},{4,6},{5,7},{6,4},{7,5},{8,10},{9,11},{10,... | collective-permute-start | bytes 147464 | tf_op jit(solution)/shard_map/ppermute | solution.py:24
  133.9 6.9 %collective-permute-start.35 = (bf16[48,512]{1,0:T(8,128)(2,1)S(1)}, bf16[48,512]{1,0:T(8,128)(2,1)S(1)}, u32[]{:S(2)}, u32[]{:S(2)}) collective-permute-start(bf16[48,512]{1,0:T(8,128)(2,1)S(1)} %get-tuple-element.54), channel_id=1, source_target_pairs={{0,1},{1,0},{2,3},{3,2},{4,5},{5,4},{6,7},{7,6},{8,9},{9,8},{10,11... | collective-permute-start | bytes 147464 | tf_op jit(solution)/shard_map/ppermute | solution.py:24
  138.0 6.0 %collective-permute-start.37 = (bf16[48,512]{1,0:T(8,128)(2,1)S(1)}, bf16[48,512]{1,0:T(8,128)(2,1)S(1)}, u32[]{:S(2)}, u32[]{:S(2)}) collective-permute-start(bf16[48,512]{1,0:T(8,128)(2,1)S(1)} %get-tuple-element.55), channel_id=1, source_target_pairs={{0,3},{1,2},{2,1},{3,0},{4,7},{5,6},{6,5},{7,4},{8,11},{9,10},{10,... | collective-permute-start | bytes 147464 | tf_op jit(solution)/shard_map/ppermute | solution.py:24
  138.0 6.9 %collective-permute-start.36 = (bf16[48,512]{1,0:T(8,128)(2,1)S(1)}, bf16[48,512]{1,0:T(8,128)(2,1)S(1)}, u32[]{:S(2)}, u32[]{:S(2)}) collective-permute-start(bf16[48,512]{1,0:T(8,128)(2,1)S(1)} %get-tuple-element.56), channel_id=1, source_target_pairs={{0,2},{1,3},{2,0},{3,1},{4,6},{5,7},{6,4},{7,5},{8,10},{9,11},{10,... | collective-permute-start | bytes 147464 | tf_op jit(solution)/shard_map/ppermute | solution.py:24

commit v3 on v2

--- a/solution.py
+++ b/solution.py
@@ -11,6 +11,8 @@
 F32 = jnp.float32
 N = 16
 CHUNKS = 3
+TURNS = [(0, 0), (1, 0), (0, 1), (2, 0), (1, 1), (2, 1), (0, 2), (1, 2)]
+TURNS += [(0, 3), (2, 2), (1, 3), (0, 4), (2, 3), (1, 4), (2, 4)]
 FIRST = (1, 3)
 SECOND = (3, 1)
 
@@ -168,15 +170,13 @@
 
 def gather_tokens(t, gate_weight, up_weight):
     t1, t2, t3 = (exchange(t, z=m) for m in (1, 2, 3))
-    first = join(t, t1)
-    gate_weight, _ = tie(gate_weight, first)
-    weight = pack(gate_weight, up_weight)
-    t3, weight = tie(t3, weight)
     pieces = []
-    for h in first, join(t2, t3):
+    for h in join(t, t1), join(t2, t3):
         p = exchange(h, masks_x=FIRST)
-        pieces += [h, p, exchange(join(h, p), masks_x=SECOND)]
-    return pieces, weight
+        both = join(h, p)
+        pieces += [h, p, exchange(both, masks_x=SECOND)]
+    gate_weight, _ = tie(gate_weight, both)
+    return pieces, pack(gate_weight, up_weight)
 
 
 def halve(stays, got, size):
@@ -185,29 +185,34 @@
 
 
 def scatter_hidden(chunks, weight, rows):
-    stays, got, sent = [None] * CHUNKS, [None] * CHUNKS, None
-    for c, picked in enumerate(chunks):
-        s = dot(picked, weight)
-        stays[c], sent = s[8 * rows :], s[: 8 * rows]
-        got[c] = exchange(sent, core=1)
-    for size, how in (4, dict(masks_y=FIRST)), (2, dict(masks_y=SECOND)), (1, dict(zhi=1)):
-        for c in range(CHUNKS):
-            got[c], _ = tie(got[c], sent)
-            stays[c], sent = halve(stays[c], got[c], size * rows)
-            got[c] = exchange(sent, **how)
-    hidden = [silu(stays[0], got[0])]
-    for c in range(1, CHUNKS):
-        got[c], _ = tie(got[c], hidden[-1])
-        hidden.append(silu(stays[c], got[c]))
-    return hidden
-
-
-def gather_hidden(hidden):
-    half = [exchange(h, zhi=1) for h in hidden]
+    stays, got = [None] * CHUNKS, [None] * CHUNKS
+
+    def step(c, k, turn):
+        if k == 0:
+            picked = chunks[c] if turn is None else tie(chunks[c], turn)[0]
+            s = dot(picked, weight)
+            stays[c], sent, how = s[8 * rows :], s[: 8 * rows], dict(core=1)
+        else:
+            got[c], _ = tie(got[c], turn)
+            if k == 4:
+                stays[c] = sent = silu(stays[c], got[c])
+                how = dict(zhi=1)
+            else:
+                size, how = [(4, dict(masks_y=FIRST)), (2, dict(masks_y=SECOND)), (1, dict(zhi=1))][k - 1]
+                stays[c], sent = halve(stays[c], got[c], size * rows)
+        got[c] = exchange(sent, **how)
+        return sent
+
+    turn = None
+    for c, k in TURNS:
+        turn = step(c, k, turn)
+    return stays, got
+
+
+def gather_hidden(own, other):
     halves = []
-    for h in join(*hidden), None:
-        if h is None:
-            h = join(*half)
+    for hidden in own, other:
+        h = join(*hidden)
         h = join(h, exchange(h, masks_y=SECOND))
         halves.append(join(h, exchange(h, masks_y=FIRST)))
     return halves + [exchange(h, core=1) for h in halves]
@@ -238,7 +243,7 @@
     rows = tokens.shape[0]
     pieces, weight = gather_tokens(tokens, gate_weight, up_weight)
     hidden = scatter_hidden(pick(pieces, rows // CHUNKS), weight, rows // CHUNKS)
-    return scatter_out(place(gather_hidden(hidden), rows), down_weight, rows)
+    return scatter_out(place(gather_hidden(*hidden), rows), down_weight, rows)
 
 
 def solution(mesh):

time: 147 us -> 140 us (0.952)
  starting transfers between devices: 62.1 us -> 57.1 us
  waiting for transfers between devices: 64.3 us -> 61.6 us
    ppermute x38, starting transfers between devices: 62.1 us -> 57.1 us  [exchange(): return lax.ppermute(value, ('gx', 'gy'), pairs)]
    ppermute x38, waiting for transfers between devices: 64.3 us -> 61.6 us  [exchange(): return lax.ppermute(value, ('gx', 'gy'), pairs)]
  transfers between devices with their start and end apart: 38 -> 38, of which waited for: 20 -> 22; matrix products, arithmetic and copies ran while one was open for 5% -> 5% of each run, Pallas kernels for 1% -> 1%
where the time goes in v3:
time: 140 us; the launch traced here: 138 us
  waiting for transfers between devices  61.6 us (44%)
  starting transfers between devices  57.1 us (41%)
  matrix products  8.99 us (6%)
  local copies, waits for them, and re-layouts  5.32 us (4%)
  Pallas kernels  2.35 us (2%)
  other arithmetic  2.07 us (1%)
    ppermute x38, waiting for transfers between devices, exchange(): return lax.ppermute(value, ('gx', 'gy'), pairs)  61.6 us
    ppermute x38, starting transfers between devices, exchange(): return lax.ppermute(value, ('gx', 'gy'), pairs)  57.1 us
    dot_general x5, matrix products, dot(): return jnp.dot(a, b, preferred_element_type=F32).astype(BF)  8.99 us
    unnamed x8, local copies, waits for them, and re-layouts  4.86 us
  transfers between devices with their start and end apart: 38, of which 22 were waited for; matrix products, arithmetic and copies ran while one was open for 5% of the time, Pallas kernels for 1%

profile of v3, /device:TPU:24, one launch (start us, length us, event | category | flops | bytes accessed | tf_op | source)
XLA Modules:
  0.0 137.9 jit_solution(4801934717452210866)
XLA Ops:
  0.0 1.9 %collective-permute-start = (bf16[48,1024]{1,0:T(8,128)(2,1)}, bf16[48,1024]{1,0:T(8,128)(2,1)S(1)}, u32[]{:S(2)}, u32[]{:S(2)}) collective-permute-start(bf16[48,1024]{1,0:T(8,128)(2,1)} %refs_0_.1), channel_id=1, source_target_pairs={{0,1},{1,0},{2,3},{3,2},{4,5},{5,4},{6,7},{7,6},{8,9},{9,8},{10,11... | collective-permute-start | bytes 294920 | tf_op jit(solution)/shard_map/ppermute | solution.py:26
  1.9 2.8 %collective-permute-start.4 = (bf16[48,1024]{1,0:T(8,128)(2,1)}, bf16[48,1024]{1,0:T(8,128)(2,1)S(1)}, u32[]{:S(2)}, u32[]{:S(2)}) collective-permute-start(bf16[48,1024]{1,0:T(8,128)(2,1)} %refs_0_.1), channel_id=1, source_target_pairs={{0,3},{1,2},{2,1},{3,0},{4,7},{5,6},{6,5},{7,4},{8,11},{9,10},{10,... | collective-permute-start | bytes 294920 | tf_op jit(solution)/shard_map/ppermute | solution.py:26
  6.1 1.6 %collective-permute-start.1 = (bf16[96,1024]{1,0:T(8,128)(2,1)S(1)}, bf16[96,1024]{1,0:T(8,128)(2,1)S(1)}, u32[]{:S(2)}, u32[]{:S(2)}) collective-permute-start(bf16[96,1024]{1,0:T(8,128)(2,1)S(1)} %join.10.refs_0_), channel_id=1, source_target_pairs={{0,4},{1,5},{2,6},{3,7},{4,0},{5,1},{6,2},{7,3},{8,12},{9,13},{10,... | collective-permute-start | bytes 589832 | tf_op jit(solution)/shard_map/ppermute | solution.py:26
  7.7 3.1 %collective-permute-done.4.refs_1_ = bf16[48,1024]{1,0:T(8,128)(2,1)S(1)} collective-permute-done((bf16[48,1024]{1,0:T(8,128)(2,1)}, bf16[48,1024]{1,0:T(8,128)(2,1)S(1)}, u32[]{:S(2)}, u32[]{:S(2)}) %collective-permute-start.4) | collective-permute-done | bytes 98336 | tf_op jit(solution)/shard_map/ppermute | solution.py:26
  10.8 3.5 %collective-permute-done.3.refs_0_ = bf16[48,1024]{1,0:T(8,128)(2,1)S(1)} collective-permute-done((bf16[48,1024]{1,0:T(8,128)(2,1)}, bf16[48,1024]{1,0:T(8,128)(2,1)S(1)}, u32[]{:S(2)}, u32[]{:S(2)}) %collective-permute-start.3) | collective-permute-done | bytes 98336 | tf_op jit(solution)/shard_map/ppermute | solution.py:26
  14.3 1.6 %collective-permute-start.5 = (bf16[96,1024]{1,0:T(8,128)(2,1)S(1)}, bf16[96,1024]{1,0:T(8,128)(2,1)S(1)}, u32[]{:S(2)}, u32[]{:S(2)}) collective-permute-start(bf16[96,1024]{1,0:T(8,128)(2,1)S(1)} %join.12.refs_0_.refs_3_), channel_id=1, source_target_pairs={{0,4},{1,5},{2,6},{3,7},{4,0},{5,1},{6,2},{7,3},{8,12},{9,13},{10,... | collective-permute-start | bytes 589832 | tf_op jit(solution)/shard_map/ppermute | solution.py:26
  15.9 2.2 %collective-permute-start.2 = (bf16[192,1024]{1,0:T(8,128)(2,1)S(1)}, bf16[192,1024]{1,0:T(8,128)(2,1)S(1)}, u32[]{:S(2)}, u32[]{:S(2)}) collective-permute-start(bf16[192,1024]{1,0:T(8,128)(2,1)S(1)} %join.11), channel_id=1, source_target_pairs={{0,12},{1,13},{2,14},{3,15},{4,8},{5,9},{6,10},{7,11},{8,4},{9,5},... | collective-permute-start | bytes 1179656 | tf_op jit(solution)/shard_map/ppermute | solution.py:26
  18.1 3.1 %collective-permute-done.5.refs_1_.refs_4_ = bf16[96,1024]{1,0:T(8,128)(2,1)S(1)} collective-permute-done((bf16[96,1024]{1,0:T(8,128)(2,1)S(1)}, bf16[96,1024]{1,0:T(8,128)(2,1)S(1)}, u32[]{:S(2)}, u32[]{:S(2)}) %collective-permute-start.5) | collective-permute-done | bytes 196640 | tf_op jit(solution)/shard_map/ppermute | solution.py:26
  21.2 3.9 %collective-permute-start.6 = (bf16[192,1024]{1,0:T(8,128)(2,1)S(1)}, bf16[192,1024]{1,0:T(8,128)(2,1)S(1)}, u32[]{:S(2)}, u32[]{:S(2)}) collective-permute-start(bf16[192,1024]{1,0:T(8,128)(2,1)S(1)} %join.13), channel_id=1, source_target_pairs={{0,12},{1,13},{2,14},{3,15},{4,8},{5,9},{6,10},{7,11},{8,4},{9,5},... | collective-permute-start | bytes 1179656 | tf_op jit(solution)/shard_map/ppermute | solution.py:26
  25.0 2.0 %copy-done = bf16[1024,1664]{1,0:T(8,128)(2,1)S(1)} copy-done((bf16[1024,1664]{1,0:T(8,128)(2,1)S(1)}, bf16[1024,1664]{1,0:T(8,128)(2,1)}, u32[]{:S(2)}) %copy-start) | copy-done | bytes 3407896
  27.0 2.0 %copy-done.1 = bf16[1024,1664]{1,0:T(8,128)(2,1)S(1)} copy-done((bf16[1024,1664]{1,0:T(8,128)(2,1)S(1)}, bf16[1024,1664]{1,0:T(8,128)(2,1)}, u32[]{:S(2)}) %copy-start.1) | copy-done | bytes 3407896
  29.0 1.5 %pack.1 = bf16[1024,3328]{1,0:T(8,128)(2,1)S(1)} custom-call(bf16[1024,1664]{1,0:T(8,128)(2,1)S(1)} %copy-done, bf16[1024,1664]{1,0:T(8,128)(2,1)S(1)} %copy-done.1), custom_call_target="tpu_custom_call" | custom-call | bytes 13631488 | tf_op jit(solution)/shard_map/pack/pallas_call | solution.py:91
  31.0 1.9 %convolution_convert_fusion.2 = bf16[256,3328]{1,0:T(8,128)(2,1)S(1)} fusion(bf16[256,1024]{1,0:T(8,128)(2,1)S(1)} %get-tuple-element.26, bf16[1024,3328]{1,0:T(8,128)(2,1)S(1)} %pack.1), kind=kOutput, calls=%fused_computation.2 | convolution fusion | flops 1745682432 | bytes 9043968 | tf_op jit(solution)/shard_map/dot_general | solution.py:164
  33.1 1.9 %convolution_convert_fusion.1 = bf16[256,3328]{1,0:T(8,128)(2,1)S(1)} fusion(bf16[256,1024]{1,0:T(8,128)(2,1)S(1)} %get-tuple-element.29, bf16[1024,3328]{1,0:T(8,128)(2,1)S(1)} %pack.1), kind=kOutput, calls=%fused_computation.1 | convolution fusion | flops 1745682432 | bytes 9043968 | tf_op jit(solution)/shard_map/dot_general | solution.py:164
  37.0 1.9 %convolution_convert_fusion = bf16[256,3328]{1,0:T(8,128)(2,1)S(1)} fusion(bf16[256,1024]{1,0:T(8,128)(2,1)S(1)} %get-tuple-element.32, bf16[1024,3328]{1,0:T(8,128)(2,1)S(1)} %pack.1), kind=kOutput, calls=%fused_computation | convolution fusion | flops 1745682432 | bytes 9043968 | tf_op jit(solution)/shard_map/dot_general | solution.py:164
  39.3 1.4 collective-permute-start.12
  41.7 1.4 collective-permute-start.15
  43.1 1.3 collective-permute-done.8
  44.8 5.7 %collective-permute-done.12 = bf16[64,3328]{1,0:T(8,128)(2,1)S(1)} collective-permute-done((bf16[64,3328]{1,0:T(8,128)(2,1)S(1)}, bf16[64,3328]{1,0:T(8,128)(2,1)S(1)}, u32[]{:S(2)}, u32[]{:S(2)}) %collective-permute-start.12) | collective-permute-done | bytes 426016 | tf_op jit(solution)/shard_map/ppermute | solution.py:26
  50.7 1.3 collective-permute-start.14
  52.0 2.0 %collective-permute-done.11 = bf16[32,3328]{1,0:T(8,128)(2,1)S(1)} collective-permute-done((bf16[32,3328]{1,0:T(8,128)(2,1)S(1)}, bf16[32,3328]{1,0:T(8,128)(2,1)S(1)}, u32[]{:S(2)}, u32[]{:S(2)}) %collective-permute-start.11) | collective-permute-done | bytes 213024 | tf_op jit(solution)/shard_map/ppermute | solution.py:26
  54.1 5.6 %collective-permute-start.13 = (bf16[16,3328]{1,0:T(8,128)(2,1)S(1)}, bf16[16,3328]{1,0:T(8,128)(2,1)S(1)}, u32[]{:S(2)}, u32[]{:S(2)}) collective-permute-start(bf16[16,3328]{1,0:T(8,128)(2,1)S(1)} %get-tuple-element.51), channel_id=1, source_target_pairs={{0,128},{1,129},{2,130},{3,131},{4,132},{5,133},{6,134},{7,135},{8... | collective-permute-start | bytes 319496 | tf_op jit(solution)/shard_map/ppermute | solution.py:26
  60.2 4.6 %collective-permute-start.16 = (bf16[16,3328]{1,0:T(8,128)(2,1)S(1)}, bf16[16,3328]{1,0:T(8,128)(2,1)S(1)}, u32[]{:S(2)}, u32[]{:S(2)}) collective-permute-start(bf16[16,3328]{1,0:T(8,128)(2,1)S(1)} %get-tuple-element.50), channel_id=1, source_target_pairs={{0,128},{1,129},{2,130},{3,131},{4,132},{5,133},{6,134},{7,135},{8... | collective-permute-start | bytes 319496 | tf_op jit(solution)/shard_map/ppermute | solution.py:26
  64.9 2.1 %collective-permute-done.17 = bf16[32,3328]{1,0:T(8,128)(2,1)S(1)} collective-permute-done((bf16[32,3328]{1,0:T(8,128)(2,1)S(1)}, bf16[32,3328]{1,0:T(8,128)(2,1)S(1)}, u32[]{:S(2)}, u32[]{:S(2)}) %collective-permute-start.17) | collective-permute-done | bytes 213024 | tf_op jit(solution)/shard_map/ppermute | solution.py:26
  67.0 4.0 %collective-permute-start.18 = (bf16[16,3328]{1,0:T(8,128)(2,1)S(1)}, bf16[16,3328]{1,0:T(8,128)(2,1)S(1)}, u32[]{:S(2)}, u32[]{:S(2)}) collective-permute-start(bf16[16,3328]{1,0:T(8,128)(2,1)S(1)} %get-tuple-element.48), channel_id=1, source_target_pairs={{0,128},{1,129},{2,130},{3,131},{4,132},{5,133},{6,134},{7,135},{8... | collective-permute-start | bytes 319496 | tf_op jit(solution)/shard_map/ppermute | solution.py:26
  71.0 2.0 %collective-permute-start.21 = (bf16[16,1664]{1,0:T(8,128)(2,1)S(1)}, bf16[16,1664]{1,0:T(8,128)(2,1)S(1)}, u32[]{:S(2)}, u32[]{:S(2)}) collective-permute-start(bf16[16,1664]{1,0:T(8,128)(2,1)S(1)} %silu.3.refs_0_), channel_id=1, source_target_pairs={{0,128},{1,129},{2,130},{3,131},{4,132},{5,133},{6,134},{7,135},{8... | collective-permute-start | bytes 159752 | tf_op jit(solution)/shard_map/ppermute | solution.py:26
  73.1 4.0 %collective-permute-start.22 = (bf16[16,1664]{1,0:T(8,128)(2,1)S(1)}, bf16[16,1664]{1,0:T(8,128)(2,1)S(1)}, u32[]{:S(2)}, u32[]{:S(2)}) collective-permute-start(bf16[16,1664]{1,0:T(8,128)(2,1)S(1)} %silu.4.refs_1_), channel_id=1, source_target_pairs={{0,128},{1,129},{2,130},{3,131},{4,132},{5,133},{6,134},{7,135},{8... | collective-permute-start | bytes 159752 | tf_op jit(solution)/shard_map/ppermute | solution.py:26
  77.1 1.8 %collective-permute-done.18.b_ref = bf16[16,3328]{1,0:T(8,128)(2,1)S(1)} collective-permute-done((bf16[16,3328]{1,0:T(8,128)(2,1)S(1)}, bf16[16,3328]{1,0:T(8,128)(2,1)S(1)}, u32[]{:S(2)}, u32[]{:S(2)}) %collective-permute-start.18) | collective-permute-done | bytes 106528 | tf_op jit(solution)/shard_map/ppermute | solution.py:26
  78.9 2.4 %collective-permute-start.23 = (bf16[16,1664]{1,0:T(8,128)(2,1)S(1)}, bf16[16,1664]{1,0:T(8,128)(2,1)S(1)}, u32[]{:S(2)}, u32[]{:S(2)}) collective-permute-start(bf16[16,1664]{1,0:T(8,128)(2,1)S(1)} %silu.5.refs_2_), channel_id=1, source_target_pairs={{0,128},{1,129},{2,130},{3,131},{4,132},{5,133},{6,134},{7,135},{8... | collective-permute-start | bytes 159752 | tf_op jit(solution)/shard_map/ppermute | solution.py:26
  82.4 4.7 %collective-permute-done.23.refs_2_ = bf16[16,1664]{1,0:T(8,128)(2,1)S(1)} collective-permute-done((bf16[16,1664]{1,0:T(8,128)(2,1)S(1)}, bf16[16,1664]{1,0:T(8,128)(2,1)S(1)}, u32[]{:S(2)}, u32[]{:S(2)}) %collective-permute-start.23) | collective-permute-done | bytes 53280 | tf_op jit(solution)/shard_map/ppermute | solution.py:26
  87.1 1.3 collective-permute-start.24
  88.3 1.3 collective-permute-done.19.refs_1_
  89.8 5.6 %collective-permute-done.24.refs_1_ = bf16[48,1664]{1,0:T(8,128)(2,1)S(1)} collective-permute-done((bf16[48,1664]{1,0:T(8,128)(2,1)S(1)}, bf16[48,1664]{1,0:T(8,128)(2,1)S(1)}, u32[]{:S(2)}, u32[]{:S(2)}) %collective-permute-start.24) | collective-permute-done | bytes 159776 | tf_op jit(solution)/shard_map/ppermute | solution.py:26
  95.5 1.3 collective-permute-done.20.refs_1_
  97.1 5.3 %collective-permute-done.25.refs_1_ = bf16[96,1664]{1,0:T(8,128)(2,1)S(1)} collective-permute-done((bf16[96,1664]{1,0:T(8,128)(2,1)S(1)}, bf16[96,1664]{1,0:T(8,128)(2,1)S(1)}, u32[]{:S(2)}, u32[]{:S(2)}) %collective-permute-start.25) | collective-permute-done | bytes 319520 | tf_op jit(solution)/shard_map/ppermute | solution.py:26
  102.6 2.1 %collective-permute-done.27.refs_3_ = bf16[192,1664]{1,0:T(8,128)(2,1)S(1)} collective-permute-done((bf16[192,1664]{1,0:T(8,128)(2,1)S(1)}, bf16[192,1664]{1,0:T(8,128)(2,1)S(1)}, u32[]{:S(2)}, u32[]{:S(2)}) %collective-permute-start.27) | collective-permute-done | bytes 639008 | tf_op jit(solution)/shard_map/ppermute | solution.py:26
  105.0 1.6 %fusion.4 = bf16[768,512]{1,0:T(8,128)(2,1)S(1)} fusion(bf16[768,1664]{1,0:T(8,128)(2,1)S(1)} %place.1, bf16[1664,1024]{1,0:T(8,128)(2,1)S(1)} %copy-done.3), kind=kOutput, calls=%fused_computation.10 | convolution fusion | flops 1309016064 | bytes 5046272 | tf_op jit(solution)/shard_map/dot_general | solution.py:164
  106.6 3.3 %collective-permute-start.28 = (bf16[384,512]{1,0:T(8,128)(2,1)S(1)}, bf16[384,512]{1,0:T(8,128)(2,1)S(1)}, u32[]{:S(2)}, u32[]{:S(2)}) collective-permute-start(bf16[384,512]{1,0:T(8,128)(2,1)S(1)} %slice.193), channel_id=1, source_target_pairs={{0,12},{1,13},{2,14},{3,15},{4,8},{5,9},{6,10},{7,11},{8,4},{9,5},... | collective-permute-start | bytes 1179656 | tf_op jit(solution)/shard_map/ppermute | solution.py:26
  109.9 1.6 %fusion.7 = bf16[768,512]{1,0:T(8,128)(2,1)S(1)} fusion(bf16[768,1664]{1,0:T(8,128)(2,1)S(1)} %place.1, bf16[1664,1024]{1,0:T(8,128)(2,1)S(1)} %copy-done.3), kind=kOutput, calls=%fused_computation.11 | convolution fusion | flops 1309016064 | bytes 5046272 | tf_op jit(solution)/shard_map/dot_general | solution.py:164
  111.6 4.0 %collective-permute-done.28 = bf16[384,512]{1,0:T(8,128)(2,1)S(1)} collective-permute-done((bf16[384,512]{1,0:T(8,128)(2,1)S(1)}, bf16[384,512]{1,0:T(8,128)(2,1)S(1)}, u32[]{:S(2)}, u32[]{:S(2)}) %collective-permute-start.28) | collective-permute-done | bytes 393248 | tf_op jit(solution)/shard_map/ppermute | solution.py:26
  115.9 6.8 %collective-permute-done.29 = bf16[384,512]{1,0:T(8,128)(2,1)S(1)} collective-permute-done((bf16[384,512]{1,0:T(8,128)(2,1)S(1)}, bf16[384,512]{1,0:T(8,128)(2,1)S(1)}, u32[]{:S(2)}, u32[]{:S(2)}) %collective-permute-start.29) | collective-permute-done | bytes 393248 | tf_op jit(solution)/shard_map/ppermute | solution.py:26
  123.1 2.0 %collective-permute-start.33 = (bf16[48,512]{1,0:T(8,128)(2,1)S(1)}, bf16[48,512]{1,0:T(8,128)(2,1)S(1)}, u32[]{:S(2)}, u32[]{:S(2)}) collective-permute-start(bf16[48,512]{1,0:T(8,128)(2,1)S(1)} %get-tuple-element.54), channel_id=1, source_target_pairs={{0,3},{1,2},{2,1},{3,0},{4,7},{5,6},{6,5},{7,4},{8,11},{9,10},{10,... | collective-permute-start | bytes 147464 | tf_op jit(solution)/shard_map/ppermute | solution.py:26
  125.1 1.5 %collective-permute-start.32 = (bf16[48,512]{1,0:T(8,128)(2,1)S(1)}, bf16[48,512]{1,0:T(8,128)(2,1)S(1)}, u32[]{:S(2)}, u32[]{:S(2)}) collective-permute-start(bf16[48,512]{1,0:T(8,128)(2,1)S(1)} %get-tuple-element.55), channel_id=1, source_target_pairs={{0,2},{1,3},{2,0},{3,1},{4,6},{5,7},{6,4},{7,5},{8,10},{9,11},{10,... | collective-permute-start | bytes 147464 | tf_op jit(solution)/shard_map/ppermute | solution.py:26
  126.6 2.1 %collective-permute-done.34 = bf16[192,512]{1,0:T(8,128)(2,1)S(1)} collective-permute-done((bf16[192,512]{1,0:T(8,128)(2,1)S(1)}, bf16[192,512]{1,0:T(8,128)(2,1)S(1)}, u32[]{:S(2)}, u32[]{:S(2)}) %collective-permute-start.34) | collective-permute-done | bytes 196640 | tf_op jit(solution)/shard_map/ppermute | solution.py:26
  128.8 2.0 %collective-permute-start.37 = (bf16[48,512]{1,0:T(8,128)(2,1)S(1)}, bf16[48,512]{1,0:T(8,128)(2,1)S(1)}, u32[]{:S(2)}, u32[]{:S(2)}) collective-permute-start(bf16[48,512]{1,0:T(8,128)(2,1)S(1)} %get-tuple-element.57), channel_id=1, source_target_pairs={{0,3},{1,2},{2,1},{3,0},{4,7},{5,6},{6,5},{7,4},{8,11},{9,10},{10,... | collective-permute-start | bytes 147464 | tf_op jit(solution)/shard_map/ppermute | solution.py:26
  130.8 1.5 %collective-permute-start.36 = (bf16[48,512]{1,0:T(8,128)(2,1)S(1)}, bf16[48,512]{1,0:T(8,128)(2,1)S(1)}, u32[]{:S(2)}, u32[]{:S(2)}) collective-permute-start(bf16[48,512]{1,0:T(8,128)(2,1)S(1)} %get-tuple-element.58), channel_id=1, source_target_pairs={{0,2},{1,3},{2,0},{3,1},{4,6},{5,7},{6,4},{7,5},{8,10},{9,11},{10,... | collective-permute-start | bytes 147464 | tf_op jit(solution)/shard_map/ppermute | solution.py:26
  133.3 2.0 %collective-permute-done.37 = bf16[48,512]{1,0:T(8,128)(2,1)S(1)} collective-permute-done((bf16[48,512]{1,0:T(8,128)(2,1)S(1)}, bf16[48,512]{1,0:T(8,128)(2,1)S(1)}, u32[]{:S(2)}, u32[]{:S(2)}) %collective-permute-start.37) | collective-permute-done | bytes 49184 | tf_op jit(solution)/shard_map/ppermute | solution.py:26
  135.3 2.0 %collective-permute-done.36 = bf16[48,512]{1,0:T(8,128)(2,1)S(1)} collective-permute-done((bf16[48,512]{1,0:T(8,128)(2,1)S(1)}, bf16[48,512]{1,0:T(8,128)(2,1)S(1)}, u32[]{:S(2)}, u32[]{:S(2)}) %collective-permute-start.36) | collective-permute-done | bytes 49184 | tf_op jit(solution)/shard_map/ppermute | solution.py:26
  (91 shorter events, 11.5 us)
Async XLA Ops:
  0.0 5.2 %collective-permute-start = (bf16[48,1024]{1,0:T(8,128)(2,1)}, bf16[48,1024]{1,0:T(8,128)(2,1)S(1)}, u32[]{:S(2)}, u32[]{:S(2)}) collective-permute-start(bf16[48,1024]{1,0:T(8,128)(2,1)} %refs_0_.1), channel_id=1, source_target_pairs={{0,1},{1,0},{2,3},{3,2},{4,5},{5,4},{6,7},{7,6},{8,9},{9,8},{10,11... | collective-permute-start | bytes 294920 | tf_op jit(solution)/shard_map/ppermute | solution.py:26
  1.9 8.9 %collective-permute-start.4 = (bf16[48,1024]{1,0:T(8,128)(2,1)}, bf16[48,1024]{1,0:T(8,128)(2,1)S(1)}, u32[]{:S(2)}, u32[]{:S(2)}) collective-permute-start(bf16[48,1024]{1,0:T(8,128)(2,1)} %refs_0_.1), channel_id=1, source_target_pairs={{0,3},{1,2},{2,1},{3,0},{4,7},{5,6},{6,5},{7,4},{8,11},{9,10},{10,... | collective-permute-start | bytes 294920 | tf_op jit(solution)/shard_map/ppermute | solution.py:26
  4.7 9.5 %collective-permute-start.3 = (bf16[48,1024]{1,0:T(8,128)(2,1)}, bf16[48,1024]{1,0:T(8,128)(2,1)S(1)}, u32[]{:S(2)}, u32[]{:S(2)}) collective-permute-start(bf16[48,1024]{1,0:T(8,128)(2,1)} %refs_0_.1), channel_id=1, source_target_pairs={{0,2},{1,3},{2,0},{3,1},{4,6},{5,7},{6,4},{7,5},{8,10},{9,11},{10,... | collective-permute-start | bytes 294920 | tf_op jit(solution)/shard_map/ppermute | solution.py:26
  5.2 0.9 copy-start.2
  6.1 9.7 %collective-permute-start.1 = (bf16[96,1024]{1,0:T(8,128)(2,1)S(1)}, bf16[96,1024]{1,0:T(8,128)(2,1)S(1)}, u32[]{:S(2)}, u32[]{:S(2)}) collective-permute-start(bf16[96,1024]{1,0:T(8,128)(2,1)S(1)} %join.10.refs_0_), channel_id=1, source_target_pairs={{0,4},{1,5},{2,6},{3,7},{4,0},{5,1},{6,2},{7,3},{8,12},{9,13},{10,... | collective-permute-start | bytes 589832 | tf_op jit(solution)/shard_map/ppermute | solution.py:26
  14.3 6.9 %collective-permute-start.5 = (bf16[96,1024]{1,0:T(8,128)(2,1)S(1)}, bf16[96,1024]{1,0:T(8,128)(2,1)S(1)}, u32[]{:S(2)}, u32[]{:S(2)}) collective-permute-start(bf16[96,1024]{1,0:T(8,128)(2,1)S(1)} %join.12.refs_0_.refs_3_), channel_id=1, source_target_pairs={{0,4},{1,5},{2,6},{3,7},{4,0},{5,1},{6,2},{7,3},{8,12},{9,13},{10,... | collective-permute-start | bytes 589832 | tf_op jit(solution)/shard_map/ppermute | solution.py:26
  15.9 14.5 %collective-permute-start.2 = (bf16[192,1024]{1,0:T(8,128)(2,1)S(1)}, bf16[192,1024]{1,0:T(8,128)(2,1)S(1)}, u32[]{:S(2)}, u32[]{:S(2)}) collective-permute-start(bf16[192,1024]{1,0:T(8,128)(2,1)S(1)} %join.11), channel_id=1, source_target_pairs={{0,12},{1,13},{2,14},{3,15},{4,8},{5,9},{6,10},{7,11},{8,4},{9,5},... | collective-permute-start | bytes 1179656 | tf_op jit(solution)/shard_map/ppermute | solution.py:26
  21.2 9.6 %collective-permute-start.6 = (bf16[192,1024]{1,0:T(8,128)(2,1)S(1)}, bf16[192,1024]{1,0:T(8,128)(2,1)S(1)}, u32[]{:S(2)}, u32[]{:S(2)}) collective-permute-start(bf16[192,1024]{1,0:T(8,128)(2,1)S(1)} %join.13), channel_id=1, source_target_pairs={{0,12},{1,13},{2,14},{3,15},{4,8},{5,9},{6,10},{7,11},{8,4},{9,5},... | collective-permute-start | bytes 1179656 | tf_op jit(solution)/shard_map/ppermute | solution.py:26
  25.0 2.0 %copy-start = (bf16[1024,1664]{1,0:T(8,128)(2,1)S(1)}, bf16[1024,1664]{1,0:T(8,128)(2,1)}, u32[]{:S(2)}) copy-start(bf16[1024,1664]{1,0:T(8,128)(2,1)} %gate_ref) | copy-start | bytes 10223620
  27.0 2.0 %copy-start.1 = (bf16[1024,1664]{1,0:T(8,128)(2,1)S(1)}, bf16[1024,1664]{1,0:T(8,128)(2,1)}, u32[]{:S(2)}) copy-start(bf16[1024,1664]{1,0:T(8,128)(2,1)} %up_ref.1) | copy-start | bytes 10223620
  33.0 2.7 %collective-permute-start.7 = (bf16[128,3328]{1,0:T(8,128)(2,1)S(1)}, bf16[128,3328]{1,0:T(8,128)(2,1)S(1)}, u32[]{:S(2)}, u32[]{:S(2)}) collective-permute-start(bf16[128,3328]{1,0:T(8,128)(2,1)S(1)} %slice.169), channel_id=1, source_target_pairs={{0,16},{1,17},{2,18},{3,19},{4,20},{5,21},{6,22},{7,23},{8,24},{9,... | collective-permute-start | bytes 2555912 | tf_op jit(solution)/shard_map/ppermute | solution.py:26
  35.1 3.9 %collective-permute-start.10 = (bf16[128,3328]{1,0:T(8,128)(2,1)S(1)}, bf16[128,3328]{1,0:T(8,128)(2,1)S(1)}, u32[]{:S(2)}, u32[]{:S(2)}) collective-permute-start(bf16[128,3328]{1,0:T(8,128)(2,1)S(1)} %slice.170), channel_id=1, source_target_pairs={{0,16},{1,17},{2,18},{3,19},{4,20},{5,21},{6,22},{7,23},{8,24},{9,... | collective-permute-start | bytes 2555912 | tf_op jit(solution)/shard_map/ppermute | solution.py:26
  36.0 8.4 %collective-permute-start.8 = (bf16[64,3328]{1,0:T(8,128)(2,1)S(1)}, bf16[64,3328]{1,0:T(8,128)(2,1)S(1)}, u32[]{:S(2)}, u32[]{:S(2)}) collective-permute-start(bf16[64,3328]{1,0:T(8,128)(2,1)S(1)} %slice.172), channel_id=1, source_target_pairs={{0,32},{1,33},{2,34},{3,35},{4,36},{5,37},{6,38},{7,39},{8,40},{9,... | collective-permute-start | bytes 1277960 | tf_op jit(solution)/shard_map/ppermute | solution.py:26
  39.0 2.5 %collective-permute-start.9 = (bf16[128,3328]{1,0:T(8,128)(2,1)S(1)}, bf16[128,3328]{1,0:T(8,128)(2,1)S(1)}, u32[]{:S(2)}, u32[]{:S(2)}) collective-permute-start(bf16[128,3328]{1,0:T(8,128)(2,1)S(1)} %slice.174), channel_id=1, source_target_pairs={{0,16},{1,17},{2,18},{3,19},{4,20},{5,21},{6,22},{7,23},{8,24},{9,... | collective-permute-start | bytes 2555912 | tf_op jit(solution)/shard_map/ppermute | solution.py:26
  39.3 11.2 %collective-permute-start.12 = (bf16[64,3328]{1,0:T(8,128)(2,1)S(1)}, bf16[64,3328]{1,0:T(8,128)(2,1)S(1)}, u32[]{:S(2)}, u32[]{:S(2)}) collective-permute-start(bf16[64,3328]{1,0:T(8,128)(2,1)S(1)} %slice.176), channel_id=1, source_target_pairs={{0,32},{1,33},{2,34},{3,35},{4,36},{5,37},{6,38},{7,39},{8,40},{9,... | collective-permute-start | bytes 1277960 | tf_op jit(solution)/shard_map/ppermute | solution.py:26
  41.7 17.9 %collective-permute-start.15 = (bf16[64,3328]{1,0:T(8,128)(2,1)S(1)}, bf16[64,3328]{1,0:T(8,128)(2,1)S(1)}, u32[]{:S(2)}, u32[]{:S(2)}) collective-permute-start(bf16[64,3328]{1,0:T(8,128)(2,1)S(1)} %slice.177), channel_id=1, source_target_pairs={{0,32},{1,33},{2,34},{3,35},{4,36},{5,37},{6,38},{7,39},{8,40},{9,... | collective-permute-start | bytes 1277960 | tf_op jit(solution)/shard_map/ppermute | solution.py:26
  44.5 9.5 %collective-permute-start.11 = (bf16[32,3328]{1,0:T(8,128)(2,1)S(1)}, bf16[32,3328]{1,0:T(8,128)(2,1)S(1)}, u32[]{:S(2)}, u32[]{:S(2)}) collective-permute-start(bf16[32,3328]{1,0:T(8,128)(2,1)S(1)} %slice.179), channel_id=1, source_target_pairs={{0,96},{1,97},{2,98},{3,99},{4,100},{5,101},{6,102},{7,103},{8,104... | collective-permute-start | bytes 638984 | tf_op jit(solution)/shard_map/ppermute | solution.py:26
  50.7 9.4 %collective-permute-start.14 = (bf16[32,3328]{1,0:T(8,128)(2,1)S(1)}, bf16[32,3328]{1,0:T(8,128)(2,1)S(1)}, u32[]{:S(2)}, u32[]{:S(2)}) collective-permute-start(bf16[32,3328]{1,0:T(8,128)(2,1)S(1)} %slice.181), channel_id=1, source_target_pairs={{0,96},{1,97},{2,98},{3,99},{4,100},{5,101},{6,102},{7,103},{8,104... | collective-permute-start | bytes 638984 | tf_op jit(solution)/shard_map/ppermute | solution.py:26
  54.1 10.7 %collective-permute-start.13 = (bf16[16,3328]{1,0:T(8,128)(2,1)S(1)}, bf16[16,3328]{1,0:T(8,128)(2,1)S(1)}, u32[]{:S(2)}, u32[]{:S(2)}) collective-permute-start(bf16[16,3328]{1,0:T(8,128)(2,1)S(1)} %get-tuple-element.51), channel_id=1, source_target_pairs={{0,128},{1,129},{2,130},{3,131},{4,132},{5,133},{6,134},{7,135},{8... | collective-permute-start | bytes 319496 | tf_op jit(solution)/shard_map/ppermute | solution.py:26
  59.8 7.1 %collective-permute-start.17 = (bf16[32,3328]{1,0:T(8,128)(2,1)S(1)}, bf16[32,3328]{1,0:T(8,128)(2,1)S(1)}, u32[]{:S(2)}, u32[]{:S(2)}) collective-permute-start(bf16[32,3328]{1,0:T(8,128)(2,1)S(1)} %slice.186), channel_id=1, source_target_pairs={{0,96},{1,97},{2,98},{3,99},{4,100},{5,101},{6,102},{7,103},{8,104... | collective-permute-start | bytes 638984 | tf_op jit(solution)/shard_map/ppermute | solution.py:26
  60.2 12.9 %collective-permute-start.16 = (bf16[16,3328]{1,0:T(8,128)(2,1)S(1)}, bf16[16,3328]{1,0:T(8,128)(2,1)S(1)}, u32[]{:S(2)}, u32[]{:S(2)}) collective-permute-start(bf16[16,3328]{1,0:T(8,128)(2,1)S(1)} %get-tuple-element.50), channel_id=1, source_target_pairs={{0,128},{1,129},{2,130},{3,131},{4,132},{5,133},{6,134},{7,135},{8... | collective-permute-start | bytes 319496 | tf_op jit(solution)/shard_map/ppermute | solution.py:26
  67.0 11.8 %collective-permute-start.18 = (bf16[16,3328]{1,0:T(8,128)(2,1)S(1)}, bf16[16,3328]{1,0:T(8,128)(2,1)S(1)}, u32[]{:S(2)}, u32[]{:S(2)}) collective-permute-start(bf16[16,3328]{1,0:T(8,128)(2,1)S(1)} %get-tuple-element.48), channel_id=1, source_target_pairs={{0,128},{1,129},{2,130},{3,131},{4,132},{5,133},{6,134},{7,135},{8... | collective-permute-start | bytes 319496 | tf_op jit(solution)/shard_map/ppermute | solution.py:26
  71.0 11.4 %collective-permute-start.21 = (bf16[16,1664]{1,0:T(8,128)(2,1)S(1)}, bf16[16,1664]{1,0:T(8,128)(2,1)S(1)}, u32[]{:S(2)}, u32[]{:S(2)}) collective-permute-start(bf16[16,1664]{1,0:T(8,128)(2,1)S(1)} %silu.3.refs_0_), channel_id=1, source_target_pairs={{0,128},{1,129},{2,130},{3,131},{4,132},{5,133},{6,134},{7,135},{8... | collective-permute-start | bytes 159752 | tf_op jit(solution)/shard_map/ppermute | solution.py:26
  73.1 9.3 %collective-permute-start.22 = (bf16[16,1664]{1,0:T(8,128)(2,1)S(1)}, bf16[16,1664]{1,0:T(8,128)(2,1)S(1)}, u32[]{:S(2)}, u32[]{:S(2)}) collective-permute-start(bf16[16,1664]{1,0:T(8,128)(2,1)S(1)} %silu.4.refs_1_), channel_id=1, source_target_pairs={{0,128},{1,129},{2,130},{3,131},{4,132},{5,133},{6,134},{7,135},{8... | collective-permute-start | bytes 159752 | tf_op jit(solution)/shard_map/ppermute | solution.py:26
  78.9 8.1 %collective-permute-start.23 = (bf16[16,1664]{1,0:T(8,128)(2,1)S(1)}, bf16[16,1664]{1,0:T(8,128)(2,1)S(1)}, u32[]{:S(2)}, u32[]{:S(2)}) collective-permute-start(bf16[16,1664]{1,0:T(8,128)(2,1)S(1)} %silu.5.refs_2_), channel_id=1, source_target_pairs={{0,128},{1,129},{2,130},{3,131},{4,132},{5,133},{6,134},{7,135},{8... | collective-permute-start | bytes 159752 | tf_op jit(solution)/shard_map/ppermute | solution.py:26
  81.4 8.3 %collective-permute-start.19 = (bf16[48,1664]{1,0:T(8,128)(2,1)S(1)}, bf16[48,1664]{1,0:T(8,128)(2,1)S(1)}, u32[]{:S(2)}, u32[]{:S(2)}) collective-permute-start(bf16[48,1664]{1,0:T(8,128)(2,1)S(1)} %join.14.refs_0_), channel_id=1, source_target_pairs={{0,96},{1,97},{2,98},{3,99},{4,100},{5,101},{6,102},{7,103},{8,104... | collective-permute-start | bytes 479240 | tf_op jit(solution)/shard_map/ppermute | solution.py:26
  87.1 8.3 %collective-permute-start.24 = (bf16[48,1664]{1,0:T(8,128)(2,1)S(1)}, bf16[48,1664]{1,0:T(8,128)(2,1)S(1)}, u32[]{:S(2)}, u32[]{:S(2)}) collective-permute-start(bf16[48,1664]{1,0:T(8,128)(2,1)S(1)} %join.17.refs_0_), channel_id=1, source_target_pairs={{0,96},{1,97},{2,98},{3,99},{4,100},{5,101},{6,102},{7,103},{8,104... | collective-permute-start | bytes 479240 | tf_op jit(solution)/shard_map/ppermute | solution.py:26
  89.7 7.1 %collective-permute-start.20 = (bf16[96,1664]{1,0:T(8,128)(2,1)S(1)}, bf16[96,1664]{1,0:T(8,128)(2,1)S(1)}, u32[]{:S(2)}, u32[]{:S(2)}) collective-permute-start(bf16[96,1664]{1,0:T(8,128)(2,1)S(1)} %join.15.refs_0_), channel_id=1, source_target_pairs={{0,32},{1,33},{2,34},{3,35},{4,36},{5,37},{6,38},{7,39},{8,40},{9,... | collective-permute-start | bytes 958472 | tf_op jit(solution)/shard_map/ppermute | solution.py:26
  95.4 7.1 %collective-permute-start.25 = (bf16[96,1664]{1,0:T(8,128)(2,1)S(1)}, bf16[96,1664]{1,0:T(8,128)(2,1)S(1)}, u32[]{:S(2)}, u32[]{:S(2)}) collective-permute-start(bf16[96,1664]{1,0:T(8,128)(2,1)S(1)} %join.18.refs_0_), channel_id=1, source_target_pairs={{0,32},{1,33},{2,34},{3,35},{4,36},{5,37},{6,38},{7,39},{8,40},{9,... | collective-permute-start | bytes 958472 | tf_op jit(solution)/shard_map/ppermute | solution.py:26
  96.8 5.8 %collective-permute-start.26 = (bf16[192,1664]{1,0:T(8,128)(2,1)S(1)}, bf16[192,1664]{1,0:T(8,128)(2,1)S(1)}, u32[]{:S(2)}, u32[]{:S(2)}) collective-permute-start(bf16[192,1664]{1,0:T(8,128)(2,1)S(1)} %join.16.refs_0_), channel_id=1, source_target_pairs={{0,16},{1,17},{2,18},{3,19},{4,20},{5,21},{6,22},{7,23},{8,24},{9,... | collective-permute-start | bytes 1916936 | tf_op jit(solution)/shard_map/ppermute | solution.py:26
  102.5 2.5 %copy-start.3 = (bf16[1664,1024]{1,0:T(8,128)(2,1)S(1)}, bf16[1664,1024]{1,0:T(8,128)(2,1)}, u32[]{:S(2)}) copy-start(bf16[1664,1024]{1,0:T(8,128)(2,1)} %param.7) | copy-start | bytes 10223620
  102.5 2.2 %collective-permute-start.27 = (bf16[192,1664]{1,0:T(8,128)(2,1)S(1)}, bf16[192,1664]{1,0:T(8,128)(2,1)S(1)}, u32[]{:S(2)}, u32[]{:S(2)}) collective-permute-start(bf16[192,1664]{1,0:T(8,128)(2,1)S(1)} %join.19.refs_1_), channel_id=1, source_target_pairs={{0,16},{1,17},{2,18},{3,19},{4,20},{5,21},{6,22},{7,23},{8,24},{9,... | collective-permute-start | bytes 1916936 | tf_op jit(solution)/shard_map/ppermute | solution.py:26
  106.6 9.1 %collective-permute-start.28 = (bf16[384,512]{1,0:T(8,128)(2,1)S(1)}, bf16[384,512]{1,0:T(8,128)(2,1)S(1)}, u32[]{:S(2)}, u32[]{:S(2)}) collective-permute-start(bf16[384,512]{1,0:T(8,128)(2,1)S(1)} %slice.193), channel_id=1, source_target_pairs={{0,12},{1,13},{2,14},{3,15},{4,8},{5,9},{6,10},{7,11},{8,4},{9,5},... | collective-permute-start | bytes 1179656 | tf_op jit(solution)/shard_map/ppermute | solution.py:26
  111.5 11.2 %collective-permute-start.29 = (bf16[384,512]{1,0:T(8,128)(2,1)S(1)}, bf16[384,512]{1,0:T(8,128)(2,1)S(1)}, u32[]{:S(2)}, u32[]{:S(2)}) collective-permute-start(bf16[384,512]{1,0:T(8,128)(2,1)S(1)} %slice.194), channel_id=1, source_target_pairs={{0,12},{1,13},{2,14},{3,15},{4,8},{5,9},{6,10},{7,11},{8,4},{9,5},... | collective-permute-start | bytes 1179656 | tf_op jit(solution)/shard_map/ppermute | solution.py:26
  115.8 6.9 %collective-permute-start.30 = (bf16[192,512]{1,0:T(8,128)(2,1)S(1)}, bf16[192,512]{1,0:T(8,128)(2,1)S(1)}, u32[]{:S(2)}, u32[]{:S(2)}) collective-permute-start(bf16[192,512]{1,0:T(8,128)(2,1)S(1)} %slice.196), channel_id=1, source_target_pairs={{0,4},{1,5},{2,6},{3,7},{4,0},{5,1},{6,2},{7,3},{8,12},{9,13},{10,... | collective-permute-start | bytes 589832 | tf_op jit(solution)/shard_map/ppermute | solution.py:26
  122.9 5.8 %collective-permute-start.34 = (bf16[192,512]{1,0:T(8,128)(2,1)S(1)}, bf16[192,512]{1,0:T(8,128)(2,1)S(1)}, u32[]{:S(2)}, u32[]{:S(2)}) collective-permute-start(bf16[192,512]{1,0:T(8,128)(2,1)S(1)} %slice.203), channel_id=1, source_target_pairs={{0,4},{1,5},{2,6},{3,7},{4,0},{5,1},{6,2},{7,3},{8,12},{9,13},{10,... | collective-permute-start | bytes 589832 | tf_op jit(solution)/shard_map/ppermute | solution.py:26
  123.0 7.8 %collective-permute-start.31 = (bf16[48,512]{1,0:T(8,128)(2,1)S(1)}, bf16[48,512]{1,0:T(8,128)(2,1)S(1)}, u32[]{:S(2)}, u32[]{:S(2)}) collective-permute-start(bf16[48,512]{1,0:T(8,128)(2,1)S(1)} %get-tuple-element.53), channel_id=1, source_target_pairs={{0,1},{1,0},{2,3},{3,2},{4,5},{5,4},{6,7},{7,6},{8,9},{9,8},{10,11... | collective-permute-start | bytes 147464 | tf_op jit(solution)/shard_map/ppermute | solution.py:26
  123.1 9.2 %collective-permute-start.33 = (bf16[48,512]{1,0:T(8,128)(2,1)S(1)}, bf16[48,512]{1,0:T(8,128)(2,1)S(1)}, u32[]{:S(2)}, u32[]{:S(2)}) collective-permute-start(bf16[48,512]{1,0:T(8,128)(2,1)S(1)} %get-tuple-element.54), channel_id=1, source_target_pairs={{0,3},{1,2},{2,1},{3,0},{4,7},{5,6},{6,5},{7,4},{8,11},{9,10},{10,... | collective-permute-start | bytes 147464 | tf_op jit(solution)/shard_map/ppermute | solution.py:26
  125.1 7.2 %collective-permute-start.32 = (bf16[48,512]{1,0:T(8,128)(2,1)S(1)}, bf16[48,512]{1,0:T(8,128)(2,1)S(1)}, u32[]{:S(2)}, u32[]{:S(2)}) collective-permute-start(bf16[48,512]{1,0:T(8,128)(2,1)S(1)} %get-tuple-element.55), channel_id=1, source_target_pairs={{0,2},{1,3},{2,0},{3,1},{4,6},{5,7},{6,4},{7,5},{8,10},{9,11},{10,... | collective-permute-start | bytes 147464 | tf_op jit(solution)/shard_map/ppermute | solution.py:26
  128.7 4.6 %collective-permute-start.35 = (bf16[48,512]{1,0:T(8,128)(2,1)S(1)}, bf16[48,512]{1,0:T(8,128)(2,1)S(1)}, u32[]{:S(2)}, u32[]{:S(2)}) collective-permute-start(bf16[48,512]{1,0:T(8,128)(2,1)S(1)} %get-tuple-element.56), channel_id=1, source_target_pairs={{0,1},{1,0},{2,3},{3,2},{4,5},{5,4},{6,7},{7,6},{8,9},{9,8},{10,11... | collective-permute-start | bytes 147464 | tf_op jit(solution)/shard_map/ppermute | solution.py:26
  128.8 6.5 %collective-permute-start.37 = (bf16[48,512]{1,0:T(8,128)(2,1)S(1)}, bf16[48,512]{1,0:T(8,128)(2,1)S(1)}, u32[]{:S(2)}, u32[]{:S(2)}) collective-permute-start(bf16[48,512]{1,0:T(8,128)(2,1)S(1)} %get-tuple-element.57), channel_id=1, source_target_pairs={{0,3},{1,2},{2,1},{3,0},{4,7},{5,6},{6,5},{7,4},{8,11},{9,10},{10,... | collective-permute-start | bytes 147464 | tf_op jit(solution)/shard_map/ppermute | solution.py:26
  130.8 6.4 %collective-permute-start.36 = (bf16[48,512]{1,0:T(8,128)(2,1)S(1)}, bf16[48,512]{1,0:T(8,128)(2,1)S(1)}, u32[]{:S(2)}, u32[]{:S(2)}) collective-permute-start(bf16[48,512]{1,0:T(8,128)(2,1)S(1)} %get-tuple-element.58), channel_id=1, source_target_pairs={{0,2},{1,3},{2,0},{3,1},{4,6},{5,7},{6,4},{7,5},{8,10},{9,11},{10,... | collective-permute-start | bytes 147464 | tf_op jit(solution)/shard_map/ppermute | solution.py:26

commit v4 on v3

--- a/solution.py
+++ b/solution.py
@@ -11,8 +11,6 @@
 F32 = jnp.float32
 N = 16
 CHUNKS = 3
-TURNS = [(0, 0), (1, 0), (0, 1), (2, 0), (1, 1), (2, 1), (0, 2), (1, 2)]
-TURNS += [(0, 3), (2, 2), (1, 3), (0, 4), (2, 3), (1, 4), (2, 4)]
 FIRST = (1, 3)
 SECOND = (3, 1)
 
@@ -62,13 +60,13 @@
             out[pl.ds(k * rows, rows), :] = whole[pl.ds(source, rows), :]
 
 
-def place_kernel(rows, *refs):
+def place_kernel(rows, segments, *refs):
     *pieces, out_ref = refs
     me = lax.axis_index("gx")
-    for piece, (gx, z) in zip(pieces, [(me, 0), (me, 1), (me ^ 1, 0), (me ^ 1, 1)]):
-        for part, blocks in enumerate(kept(gx)):
+    for piece, core, z, stride, offset in segments:
+        for part, blocks in enumerate(kept(me ^ core)):
             target = pl.multiple_of(scattered_slot(me, blocks[z]) * rows, 16)
-            out_ref[pl.ds(target, rows), :] = piece[pl.ds(part * rows, rows), :]
+            out_ref[pl.ds(target, rows), :] = pieces[piece][pl.ds(part * stride + offset, rows), :]
 
 
 def pack_kernel(gate_ref, up_ref, out_ref, sems):
@@ -127,9 +125,9 @@
     )
 
 
-def place(pieces, rows):
+def place(pieces, rows, segments):
     shape = (N * rows, pieces[0].shape[1])
-    return in_vmem(functools.partial(place_kernel, rows), [shape], "place", *pieces)
+    return in_vmem(functools.partial(place_kernel, rows, segments), [shape], "place", *pieces)
 
 
 def silu_kernel(a_ref, b_ref, out_ref):
@@ -184,66 +182,98 @@
     return v[:size], v[size:]
 
 
-def scatter_hidden(chunks, weight, rows):
-    stays, got = [None] * CHUNKS, [None] * CHUNKS
-
-    def step(c, k, turn):
-        if k == 0:
-            picked = chunks[c] if turn is None else tie(chunks[c], turn)[0]
-            s = dot(picked, weight)
-            stays[c], sent, how = s[8 * rows :], s[: 8 * rows], dict(core=1)
-        else:
-            got[c], _ = tie(got[c], turn)
-            if k == 4:
-                stays[c] = sent = silu(stays[c], got[c])
-                how = dict(zhi=1)
-            else:
-                size, how = [(4, dict(masks_y=FIRST)), (2, dict(masks_y=SECOND)), (1, dict(zhi=1))][k - 1]
-                stays[c], sent = halve(stays[c], got[c], size * rows)
-        got[c] = exchange(sent, **how)
-        return sent
-
-    turn = None
-    for c, k in TURNS:
-        turn = step(c, k, turn)
-    return stays, got
-
-
-def gather_hidden(own, other):
-    halves = []
-    for hidden in own, other:
-        h = join(*hidden)
-        h = join(h, exchange(h, masks_y=SECOND))
-        halves.append(join(h, exchange(h, masks_y=FIRST)))
-    return halves + [exchange(h, core=1) for h in halves]
-
-
-def scatter_out(hidden, weight, rows):
-    width = weight.shape[1] // 2
-    stays, got = [None, None], [None, None]
-    for c in range(2):
-        s = dot(hidden, weight[:, c * width : (c + 1) * width])
-        stays[c], sent = s[: 8 * rows], s[8 * rows :]
-        got[c] = exchange(sent, masks_x=SECOND)
-    got[0], _ = tie(got[0], sent)
-    for c in range(2):
-        if c == 1:
-            got[1], got[0] = tie(got[1], got[0])
-        stays[c], sent = halve(stays[c], got[c], 4 * rows)
-        got[c] = exchange(sent, masks_x=FIRST)
-    columns = []
-    for c in range(2):
-        v = add(stays[c], got[c])
-        parts = [v[:rows]] + [exchange(v[m * rows : (m + 1) * rows], z=m) for m in (1, 2, 3)]
-        columns.append(functools.reduce(jnp.add, [p.astype(F32) for p in parts]).astype(BF))
-    return jnp.concatenate(columns, axis=1)
+def feed_forward(chunks, gate_up_weight, down_weight, rows):
+    own, got, other, waves, turn = {}, {}, {}, {}, [None]
+
+    def after(value):
+        return value if turn[0] is None else tie(value, turn[0])[0]
+
+    def send(value, **how):
+        turn[0] = value
+        return exchange(value, **how)
+
+    def product(c):
+        s = dot(after(chunks[c]), gate_up_weight)
+        own[c], got[c] = s[8 * rows :], send(s[: 8 * rows], core=1)
+
+    def sums(c, size, **how):
+        own[c], sent = halve(own[c], after(got[c]), size * rows)
+        got[c] = send(sent, **how)
+
+    def y_first(c):
+        sums(c, 4, masks_y=FIRST)
+
+    def y_second(c):
+        sums(c, 2, masks_y=SECOND)
+
+    def z_hi(c):
+        sums(c, 1, zhi=1)
+
+    def hidden(c):
+        own[c] = silu(own[c], after(got[c]))
+        other[c] = send(own[c], zhi=1)
+
+    def start(wave, *parts):
+        h = after(parts[-1]) if len(parts) == 1 else join(*parts[:-1], after(parts[-1]))
+        waves[wave] = h, send(h, masks_y=SECOND)
+
+    def widen(wave, **how):
+        h, more = waves[wave]
+        h = join(h, after(more))
+        waves[wave] = h, send(h, **how)
+
+    product(0)
+    product(1)
+    y_first(0)
+    product(2)
+    y_first(1)
+    y_first(2)
+    y_second(0)
+    y_second(1)
+    z_hi(0)
+    y_second(2)
+    z_hi(1)
+    hidden(0)
+    z_hi(2)
+    hidden(1)
+    hidden(2)
+    own[2], other[0], other[1] = tie(own[2], other[0], other[1])
+    start(0, own[0], own[1], own[2], other[0], other[1])
+    start(1, other[2])
+    widen(0, masks_y=FIRST)
+    widen(1, masks_y=FIRST)
+    (h, more), (first, last) = waves[0], waves[1]
+    more, last = tie(more, last)
+    waves[0], waves[1] = (h, more), (first, last)
+    widen(0, core=1)
+    widen(1, core=1)
+
+    groups = (2 * rows, [(0, 0, 5 * rows, 0), (0, 1, 5 * rows, 3 * rows)]), (
+        rows,
+        [(0, 0, 5 * rows, 2 * rows), (1, 1, rows, 0)],
+    )
+    stays, got, output = [], [], []
+    for size, sources in groups:
+        used = sorted({wave for wave, *_ in sources})
+        pieces = [piece for wave in used for piece in waves[wave]]
+        segments = [(2 * used.index(wave) + core, core, *where) for wave, *where in sources for core in (0, 1)]
+        s = dot(place(pieces, size, segments), down_weight)
+        stays.append(s[: 8 * size])
+        got.append(send(s[8 * size :], masks_x=SECOND))
+    for g, (size, _) in enumerate(groups):
+        stays[g], sent = halve(stays[g], after(got[g]), 4 * size)
+        got[g] = send(sent, masks_x=FIRST)
+    for g, (size, _) in enumerate(groups):
+        v = turn[0] = add(stays[g], after(got[g]))
+        parts = [v[:size]] + [exchange(v[m * size : (m + 1) * size], z=m) for m in (1, 2, 3)]
+        output.append(functools.reduce(jnp.add, [p.astype(F32) for p in parts]).astype(BF))
+    return jnp.concatenate(output)
 
 
 def shards(tokens, gate_weight, up_weight, down_weight):
-    rows = tokens.shape[0]
+    rows = tokens.shape[0] // CHUNKS
     pieces, weight = gather_tokens(tokens, gate_weight, up_weight)
-    hidden = scatter_hidden(pick(pieces, rows // CHUNKS), weight, rows // CHUNKS)
-    return scatter_out(place(gather_hidden(*hidden), rows), down_weight, rows)
+    return feed_forward(pick(pieces, rows), weight, down_weight, rows)
 
 
 def solution(mesh):

time: 140 us -> 142 us (1.014)
  starting transfers between devices: 57.1 us -> 61.1 us
  waiting for transfers between devices: 61.6 us -> 59.3 us
    ppermute x38, starting transfers between devices: 57.1 us -> 61.1 us  [exchange(): return lax.ppermute(value, ('gx', 'gy'), pairs)]
    ppermute x38, waiting for transfers between devices: 61.6 us -> 59.3 us  [exchange(): return lax.ppermute(value, ('gx', 'gy'), pairs)]
  transfers between devices with their start and end apart: 38 -> 38, of which waited for: 22 -> 23; matrix products, arithmetic and copies ran while one was open for 5% -> 6% of each run, Pallas kernels for 1% -> 1%
where the time goes in v4:
time: 142 us; the launch traced here: 140 us
  starting transfers between devices  61.1 us (43%)
  waiting for transfers between devices  59.3 us (42%)
  matrix products  9.12 us (6%)
  local copies, waits for them, and re-layouts  5.32 us (4%)
  Pallas kernels  2.4 us (2%)
  other arithmetic  2.12 us (1%)
    ppermute x38, starting transfers between devices, exchange(): return lax.ppermute(value, ('gx', 'gy'), pairs)  61.1 us
    ppermute x38, waiting for transfers between devices, exchange(): return lax.ppermute(value, ('gx', 'gy'), pairs)  59.3 us
    dot_general x5, matrix products, dot(): return jnp.dot(a, b, preferred_element_type=F32).astype(BF)  9.12 us
    unnamed x8, local copies, waits for them, and re-layouts  4.85 us
  transfers between devices with their start and end apart: 38, of which 23 were waited for; matrix products, arithmetic and copies ran while one was open for 6% of the time, Pallas kernels for 1%

profile of v4, /device:TPU:24, one launch (start us, length us, event | category | flops | bytes accessed | tf_op | source)
XLA Modules:
  0.0 139.8 jit_solution(4547150437540700162)
XLA Ops:
  0.0 1.9 %collective-permute-start = (bf16[48,1024]{1,0:T(8,128)(2,1)}, bf16[48,1024]{1,0:T(8,128)(2,1)S(1)}, u32[]{:S(2)}, u32[]{:S(2)}) collective-permute-start(bf16[48,1024]{1,0:T(8,128)(2,1)} %refs_0_.1), channel_id=1, source_target_pairs={{0,1},{1,0},{2,3},{3,2},{4,5},{5,4},{6,7},{7,6},{8,9},{9,8},{10,11... | collective-permute-start | bytes 294920 | tf_op jit(solution)/shard_map/ppermute | solution.py:24
  1.9 2.8 %collective-permute-start.4 = (bf16[48,1024]{1,0:T(8,128)(2,1)}, bf16[48,1024]{1,0:T(8,128)(2,1)S(1)}, u32[]{:S(2)}, u32[]{:S(2)}) collective-permute-start(bf16[48,1024]{1,0:T(8,128)(2,1)} %refs_0_.1), channel_id=1, source_target_pairs={{0,3},{1,2},{2,1},{3,0},{4,7},{5,6},{6,5},{7,4},{8,11},{9,10},{10,... | collective-permute-start | bytes 294920 | tf_op jit(solution)/shard_map/ppermute | solution.py:24
  6.1 1.6 %collective-permute-start.1 = (bf16[96,1024]{1,0:T(8,128)(2,1)S(1)}, bf16[96,1024]{1,0:T(8,128)(2,1)S(1)}, u32[]{:S(2)}, u32[]{:S(2)}) collective-permute-start(bf16[96,1024]{1,0:T(8,128)(2,1)S(1)} %join.9.refs_0_), channel_id=1, source_target_pairs={{0,4},{1,5},{2,6},{3,7},{4,0},{5,1},{6,2},{7,3},{8,12},{9,13},{10,... | collective-permute-start | bytes 589832 | tf_op jit(solution)/shard_map/ppermute | solution.py:24
  7.7 3.1 %collective-permute-done.4.refs_1_ = bf16[48,1024]{1,0:T(8,128)(2,1)S(1)} collective-permute-done((bf16[48,1024]{1,0:T(8,128)(2,1)}, bf16[48,1024]{1,0:T(8,128)(2,1)S(1)}, u32[]{:S(2)}, u32[]{:S(2)}) %collective-permute-start.4) | collective-permute-done | bytes 98336 | tf_op jit(solution)/shard_map/ppermute | solution.py:24
  10.8 3.5 %collective-permute-done.3.refs_0_ = bf16[48,1024]{1,0:T(8,128)(2,1)S(1)} collective-permute-done((bf16[48,1024]{1,0:T(8,128)(2,1)}, bf16[48,1024]{1,0:T(8,128)(2,1)S(1)}, u32[]{:S(2)}, u32[]{:S(2)}) %collective-permute-start.3) | collective-permute-done | bytes 98336 | tf_op jit(solution)/shard_map/ppermute | solution.py:24
  14.3 1.6 %collective-permute-start.5 = (bf16[96,1024]{1,0:T(8,128)(2,1)S(1)}, bf16[96,1024]{1,0:T(8,128)(2,1)S(1)}, u32[]{:S(2)}, u32[]{:S(2)}) collective-permute-start(bf16[96,1024]{1,0:T(8,128)(2,1)S(1)} %join.11.refs_0_.refs_3_), channel_id=1, source_target_pairs={{0,4},{1,5},{2,6},{3,7},{4,0},{5,1},{6,2},{7,3},{8,12},{9,13},{10,... | collective-permute-start | bytes 589832 | tf_op jit(solution)/shard_map/ppermute | solution.py:24
  15.9 2.2 %collective-permute-start.2 = (bf16[192,1024]{1,0:T(8,128)(2,1)S(1)}, bf16[192,1024]{1,0:T(8,128)(2,1)S(1)}, u32[]{:S(2)}, u32[]{:S(2)}) collective-permute-start(bf16[192,1024]{1,0:T(8,128)(2,1)S(1)} %join.10), channel_id=1, source_target_pairs={{0,12},{1,13},{2,14},{3,15},{4,8},{5,9},{6,10},{7,11},{8,4},{9,5},... | collective-permute-start | bytes 1179656 | tf_op jit(solution)/shard_map/ppermute | solution.py:24
  18.1 3.1 %collective-permute-done.5.refs_1_.refs_4_ = bf16[96,1024]{1,0:T(8,128)(2,1)S(1)} collective-permute-done((bf16[96,1024]{1,0:T(8,128)(2,1)S(1)}, bf16[96,1024]{1,0:T(8,128)(2,1)S(1)}, u32[]{:S(2)}, u32[]{:S(2)}) %collective-permute-start.5) | collective-permute-done | bytes 196640 | tf_op jit(solution)/shard_map/ppermute | solution.py:24
  21.2 3.9 %collective-permute-start.6 = (bf16[192,1024]{1,0:T(8,128)(2,1)S(1)}, bf16[192,1024]{1,0:T(8,128)(2,1)S(1)}, u32[]{:S(2)}, u32[]{:S(2)}) collective-permute-start(bf16[192,1024]{1,0:T(8,128)(2,1)S(1)} %join.12), channel_id=1, source_target_pairs={{0,12},{1,13},{2,14},{3,15},{4,8},{5,9},{6,10},{7,11},{8,4},{9,5},... | collective-permute-start | bytes 1179656 | tf_op jit(solution)/shard_map/ppermute | solution.py:24
  25.0 2.0 %copy-done.1 = bf16[1024,1664]{1,0:T(8,128)(2,1)S(1)} copy-done((bf16[1024,1664]{1,0:T(8,128)(2,1)S(1)}, bf16[1024,1664]{1,0:T(8,128)(2,1)}, u32[]{:S(2)}) %copy-start.1) | copy-done | bytes 3407896
  27.0 2.0 %copy-done.2 = bf16[1024,1664]{1,0:T(8,128)(2,1)S(1)} copy-done((bf16[1024,1664]{1,0:T(8,128)(2,1)S(1)}, bf16[1024,1664]{1,0:T(8,128)(2,1)}, u32[]{:S(2)}) %copy-start.2) | copy-done | bytes 3407896
  29.0 1.5 %pack.1 = bf16[1024,3328]{1,0:T(8,128)(2,1)S(1)} custom-call(bf16[1024,1664]{1,0:T(8,128)(2,1)S(1)} %copy-done.1, bf16[1024,1664]{1,0:T(8,128)(2,1)S(1)} %copy-done.2), custom_call_target="tpu_custom_call" | custom-call | bytes 13631488 | tf_op jit(solution)/shard_map/pack/pallas_call | solution.py:89
  31.0 1.9 %convolution_convert_fusion.2 = bf16[256,3328]{1,0:T(8,128)(2,1)S(1)} fusion(bf16[256,1024]{1,0:T(8,128)(2,1)S(1)} %get-tuple-element.38, bf16[1024,3328]{1,0:T(8,128)(2,1)S(1)} %pack.1), kind=kOutput, calls=%fused_computation.2 | convolution fusion | flops 1745682432 | bytes 9043968 | tf_op jit(solution)/shard_map/dot_general | solution.py:162
  33.1 1.9 %convolution_convert_fusion.1 = bf16[256,3328]{1,0:T(8,128)(2,1)S(1)} fusion(bf16[256,1024]{1,0:T(8,128)(2,1)S(1)} %get-tuple-element.41, bf16[1024,3328]{1,0:T(8,128)(2,1)S(1)} %pack.1), kind=kOutput, calls=%fused_computation.1 | convolution fusion | flops 1745682432 | bytes 9043968 | tf_op jit(solution)/shard_map/dot_general | solution.py:162
  37.0 1.9 %convolution_convert_fusion = bf16[256,3328]{1,0:T(8,128)(2,1)S(1)} fusion(bf16[256,1024]{1,0:T(8,128)(2,1)S(1)} %get-tuple-element.44, bf16[1024,3328]{1,0:T(8,128)(2,1)S(1)} %pack.1), kind=kOutput, calls=%fused_computation | convolution fusion | flops 1745682432 | bytes 9043968 | tf_op jit(solution)/shard_map/dot_general | solution.py:162
  39.3 1.4 collective-permute-start.12
  41.7 1.4 collective-permute-start.15
  43.1 1.3 collective-permute-done.8
  44.8 5.7 %collective-permute-done.12 = bf16[64,3328]{1,0:T(8,128)(2,1)S(1)} collective-permute-done((bf16[64,3328]{1,0:T(8,128)(2,1)S(1)}, bf16[64,3328]{1,0:T(8,128)(2,1)S(1)}, u32[]{:S(2)}, u32[]{:S(2)}) %collective-permute-start.12) | collective-permute-done | bytes 426016 | tf_op jit(solution)/shard_map/ppermute | solution.py:24
  50.7 1.3 collective-permute-start.14
  52.0 2.0 %collective-permute-done.11 = bf16[32,3328]{1,0:T(8,128)(2,1)S(1)} collective-permute-done((bf16[32,3328]{1,0:T(8,128)(2,1)S(1)}, bf16[32,3328]{1,0:T(8,128)(2,1)S(1)}, u32[]{:S(2)}, u32[]{:S(2)}) %collective-permute-start.11) | collective-permute-done | bytes 213024 | tf_op jit(solution)/shard_map/ppermute | solution.py:24
  54.1 5.6 %collective-permute-start.13 = (bf16[16,3328]{1,0:T(8,128)(2,1)S(1)}, bf16[16,3328]{1,0:T(8,128)(2,1)S(1)}, u32[]{:S(2)}, u32[]{:S(2)}) collective-permute-start(bf16[16,3328]{1,0:T(8,128)(2,1)S(1)} %get-tuple-element.78), channel_id=1, source_target_pairs={{0,128},{1,129},{2,130},{3,131},{4,132},{5,133},{6,134},{7,135},{8... | collective-permute-start | bytes 319496 | tf_op jit(solution)/shard_map/ppermute | solution.py:24
  60.2 4.6 %collective-permute-start.16 = (bf16[16,3328]{1,0:T(8,128)(2,1)S(1)}, bf16[16,3328]{1,0:T(8,128)(2,1)S(1)}, u32[]{:S(2)}, u32[]{:S(2)}) collective-permute-start(bf16[16,3328]{1,0:T(8,128)(2,1)S(1)} %get-tuple-element.77), channel_id=1, source_target_pairs={{0,128},{1,129},{2,130},{3,131},{4,132},{5,133},{6,134},{7,135},{8... | collective-permute-start | bytes 319496 | tf_op jit(solution)/shard_map/ppermute | solution.py:24
  64.9 2.1 %collective-permute-done.17 = bf16[32,3328]{1,0:T(8,128)(2,1)S(1)} collective-permute-done((bf16[32,3328]{1,0:T(8,128)(2,1)S(1)}, bf16[32,3328]{1,0:T(8,128)(2,1)S(1)}, u32[]{:S(2)}, u32[]{:S(2)}) %collective-permute-start.17) | collective-permute-done | bytes 213024 | tf_op jit(solution)/shard_map/ppermute | solution.py:24
  67.0 4.0 %collective-permute-start.18 = (bf16[16,3328]{1,0:T(8,128)(2,1)S(1)}, bf16[16,3328]{1,0:T(8,128)(2,1)S(1)}, u32[]{:S(2)}, u32[]{:S(2)}) collective-permute-start(bf16[16,3328]{1,0:T(8,128)(2,1)S(1)} %get-tuple-element.75), channel_id=1, source_target_pairs={{0,128},{1,129},{2,130},{3,131},{4,132},{5,133},{6,134},{7,135},{8... | collective-permute-start | bytes 319496 | tf_op jit(solution)/shard_map/ppermute | solution.py:24
  71.0 2.0 %collective-permute-start.19 = (bf16[16,1664]{1,0:T(8,128)(2,1)S(1)}, bf16[16,1664]{1,0:T(8,128)(2,1)S(1)}, u32[]{:S(2)}, u32[]{:S(2)}) collective-permute-start(bf16[16,1664]{1,0:T(8,128)(2,1)S(1)} %silu.3.refs_0_), channel_id=1, source_target_pairs={{0,128},{1,129},{2,130},{3,131},{4,132},{5,133},{6,134},{7,135},{8... | collective-permute-start | bytes 159752 | tf_op jit(solution)/shard_map/ppermute | solution.py:24
  73.1 4.0 %collective-permute-start.20 = (bf16[16,1664]{1,0:T(8,128)(2,1)S(1)}, bf16[16,1664]{1,0:T(8,128)(2,1)S(1)}, u32[]{:S(2)}, u32[]{:S(2)}) collective-permute-start(bf16[16,1664]{1,0:T(8,128)(2,1)S(1)} %silu.4.refs_1_), channel_id=1, source_target_pairs={{0,128},{1,129},{2,130},{3,131},{4,132},{5,133},{6,134},{7,135},{8... | collective-permute-start | bytes 159752 | tf_op jit(solution)/shard_map/ppermute | solution.py:24
  77.1 1.9 %collective-permute-done.18.b_ref = bf16[16,3328]{1,0:T(8,128)(2,1)S(1)} collective-permute-done((bf16[16,3328]{1,0:T(8,128)(2,1)S(1)}, bf16[16,3328]{1,0:T(8,128)(2,1)S(1)}, u32[]{:S(2)}, u32[]{:S(2)}) %collective-permute-start.18) | collective-permute-done | bytes 106528 | tf_op jit(solution)/shard_map/ppermute | solution.py:24
  79.5 1.7 %collective-permute-done.20.refs_4_ = bf16[16,1664]{1,0:T(8,128)(2,1)S(1)} collective-permute-done((bf16[16,1664]{1,0:T(8,128)(2,1)S(1)}, bf16[16,1664]{1,0:T(8,128)(2,1)S(1)}, u32[]{:S(2)}, u32[]{:S(2)}) %collective-permute-start.20) | collective-permute-done | bytes 53280 | tf_op jit(solution)/shard_map/ppermute | solution.py:24
  81.2 2.9 %collective-permute-start.21 = (bf16[80,1664]{1,0:T(8,128)(2,1)S(1)}, bf16[80,1664]{1,0:T(8,128)(2,1)S(1)}, u32[]{:S(2)}, u32[]{:S(2)}) collective-permute-start(bf16[80,1664]{1,0:T(8,128)(2,1)S(1)} %join.13.refs_0_), channel_id=1, source_target_pairs={{0,96},{1,97},{2,98},{3,99},{4,100},{5,101},{6,102},{7,103},{8,104... | collective-permute-start | bytes 798728 | tf_op jit(solution)/shard_map/ppermute | solution.py:24
  84.1 3.9 %collective-permute-start.22 = (bf16[16,1664]{1,0:T(8,128)(2,1)S(1)}, bf16[16,1664]{1,0:T(8,128)(2,1)S(1)}, u32[]{:S(2)}, u32[]{:S(2)}) collective-permute-start(bf16[16,1664]{1,0:T(8,128)(2,1)S(1)} %silu.5.refs_2_), channel_id=1, source_target_pairs={{0,128},{1,129},{2,130},{3,131},{4,132},{5,133},{6,134},{7,135},{8... | collective-permute-start | bytes 159752 | tf_op jit(solution)/shard_map/ppermute | solution.py:24
  88.0 4.1 %collective-permute-done.22.refs_0_ = bf16[16,1664]{1,0:T(8,128)(2,1)S(1)} collective-permute-done((bf16[16,1664]{1,0:T(8,128)(2,1)S(1)}, bf16[16,1664]{1,0:T(8,128)(2,1)S(1)}, u32[]{:S(2)}, u32[]{:S(2)}) %collective-permute-start.22) | collective-permute-done | bytes 53280 | tf_op jit(solution)/shard_map/ppermute | solution.py:24
  92.9 4.8 %collective-permute-done.24.refs_1_ = bf16[16,1664]{1,0:T(8,128)(2,1)S(1)} collective-permute-done((bf16[16,1664]{1,0:T(8,128)(2,1)S(1)}, bf16[16,1664]{1,0:T(8,128)(2,1)S(1)}, u32[]{:S(2)}, u32[]{:S(2)}) %collective-permute-start.24) | collective-permute-done | bytes 53280 | tf_op jit(solution)/shard_map/ppermute | solution.py:24
  98.5 4.1 %collective-permute-done.25.refs_1_ = bf16[32,1664]{1,0:T(8,128)(2,1)S(1)} collective-permute-done((bf16[32,1664]{1,0:T(8,128)(2,1)S(1)}, bf16[32,1664]{1,0:T(8,128)(2,1)S(1)}, u32[]{:S(2)}, u32[]{:S(2)}) %collective-permute-start.25) | collective-permute-done | bytes 106528 | tf_op jit(solution)/shard_map/ppermute | solution.py:24
  103.7 2.1 %collective-permute-done.26.refs_1_ = bf16[320,1664]{1,0:T(8,128)(2,1)S(1)} collective-permute-done((bf16[320,1664]{1,0:T(8,128)(2,1)S(1)}, bf16[320,1664]{1,0:T(8,128)(2,1)S(1)}, u32[]{:S(2)}, u32[]{:S(2)}) %collective-permute-start.26) | collective-permute-done | bytes 1064992 | tf_op jit(solution)/shard_map/ppermute | solution.py:24
  106.0 2.1 %convolution_convert_fusion.3 = bf16[512,1024]{1,0:T(8,128)(2,1)S(1)} fusion(bf16[512,1664]{1,0:T(8,128)(2,1)S(1)} %place.2, bf16[1664,1024]{1,0:T(8,128)(2,1)S(1)} %copy-done), kind=kOutput, calls=%fused_computation.6 | convolution fusion | flops 1745354752 | bytes 6160384 | tf_op jit(solution)/shard_map/dot_general | solution.py:162
  108.2 3.3 %collective-permute-start.27 = (bf16[256,1024]{1,0:T(8,128)(2,1)S(1)}, bf16[256,1024]{1,0:T(8,128)(2,1)S(1)}, u32[]{:S(2)}, u32[]{:S(2)}) collective-permute-start(bf16[256,1024]{1,0:T(8,128)(2,1)S(1)} %slice.185), channel_id=1, source_target_pairs={{0,12},{1,13},{2,14},{3,15},{4,8},{5,9},{6,10},{7,11},{8,4},{9,5},... | collective-permute-start | bytes 1572872 | tf_op jit(solution)/shard_map/ppermute | solution.py:24
  111.6 1.2 convolution_convert_fusion.4
  112.9 5.7 %collective-permute-done.27 = bf16[256,1024]{1,0:T(8,128)(2,1)S(1)} collective-permute-done((bf16[256,1024]{1,0:T(8,128)(2,1)S(1)}, bf16[256,1024]{1,0:T(8,128)(2,1)S(1)}, u32[]{:S(2)}, u32[]{:S(2)}) %collective-permute-start.27) | collective-permute-done | bytes 524320 | tf_op jit(solution)/shard_map/ppermute | solution.py:24
  119.0 2.8 %collective-permute-done.30 = bf16[128,1024]{1,0:T(8,128)(2,1)S(1)} collective-permute-done((bf16[128,1024]{1,0:T(8,128)(2,1)S(1)}, bf16[128,1024]{1,0:T(8,128)(2,1)S(1)}, u32[]{:S(2)}, u32[]{:S(2)}) %collective-permute-start.30) | collective-permute-done | bytes 262176 | tf_op jit(solution)/shard_map/ppermute | solution.py:24
  121.9 3.4 %collective-permute-done.29 = bf16[128,1024]{1,0:T(8,128)(2,1)S(1)} collective-permute-done((bf16[128,1024]{1,0:T(8,128)(2,1)S(1)}, bf16[128,1024]{1,0:T(8,128)(2,1)S(1)}, u32[]{:S(2)}, u32[]{:S(2)}) %collective-permute-start.29) | collective-permute-done | bytes 262176 | tf_op jit(solution)/shard_map/ppermute | solution.py:24
  125.4 1.5 %collective-permute-done.34 = bf16[64,1024]{1,0:T(8,128)(2,1)S(1)} collective-permute-done((bf16[64,1024]{1,0:T(8,128)(2,1)S(1)}, bf16[64,1024]{1,0:T(8,128)(2,1)S(1)}, u32[]{:S(2)}, u32[]{:S(2)}) %collective-permute-start.34) | collective-permute-done | bytes 131104 | tf_op jit(solution)/shard_map/ppermute | solution.py:24
  127.0 2.0 %collective-permute-start.37 = (bf16[16,1024]{1,0:T(8,128)(2,1)S(1)}, bf16[16,1024]{1,0:T(8,128)(2,1)S(1)}, u32[]{:S(2)}, u32[]{:S(2)}) collective-permute-start(bf16[16,1024]{1,0:T(8,128)(2,1)S(1)} %get-tuple-element.81), channel_id=1, source_target_pairs={{0,3},{1,2},{2,1},{3,0},{4,7},{5,6},{6,5},{7,4},{8,11},{9,10},{10,... | collective-permute-start | bytes 98312 | tf_op jit(solution)/shard_map/ppermute | solution.py:24
  129.0 1.5 %collective-permute-start.36 = (bf16[16,1024]{1,0:T(8,128)(2,1)S(1)}, bf16[16,1024]{1,0:T(8,128)(2,1)S(1)}, u32[]{:S(2)}, u32[]{:S(2)}) collective-permute-start(bf16[16,1024]{1,0:T(8,128)(2,1)S(1)} %get-tuple-element.82), channel_id=1, source_target_pairs={{0,2},{1,3},{2,0},{3,1},{4,6},{5,7},{6,4},{7,5},{8,10},{9,11},{10,... | collective-permute-start | bytes 98312 | tf_op jit(solution)/shard_map/ppermute | solution.py:24
  131.6 1.9 %collective-permute-start.33 = (bf16[32,1024]{1,0:T(8,128)(2,1)S(1)}, bf16[32,1024]{1,0:T(8,128)(2,1)S(1)}, u32[]{:S(2)}, u32[]{:S(2)}) collective-permute-start(bf16[32,1024]{1,0:T(8,128)(2,1)S(1)} %get-tuple-element.72), channel_id=1, source_target_pairs={{0,3},{1,2},{2,1},{3,0},{4,7},{5,6},{6,5},{7,4},{8,11},{9,10},{10,... | collective-permute-start | bytes 196616 | tf_op jit(solution)/shard_map/ppermute | solution.py:24
  134.1 1.3 collective-permute-done.31
  135.4 2.3 %collective-permute-done.33 = bf16[32,1024]{1,0:T(8,128)(2,1)S(1)} collective-permute-done((bf16[32,1024]{1,0:T(8,128)(2,1)S(1)}, bf16[32,1024]{1,0:T(8,128)(2,1)S(1)}, u32[]{:S(2)}, u32[]{:S(2)}) %collective-permute-start.33) | collective-permute-done | bytes 65568 | tf_op jit(solution)/shard_map/ppermute | solution.py:24
  137.7 1.4 %collective-permute-done.32 = bf16[32,1024]{1,0:T(8,128)(2,1)S(1)} collective-permute-done((bf16[32,1024]{1,0:T(8,128)(2,1)S(1)}, bf16[32,1024]{1,0:T(8,128)(2,1)S(1)}, u32[]{:S(2)}, u32[]{:S(2)}) %collective-permute-start.32) | collective-permute-done | bytes 65568 | tf_op jit(solution)/shard_map/ppermute | solution.py:24
  (91 shorter events, 13.5 us)
Async XLA Ops:
  0.0 106.0 %copy-start = (bf16[1664,1024]{1,0:T(8,128)(2,1)S(1)}, bf16[1664,1024]{1,0:T(8,128)(2,1)}, u32[]{:S(2)}) copy-start(bf16[1664,1024]{1,0:T(8,128)(2,1)} %param.7) | copy-start | bytes 10223620
  0.0 5.2 %collective-permute-start = (bf16[48,1024]{1,0:T(8,128)(2,1)}, bf16[48,1024]{1,0:T(8,128)(2,1)S(1)}, u32[]{:S(2)}, u32[]{:S(2)}) collective-permute-start(bf16[48,1024]{1,0:T(8,128)(2,1)} %refs_0_.1), channel_id=1, source_target_pairs={{0,1},{1,0},{2,3},{3,2},{4,5},{5,4},{6,7},{7,6},{8,9},{9,8},{10,11... | collective-permute-start | bytes 294920 | tf_op jit(solution)/shard_map/ppermute | solution.py:24
  1.9 8.9 %collective-permute-start.4 = (bf16[48,1024]{1,0:T(8,128)(2,1)}, bf16[48,1024]{1,0:T(8,128)(2,1)S(1)}, u32[]{:S(2)}, u32[]{:S(2)}) collective-permute-start(bf16[48,1024]{1,0:T(8,128)(2,1)} %refs_0_.1), channel_id=1, source_target_pairs={{0,3},{1,2},{2,1},{3,0},{4,7},{5,6},{6,5},{7,4},{8,11},{9,10},{10,... | collective-permute-start | bytes 294920 | tf_op jit(solution)/shard_map/ppermute | solution.py:24
  4.7 9.5 %collective-permute-start.3 = (bf16[48,1024]{1,0:T(8,128)(2,1)}, bf16[48,1024]{1,0:T(8,128)(2,1)S(1)}, u32[]{:S(2)}, u32[]{:S(2)}) collective-permute-start(bf16[48,1024]{1,0:T(8,128)(2,1)} %refs_0_.1), channel_id=1, source_target_pairs={{0,2},{1,3},{2,0},{3,1},{4,6},{5,7},{6,4},{7,5},{8,10},{9,11},{10,... | collective-permute-start | bytes 294920 | tf_op jit(solution)/shard_map/ppermute | solution.py:24
  5.2 0.9 copy-start.3
  6.1 9.7 %collective-permute-start.1 = (bf16[96,1024]{1,0:T(8,128)(2,1)S(1)}, bf16[96,1024]{1,0:T(8,128)(2,1)S(1)}, u32[]{:S(2)}, u32[]{:S(2)}) collective-permute-start(bf16[96,1024]{1,0:T(8,128)(2,1)S(1)} %join.9.refs_0_), channel_id=1, source_target_pairs={{0,4},{1,5},{2,6},{3,7},{4,0},{5,1},{6,2},{7,3},{8,12},{9,13},{10,... | collective-permute-start | bytes 589832 | tf_op jit(solution)/shard_map/ppermute | solution.py:24
  14.3 6.9 %collective-permute-start.5 = (bf16[96,1024]{1,0:T(8,128)(2,1)S(1)}, bf16[96,1024]{1,0:T(8,128)(2,1)S(1)}, u32[]{:S(2)}, u32[]{:S(2)}) collective-permute-start(bf16[96,1024]{1,0:T(8,128)(2,1)S(1)} %join.11.refs_0_.refs_3_), channel_id=1, source_target_pairs={{0,4},{1,5},{2,6},{3,7},{4,0},{5,1},{6,2},{7,3},{8,12},{9,13},{10,... | collective-permute-start | bytes 589832 | tf_op jit(solution)/shard_map/ppermute | solution.py:24
  15.9 14.5 %collective-permute-start.2 = (bf16[192,1024]{1,0:T(8,128)(2,1)S(1)}, bf16[192,1024]{1,0:T(8,128)(2,1)S(1)}, u32[]{:S(2)}, u32[]{:S(2)}) collective-permute-start(bf16[192,1024]{1,0:T(8,128)(2,1)S(1)} %join.10), channel_id=1, source_target_pairs={{0,12},{1,13},{2,14},{3,15},{4,8},{5,9},{6,10},{7,11},{8,4},{9,5},... | collective-permute-start | bytes 1179656 | tf_op jit(solution)/shard_map/ppermute | solution.py:24
  21.2 9.6 %collective-permute-start.6 = (bf16[192,1024]{1,0:T(8,128)(2,1)S(1)}, bf16[192,1024]{1,0:T(8,128)(2,1)S(1)}, u32[]{:S(2)}, u32[]{:S(2)}) collective-permute-start(bf16[192,1024]{1,0:T(8,128)(2,1)S(1)} %join.12), channel_id=1, source_target_pairs={{0,12},{1,13},{2,14},{3,15},{4,8},{5,9},{6,10},{7,11},{8,4},{9,5},... | collective-permute-start | bytes 1179656 | tf_op jit(solution)/shard_map/ppermute | solution.py:24
  25.0 2.0 %copy-start.1 = (bf16[1024,1664]{1,0:T(8,128)(2,1)S(1)}, bf16[1024,1664]{1,0:T(8,128)(2,1)}, u32[]{:S(2)}) copy-start(bf16[1024,1664]{1,0:T(8,128)(2,1)} %gate_ref) | copy-start | bytes 10223620
  27.0 2.0 %copy-start.2 = (bf16[1024,1664]{1,0:T(8,128)(2,1)S(1)}, bf16[1024,1664]{1,0:T(8,128)(2,1)}, u32[]{:S(2)}) copy-start(bf16[1024,1664]{1,0:T(8,128)(2,1)} %up_ref.1) | copy-start | bytes 10223620
  33.0 2.7 %collective-permute-start.7 = (bf16[128,3328]{1,0:T(8,128)(2,1)S(1)}, bf16[128,3328]{1,0:T(8,128)(2,1)S(1)}, u32[]{:S(2)}, u32[]{:S(2)}) collective-permute-start(bf16[128,3328]{1,0:T(8,128)(2,1)S(1)} %slice.161), channel_id=1, source_target_pairs={{0,16},{1,17},{2,18},{3,19},{4,20},{5,21},{6,22},{7,23},{8,24},{9,... | collective-permute-start | bytes 2555912 | tf_op jit(solution)/shard_map/ppermute | solution.py:24
  35.1 4.0 %collective-permute-start.10 = (bf16[128,3328]{1,0:T(8,128)(2,1)S(1)}, bf16[128,3328]{1,0:T(8,128)(2,1)S(1)}, u32[]{:S(2)}, u32[]{:S(2)}) collective-permute-start(bf16[128,3328]{1,0:T(8,128)(2,1)S(1)} %slice.162), channel_id=1, source_target_pairs={{0,16},{1,17},{2,18},{3,19},{4,20},{5,21},{6,22},{7,23},{8,24},{9,... | collective-permute-start | bytes 2555912 | tf_op jit(solution)/shard_map/ppermute | solution.py:24
  36.0 8.4 %collective-permute-start.8 = (bf16[64,3328]{1,0:T(8,128)(2,1)S(1)}, bf16[64,3328]{1,0:T(8,128)(2,1)S(1)}, u32[]{:S(2)}, u32[]{:S(2)}) collective-permute-start(bf16[64,3328]{1,0:T(8,128)(2,1)S(1)} %slice.164), channel_id=1, source_target_pairs={{0,32},{1,33},{2,34},{3,35},{4,36},{5,37},{6,38},{7,39},{8,40},{9,... | collective-permute-start | bytes 1277960 | tf_op jit(solution)/shard_map/ppermute | solution.py:24
  39.0 2.5 %collective-permute-start.9 = (bf16[128,3328]{1,0:T(8,128)(2,1)S(1)}, bf16[128,3328]{1,0:T(8,128)(2,1)S(1)}, u32[]{:S(2)}, u32[]{:S(2)}) collective-permute-start(bf16[128,3328]{1,0:T(8,128)(2,1)S(1)} %slice.166), channel_id=1, source_target_pairs={{0,16},{1,17},{2,18},{3,19},{4,20},{5,21},{6,22},{7,23},{8,24},{9,... | collective-permute-start | bytes 2555912 | tf_op jit(solution)/shard_map/ppermute | solution.py:24
  39.3 11.2 %collective-permute-start.12 = (bf16[64,3328]{1,0:T(8,128)(2,1)S(1)}, bf16[64,3328]{1,0:T(8,128)(2,1)S(1)}, u32[]{:S(2)}, u32[]{:S(2)}) collective-permute-start(bf16[64,3328]{1,0:T(8,128)(2,1)S(1)} %slice.168), channel_id=1, source_target_pairs={{0,32},{1,33},{2,34},{3,35},{4,36},{5,37},{6,38},{7,39},{8,40},{9,... | collective-permute-start | bytes 1277960 | tf_op jit(solution)/shard_map/ppermute | solution.py:24
  41.7 17.9 %collective-permute-start.15 = (bf16[64,3328]{1,0:T(8,128)(2,1)S(1)}, bf16[64,3328]{1,0:T(8,128)(2,1)S(1)}, u32[]{:S(2)}, u32[]{:S(2)}) collective-permute-start(bf16[64,3328]{1,0:T(8,128)(2,1)S(1)} %slice.169), channel_id=1, source_target_pairs={{0,32},{1,33},{2,34},{3,35},{4,36},{5,37},{6,38},{7,39},{8,40},{9,... | collective-permute-start | bytes 1277960 | tf_op jit(solution)/shard_map/ppermute | solution.py:24
  44.5 9.5 %collective-permute-start.11 = (bf16[32,3328]{1,0:T(8,128)(2,1)S(1)}, bf16[32,3328]{1,0:T(8,128)(2,1)S(1)}, u32[]{:S(2)}, u32[]{:S(2)}) collective-permute-start(bf16[32,3328]{1,0:T(8,128)(2,1)S(1)} %slice.171), channel_id=1, source_target_pairs={{0,96},{1,97},{2,98},{3,99},{4,100},{5,101},{6,102},{7,103},{8,104... | collective-permute-start | bytes 638984 | tf_op jit(solution)/shard_map/ppermute | solution.py:24
  50.7 9.4 %collective-permute-start.14 = (bf16[32,3328]{1,0:T(8,128)(2,1)S(1)}, bf16[32,3328]{1,0:T(8,128)(2,1)S(1)}, u32[]{:S(2)}, u32[]{:S(2)}) collective-permute-start(bf16[32,3328]{1,0:T(8,128)(2,1)S(1)} %slice.173), channel_id=1, source_target_pairs={{0,96},{1,97},{2,98},{3,99},{4,100},{5,101},{6,102},{7,103},{8,104... | collective-permute-start | bytes 638984 | tf_op jit(solution)/shard_map/ppermute | solution.py:24
  54.1 10.7 %collective-permute-start.13 = (bf16[16,3328]{1,0:T(8,128)(2,1)S(1)}, bf16[16,3328]{1,0:T(8,128)(2,1)S(1)}, u32[]{:S(2)}, u32[]{:S(2)}) collective-permute-start(bf16[16,3328]{1,0:T(8,128)(2,1)S(1)} %get-tuple-element.78), channel_id=1, source_target_pairs={{0,128},{1,129},{2,130},{3,131},{4,132},{5,133},{6,134},{7,135},{8... | collective-permute-start | bytes 319496 | tf_op jit(solution)/shard_map/ppermute | solution.py:24
  59.8 7.1 %collective-permute-start.17 = (bf16[32,3328]{1,0:T(8,128)(2,1)S(1)}, bf16[32,3328]{1,0:T(8,128)(2,1)S(1)}, u32[]{:S(2)}, u32[]{:S(2)}) collective-permute-start(bf16[32,3328]{1,0:T(8,128)(2,1)S(1)} %slice.178), channel_id=1, source_target_pairs={{0,96},{1,97},{2,98},{3,99},{4,100},{5,101},{6,102},{7,103},{8,104... | collective-permute-start | bytes 638984 | tf_op jit(solution)/shard_map/ppermute | solution.py:24
  60.2 12.9 %collective-permute-start.16 = (bf16[16,3328]{1,0:T(8,128)(2,1)S(1)}, bf16[16,3328]{1,0:T(8,128)(2,1)S(1)}, u32[]{:S(2)}, u32[]{:S(2)}) collective-permute-start(bf16[16,3328]{1,0:T(8,128)(2,1)S(1)} %get-tuple-element.77), channel_id=1, source_target_pairs={{0,128},{1,129},{2,130},{3,131},{4,132},{5,133},{6,134},{7,135},{8... | collective-permute-start | bytes 319496 | tf_op jit(solution)/shard_map/ppermute | solution.py:24
  67.0 11.9 %collective-permute-start.18 = (bf16[16,3328]{1,0:T(8,128)(2,1)S(1)}, bf16[16,3328]{1,0:T(8,128)(2,1)S(1)}, u32[]{:S(2)}, u32[]{:S(2)}) collective-permute-start(bf16[16,3328]{1,0:T(8,128)(2,1)S(1)} %get-tuple-element.75), channel_id=1, source_target_pairs={{0,128},{1,129},{2,130},{3,131},{4,132},{5,133},{6,134},{7,135},{8... | collective-permute-start | bytes 319496 | tf_op jit(solution)/shard_map/ppermute | solution.py:24
  71.0 8.5 %collective-permute-start.19 = (bf16[16,1664]{1,0:T(8,128)(2,1)S(1)}, bf16[16,1664]{1,0:T(8,128)(2,1)S(1)}, u32[]{:S(2)}, u32[]{:S(2)}) collective-permute-start(bf16[16,1664]{1,0:T(8,128)(2,1)S(1)} %silu.3.refs_0_), channel_id=1, source_target_pairs={{0,128},{1,129},{2,130},{3,131},{4,132},{5,133},{6,134},{7,135},{8... | collective-permute-start | bytes 159752 | tf_op jit(solution)/shard_map/ppermute | solution.py:24
  73.1 8.1 %collective-permute-start.20 = (bf16[16,1664]{1,0:T(8,128)(2,1)S(1)}, bf16[16,1664]{1,0:T(8,128)(2,1)S(1)}, u32[]{:S(2)}, u32[]{:S(2)}) collective-permute-start(bf16[16,1664]{1,0:T(8,128)(2,1)S(1)} %silu.4.refs_1_), channel_id=1, source_target_pairs={{0,128},{1,129},{2,130},{3,131},{4,132},{5,133},{6,134},{7,135},{8... | collective-permute-start | bytes 159752 | tf_op jit(solution)/shard_map/ppermute | solution.py:24
  81.2 10.9 %collective-permute-start.21 = (bf16[80,1664]{1,0:T(8,128)(2,1)S(1)}, bf16[80,1664]{1,0:T(8,128)(2,1)S(1)}, u32[]{:S(2)}, u32[]{:S(2)}) collective-permute-start(bf16[80,1664]{1,0:T(8,128)(2,1)S(1)} %join.13.refs_0_), channel_id=1, source_target_pairs={{0,96},{1,97},{2,98},{3,99},{4,100},{5,101},{6,102},{7,103},{8,104... | collective-permute-start | bytes 798728 | tf_op jit(solution)/shard_map/ppermute | solution.py:24
  84.1 8.0 %collective-permute-start.22 = (bf16[16,1664]{1,0:T(8,128)(2,1)S(1)}, bf16[16,1664]{1,0:T(8,128)(2,1)S(1)}, u32[]{:S(2)}, u32[]{:S(2)}) collective-permute-start(bf16[16,1664]{1,0:T(8,128)(2,1)S(1)} %silu.5.refs_2_), channel_id=1, source_target_pairs={{0,128},{1,129},{2,130},{3,131},{4,132},{5,133},{6,134},{7,135},{8... | collective-permute-start | bytes 159752 | tf_op jit(solution)/shard_map/ppermute | solution.py:24
  92.2 10.5 %collective-permute-start.23 = (bf16[160,1664]{1,0:T(8,128)(2,1)S(1)}, bf16[160,1664]{1,0:T(8,128)(2,1)S(1)}, u32[]{:S(2)}, u32[]{:S(2)}) collective-permute-start(bf16[160,1664]{1,0:T(8,128)(2,1)S(1)} %join.14.refs_0_), channel_id=1, source_target_pairs={{0,32},{1,33},{2,34},{3,35},{4,36},{5,37},{6,38},{7,39},{8,40},{9,... | collective-permute-start | bytes 1597448 | tf_op jit(solution)/shard_map/ppermute | solution.py:24
  92.3 5.4 %collective-permute-start.24 = (bf16[16,1664]{1,0:T(8,128)(2,1)S(1)}, bf16[16,1664]{1,0:T(8,128)(2,1)S(1)}, u32[]{:S(2)}, u32[]{:S(2)}) collective-permute-start(bf16[16,1664]{1,0:T(8,128)(2,1)S(1)} %collective-permute-done.22.refs_0_), channel_id=1, source_target_pairs={{0,96},{1,97},{2,98},{3,99},{4,100},{5,101},{6,102},{7,103},{8,104... | collective-permute-start | bytes 159752 | tf_op jit(solution)/shard_map/ppermute | solution.py:24
  97.7 5.0 %collective-permute-start.25 = (bf16[32,1664]{1,0:T(8,128)(2,1)S(1)}, bf16[32,1664]{1,0:T(8,128)(2,1)S(1)}, u32[]{:S(2)}, u32[]{:S(2)}) collective-permute-start(bf16[32,1664]{1,0:T(8,128)(2,1)S(1)} %join.15.refs_0_), channel_id=1, source_target_pairs={{0,32},{1,33},{2,34},{3,35},{4,36},{5,37},{6,38},{7,39},{8,40},{9,... | collective-permute-start | bytes 319496 | tf_op jit(solution)/shard_map/ppermute | solution.py:24
  102.8 3.0 %collective-permute-start.26 = (bf16[320,1664]{1,0:T(8,128)(2,1)S(1)}, bf16[320,1664]{1,0:T(8,128)(2,1)S(1)}, u32[]{:S(2)}, u32[]{:S(2)}) collective-permute-start(bf16[320,1664]{1,0:T(8,128)(2,1)S(1)} %join.16.refs_0_), channel_id=1, source_target_pairs={{0,16},{1,17},{2,18},{3,19},{4,20},{5,21},{6,22},{7,23},{8,24},{9,... | collective-permute-start | bytes 3194888 | tf_op jit(solution)/shard_map/ppermute | solution.py:24
  103.1 8.4 %collective-permute-start.28 = (bf16[64,1664]{1,0:T(8,128)(2,1)S(1)}, bf16[64,1664]{1,0:T(8,128)(2,1)S(1)}, u32[]{:S(2)}, u32[]{:S(2)}) collective-permute-start(bf16[64,1664]{1,0:T(8,128)(2,1)S(1)} %join.17.refs_2_), channel_id=1, source_target_pairs={{0,16},{1,17},{2,18},{3,19},{4,20},{5,21},{6,22},{7,23},{8,24},{9,... | collective-permute-start | bytes 638984 | tf_op jit(solution)/shard_map/ppermute | solution.py:24
  108.2 10.5 %collective-permute-start.27 = (bf16[256,1024]{1,0:T(8,128)(2,1)S(1)}, bf16[256,1024]{1,0:T(8,128)(2,1)S(1)}, u32[]{:S(2)}, u32[]{:S(2)}) collective-permute-start(bf16[256,1024]{1,0:T(8,128)(2,1)S(1)} %slice.185), channel_id=1, source_target_pairs={{0,12},{1,13},{2,14},{3,15},{4,8},{5,9},{6,10},{7,11},{8,4},{9,5},... | collective-permute-start | bytes 1572872 | tf_op jit(solution)/shard_map/ppermute | solution.py:24
  112.8 8.9 %collective-permute-start.30 = (bf16[128,1024]{1,0:T(8,128)(2,1)S(1)}, bf16[128,1024]{1,0:T(8,128)(2,1)S(1)}, u32[]{:S(2)}, u32[]{:S(2)}) collective-permute-start(bf16[128,1024]{1,0:T(8,128)(2,1)S(1)} %slice.186), channel_id=1, source_target_pairs={{0,12},{1,13},{2,14},{3,15},{4,8},{5,9},{6,10},{7,11},{8,4},{9,5},... | collective-permute-start | bytes 786440 | tf_op jit(solution)/shard_map/ppermute | solution.py:24
  118.9 6.5 %collective-permute-start.29 = (bf16[128,1024]{1,0:T(8,128)(2,1)S(1)}, bf16[128,1024]{1,0:T(8,128)(2,1)S(1)}, u32[]{:S(2)}, u32[]{:S(2)}) collective-permute-start(bf16[128,1024]{1,0:T(8,128)(2,1)S(1)} %slice.188), channel_id=1, source_target_pairs={{0,4},{1,5},{2,6},{3,7},{4,0},{5,1},{6,2},{7,3},{8,12},{9,13},{10,... | collective-permute-start | bytes 786440 | tf_op jit(solution)/shard_map/ppermute | solution.py:24
  121.8 5.1 %collective-permute-start.34 = (bf16[64,1024]{1,0:T(8,128)(2,1)S(1)}, bf16[64,1024]{1,0:T(8,128)(2,1)S(1)}, u32[]{:S(2)}, u32[]{:S(2)}) collective-permute-start(bf16[64,1024]{1,0:T(8,128)(2,1)S(1)} %slice.190), channel_id=1, source_target_pairs={{0,4},{1,5},{2,6},{3,7},{4,0},{5,1},{6,2},{7,3},{8,12},{9,13},{10,... | collective-permute-start | bytes 393224 | tf_op jit(solution)/shard_map/ppermute | solution.py:24
  126.9 6.6 %collective-permute-start.35 = (bf16[16,1024]{1,0:T(8,128)(2,1)S(1)}, bf16[16,1024]{1,0:T(8,128)(2,1)S(1)}, u32[]{:S(2)}, u32[]{:S(2)}) collective-permute-start(bf16[16,1024]{1,0:T(8,128)(2,1)S(1)} %get-tuple-element.80), channel_id=1, source_target_pairs={{0,1},{1,0},{2,3},{3,2},{4,5},{5,4},{6,7},{7,6},{8,9},{9,8},{10,11... | collective-permute-start | bytes 98312 | tf_op jit(solution)/shard_map/ppermute | solution.py:24
  127.0 7.1 %collective-permute-start.37 = (bf16[16,1024]{1,0:T(8,128)(2,1)S(1)}, bf16[16,1024]{1,0:T(8,128)(2,1)S(1)}, u32[]{:S(2)}, u32[]{:S(2)}) collective-permute-start(bf16[16,1024]{1,0:T(8,128)(2,1)S(1)} %get-tuple-element.81), channel_id=1, source_target_pairs={{0,3},{1,2},{2,1},{3,0},{4,7},{5,6},{6,5},{7,4},{8,11},{9,10},{10,... | collective-permute-start | bytes 98312 | tf_op jit(solution)/shard_map/ppermute | solution.py:24
  129.0 5.1 %collective-permute-start.36 = (bf16[16,1024]{1,0:T(8,128)(2,1)S(1)}, bf16[16,1024]{1,0:T(8,128)(2,1)S(1)}, u32[]{:S(2)}, u32[]{:S(2)}) collective-permute-start(bf16[16,1024]{1,0:T(8,128)(2,1)S(1)} %get-tuple-element.82), channel_id=1, source_target_pairs={{0,2},{1,3},{2,0},{3,1},{4,6},{5,7},{6,4},{7,5},{8,10},{9,11},{10,... | collective-permute-start | bytes 98312 | tf_op jit(solution)/shard_map/ppermute | solution.py:24
  130.5 4.9 %collective-permute-start.31 = (bf16[32,1024]{1,0:T(8,128)(2,1)S(1)}, bf16[32,1024]{1,0:T(8,128)(2,1)S(1)}, u32[]{:S(2)}, u32[]{:S(2)}) collective-permute-start(bf16[32,1024]{1,0:T(8,128)(2,1)S(1)} %get-tuple-element.71), channel_id=1, source_target_pairs={{0,1},{1,0},{2,3},{3,2},{4,5},{5,4},{6,7},{7,6},{8,9},{9,8},{10,11... | collective-permute-start | bytes 196616 | tf_op jit(solution)/shard_map/ppermute | solution.py:24
  131.6 6.1 %collective-permute-start.33 = (bf16[32,1024]{1,0:T(8,128)(2,1)S(1)}, bf16[32,1024]{1,0:T(8,128)(2,1)S(1)}, u32[]{:S(2)}, u32[]{:S(2)}) collective-permute-start(bf16[32,1024]{1,0:T(8,128)(2,1)S(1)} %get-tuple-element.72), channel_id=1, source_target_pairs={{0,3},{1,2},{2,1},{3,0},{4,7},{5,6},{6,5},{7,4},{8,11},{9,10},{10,... | collective-permute-start | bytes 196616 | tf_op jit(solution)/shard_map/ppermute | solution.py:24
  133.5 5.6 %collective-permute-start.32 = (bf16[32,1024]{1,0:T(8,128)(2,1)S(1)}, bf16[32,1024]{1,0:T(8,128)(2,1)S(1)}, u32[]{:S(2)}, u32[]{:S(2)}) collective-permute-start(bf16[32,1024]{1,0:T(8,128)(2,1)S(1)} %get-tuple-element.73), channel_id=1, source_target_pairs={{0,2},{1,3},{2,0},{3,1},{4,6},{5,7},{6,4},{7,5},{8,10},{9,11},{10,... | collective-permute-start | bytes 196616 | tf_op jit(solution)/shard_map/ppermute | solution.py:24

commit v5 on v3

--- a/solution.py
+++ b/solution.py
@@ -219,23 +219,23 @@
 
 
 def scatter_out(hidden, weight, rows):
-    width = weight.shape[1] // 2
-    stays, got = [None, None], [None, None]
+    parts, stays, got = (slice(0, 640), slice(640, None)), [None, None], [None, None]
+    for c, part in enumerate(parts):
+        s = dot(hidden, weight[:, part])
+        stays[c], turn = s[: 8 * rows], s[8 * rows :]
+        got[c] = exchange(turn, masks_x=SECOND)
     for c in range(2):
-        s = dot(hidden, weight[:, c * width : (c + 1) * width])
-        stays[c], sent = s[: 8 * rows], s[8 * rows :]
-        got[c] = exchange(sent, masks_x=SECOND)
-    got[0], _ = tie(got[0], sent)
+        got[c], _ = tie(got[c], turn)
+        stays[c], turn = halve(stays[c], got[c], 4 * rows)
+        got[c] = exchange(turn, masks_x=FIRST)
+    columns = []
     for c in range(2):
         if c == 1:
-            got[1], got[0] = tie(got[1], got[0])
-        stays[c], sent = halve(stays[c], got[c], 4 * rows)
-        got[c] = exchange(sent, masks_x=FIRST)
-    columns = []
-    for c in range(2):
+            got[1], z[1] = tie(got[1], z[1])
         v = add(stays[c], got[c])
-        parts = [v[:rows]] + [exchange(v[m * rows : (m + 1) * rows], z=m) for m in (1, 2, 3)]
-        columns.append(functools.reduce(jnp.add, [p.astype(F32) for p in parts]).astype(BF))
+        z = [v[:rows]] + [exchange(v[m * rows : (m + 1) * rows], z=m) for m in (1, 2, 3)]
+        columns.append(z)
+    columns = [functools.reduce(jnp.add, [p.astype(F32) for p in z]).astype(BF) for z in columns]
     return jnp.concatenate(columns, axis=1)
 
 

time: 140 us -> 138 us (0.986)
  waiting for transfers between devices: 61.6 us -> 58.4 us
    ppermute x38, waiting for transfers between devices: 61.6 us -> 58.4 us  [exchange(): return lax.ppermute(value, ('gx', 'gy'), pairs)]
where the time goes in v5:
time: 138 us; the launch traced here: 136 us
  waiting for transfers between devices  58.4 us (42%)
  starting transfers between devices  58 us (42%)
  matrix products  9.62 us (7%)
  local copies, waits for them, and re-layouts  5.36 us (4%)
  Pallas kernels  2.35 us (2%)
  other arithmetic  2.08 us (2%)
    ppermute x38, waiting for transfers between devices, exchange(): return lax.ppermute(value, ('gx', 'gy'), pairs)  58.4 us
    ppermute x38, starting transfers between devices, exchange(): return lax.ppermute(value, ('gx', 'gy'), pairs)  58 us
    dot_general x5, matrix products, dot(): return jnp.dot(a, b, preferred_element_type=F32).astype(BF)  9.62 us
    unnamed x8, local copies, waits for them, and re-layouts  4.86 us
  transfers between devices with their start and end apart: 38, of which 22 were waited for; matrix products, arithmetic and copies ran while one was open for 5% of the time, Pallas kernels for 1%

profile of v5, /device:TPU:24, one launch (start us, length us, event | category | flops | bytes accessed | tf_op | source)
XLA Modules:
  0.0 136.3 jit_solution(5595381627017869323)
XLA Ops:
  0.0 1.9 %collective-permute-start = (bf16[48,1024]{1,0:T(8,128)(2,1)}, bf16[48,1024]{1,0:T(8,128)(2,1)S(1)}, u32[]{:S(2)}, u32[]{:S(2)}) collective-permute-start(bf16[48,1024]{1,0:T(8,128)(2,1)} %refs_0_.1), channel_id=1, source_target_pairs={{0,1},{1,0},{2,3},{3,2},{4,5},{5,4},{6,7},{7,6},{8,9},{9,8},{10,11... | collective-permute-start | bytes 294920 | tf_op jit(solution)/shard_map/ppermute | solution.py:26
  1.9 2.8 %collective-permute-start.4 = (bf16[48,1024]{1,0:T(8,128)(2,1)}, bf16[48,1024]{1,0:T(8,128)(2,1)S(1)}, u32[]{:S(2)}, u32[]{:S(2)}) collective-permute-start(bf16[48,1024]{1,0:T(8,128)(2,1)} %refs_0_.1), channel_id=1, source_target_pairs={{0,3},{1,2},{2,1},{3,0},{4,7},{5,6},{6,5},{7,4},{8,11},{9,10},{10,... | collective-permute-start | bytes 294920 | tf_op jit(solution)/shard_map/ppermute | solution.py:26
  6.1 1.6 %collective-permute-start.1 = (bf16[96,1024]{1,0:T(8,128)(2,1)S(1)}, bf16[96,1024]{1,0:T(8,128)(2,1)S(1)}, u32[]{:S(2)}, u32[]{:S(2)}) collective-permute-start(bf16[96,1024]{1,0:T(8,128)(2,1)S(1)} %join.10.refs_0_), channel_id=1, source_target_pairs={{0,4},{1,5},{2,6},{3,7},{4,0},{5,1},{6,2},{7,3},{8,12},{9,13},{10,... | collective-permute-start | bytes 589832 | tf_op jit(solution)/shard_map/ppermute | solution.py:26
  7.7 3.1 %collective-permute-done.4.refs_1_ = bf16[48,1024]{1,0:T(8,128)(2,1)S(1)} collective-permute-done((bf16[48,1024]{1,0:T(8,128)(2,1)}, bf16[48,1024]{1,0:T(8,128)(2,1)S(1)}, u32[]{:S(2)}, u32[]{:S(2)}) %collective-permute-start.4) | collective-permute-done | bytes 98336 | tf_op jit(solution)/shard_map/ppermute | solution.py:26
  10.8 3.5 %collective-permute-done.3.refs_0_ = bf16[48,1024]{1,0:T(8,128)(2,1)S(1)} collective-permute-done((bf16[48,1024]{1,0:T(8,128)(2,1)}, bf16[48,1024]{1,0:T(8,128)(2,1)S(1)}, u32[]{:S(2)}, u32[]{:S(2)}) %collective-permute-start.3) | collective-permute-done | bytes 98336 | tf_op jit(solution)/shard_map/ppermute | solution.py:26
  14.3 1.6 %collective-permute-start.5 = (bf16[96,1024]{1,0:T(8,128)(2,1)S(1)}, bf16[96,1024]{1,0:T(8,128)(2,1)S(1)}, u32[]{:S(2)}, u32[]{:S(2)}) collective-permute-start(bf16[96,1024]{1,0:T(8,128)(2,1)S(1)} %join.12.refs_0_.refs_3_), channel_id=1, source_target_pairs={{0,4},{1,5},{2,6},{3,7},{4,0},{5,1},{6,2},{7,3},{8,12},{9,13},{10,... | collective-permute-start | bytes 589832 | tf_op jit(solution)/shard_map/ppermute | solution.py:26
  15.9 2.2 %collective-permute-start.2 = (bf16[192,1024]{1,0:T(8,128)(2,1)S(1)}, bf16[192,1024]{1,0:T(8,128)(2,1)S(1)}, u32[]{:S(2)}, u32[]{:S(2)}) collective-permute-start(bf16[192,1024]{1,0:T(8,128)(2,1)S(1)} %join.11), channel_id=1, source_target_pairs={{0,12},{1,13},{2,14},{3,15},{4,8},{5,9},{6,10},{7,11},{8,4},{9,5},... | collective-permute-start | bytes 1179656 | tf_op jit(solution)/shard_map/ppermute | solution.py:26
  18.1 3.1 %collective-permute-done.5.refs_1_.refs_4_ = bf16[96,1024]{1,0:T(8,128)(2,1)S(1)} collective-permute-done((bf16[96,1024]{1,0:T(8,128)(2,1)S(1)}, bf16[96,1024]{1,0:T(8,128)(2,1)S(1)}, u32[]{:S(2)}, u32[]{:S(2)}) %collective-permute-start.5) | collective-permute-done | bytes 196640 | tf_op jit(solution)/shard_map/ppermute | solution.py:26
  21.2 3.9 %collective-permute-start.6 = (bf16[192,1024]{1,0:T(8,128)(2,1)S(1)}, bf16[192,1024]{1,0:T(8,128)(2,1)S(1)}, u32[]{:S(2)}, u32[]{:S(2)}) collective-permute-start(bf16[192,1024]{1,0:T(8,128)(2,1)S(1)} %join.13), channel_id=1, source_target_pairs={{0,12},{1,13},{2,14},{3,15},{4,8},{5,9},{6,10},{7,11},{8,4},{9,5},... | collective-permute-start | bytes 1179656 | tf_op jit(solution)/shard_map/ppermute | solution.py:26
  25.0 2.0 %copy-done = bf16[1024,1664]{1,0:T(8,128)(2,1)S(1)} copy-done((bf16[1024,1664]{1,0:T(8,128)(2,1)S(1)}, bf16[1024,1664]{1,0:T(8,128)(2,1)}, u32[]{:S(2)}) %copy-start) | copy-done | bytes 3407896
  27.0 2.0 %copy-done.1 = bf16[1024,1664]{1,0:T(8,128)(2,1)S(1)} copy-done((bf16[1024,1664]{1,0:T(8,128)(2,1)S(1)}, bf16[1024,1664]{1,0:T(8,128)(2,1)}, u32[]{:S(2)}) %copy-start.1) | copy-done | bytes 3407896
  29.0 1.5 %pack.1 = bf16[1024,3328]{1,0:T(8,128)(2,1)S(1)} custom-call(bf16[1024,1664]{1,0:T(8,128)(2,1)S(1)} %copy-done, bf16[1024,1664]{1,0:T(8,128)(2,1)S(1)} %copy-done.1), custom_call_target="tpu_custom_call" | custom-call | bytes 13631488 | tf_op jit(solution)/shard_map/pack/pallas_call | solution.py:91
  31.0 1.9 %convolution_convert_fusion.2 = bf16[256,3328]{1,0:T(8,128)(2,1)S(1)} fusion(bf16[256,1024]{1,0:T(8,128)(2,1)S(1)} %get-tuple-element.27, bf16[1024,3328]{1,0:T(8,128)(2,1)S(1)} %pack.1), kind=kOutput, calls=%fused_computation.2 | convolution fusion | flops 1745682432 | bytes 9043968 | tf_op jit(solution)/shard_map/dot_general | solution.py:164
  33.1 1.9 %convolution_convert_fusion.1 = bf16[256,3328]{1,0:T(8,128)(2,1)S(1)} fusion(bf16[256,1024]{1,0:T(8,128)(2,1)S(1)} %get-tuple-element.30, bf16[1024,3328]{1,0:T(8,128)(2,1)S(1)} %pack.1), kind=kOutput, calls=%fused_computation.1 | convolution fusion | flops 1745682432 | bytes 9043968 | tf_op jit(solution)/shard_map/dot_general | solution.py:164
  37.0 1.9 %convolution_convert_fusion = bf16[256,3328]{1,0:T(8,128)(2,1)S(1)} fusion(bf16[256,1024]{1,0:T(8,128)(2,1)S(1)} %get-tuple-element.33, bf16[1024,3328]{1,0:T(8,128)(2,1)S(1)} %pack.1), kind=kOutput, calls=%fused_computation | convolution fusion | flops 1745682432 | bytes 9043968 | tf_op jit(solution)/shard_map/dot_general | solution.py:164
  39.3 1.4 %collective-permute-start.12 = (bf16[64,3328]{1,0:T(8,128)(2,1)S(1)}, bf16[64,3328]{1,0:T(8,128)(2,1)S(1)}, u32[]{:S(2)}, u32[]{:S(2)}) collective-permute-start(bf16[64,3328]{1,0:T(8,128)(2,1)S(1)} %slice.176), channel_id=1, source_target_pairs={{0,32},{1,33},{2,34},{3,35},{4,36},{5,37},{6,38},{7,39},{8,40},{9,... | collective-permute-start | bytes 1277960 | tf_op jit(solution)/shard_map/ppermute | solution.py:26
  41.7 1.4 %collective-permute-start.15 = (bf16[64,3328]{1,0:T(8,128)(2,1)S(1)}, bf16[64,3328]{1,0:T(8,128)(2,1)S(1)}, u32[]{:S(2)}, u32[]{:S(2)}) collective-permute-start(bf16[64,3328]{1,0:T(8,128)(2,1)S(1)} %slice.177), channel_id=1, source_target_pairs={{0,32},{1,33},{2,34},{3,35},{4,36},{5,37},{6,38},{7,39},{8,40},{9,... | collective-permute-start | bytes 1277960 | tf_op jit(solution)/shard_map/ppermute | solution.py:26
  43.1 1.3 collective-permute-done.8
  44.8 5.7 %collective-permute-done.12 = bf16[64,3328]{1,0:T(8,128)(2,1)S(1)} collective-permute-done((bf16[64,3328]{1,0:T(8,128)(2,1)S(1)}, bf16[64,3328]{1,0:T(8,128)(2,1)S(1)}, u32[]{:S(2)}, u32[]{:S(2)}) %collective-permute-start.12) | collective-permute-done | bytes 426016 | tf_op jit(solution)/shard_map/ppermute | solution.py:26
  50.7 1.3 collective-permute-start.14
  52.0 2.0 %collective-permute-done.11 = bf16[32,3328]{1,0:T(8,128)(2,1)S(1)} collective-permute-done((bf16[32,3328]{1,0:T(8,128)(2,1)S(1)}, bf16[32,3328]{1,0:T(8,128)(2,1)S(1)}, u32[]{:S(2)}, u32[]{:S(2)}) %collective-permute-start.11) | collective-permute-done | bytes 213024 | tf_op jit(solution)/shard_map/ppermute | solution.py:26
  54.1 5.6 %collective-permute-start.13 = (bf16[16,3328]{1,0:T(8,128)(2,1)S(1)}, bf16[16,3328]{1,0:T(8,128)(2,1)S(1)}, u32[]{:S(2)}, u32[]{:S(2)}) collective-permute-start(bf16[16,3328]{1,0:T(8,128)(2,1)S(1)} %get-tuple-element.56), channel_id=1, source_target_pairs={{0,128},{1,129},{2,130},{3,131},{4,132},{5,133},{6,134},{7,135},{8... | collective-permute-start | bytes 319496 | tf_op jit(solution)/shard_map/ppermute | solution.py:26
  60.2 4.6 %collective-permute-start.16 = (bf16[16,3328]{1,0:T(8,128)(2,1)S(1)}, bf16[16,3328]{1,0:T(8,128)(2,1)S(1)}, u32[]{:S(2)}, u32[]{:S(2)}) collective-permute-start(bf16[16,3328]{1,0:T(8,128)(2,1)S(1)} %get-tuple-element.55), channel_id=1, source_target_pairs={{0,128},{1,129},{2,130},{3,131},{4,132},{5,133},{6,134},{7,135},{8... | collective-permute-start | bytes 319496 | tf_op jit(solution)/shard_map/ppermute | solution.py:26
  64.9 2.1 %collective-permute-done.17 = bf16[32,3328]{1,0:T(8,128)(2,1)S(1)} collective-permute-done((bf16[32,3328]{1,0:T(8,128)(2,1)S(1)}, bf16[32,3328]{1,0:T(8,128)(2,1)S(1)}, u32[]{:S(2)}, u32[]{:S(2)}) %collective-permute-start.17) | collective-permute-done | bytes 213024 | tf_op jit(solution)/shard_map/ppermute | solution.py:26
  67.0 4.0 %collective-permute-start.18 = (bf16[16,3328]{1,0:T(8,128)(2,1)S(1)}, bf16[16,3328]{1,0:T(8,128)(2,1)S(1)}, u32[]{:S(2)}, u32[]{:S(2)}) collective-permute-start(bf16[16,3328]{1,0:T(8,128)(2,1)S(1)} %get-tuple-element.53), channel_id=1, source_target_pairs={{0,128},{1,129},{2,130},{3,131},{4,132},{5,133},{6,134},{7,135},{8... | collective-permute-start | bytes 319496 | tf_op jit(solution)/shard_map/ppermute | solution.py:26
  71.0 2.0 %collective-permute-start.21 = (bf16[16,1664]{1,0:T(8,128)(2,1)S(1)}, bf16[16,1664]{1,0:T(8,128)(2,1)S(1)}, u32[]{:S(2)}, u32[]{:S(2)}) collective-permute-start(bf16[16,1664]{1,0:T(8,128)(2,1)S(1)} %silu.3.refs_0_), channel_id=1, source_target_pairs={{0,128},{1,129},{2,130},{3,131},{4,132},{5,133},{6,134},{7,135},{8... | collective-permute-start | bytes 159752 | tf_op jit(solution)/shard_map/ppermute | solution.py:26
  73.1 4.0 %collective-permute-start.22 = (bf16[16,1664]{1,0:T(8,128)(2,1)S(1)}, bf16[16,1664]{1,0:T(8,128)(2,1)S(1)}, u32[]{:S(2)}, u32[]{:S(2)}) collective-permute-start(bf16[16,1664]{1,0:T(8,128)(2,1)S(1)} %silu.4.refs_1_), channel_id=1, source_target_pairs={{0,128},{1,129},{2,130},{3,131},{4,132},{5,133},{6,134},{7,135},{8... | collective-permute-start | bytes 159752 | tf_op jit(solution)/shard_map/ppermute | solution.py:26
  77.1 1.8 %collective-permute-done.18.b_ref = bf16[16,3328]{1,0:T(8,128)(2,1)S(1)} collective-permute-done((bf16[16,3328]{1,0:T(8,128)(2,1)S(1)}, bf16[16,3328]{1,0:T(8,128)(2,1)S(1)}, u32[]{:S(2)}, u32[]{:S(2)}) %collective-permute-start.18) | collective-permute-done | bytes 106528 | tf_op jit(solution)/shard_map/ppermute | solution.py:26
  78.9 2.4 %collective-permute-start.23 = (bf16[16,1664]{1,0:T(8,128)(2,1)S(1)}, bf16[16,1664]{1,0:T(8,128)(2,1)S(1)}, u32[]{:S(2)}, u32[]{:S(2)}) collective-permute-start(bf16[16,1664]{1,0:T(8,128)(2,1)S(1)} %silu.5.refs_2_), channel_id=1, source_target_pairs={{0,128},{1,129},{2,130},{3,131},{4,132},{5,133},{6,134},{7,135},{8... | collective-permute-start | bytes 159752 | tf_op jit(solution)/shard_map/ppermute | solution.py:26
  82.4 4.7 %collective-permute-done.23.refs_2_ = bf16[16,1664]{1,0:T(8,128)(2,1)S(1)} collective-permute-done((bf16[16,1664]{1,0:T(8,128)(2,1)S(1)}, bf16[16,1664]{1,0:T(8,128)(2,1)S(1)}, u32[]{:S(2)}, u32[]{:S(2)}) %collective-permute-start.23) | collective-permute-done | bytes 53280 | tf_op jit(solution)/shard_map/ppermute | solution.py:26
  87.1 1.3 collective-permute-start.24
  88.3 1.3 collective-permute-done.19.refs_1_
  89.8 5.6 %collective-permute-done.24.refs_1_ = bf16[48,1664]{1,0:T(8,128)(2,1)S(1)} collective-permute-done((bf16[48,1664]{1,0:T(8,128)(2,1)S(1)}, bf16[48,1664]{1,0:T(8,128)(2,1)S(1)}, u32[]{:S(2)}, u32[]{:S(2)}) %collective-permute-start.24) | collective-permute-done | bytes 159776 | tf_op jit(solution)/shard_map/ppermute | solution.py:26
  95.5 1.3 collective-permute-done.20.refs_1_
  97.1 5.3 %collective-permute-done.25.refs_1_ = bf16[96,1664]{1,0:T(8,128)(2,1)S(1)} collective-permute-done((bf16[96,1664]{1,0:T(8,128)(2,1)S(1)}, bf16[96,1664]{1,0:T(8,128)(2,1)S(1)}, u32[]{:S(2)}, u32[]{:S(2)}) %collective-permute-start.25) | collective-permute-done | bytes 319520 | tf_op jit(solution)/shard_map/ppermute | solution.py:26
  102.6 2.1 %collective-permute-done.27.refs_3_ = bf16[192,1664]{1,0:T(8,128)(2,1)S(1)} collective-permute-done((bf16[192,1664]{1,0:T(8,128)(2,1)S(1)}, bf16[192,1664]{1,0:T(8,128)(2,1)S(1)}, u32[]{:S(2)}, u32[]{:S(2)}) %collective-permute-start.27) | collective-permute-done | bytes 639008 | tf_op jit(solution)/shard_map/ppermute | solution.py:26
  105.0 2.3 %fusion.2 = bf16[768,640]{1,0:T(8,128)(2,1)S(1)} fusion(bf16[768,1664]{1,0:T(8,128)(2,1)S(1)} %place.1, bf16[1664,1024]{1,0:T(8,128)(2,1)S(1)} %copy-done.3), kind=kOutput, calls=%fused_computation.8 | convolution fusion | flops 1636270080 | bytes 5668864 | tf_op jit(solution)/shard_map/dot_general | solution.py:164
  107.3 3.3 %collective-permute-start.28 = (bf16[384,640]{1,0:T(8,128)(2,1)S(1)}, bf16[384,640]{1,0:T(8,128)(2,1)S(1)}, u32[]{:S(2)}, u32[]{:S(2)}) collective-permute-start(bf16[384,640]{1,0:T(8,128)(2,1)S(1)} %slice.193), channel_id=1, source_target_pairs={{0,12},{1,13},{2,14},{3,15},{4,8},{5,9},{6,10},{7,11},{8,4},{9,5},... | collective-permute-start | bytes 1474568 | tf_op jit(solution)/shard_map/ppermute | solution.py:26
  110.6 1.5 %convolution_convert_fusion.3 = bf16[768,384]{1,0:T(8,128)(2,1)S(1)} fusion(bf16[768,1664]{1,0:T(8,128)(2,1)S(1)} %place.1, bf16[1664,1024]{1,0:T(8,128)(2,1)S(1)} %copy-done.3), kind=kOutput, calls=%fused_computation.9 | convolution fusion | flops 981762048 | bytes 4423680 | tf_op jit(solution)/shard_map/dot_general | solution.py:164
  112.3 5.1 %collective-permute-done.28 = bf16[384,640]{1,0:T(8,128)(2,1)S(1)} collective-permute-done((bf16[384,640]{1,0:T(8,128)(2,1)S(1)}, bf16[384,640]{1,0:T(8,128)(2,1)S(1)}, u32[]{:S(2)}, u32[]{:S(2)}) %collective-permute-start.28) | collective-permute-done | bytes 491552 | tf_op jit(solution)/shard_map/ppermute | solution.py:26
  117.7 3.6 %collective-permute-done.30 = bf16[384,384]{1,0:T(8,128)(2,1)S(1)} collective-permute-done((bf16[384,384]{1,0:T(8,128)(2,1)S(1)}, bf16[384,384]{1,0:T(8,128)(2,1)S(1)}, u32[]{:S(2)}, u32[]{:S(2)}) %collective-permute-start.30) | collective-permute-done | bytes 294944 | tf_op jit(solution)/shard_map/ppermute | solution.py:26
  121.5 2.4 %collective-permute-done.29 = bf16[192,640]{1,0:T(8,128)(2,1)S(1)} collective-permute-done((bf16[192,640]{1,0:T(8,128)(2,1)S(1)}, bf16[192,640]{1,0:T(8,128)(2,1)S(1)}, u32[]{:S(2)}, u32[]{:S(2)}) %collective-permute-start.29) | collective-permute-done | bytes 245792 | tf_op jit(solution)/shard_map/ppermute | solution.py:26
  124.1 2.5 %collective-permute-start.33 = (bf16[48,640]{1,0:T(8,128)(2,1)S(1)}, bf16[48,640]{1,0:T(8,128)(2,1)S(1)}, u32[]{:S(2)}, u32[]{:S(2)}) collective-permute-start(bf16[48,640]{1,0:T(8,128)(2,1)S(1)} %get-tuple-element.49), channel_id=1, source_target_pairs={{0,2},{1,3},{2,0},{3,1},{4,6},{5,7},{6,4},{7,5},{8,10},{9,11},{10,... | collective-permute-start | bytes 184328 | tf_op jit(solution)/shard_map/ppermute | solution.py:26
  126.5 1.9 %collective-permute-start.34 = (bf16[48,640]{1,0:T(8,128)(2,1)S(1)}, bf16[48,640]{1,0:T(8,128)(2,1)S(1)}, u32[]{:S(2)}, u32[]{:S(2)}) collective-permute-start(bf16[48,640]{1,0:T(8,128)(2,1)S(1)} %get-tuple-element.50), channel_id=1, source_target_pairs={{0,3},{1,2},{2,1},{3,0},{4,7},{5,6},{6,5},{7,4},{8,11},{9,10},{10,... | collective-permute-start | bytes 184328 | tf_op jit(solution)/shard_map/ppermute | solution.py:26
  128.8 1.9 %collective-permute-start.37 = (bf16[48,384]{1,0:T(8,128)(2,1)S(1)}, bf16[48,384]{1,0:T(8,128)(2,1)S(1)}, u32[]{:S(2)}, u32[]{:S(2)}) collective-permute-start(bf16[48,384]{1,0:T(8,128)(2,1)S(1)} %get-tuple-element.59), channel_id=1, source_target_pairs={{0,3},{1,2},{2,1},{3,0},{4,7},{5,6},{6,5},{7,4},{8,11},{9,10},{10,... | collective-permute-start | bytes 110600 | tf_op jit(solution)/shard_map/ppermute | solution.py:26
  130.7 1.4 %collective-permute-start.36 = (bf16[48,384]{1,0:T(8,128)(2,1)S(1)}, bf16[48,384]{1,0:T(8,128)(2,1)S(1)}, u32[]{:S(2)}, u32[]{:S(2)}) collective-permute-start(bf16[48,384]{1,0:T(8,128)(2,1)S(1)} %get-tuple-element.60), channel_id=1, source_target_pairs={{0,2},{1,3},{2,0},{3,1},{4,6},{5,7},{6,4},{7,5},{8,10},{9,11},{10,... | collective-permute-start | bytes 110600 | tf_op jit(solution)/shard_map/ppermute | solution.py:26
  133.0 1.6 %collective-permute-done.37 = bf16[48,384]{1,0:T(8,128)(2,1)S(1)} collective-permute-done((bf16[48,384]{1,0:T(8,128)(2,1)S(1)}, bf16[48,384]{1,0:T(8,128)(2,1)S(1)}, u32[]{:S(2)}, u32[]{:S(2)}) %collective-permute-start.37) | collective-permute-done | bytes 36896 | tf_op jit(solution)/shard_map/ppermute | solution.py:26
  134.5 1.0 collective-permute-done.36
  (91 shorter events, 11.5 us)
Async XLA Ops:
  0.0 5.2 %collective-permute-start = (bf16[48,1024]{1,0:T(8,128)(2,1)}, bf16[48,1024]{1,0:T(8,128)(2,1)S(1)}, u32[]{:S(2)}, u32[]{:S(2)}) collective-permute-start(bf16[48,1024]{1,0:T(8,128)(2,1)} %refs_0_.1), channel_id=1, source_target_pairs={{0,1},{1,0},{2,3},{3,2},{4,5},{5,4},{6,7},{7,6},{8,9},{9,8},{10,11... | collective-permute-start | bytes 294920 | tf_op jit(solution)/shard_map/ppermute | solution.py:26
  1.9 8.9 %collective-permute-start.4 = (bf16[48,1024]{1,0:T(8,128)(2,1)}, bf16[48,1024]{1,0:T(8,128)(2,1)S(1)}, u32[]{:S(2)}, u32[]{:S(2)}) collective-permute-start(bf16[48,1024]{1,0:T(8,128)(2,1)} %refs_0_.1), channel_id=1, source_target_pairs={{0,3},{1,2},{2,1},{3,0},{4,7},{5,6},{6,5},{7,4},{8,11},{9,10},{10,... | collective-permute-start | bytes 294920 | tf_op jit(solution)/shard_map/ppermute | solution.py:26
  4.7 9.5 %collective-permute-start.3 = (bf16[48,1024]{1,0:T(8,128)(2,1)}, bf16[48,1024]{1,0:T(8,128)(2,1)S(1)}, u32[]{:S(2)}, u32[]{:S(2)}) collective-permute-start(bf16[48,1024]{1,0:T(8,128)(2,1)} %refs_0_.1), channel_id=1, source_target_pairs={{0,2},{1,3},{2,0},{3,1},{4,6},{5,7},{6,4},{7,5},{8,10},{9,11},{10,... | collective-permute-start | bytes 294920 | tf_op jit(solution)/shard_map/ppermute | solution.py:26
  5.2 0.9 copy-start.2
  6.1 9.7 %collective-permute-start.1 = (bf16[96,1024]{1,0:T(8,128)(2,1)S(1)}, bf16[96,1024]{1,0:T(8,128)(2,1)S(1)}, u32[]{:S(2)}, u32[]{:S(2)}) collective-permute-start(bf16[96,1024]{1,0:T(8,128)(2,1)S(1)} %join.10.refs_0_), channel_id=1, source_target_pairs={{0,4},{1,5},{2,6},{3,7},{4,0},{5,1},{6,2},{7,3},{8,12},{9,13},{10,... | collective-permute-start | bytes 589832 | tf_op jit(solution)/shard_map/ppermute | solution.py:26
  14.3 6.9 %collective-permute-start.5 = (bf16[96,1024]{1,0:T(8,128)(2,1)S(1)}, bf16[96,1024]{1,0:T(8,128)(2,1)S(1)}, u32[]{:S(2)}, u32[]{:S(2)}) collective-permute-start(bf16[96,1024]{1,0:T(8,128)(2,1)S(1)} %join.12.refs_0_.refs_3_), channel_id=1, source_target_pairs={{0,4},{1,5},{2,6},{3,7},{4,0},{5,1},{6,2},{7,3},{8,12},{9,13},{10,... | collective-permute-start | bytes 589832 | tf_op jit(solution)/shard_map/ppermute | solution.py:26
  15.9 14.5 %collective-permute-start.2 = (bf16[192,1024]{1,0:T(8,128)(2,1)S(1)}, bf16[192,1024]{1,0:T(8,128)(2,1)S(1)}, u32[]{:S(2)}, u32[]{:S(2)}) collective-permute-start(bf16[192,1024]{1,0:T(8,128)(2,1)S(1)} %join.11), channel_id=1, source_target_pairs={{0,12},{1,13},{2,14},{3,15},{4,8},{5,9},{6,10},{7,11},{8,4},{9,5},... | collective-permute-start | bytes 1179656 | tf_op jit(solution)/shard_map/ppermute | solution.py:26
  21.2 9.6 %collective-permute-start.6 = (bf16[192,1024]{1,0:T(8,128)(2,1)S(1)}, bf16[192,1024]{1,0:T(8,128)(2,1)S(1)}, u32[]{:S(2)}, u32[]{:S(2)}) collective-permute-start(bf16[192,1024]{1,0:T(8,128)(2,1)S(1)} %join.13), channel_id=1, source_target_pairs={{0,12},{1,13},{2,14},{3,15},{4,8},{5,9},{6,10},{7,11},{8,4},{9,5},... | collective-permute-start | bytes 1179656 | tf_op jit(solution)/shard_map/ppermute | solution.py:26
  25.0 2.0 %copy-start = (bf16[1024,1664]{1,0:T(8,128)(2,1)S(1)}, bf16[1024,1664]{1,0:T(8,128)(2,1)}, u32[]{:S(2)}) copy-start(bf16[1024,1664]{1,0:T(8,128)(2,1)} %gate_ref) | copy-start | bytes 10223620
  27.0 2.0 %copy-start.1 = (bf16[1024,1664]{1,0:T(8,128)(2,1)S(1)}, bf16[1024,1664]{1,0:T(8,128)(2,1)}, u32[]{:S(2)}) copy-start(bf16[1024,1664]{1,0:T(8,128)(2,1)} %up_ref.1) | copy-start | bytes 10223620
  33.0 2.7 %collective-permute-start.7 = (bf16[128,3328]{1,0:T(8,128)(2,1)S(1)}, bf16[128,3328]{1,0:T(8,128)(2,1)S(1)}, u32[]{:S(2)}, u32[]{:S(2)}) collective-permute-start(bf16[128,3328]{1,0:T(8,128)(2,1)S(1)} %slice.169), channel_id=1, source_target_pairs={{0,16},{1,17},{2,18},{3,19},{4,20},{5,21},{6,22},{7,23},{8,24},{9,... | collective-permute-start | bytes 2555912 | tf_op jit(solution)/shard_map/ppermute | solution.py:26
  35.1 3.9 %collective-permute-start.10 = (bf16[128,3328]{1,0:T(8,128)(2,1)S(1)}, bf16[128,3328]{1,0:T(8,128)(2,1)S(1)}, u32[]{:S(2)}, u32[]{:S(2)}) collective-permute-start(bf16[128,3328]{1,0:T(8,128)(2,1)S(1)} %slice.170), channel_id=1, source_target_pairs={{0,16},{1,17},{2,18},{3,19},{4,20},{5,21},{6,22},{7,23},{8,24},{9,... | collective-permute-start | bytes 2555912 | tf_op jit(solution)/shard_map/ppermute | solution.py:26
  36.0 8.4 %collective-permute-start.8 = (bf16[64,3328]{1,0:T(8,128)(2,1)S(1)}, bf16[64,3328]{1,0:T(8,128)(2,1)S(1)}, u32[]{:S(2)}, u32[]{:S(2)}) collective-permute-start(bf16[64,3328]{1,0:T(8,128)(2,1)S(1)} %slice.172), channel_id=1, source_target_pairs={{0,32},{1,33},{2,34},{3,35},{4,36},{5,37},{6,38},{7,39},{8,40},{9,... | collective-permute-start | bytes 1277960 | tf_op jit(solution)/shard_map/ppermute | solution.py:26
  39.0 2.5 %collective-permute-start.9 = (bf16[128,3328]{1,0:T(8,128)(2,1)S(1)}, bf16[128,3328]{1,0:T(8,128)(2,1)S(1)}, u32[]{:S(2)}, u32[]{:S(2)}) collective-permute-start(bf16[128,3328]{1,0:T(8,128)(2,1)S(1)} %slice.174), channel_id=1, source_target_pairs={{0,16},{1,17},{2,18},{3,19},{4,20},{5,21},{6,22},{7,23},{8,24},{9,... | collective-permute-start | bytes 2555912 | tf_op jit(solution)/shard_map/ppermute | solution.py:26
  39.3 11.2 %collective-permute-start.12 = (bf16[64,3328]{1,0:T(8,128)(2,1)S(1)}, bf16[64,3328]{1,0:T(8,128)(2,1)S(1)}, u32[]{:S(2)}, u32[]{:S(2)}) collective-permute-start(bf16[64,3328]{1,0:T(8,128)(2,1)S(1)} %slice.176), channel_id=1, source_target_pairs={{0,32},{1,33},{2,34},{3,35},{4,36},{5,37},{6,38},{7,39},{8,40},{9,... | collective-permute-start | bytes 1277960 | tf_op jit(solution)/shard_map/ppermute | solution.py:26
  41.7 17.9 %collective-permute-start.15 = (bf16[64,3328]{1,0:T(8,128)(2,1)S(1)}, bf16[64,3328]{1,0:T(8,128)(2,1)S(1)}, u32[]{:S(2)}, u32[]{:S(2)}) collective-permute-start(bf16[64,3328]{1,0:T(8,128)(2,1)S(1)} %slice.177), channel_id=1, source_target_pairs={{0,32},{1,33},{2,34},{3,35},{4,36},{5,37},{6,38},{7,39},{8,40},{9,... | collective-permute-start | bytes 1277960 | tf_op jit(solution)/shard_map/ppermute | solution.py:26
  44.5 9.5 %collective-permute-start.11 = (bf16[32,3328]{1,0:T(8,128)(2,1)S(1)}, bf16[32,3328]{1,0:T(8,128)(2,1)S(1)}, u32[]{:S(2)}, u32[]{:S(2)}) collective-permute-start(bf16[32,3328]{1,0:T(8,128)(2,1)S(1)} %slice.179), channel_id=1, source_target_pairs={{0,96},{1,97},{2,98},{3,99},{4,100},{5,101},{6,102},{7,103},{8,104... | collective-permute-start | bytes 638984 | tf_op jit(solution)/shard_map/ppermute | solution.py:26
  50.7 9.4 %collective-permute-start.14 = (bf16[32,3328]{1,0:T(8,128)(2,1)S(1)}, bf16[32,3328]{1,0:T(8,128)(2,1)S(1)}, u32[]{:S(2)}, u32[]{:S(2)}) collective-permute-start(bf16[32,3328]{1,0:T(8,128)(2,1)S(1)} %slice.181), channel_id=1, source_target_pairs={{0,96},{1,97},{2,98},{3,99},{4,100},{5,101},{6,102},{7,103},{8,104... | collective-permute-start | bytes 638984 | tf_op jit(solution)/shard_map/ppermute | solution.py:26
  54.1 10.7 %collective-permute-start.13 = (bf16[16,3328]{1,0:T(8,128)(2,1)S(1)}, bf16[16,3328]{1,0:T(8,128)(2,1)S(1)}, u32[]{:S(2)}, u32[]{:S(2)}) collective-permute-start(bf16[16,3328]{1,0:T(8,128)(2,1)S(1)} %get-tuple-element.56), channel_id=1, source_target_pairs={{0,128},{1,129},{2,130},{3,131},{4,132},{5,133},{6,134},{7,135},{8... | collective-permute-start | bytes 319496 | tf_op jit(solution)/shard_map/ppermute | solution.py:26
  59.8 7.1 %collective-permute-start.17 = (bf16[32,3328]{1,0:T(8,128)(2,1)S(1)}, bf16[32,3328]{1,0:T(8,128)(2,1)S(1)}, u32[]{:S(2)}, u32[]{:S(2)}) collective-permute-start(bf16[32,3328]{1,0:T(8,128)(2,1)S(1)} %slice.186), channel_id=1, source_target_pairs={{0,96},{1,97},{2,98},{3,99},{4,100},{5,101},{6,102},{7,103},{8,104... | collective-permute-start | bytes 638984 | tf_op jit(solution)/shard_map/ppermute | solution.py:26
  60.2 12.9 %collective-permute-start.16 = (bf16[16,3328]{1,0:T(8,128)(2,1)S(1)}, bf16[16,3328]{1,0:T(8,128)(2,1)S(1)}, u32[]{:S(2)}, u32[]{:S(2)}) collective-permute-start(bf16[16,3328]{1,0:T(8,128)(2,1)S(1)} %get-tuple-element.55), channel_id=1, source_target_pairs={{0,128},{1,129},{2,130},{3,131},{4,132},{5,133},{6,134},{7,135},{8... | collective-permute-start | bytes 319496 | tf_op jit(solution)/shard_map/ppermute | solution.py:26
  67.0 11.8 %collective-permute-start.18 = (bf16[16,3328]{1,0:T(8,128)(2,1)S(1)}, bf16[16,3328]{1,0:T(8,128)(2,1)S(1)}, u32[]{:S(2)}, u32[]{:S(2)}) collective-permute-start(bf16[16,3328]{1,0:T(8,128)(2,1)S(1)} %get-tuple-element.53), channel_id=1, source_target_pairs={{0,128},{1,129},{2,130},{3,131},{4,132},{5,133},{6,134},{7,135},{8... | collective-permute-start | bytes 319496 | tf_op jit(solution)/shard_map/ppermute | solution.py:26
  71.0 11.4 %collective-permute-start.21 = (bf16[16,1664]{1,0:T(8,128)(2,1)S(1)}, bf16[16,1664]{1,0:T(8,128)(2,1)S(1)}, u32[]{:S(2)}, u32[]{:S(2)}) collective-permute-start(bf16[16,1664]{1,0:T(8,128)(2,1)S(1)} %silu.3.refs_0_), channel_id=1, source_target_pairs={{0,128},{1,129},{2,130},{3,131},{4,132},{5,133},{6,134},{7,135},{8... | collective-permute-start | bytes 159752 | tf_op jit(solution)/shard_map/ppermute | solution.py:26
  73.1 9.3 %collective-permute-start.22 = (bf16[16,1664]{1,0:T(8,128)(2,1)S(1)}, bf16[16,1664]{1,0:T(8,128)(2,1)S(1)}, u32[]{:S(2)}, u32[]{:S(2)}) collective-permute-start(bf16[16,1664]{1,0:T(8,128)(2,1)S(1)} %silu.4.refs_1_), channel_id=1, source_target_pairs={{0,128},{1,129},{2,130},{3,131},{4,132},{5,133},{6,134},{7,135},{8... | collective-permute-start | bytes 159752 | tf_op jit(solution)/shard_map/ppermute | solution.py:26
  78.9 8.1 %collective-permute-start.23 = (bf16[16,1664]{1,0:T(8,128)(2,1)S(1)}, bf16[16,1664]{1,0:T(8,128)(2,1)S(1)}, u32[]{:S(2)}, u32[]{:S(2)}) collective-permute-start(bf16[16,1664]{1,0:T(8,128)(2,1)S(1)} %silu.5.refs_2_), channel_id=1, source_target_pairs={{0,128},{1,129},{2,130},{3,131},{4,132},{5,133},{6,134},{7,135},{8... | collective-permute-start | bytes 159752 | tf_op jit(solution)/shard_map/ppermute | solution.py:26
  81.4 8.3 %collective-permute-start.19 = (bf16[48,1664]{1,0:T(8,128)(2,1)S(1)}, bf16[48,1664]{1,0:T(8,128)(2,1)S(1)}, u32[]{:S(2)}, u32[]{:S(2)}) collective-permute-start(bf16[48,1664]{1,0:T(8,128)(2,1)S(1)} %join.14.refs_0_), channel_id=1, source_target_pairs={{0,96},{1,97},{2,98},{3,99},{4,100},{5,101},{6,102},{7,103},{8,104... | collective-permute-start | bytes 479240 | tf_op jit(solution)/shard_map/ppermute | solution.py:26
  87.1 8.3 %collective-permute-start.24 = (bf16[48,1664]{1,0:T(8,128)(2,1)S(1)}, bf16[48,1664]{1,0:T(8,128)(2,1)S(1)}, u32[]{:S(2)}, u32[]{:S(2)}) collective-permute-start(bf16[48,1664]{1,0:T(8,128)(2,1)S(1)} %join.17.refs_0_), channel_id=1, source_target_pairs={{0,96},{1,97},{2,98},{3,99},{4,100},{5,101},{6,102},{7,103},{8,104... | collective-permute-start | bytes 479240 | tf_op jit(solution)/shard_map/ppermute | solution.py:26
  89.7 7.1 %collective-permute-start.20 = (bf16[96,1664]{1,0:T(8,128)(2,1)S(1)}, bf16[96,1664]{1,0:T(8,128)(2,1)S(1)}, u32[]{:S(2)}, u32[]{:S(2)}) collective-permute-start(bf16[96,1664]{1,0:T(8,128)(2,1)S(1)} %join.15.refs_0_), channel_id=1, source_target_pairs={{0,32},{1,33},{2,34},{3,35},{4,36},{5,37},{6,38},{7,39},{8,40},{9,... | collective-permute-start | bytes 958472 | tf_op jit(solution)/shard_map/ppermute | solution.py:26
  95.4 7.1 %collective-permute-start.25 = (bf16[96,1664]{1,0:T(8,128)(2,1)S(1)}, bf16[96,1664]{1,0:T(8,128)(2,1)S(1)}, u32[]{:S(2)}, u32[]{:S(2)}) collective-permute-start(bf16[96,1664]{1,0:T(8,128)(2,1)S(1)} %join.18.refs_0_), channel_id=1, source_target_pairs={{0,32},{1,33},{2,34},{3,35},{4,36},{5,37},{6,38},{7,39},{8,40},{9,... | collective-permute-start | bytes 958472 | tf_op jit(solution)/shard_map/ppermute | solution.py:26
  96.8 5.8 %collective-permute-start.26 = (bf16[192,1664]{1,0:T(8,128)(2,1)S(1)}, bf16[192,1664]{1,0:T(8,128)(2,1)S(1)}, u32[]{:S(2)}, u32[]{:S(2)}) collective-permute-start(bf16[192,1664]{1,0:T(8,128)(2,1)S(1)} %join.16.refs_0_), channel_id=1, source_target_pairs={{0,16},{1,17},{2,18},{3,19},{4,20},{5,21},{6,22},{7,23},{8,24},{9,... | collective-permute-start | bytes 1916936 | tf_op jit(solution)/shard_map/ppermute | solution.py:26
  102.5 2.5 %copy-start.3 = (bf16[1664,1024]{1,0:T(8,128)(2,1)S(1)}, bf16[1664,1024]{1,0:T(8,128)(2,1)}, u32[]{:S(2)}) copy-start(bf16[1664,1024]{1,0:T(8,128)(2,1)} %param.7) | copy-start | bytes 10223620
  102.5 2.2 %collective-permute-start.27 = (bf16[192,1664]{1,0:T(8,128)(2,1)S(1)}, bf16[192,1664]{1,0:T(8,128)(2,1)S(1)}, u32[]{:S(2)}, u32[]{:S(2)}) collective-permute-start(bf16[192,1664]{1,0:T(8,128)(2,1)S(1)} %join.19.refs_1_), channel_id=1, source_target_pairs={{0,16},{1,17},{2,18},{3,19},{4,20},{5,21},{6,22},{7,23},{8,24},{9,... | collective-permute-start | bytes 1916936 | tf_op jit(solution)/shard_map/ppermute | solution.py:26
  107.3 10.1 %collective-permute-start.28 = (bf16[384,640]{1,0:T(8,128)(2,1)S(1)}, bf16[384,640]{1,0:T(8,128)(2,1)S(1)}, u32[]{:S(2)}, u32[]{:S(2)}) collective-permute-start(bf16[384,640]{1,0:T(8,128)(2,1)S(1)} %slice.193), channel_id=1, source_target_pairs={{0,12},{1,13},{2,14},{3,15},{4,8},{5,9},{6,10},{7,11},{8,4},{9,5},... | collective-permute-start | bytes 1474568 | tf_op jit(solution)/shard_map/ppermute | solution.py:26
  112.2 9.1 %collective-permute-start.30 = (bf16[384,384]{1,0:T(8,128)(2,1)S(1)}, bf16[384,384]{1,0:T(8,128)(2,1)S(1)}, u32[]{:S(2)}, u32[]{:S(2)}) collective-permute-start(bf16[384,384]{1,0:T(8,128)(2,1)S(1)} %slice.194), channel_id=1, source_target_pairs={{0,12},{1,13},{2,14},{3,15},{4,8},{5,9},{6,10},{7,11},{8,4},{9,5},... | collective-permute-start | bytes 884744 | tf_op jit(solution)/shard_map/ppermute | solution.py:26
  117.6 6.3 %collective-permute-start.29 = (bf16[192,640]{1,0:T(8,128)(2,1)S(1)}, bf16[192,640]{1,0:T(8,128)(2,1)S(1)}, u32[]{:S(2)}, u32[]{:S(2)}) collective-permute-start(bf16[192,640]{1,0:T(8,128)(2,1)S(1)} %slice.196), channel_id=1, source_target_pairs={{0,4},{1,5},{2,6},{3,7},{4,0},{5,1},{6,2},{7,3},{8,12},{9,13},{10,... | collective-permute-start | bytes 737288 | tf_op jit(solution)/shard_map/ppermute | solution.py:26
  121.4 7.1 %collective-permute-start.31 = (bf16[192,384]{1,0:T(8,128)(2,1)S(1)}, bf16[192,384]{1,0:T(8,128)(2,1)S(1)}, u32[]{:S(2)}, u32[]{:S(2)}) collective-permute-start(bf16[192,384]{1,0:T(8,128)(2,1)S(1)} %slice.199), channel_id=1, source_target_pairs={{0,4},{1,5},{2,6},{3,7},{4,0},{5,1},{6,2},{7,3},{8,12},{9,13},{10,... | collective-permute-start | bytes 442376 | tf_op jit(solution)/shard_map/ppermute | solution.py:26
  124.0 4.5 %collective-permute-start.32 = (bf16[48,640]{1,0:T(8,128)(2,1)S(1)}, bf16[48,640]{1,0:T(8,128)(2,1)S(1)}, u32[]{:S(2)}, u32[]{:S(2)}) collective-permute-start(bf16[48,640]{1,0:T(8,128)(2,1)S(1)} %get-tuple-element.51), channel_id=1, source_target_pairs={{0,1},{1,0},{2,3},{3,2},{4,5},{5,4},{6,7},{7,6},{8,9},{9,8},{10,11... | collective-permute-start | bytes 184328 | tf_op jit(solution)/shard_map/ppermute | solution.py:26
  124.1 8.0 %collective-permute-start.33 = (bf16[48,640]{1,0:T(8,128)(2,1)S(1)}, bf16[48,640]{1,0:T(8,128)(2,1)S(1)}, u32[]{:S(2)}, u32[]{:S(2)}) collective-permute-start(bf16[48,640]{1,0:T(8,128)(2,1)S(1)} %get-tuple-element.49), channel_id=1, source_target_pairs={{0,2},{1,3},{2,0},{3,1},{4,6},{5,7},{6,4},{7,5},{8,10},{9,11},{10,... | collective-permute-start | bytes 184328 | tf_op jit(solution)/shard_map/ppermute | solution.py:26
  126.5 6.4 %collective-permute-start.34 = (bf16[48,640]{1,0:T(8,128)(2,1)S(1)}, bf16[48,640]{1,0:T(8,128)(2,1)S(1)}, u32[]{:S(2)}, u32[]{:S(2)}) collective-permute-start(bf16[48,640]{1,0:T(8,128)(2,1)S(1)} %get-tuple-element.50), channel_id=1, source_target_pairs={{0,3},{1,2},{2,1},{3,0},{4,7},{5,6},{6,5},{7,4},{8,11},{9,10},{10,... | collective-permute-start | bytes 184328 | tf_op jit(solution)/shard_map/ppermute | solution.py:26
  128.5 4.5 %collective-permute-start.35 = (bf16[48,384]{1,0:T(8,128)(2,1)S(1)}, bf16[48,384]{1,0:T(8,128)(2,1)S(1)}, u32[]{:S(2)}, u32[]{:S(2)}) collective-permute-start(bf16[48,384]{1,0:T(8,128)(2,1)S(1)} %get-tuple-element.58), channel_id=1, source_target_pairs={{0,1},{1,0},{2,3},{3,2},{4,5},{5,4},{6,7},{7,6},{8,9},{9,8},{10,11... | collective-permute-start | bytes 110600 | tf_op jit(solution)/shard_map/ppermute | solution.py:26
  128.8 5.8 %collective-permute-start.37 = (bf16[48,384]{1,0:T(8,128)(2,1)S(1)}, bf16[48,384]{1,0:T(8,128)(2,1)S(1)}, u32[]{:S(2)}, u32[]{:S(2)}) collective-permute-start(bf16[48,384]{1,0:T(8,128)(2,1)S(1)} %get-tuple-element.59), channel_id=1, source_target_pairs={{0,3},{1,2},{2,1},{3,0},{4,7},{5,6},{6,5},{7,4},{8,11},{9,10},{10,... | collective-permute-start | bytes 110600 | tf_op jit(solution)/shard_map/ppermute | solution.py:26
  130.7 4.9 %collective-permute-start.36 = (bf16[48,384]{1,0:T(8,128)(2,1)S(1)}, bf16[48,384]{1,0:T(8,128)(2,1)S(1)}, u32[]{:S(2)}, u32[]{:S(2)}) collective-permute-start(bf16[48,384]{1,0:T(8,128)(2,1)S(1)} %get-tuple-element.60), channel_id=1, source_target_pairs={{0,2},{1,3},{2,0},{3,1},{4,6},{5,7},{6,4},{7,5},{8,10},{9,11},{10,... | collective-permute-start | bytes 110600 | tf_op jit(solution)/shard_map/ppermute | solution.py:26

commit v6 on v5

--- a/solution.py
+++ b/solution.py
@@ -11,8 +11,8 @@
 F32 = jnp.float32
 N = 16
 CHUNKS = 3
-TURNS = [(0, 0), (1, 0), (0, 1), (2, 0), (1, 1), (2, 1), (0, 2), (1, 2)]
-TURNS += [(0, 3), (2, 2), (1, 3), (0, 4), (2, 3), (1, 4), (2, 4)]
+TURNS = [(0, 0), (1, 0), (0, 1), (2, 0), (1, 1), (0, 2), (2, 1), (0, 3)]
+TURNS += [(1, 2), (2, 2), (1, 3), (0, 4), (2, 3), (1, 4), (2, 4)]
 FIRST = (1, 3)
 SECOND = (3, 1)
 
@@ -219,7 +219,7 @@
 
 
 def scatter_out(hidden, weight, rows):
-    parts, stays, got = (slice(0, 640), slice(640, None)), [None, None], [None, None]
+    parts, stays, got = (slice(0, 512), slice(512, None)), [None, None], [None, None]
     for c, part in enumerate(parts):
         s = dot(hidden, weight[:, part])
         stays[c], turn = s[: 8 * rows], s[8 * rows :]

time: 138 us -> 140 us (1.014)
  waiting for transfers between devices: 58.4 us -> 67 us
  starting transfers between devices: 58 us -> 53.1 us
    ppermute x38, waiting for transfers between devices: 58.4 us -> 67 us  [exchange(): return lax.ppermute(value, ('gx', 'gy'), pairs)]
    ppermute x38, starting transfers between devices: 58 us -> 53.1 us  [exchange(): return lax.ppermute(value, ('gx', 'gy'), pairs)]
  transfers between devices with their start and end apart: 38 -> 38, of which waited for: 22 -> 23; matrix products, arithmetic and copies ran while one was open for 5% -> 5% of each run, Pallas kernels for 1% -> 1%
where the time goes in v6:
time: 140 us; the launch traced here: 139 us
  waiting for transfers between devices  67 us (48%)
  starting transfers between devices  53.1 us (38%)
  matrix products  8.99 us (6%)
  local copies, waits for them, and re-layouts  5.32 us (4%)
  Pallas kernels  2.35 us (2%)
  other arithmetic  2.08 us (1%)
    ppermute x38, waiting for transfers between devices, exchange(): return lax.ppermute(value, ('gx', 'gy'), pairs)  67 us
    ppermute x38, starting transfers between devices, exchange(): return lax.ppermute(value, ('gx', 'gy'), pairs)  53.1 us
    dot_general x5, matrix products, dot(): return jnp.dot(a, b, preferred_element_type=F32).astype(BF)  8.99 us
    unnamed x8, local copies, waits for them, and re-layouts  4.86 us
  transfers between devices with their start and end apart: 38, of which 23 were waited for; matrix products, arithmetic and copies ran while one was open for 5% of the time, Pallas kernels for 1%

profile of v6, /device:TPU:24, one launch (start us, length us, event | category | flops | bytes accessed | tf_op | source)
XLA Modules:
  0.0 139.3 jit_solution(14904602647759579531)
XLA Ops:
  0.0 1.9 %collective-permute-start = (bf16[48,1024]{1,0:T(8,128)(2,1)}, bf16[48,1024]{1,0:T(8,128)(2,1)S(1)}, u32[]{:S(2)}, u32[]{:S(2)}) collective-permute-start(bf16[48,1024]{1,0:T(8,128)(2,1)} %refs_0_.1), channel_id=1, source_target_pairs={{0,1},{1,0},{2,3},{3,2},{4,5},{5,4},{6,7},{7,6},{8,9},{9,8},{10,11... | collective-permute-start | bytes 294920 | tf_op jit(solution)/shard_map/ppermute | solution.py:26
  1.9 2.8 %collective-permute-start.4 = (bf16[48,1024]{1,0:T(8,128)(2,1)}, bf16[48,1024]{1,0:T(8,128)(2,1)S(1)}, u32[]{:S(2)}, u32[]{:S(2)}) collective-permute-start(bf16[48,1024]{1,0:T(8,128)(2,1)} %refs_0_.1), channel_id=1, source_target_pairs={{0,3},{1,2},{2,1},{3,0},{4,7},{5,6},{6,5},{7,4},{8,11},{9,10},{10,... | collective-permute-start | bytes 294920 | tf_op jit(solution)/shard_map/ppermute | solution.py:26
  6.1 1.6 %collective-permute-start.1 = (bf16[96,1024]{1,0:T(8,128)(2,1)S(1)}, bf16[96,1024]{1,0:T(8,128)(2,1)S(1)}, u32[]{:S(2)}, u32[]{:S(2)}) collective-permute-start(bf16[96,1024]{1,0:T(8,128)(2,1)S(1)} %join.10.refs_0_), channel_id=1, source_target_pairs={{0,4},{1,5},{2,6},{3,7},{4,0},{5,1},{6,2},{7,3},{8,12},{9,13},{10,... | collective-permute-start | bytes 589832 | tf_op jit(solution)/shard_map/ppermute | solution.py:26
  7.7 3.1 %collective-permute-done.4.refs_1_ = bf16[48,1024]{1,0:T(8,128)(2,1)S(1)} collective-permute-done((bf16[48,1024]{1,0:T(8,128)(2,1)}, bf16[48,1024]{1,0:T(8,128)(2,1)S(1)}, u32[]{:S(2)}, u32[]{:S(2)}) %collective-permute-start.4) | collective-permute-done | bytes 98336 | tf_op jit(solution)/shard_map/ppermute | solution.py:26
  10.8 3.5 %collective-permute-done.3.refs_0_ = bf16[48,1024]{1,0:T(8,128)(2,1)S(1)} collective-permute-done((bf16[48,1024]{1,0:T(8,128)(2,1)}, bf16[48,1024]{1,0:T(8,128)(2,1)S(1)}, u32[]{:S(2)}, u32[]{:S(2)}) %collective-permute-start.3) | collective-permute-done | bytes 98336 | tf_op jit(solution)/shard_map/ppermute | solution.py:26
  14.3 1.6 %collective-permute-start.5 = (bf16[96,1024]{1,0:T(8,128)(2,1)S(1)}, bf16[96,1024]{1,0:T(8,128)(2,1)S(1)}, u32[]{:S(2)}, u32[]{:S(2)}) collective-permute-start(bf16[96,1024]{1,0:T(8,128)(2,1)S(1)} %join.12.refs_0_.refs_3_), channel_id=1, source_target_pairs={{0,4},{1,5},{2,6},{3,7},{4,0},{5,1},{6,2},{7,3},{8,12},{9,13},{10,... | collective-permute-start | bytes 589832 | tf_op jit(solution)/shard_map/ppermute | solution.py:26
  15.9 2.2 %collective-permute-start.2 = (bf16[192,1024]{1,0:T(8,128)(2,1)S(1)}, bf16[192,1024]{1,0:T(8,128)(2,1)S(1)}, u32[]{:S(2)}, u32[]{:S(2)}) collective-permute-start(bf16[192,1024]{1,0:T(8,128)(2,1)S(1)} %join.11), channel_id=1, source_target_pairs={{0,12},{1,13},{2,14},{3,15},{4,8},{5,9},{6,10},{7,11},{8,4},{9,5},... | collective-permute-start | bytes 1179656 | tf_op jit(solution)/shard_map/ppermute | solution.py:26
  18.1 3.1 %collective-permute-done.5.refs_1_.refs_4_ = bf16[96,1024]{1,0:T(8,128)(2,1)S(1)} collective-permute-done((bf16[96,1024]{1,0:T(8,128)(2,1)S(1)}, bf16[96,1024]{1,0:T(8,128)(2,1)S(1)}, u32[]{:S(2)}, u32[]{:S(2)}) %collective-permute-start.5) | collective-permute-done | bytes 196640 | tf_op jit(solution)/shard_map/ppermute | solution.py:26
  21.2 3.9 %collective-permute-start.6 = (bf16[192,1024]{1,0:T(8,128)(2,1)S(1)}, bf16[192,1024]{1,0:T(8,128)(2,1)S(1)}, u32[]{:S(2)}, u32[]{:S(2)}) collective-permute-start(bf16[192,1024]{1,0:T(8,128)(2,1)S(1)} %join.13), channel_id=1, source_target_pairs={{0,12},{1,13},{2,14},{3,15},{4,8},{5,9},{6,10},{7,11},{8,4},{9,5},... | collective-permute-start | bytes 1179656 | tf_op jit(solution)/shard_map/ppermute | solution.py:26
  25.0 2.0 %copy-done = bf16[1024,1664]{1,0:T(8,128)(2,1)S(1)} copy-done((bf16[1024,1664]{1,0:T(8,128)(2,1)S(1)}, bf16[1024,1664]{1,0:T(8,128)(2,1)}, u32[]{:S(2)}) %copy-start) | copy-done | bytes 3407896
  27.0 2.0 %copy-done.1 = bf16[1024,1664]{1,0:T(8,128)(2,1)S(1)} copy-done((bf16[1024,1664]{1,0:T(8,128)(2,1)S(1)}, bf16[1024,1664]{1,0:T(8,128)(2,1)}, u32[]{:S(2)}) %copy-start.1) | copy-done | bytes 3407896
  29.0 1.5 %pack.1 = bf16[1024,3328]{1,0:T(8,128)(2,1)S(1)} custom-call(bf16[1024,1664]{1,0:T(8,128)(2,1)S(1)} %copy-done, bf16[1024,1664]{1,0:T(8,128)(2,1)S(1)} %copy-done.1), custom_call_target="tpu_custom_call" | custom-call | bytes 13631488 | tf_op jit(solution)/shard_map/pack/pallas_call | solution.py:91
  31.0 1.9 %convolution_convert_fusion.2 = bf16[256,3328]{1,0:T(8,128)(2,1)S(1)} fusion(bf16[256,1024]{1,0:T(8,128)(2,1)S(1)} %get-tuple-element.27, bf16[1024,3328]{1,0:T(8,128)(2,1)S(1)} %pack.1), kind=kOutput, calls=%fused_computation.2 | convolution fusion | flops 1745682432 | bytes 9043968 | tf_op jit(solution)/shard_map/dot_general | solution.py:164
  33.1 1.9 %convolution_convert_fusion.1 = bf16[256,3328]{1,0:T(8,128)(2,1)S(1)} fusion(bf16[256,1024]{1,0:T(8,128)(2,1)S(1)} %get-tuple-element.30, bf16[1024,3328]{1,0:T(8,128)(2,1)S(1)} %pack.1), kind=kOutput, calls=%fused_computation.1 | convolution fusion | flops 1745682432 | bytes 9043968 | tf_op jit(solution)/shard_map/dot_general | solution.py:164
  37.0 1.9 %convolution_convert_fusion = bf16[256,3328]{1,0:T(8,128)(2,1)S(1)} fusion(bf16[256,1024]{1,0:T(8,128)(2,1)S(1)} %get-tuple-element.33, bf16[1024,3328]{1,0:T(8,128)(2,1)S(1)} %pack.1), kind=kOutput, calls=%fused_computation | convolution fusion | flops 1745682432 | bytes 9043968 | tf_op jit(solution)/shard_map/dot_general | solution.py:164
  39.3 1.4 collective-permute-start.13
  40.7 3.6 %collective-permute-done.8 = bf16[64,3328]{1,0:T(8,128)(2,1)S(1)} collective-permute-done((bf16[64,3328]{1,0:T(8,128)(2,1)S(1)}, bf16[64,3328]{1,0:T(8,128)(2,1)S(1)}, u32[]{:S(2)}, u32[]{:S(2)}) %collective-permute-start.8) | collective-permute-done | bytes 426016 | tf_op jit(solution)/shard_map/ppermute | solution.py:26
  45.0 1.1 collective-permute-start.15
  46.1 7.9 %collective-permute-done.10 = bf16[32,3328]{1,0:T(8,128)(2,1)S(1)} collective-permute-done((bf16[32,3328]{1,0:T(8,128)(2,1)S(1)}, bf16[32,3328]{1,0:T(8,128)(2,1)S(1)}, u32[]{:S(2)}, u32[]{:S(2)}) %collective-permute-start.10) | collective-permute-done | bytes 213024 | tf_op jit(solution)/shard_map/ppermute | solution.py:26
  54.1 5.6 %collective-permute-start.12 = (bf16[16,3328]{1,0:T(8,128)(2,1)S(1)}, bf16[16,3328]{1,0:T(8,128)(2,1)S(1)}, u32[]{:S(2)}, u32[]{:S(2)}) collective-permute-start(bf16[16,3328]{1,0:T(8,128)(2,1)S(1)} %get-tuple-element.53), channel_id=1, source_target_pairs={{0,128},{1,129},{2,130},{3,131},{4,132},{5,133},{6,134},{7,135},{8... | collective-permute-start | bytes 319496 | tf_op jit(solution)/shard_map/ppermute | solution.py:26
  60.2 3.1 %collective-permute-start.17 = (bf16[32,3328]{1,0:T(8,128)(2,1)S(1)}, bf16[32,3328]{1,0:T(8,128)(2,1)S(1)}, u32[]{:S(2)}, u32[]{:S(2)}) collective-permute-start(bf16[32,3328]{1,0:T(8,128)(2,1)S(1)} %slice.186), channel_id=1, source_target_pairs={{0,96},{1,97},{2,98},{3,99},{4,100},{5,101},{6,102},{7,103},{8,104... | collective-permute-start | bytes 638984 | tf_op jit(solution)/shard_map/ppermute | solution.py:26
  63.3 3.6 %collective-permute-done.14 = bf16[32,3328]{1,0:T(8,128)(2,1)S(1)} collective-permute-done((bf16[32,3328]{1,0:T(8,128)(2,1)S(1)}, bf16[32,3328]{1,0:T(8,128)(2,1)S(1)}, u32[]{:S(2)}, u32[]{:S(2)}) %collective-permute-start.14) | collective-permute-done | bytes 213024 | tf_op jit(solution)/shard_map/ppermute | solution.py:26
  67.6 1.6 %collective-permute-done.17 = bf16[32,3328]{1,0:T(8,128)(2,1)S(1)} collective-permute-done((bf16[32,3328]{1,0:T(8,128)(2,1)S(1)}, bf16[32,3328]{1,0:T(8,128)(2,1)S(1)}, u32[]{:S(2)}, u32[]{:S(2)}) %collective-permute-start.17) | collective-permute-done | bytes 213024 | tf_op jit(solution)/shard_map/ppermute | solution.py:26
  69.3 4.0 %collective-permute-start.18 = (bf16[16,3328]{1,0:T(8,128)(2,1)S(1)}, bf16[16,3328]{1,0:T(8,128)(2,1)S(1)}, u32[]{:S(2)}, u32[]{:S(2)}) collective-permute-start(bf16[16,3328]{1,0:T(8,128)(2,1)S(1)} %get-tuple-element.50), channel_id=1, source_target_pairs={{0,128},{1,129},{2,130},{3,131},{4,132},{5,133},{6,134},{7,135},{8... | collective-permute-start | bytes 319496 | tf_op jit(solution)/shard_map/ppermute | solution.py:26
  73.3 2.0 %collective-permute-start.21 = (bf16[16,1664]{1,0:T(8,128)(2,1)S(1)}, bf16[16,1664]{1,0:T(8,128)(2,1)S(1)}, u32[]{:S(2)}, u32[]{:S(2)}) collective-permute-start(bf16[16,1664]{1,0:T(8,128)(2,1)S(1)} %silu.3.refs_0_), channel_id=1, source_target_pairs={{0,128},{1,129},{2,130},{3,131},{4,132},{5,133},{6,134},{7,135},{8... | collective-permute-start | bytes 159752 | tf_op jit(solution)/shard_map/ppermute | solution.py:26
  75.3 1.9 %collective-permute-done.16.b_ref = bf16[16,3328]{1,0:T(8,128)(2,1)S(1)} collective-permute-done((bf16[16,3328]{1,0:T(8,128)(2,1)S(1)}, bf16[16,3328]{1,0:T(8,128)(2,1)S(1)}, u32[]{:S(2)}, u32[]{:S(2)}) %collective-permute-start.16) | collective-permute-done | bytes 106528 | tf_op jit(solution)/shard_map/ppermute | solution.py:26
  77.3 2.4 %collective-permute-start.22 = (bf16[16,1664]{1,0:T(8,128)(2,1)S(1)}, bf16[16,1664]{1,0:T(8,128)(2,1)S(1)}, u32[]{:S(2)}, u32[]{:S(2)}) collective-permute-start(bf16[16,1664]{1,0:T(8,128)(2,1)S(1)} %silu.4.refs_1_), channel_id=1, source_target_pairs={{0,128},{1,129},{2,130},{3,131},{4,132},{5,133},{6,134},{7,135},{8... | collective-permute-start | bytes 159752 | tf_op jit(solution)/shard_map/ppermute | solution.py:26
  79.7 1.2 collective-permute-done.18.b_ref
  80.9 2.5 %collective-permute-start.23 = (bf16[16,1664]{1,0:T(8,128)(2,1)S(1)}, bf16[16,1664]{1,0:T(8,128)(2,1)S(1)}, u32[]{:S(2)}, u32[]{:S(2)}) collective-permute-start(bf16[16,1664]{1,0:T(8,128)(2,1)S(1)} %silu.5.refs_2_), channel_id=1, source_target_pairs={{0,128},{1,129},{2,130},{3,131},{4,132},{5,133},{6,134},{7,135},{8... | collective-permute-start | bytes 159752 | tf_op jit(solution)/shard_map/ppermute | solution.py:26
  83.8 1.6 %collective-permute-done.22.refs_1_ = bf16[16,1664]{1,0:T(8,128)(2,1)S(1)} collective-permute-done((bf16[16,1664]{1,0:T(8,128)(2,1)S(1)}, bf16[16,1664]{1,0:T(8,128)(2,1)S(1)}, u32[]{:S(2)}, u32[]{:S(2)}) %collective-permute-start.22) | collective-permute-done | bytes 53280 | tf_op jit(solution)/shard_map/ppermute | solution.py:26
  85.4 3.8 %collective-permute-done.23.refs_2_ = bf16[16,1664]{1,0:T(8,128)(2,1)S(1)} collective-permute-done((bf16[16,1664]{1,0:T(8,128)(2,1)S(1)}, bf16[16,1664]{1,0:T(8,128)(2,1)S(1)}, u32[]{:S(2)}, u32[]{:S(2)}) %collective-permute-start.23) | collective-permute-done | bytes 53280 | tf_op jit(solution)/shard_map/ppermute | solution.py:26
  89.6 1.3 collective-permute-done.19.refs_1_
  91.8 5.8 %collective-permute-done.24.refs_1_ = bf16[48,1664]{1,0:T(8,128)(2,1)S(1)} collective-permute-done((bf16[48,1664]{1,0:T(8,128)(2,1)S(1)}, bf16[48,1664]{1,0:T(8,128)(2,1)S(1)}, u32[]{:S(2)}, u32[]{:S(2)}) %collective-permute-start.24) | collective-permute-done | bytes 159776 | tf_op jit(solution)/shard_map/ppermute | solution.py:26
  98.4 6.3 %collective-permute-done.25.refs_1_ = bf16[96,1664]{1,0:T(8,128)(2,1)S(1)} collective-permute-done((bf16[96,1664]{1,0:T(8,128)(2,1)S(1)}, bf16[96,1664]{1,0:T(8,128)(2,1)S(1)}, u32[]{:S(2)}, u32[]{:S(2)}) %collective-permute-start.25) | collective-permute-done | bytes 319520 | tf_op jit(solution)/shard_map/ppermute | solution.py:26
  104.9 2.1 %collective-permute-done.27.refs_3_ = bf16[192,1664]{1,0:T(8,128)(2,1)S(1)} collective-permute-done((bf16[192,1664]{1,0:T(8,128)(2,1)S(1)}, bf16[192,1664]{1,0:T(8,128)(2,1)S(1)}, u32[]{:S(2)}, u32[]{:S(2)}) %collective-permute-start.27) | collective-permute-done | bytes 639008 | tf_op jit(solution)/shard_map/ppermute | solution.py:26
  107.2 1.6 %fusion.4 = bf16[768,512]{1,0:T(8,128)(2,1)S(1)} fusion(bf16[768,1664]{1,0:T(8,128)(2,1)S(1)} %place.1, bf16[1664,1024]{1,0:T(8,128)(2,1)S(1)} %copy-done.3), kind=kOutput, calls=%fused_computation.10 | convolution fusion | flops 1309016064 | bytes 5046272 | tf_op jit(solution)/shard_map/dot_general | solution.py:164
  108.8 3.3 %collective-permute-start.28 = (bf16[384,512]{1,0:T(8,128)(2,1)S(1)}, bf16[384,512]{1,0:T(8,128)(2,1)S(1)}, u32[]{:S(2)}, u32[]{:S(2)}) collective-permute-start(bf16[384,512]{1,0:T(8,128)(2,1)S(1)} %slice.193), channel_id=1, source_target_pairs={{0,12},{1,13},{2,14},{3,15},{4,8},{5,9},{6,10},{7,11},{8,4},{9,5},... | collective-permute-start | bytes 1179656 | tf_op jit(solution)/shard_map/ppermute | solution.py:26
  112.2 1.6 %fusion.7 = bf16[768,512]{1,0:T(8,128)(2,1)S(1)} fusion(bf16[768,1664]{1,0:T(8,128)(2,1)S(1)} %place.1, bf16[1664,1024]{1,0:T(8,128)(2,1)S(1)} %copy-done.3), kind=kOutput, calls=%fused_computation.11 | convolution fusion | flops 1309016064 | bytes 5046272 | tf_op jit(solution)/shard_map/dot_general | solution.py:164
  113.9 4.0 %collective-permute-done.28 = bf16[384,512]{1,0:T(8,128)(2,1)S(1)} collective-permute-done((bf16[384,512]{1,0:T(8,128)(2,1)S(1)}, bf16[384,512]{1,0:T(8,128)(2,1)S(1)}, u32[]{:S(2)}, u32[]{:S(2)}) %collective-permute-start.28) | collective-permute-done | bytes 393248 | tf_op jit(solution)/shard_map/ppermute | solution.py:26
  118.2 7.2 %collective-permute-done.30 = bf16[384,512]{1,0:T(8,128)(2,1)S(1)} collective-permute-done((bf16[384,512]{1,0:T(8,128)(2,1)S(1)}, bf16[384,512]{1,0:T(8,128)(2,1)S(1)}, u32[]{:S(2)}, u32[]{:S(2)}) %collective-permute-start.30) | collective-permute-done | bytes 393248 | tf_op jit(solution)/shard_map/ppermute | solution.py:26
  125.8 2.6 %collective-permute-start.33 = (bf16[48,512]{1,0:T(8,128)(2,1)S(1)}, bf16[48,512]{1,0:T(8,128)(2,1)S(1)}, u32[]{:S(2)}, u32[]{:S(2)}) collective-permute-start(bf16[48,512]{1,0:T(8,128)(2,1)S(1)} %get-tuple-element.55), channel_id=1, source_target_pairs={{0,2},{1,3},{2,0},{3,1},{4,6},{5,7},{6,4},{7,5},{8,10},{9,11},{10,... | collective-permute-start | bytes 147464 | tf_op jit(solution)/shard_map/ppermute | solution.py:26
  128.4 1.8 %collective-permute-start.34 = (bf16[48,512]{1,0:T(8,128)(2,1)S(1)}, bf16[48,512]{1,0:T(8,128)(2,1)S(1)}, u32[]{:S(2)}, u32[]{:S(2)}) collective-permute-start(bf16[48,512]{1,0:T(8,128)(2,1)S(1)} %get-tuple-element.56), channel_id=1, source_target_pairs={{0,3},{1,2},{2,1},{3,0},{4,7},{5,6},{6,5},{7,4},{8,11},{9,10},{10,... | collective-permute-start | bytes 147464 | tf_op jit(solution)/shard_map/ppermute | solution.py:26
  130.2 1.1 collective-permute-done.31
  131.4 2.1 %collective-permute-start.37 = (bf16[48,512]{1,0:T(8,128)(2,1)S(1)}, bf16[48,512]{1,0:T(8,128)(2,1)S(1)}, u32[]{:S(2)}, u32[]{:S(2)}) collective-permute-start(bf16[48,512]{1,0:T(8,128)(2,1)S(1)} %get-tuple-element.59), channel_id=1, source_target_pairs={{0,3},{1,2},{2,1},{3,0},{4,7},{5,6},{6,5},{7,4},{8,11},{9,10},{10,... | collective-permute-start | bytes 147464 | tf_op jit(solution)/shard_map/ppermute | solution.py:26
  133.6 1.3 collective-permute-start.36
  135.0 1.0 collective-permute-done.35
  136.0 1.5 %collective-permute-done.37 = bf16[48,512]{1,0:T(8,128)(2,1)S(1)} collective-permute-done((bf16[48,512]{1,0:T(8,128)(2,1)S(1)}, bf16[48,512]{1,0:T(8,128)(2,1)S(1)}, u32[]{:S(2)}, u32[]{:S(2)}) %collective-permute-start.37) | collective-permute-done | bytes 49184 | tf_op jit(solution)/shard_map/ppermute | solution.py:26
  137.5 1.1 collective-permute-done.36
  (91 shorter events, 10.9 us)
Async XLA Ops:
  0.0 5.2 %collective-permute-start = (bf16[48,1024]{1,0:T(8,128)(2,1)}, bf16[48,1024]{1,0:T(8,128)(2,1)S(1)}, u32[]{:S(2)}, u32[]{:S(2)}) collective-permute-start(bf16[48,1024]{1,0:T(8,128)(2,1)} %refs_0_.1), channel_id=1, source_target_pairs={{0,1},{1,0},{2,3},{3,2},{4,5},{5,4},{6,7},{7,6},{8,9},{9,8},{10,11... | collective-permute-start | bytes 294920 | tf_op jit(solution)/shard_map/ppermute | solution.py:26
  1.9 8.9 %collective-permute-start.4 = (bf16[48,1024]{1,0:T(8,128)(2,1)}, bf16[48,1024]{1,0:T(8,128)(2,1)S(1)}, u32[]{:S(2)}, u32[]{:S(2)}) collective-permute-start(bf16[48,1024]{1,0:T(8,128)(2,1)} %refs_0_.1), channel_id=1, source_target_pairs={{0,3},{1,2},{2,1},{3,0},{4,7},{5,6},{6,5},{7,4},{8,11},{9,10},{10,... | collective-permute-start | bytes 294920 | tf_op jit(solution)/shard_map/ppermute | solution.py:26
  4.7 9.5 %collective-permute-start.3 = (bf16[48,1024]{1,0:T(8,128)(2,1)}, bf16[48,1024]{1,0:T(8,128)(2,1)S(1)}, u32[]{:S(2)}, u32[]{:S(2)}) collective-permute-start(bf16[48,1024]{1,0:T(8,128)(2,1)} %refs_0_.1), channel_id=1, source_target_pairs={{0,2},{1,3},{2,0},{3,1},{4,6},{5,7},{6,4},{7,5},{8,10},{9,11},{10,... | collective-permute-start | bytes 294920 | tf_op jit(solution)/shard_map/ppermute | solution.py:26
  5.2 0.9 copy-start.2
  6.1 9.7 %collective-permute-start.1 = (bf16[96,1024]{1,0:T(8,128)(2,1)S(1)}, bf16[96,1024]{1,0:T(8,128)(2,1)S(1)}, u32[]{:S(2)}, u32[]{:S(2)}) collective-permute-start(bf16[96,1024]{1,0:T(8,128)(2,1)S(1)} %join.10.refs_0_), channel_id=1, source_target_pairs={{0,4},{1,5},{2,6},{3,7},{4,0},{5,1},{6,2},{7,3},{8,12},{9,13},{10,... | collective-permute-start | bytes 589832 | tf_op jit(solution)/shard_map/ppermute | solution.py:26
  14.3 6.9 %collective-permute-start.5 = (bf16[96,1024]{1,0:T(8,128)(2,1)S(1)}, bf16[96,1024]{1,0:T(8,128)(2,1)S(1)}, u32[]{:S(2)}, u32[]{:S(2)}) collective-permute-start(bf16[96,1024]{1,0:T(8,128)(2,1)S(1)} %join.12.refs_0_.refs_3_), channel_id=1, source_target_pairs={{0,4},{1,5},{2,6},{3,7},{4,0},{5,1},{6,2},{7,3},{8,12},{9,13},{10,... | collective-permute-start | bytes 589832 | tf_op jit(solution)/shard_map/ppermute | solution.py:26
  15.9 14.5 %collective-permute-start.2 = (bf16[192,1024]{1,0:T(8,128)(2,1)S(1)}, bf16[192,1024]{1,0:T(8,128)(2,1)S(1)}, u32[]{:S(2)}, u32[]{:S(2)}) collective-permute-start(bf16[192,1024]{1,0:T(8,128)(2,1)S(1)} %join.11), channel_id=1, source_target_pairs={{0,12},{1,13},{2,14},{3,15},{4,8},{5,9},{6,10},{7,11},{8,4},{9,5},... | collective-permute-start | bytes 1179656 | tf_op jit(solution)/shard_map/ppermute | solution.py:26
  21.2 9.6 %collective-permute-start.6 = (bf16[192,1024]{1,0:T(8,128)(2,1)S(1)}, bf16[192,1024]{1,0:T(8,128)(2,1)S(1)}, u32[]{:S(2)}, u32[]{:S(2)}) collective-permute-start(bf16[192,1024]{1,0:T(8,128)(2,1)S(1)} %join.13), channel_id=1, source_target_pairs={{0,12},{1,13},{2,14},{3,15},{4,8},{5,9},{6,10},{7,11},{8,4},{9,5},... | collective-permute-start | bytes 1179656 | tf_op jit(solution)/shard_map/ppermute | solution.py:26
  25.0 2.0 %copy-start = (bf16[1024,1664]{1,0:T(8,128)(2,1)S(1)}, bf16[1024,1664]{1,0:T(8,128)(2,1)}, u32[]{:S(2)}) copy-start(bf16[1024,1664]{1,0:T(8,128)(2,1)} %gate_ref) | copy-start | bytes 10223620
  27.0 2.0 %copy-start.1 = (bf16[1024,1664]{1,0:T(8,128)(2,1)S(1)}, bf16[1024,1664]{1,0:T(8,128)(2,1)}, u32[]{:S(2)}) copy-start(bf16[1024,1664]{1,0:T(8,128)(2,1)} %up_ref.1) | copy-start | bytes 10223620
  33.0 2.7 %collective-permute-start.7 = (bf16[128,3328]{1,0:T(8,128)(2,1)S(1)}, bf16[128,3328]{1,0:T(8,128)(2,1)S(1)}, u32[]{:S(2)}, u32[]{:S(2)}) collective-permute-start(bf16[128,3328]{1,0:T(8,128)(2,1)S(1)} %slice.169), channel_id=1, source_target_pairs={{0,16},{1,17},{2,18},{3,19},{4,20},{5,21},{6,22},{7,23},{8,24},{9,... | collective-permute-start | bytes 2555912 | tf_op jit(solution)/shard_map/ppermute | solution.py:26
  35.1 3.9 %collective-permute-start.9 = (bf16[128,3328]{1,0:T(8,128)(2,1)S(1)}, bf16[128,3328]{1,0:T(8,128)(2,1)S(1)}, u32[]{:S(2)}, u32[]{:S(2)}) collective-permute-start(bf16[128,3328]{1,0:T(8,128)(2,1)S(1)} %slice.170), channel_id=1, source_target_pairs={{0,16},{1,17},{2,18},{3,19},{4,20},{5,21},{6,22},{7,23},{8,24},{9,... | collective-permute-start | bytes 2555912 | tf_op jit(solution)/shard_map/ppermute | solution.py:26
  36.0 8.4 %collective-permute-start.8 = (bf16[64,3328]{1,0:T(8,128)(2,1)S(1)}, bf16[64,3328]{1,0:T(8,128)(2,1)S(1)}, u32[]{:S(2)}, u32[]{:S(2)}) collective-permute-start(bf16[64,3328]{1,0:T(8,128)(2,1)S(1)} %slice.172), channel_id=1, source_target_pairs={{0,32},{1,33},{2,34},{3,35},{4,36},{5,37},{6,38},{7,39},{8,40},{9,... | collective-permute-start | bytes 1277960 | tf_op jit(solution)/shard_map/ppermute | solution.py:26
  39.0 5.8 %collective-permute-start.11 = (bf16[128,3328]{1,0:T(8,128)(2,1)S(1)}, bf16[128,3328]{1,0:T(8,128)(2,1)S(1)}, u32[]{:S(2)}, u32[]{:S(2)}) collective-permute-start(bf16[128,3328]{1,0:T(8,128)(2,1)S(1)} %slice.174), channel_id=1, source_target_pairs={{0,16},{1,17},{2,18},{3,19},{4,20},{5,21},{6,22},{7,23},{8,24},{9,... | collective-permute-start | bytes 2555912 | tf_op jit(solution)/shard_map/ppermute | solution.py:26
  39.3 20.3 %collective-permute-start.13 = (bf16[64,3328]{1,0:T(8,128)(2,1)S(1)}, bf16[64,3328]{1,0:T(8,128)(2,1)S(1)}, u32[]{:S(2)}, u32[]{:S(2)}) collective-permute-start(bf16[64,3328]{1,0:T(8,128)(2,1)S(1)} %slice.175), channel_id=1, source_target_pairs={{0,32},{1,33},{2,34},{3,35},{4,36},{5,37},{6,38},{7,39},{8,40},{9,... | collective-permute-start | bytes 1277960 | tf_op jit(solution)/shard_map/ppermute | solution.py:26
  44.5 9.5 %collective-permute-start.10 = (bf16[32,3328]{1,0:T(8,128)(2,1)S(1)}, bf16[32,3328]{1,0:T(8,128)(2,1)S(1)}, u32[]{:S(2)}, u32[]{:S(2)}) collective-permute-start(bf16[32,3328]{1,0:T(8,128)(2,1)S(1)} %slice.177), channel_id=1, source_target_pairs={{0,96},{1,97},{2,98},{3,99},{4,100},{5,101},{6,102},{7,103},{8,104... | collective-permute-start | bytes 638984 | tf_op jit(solution)/shard_map/ppermute | solution.py:26
  45.0 15.0 %collective-permute-start.15 = (bf16[64,3328]{1,0:T(8,128)(2,1)S(1)}, bf16[64,3328]{1,0:T(8,128)(2,1)S(1)}, u32[]{:S(2)}, u32[]{:S(2)}) collective-permute-start(bf16[64,3328]{1,0:T(8,128)(2,1)S(1)} %slice.179), channel_id=1, source_target_pairs={{0,32},{1,33},{2,34},{3,35},{4,36},{5,37},{6,38},{7,39},{8,40},{9,... | collective-permute-start | bytes 1277960 | tf_op jit(solution)/shard_map/ppermute | solution.py:26
  54.1 13.5 %collective-permute-start.12 = (bf16[16,3328]{1,0:T(8,128)(2,1)S(1)}, bf16[16,3328]{1,0:T(8,128)(2,1)S(1)}, u32[]{:S(2)}, u32[]{:S(2)}) collective-permute-start(bf16[16,3328]{1,0:T(8,128)(2,1)S(1)} %get-tuple-element.53), channel_id=1, source_target_pairs={{0,128},{1,129},{2,130},{3,131},{4,132},{5,133},{6,134},{7,135},{8... | collective-permute-start | bytes 319496 | tf_op jit(solution)/shard_map/ppermute | solution.py:26
  59.8 7.1 %collective-permute-start.14 = (bf16[32,3328]{1,0:T(8,128)(2,1)S(1)}, bf16[32,3328]{1,0:T(8,128)(2,1)S(1)}, u32[]{:S(2)}, u32[]{:S(2)}) collective-permute-start(bf16[32,3328]{1,0:T(8,128)(2,1)S(1)} %slice.184), channel_id=1, source_target_pairs={{0,96},{1,97},{2,98},{3,99},{4,100},{5,101},{6,102},{7,103},{8,104... | collective-permute-start | bytes 638984 | tf_op jit(solution)/shard_map/ppermute | solution.py:26
  60.2 9.0 %collective-permute-start.17 = (bf16[32,3328]{1,0:T(8,128)(2,1)S(1)}, bf16[32,3328]{1,0:T(8,128)(2,1)S(1)}, u32[]{:S(2)}, u32[]{:S(2)}) collective-permute-start(bf16[32,3328]{1,0:T(8,128)(2,1)S(1)} %slice.186), channel_id=1, source_target_pairs={{0,96},{1,97},{2,98},{3,99},{4,100},{5,101},{6,102},{7,103},{8,104... | collective-permute-start | bytes 638984 | tf_op jit(solution)/shard_map/ppermute | solution.py:26
  67.0 10.2 %collective-permute-start.16 = (bf16[16,3328]{1,0:T(8,128)(2,1)S(1)}, bf16[16,3328]{1,0:T(8,128)(2,1)S(1)}, u32[]{:S(2)}, u32[]{:S(2)}) collective-permute-start(bf16[16,3328]{1,0:T(8,128)(2,1)S(1)} %get-tuple-element.52), channel_id=1, source_target_pairs={{0,128},{1,129},{2,130},{3,131},{4,132},{5,133},{6,134},{7,135},{8... | collective-permute-start | bytes 319496 | tf_op jit(solution)/shard_map/ppermute | solution.py:26
  69.3 11.6 %collective-permute-start.18 = (bf16[16,3328]{1,0:T(8,128)(2,1)S(1)}, bf16[16,3328]{1,0:T(8,128)(2,1)S(1)}, u32[]{:S(2)}, u32[]{:S(2)}) collective-permute-start(bf16[16,3328]{1,0:T(8,128)(2,1)S(1)} %get-tuple-element.50), channel_id=1, source_target_pairs={{0,128},{1,129},{2,130},{3,131},{4,132},{5,133},{6,134},{7,135},{8... | collective-permute-start | bytes 319496 | tf_op jit(solution)/shard_map/ppermute | solution.py:26
  73.3 10.6 %collective-permute-start.21 = (bf16[16,1664]{1,0:T(8,128)(2,1)S(1)}, bf16[16,1664]{1,0:T(8,128)(2,1)S(1)}, u32[]{:S(2)}, u32[]{:S(2)}) collective-permute-start(bf16[16,1664]{1,0:T(8,128)(2,1)S(1)} %silu.3.refs_0_), channel_id=1, source_target_pairs={{0,128},{1,129},{2,130},{3,131},{4,132},{5,133},{6,134},{7,135},{8... | collective-permute-start | bytes 159752 | tf_op jit(solution)/shard_map/ppermute | solution.py:26
  77.3 8.1 %collective-permute-start.22 = (bf16[16,1664]{1,0:T(8,128)(2,1)S(1)}, bf16[16,1664]{1,0:T(8,128)(2,1)S(1)}, u32[]{:S(2)}, u32[]{:S(2)}) collective-permute-start(bf16[16,1664]{1,0:T(8,128)(2,1)S(1)} %silu.4.refs_1_), channel_id=1, source_target_pairs={{0,128},{1,129},{2,130},{3,131},{4,132},{5,133},{6,134},{7,135},{8... | collective-permute-start | bytes 159752 | tf_op jit(solution)/shard_map/ppermute | solution.py:26
  80.9 8.3 %collective-permute-start.23 = (bf16[16,1664]{1,0:T(8,128)(2,1)S(1)}, bf16[16,1664]{1,0:T(8,128)(2,1)S(1)}, u32[]{:S(2)}, u32[]{:S(2)}) collective-permute-start(bf16[16,1664]{1,0:T(8,128)(2,1)S(1)} %silu.5.refs_2_), channel_id=1, source_target_pairs={{0,128},{1,129},{2,130},{3,131},{4,132},{5,133},{6,134},{7,135},{8... | collective-permute-start | bytes 159752 | tf_op jit(solution)/shard_map/ppermute | solution.py:26
  83.5 7.4 %collective-permute-start.19 = (bf16[48,1664]{1,0:T(8,128)(2,1)S(1)}, bf16[48,1664]{1,0:T(8,128)(2,1)S(1)}, u32[]{:S(2)}, u32[]{:S(2)}) collective-permute-start(bf16[48,1664]{1,0:T(8,128)(2,1)S(1)} %join.14.refs_0_), channel_id=1, source_target_pairs={{0,96},{1,97},{2,98},{3,99},{4,100},{5,101},{6,102},{7,103},{8,104... | collective-permute-start | bytes 479240 | tf_op jit(solution)/shard_map/ppermute | solution.py:26
  89.3 8.3 %collective-permute-start.24 = (bf16[48,1664]{1,0:T(8,128)(2,1)S(1)}, bf16[48,1664]{1,0:T(8,128)(2,1)S(1)}, u32[]{:S(2)}, u32[]{:S(2)}) collective-permute-start(bf16[48,1664]{1,0:T(8,128)(2,1)S(1)} %join.17.refs_0_), channel_id=1, source_target_pairs={{0,96},{1,97},{2,98},{3,99},{4,100},{5,101},{6,102},{7,103},{8,104... | collective-permute-start | bytes 479240 | tf_op jit(solution)/shard_map/ppermute | solution.py:26
  90.9 7.1 %collective-permute-start.20 = (bf16[96,1664]{1,0:T(8,128)(2,1)S(1)}, bf16[96,1664]{1,0:T(8,128)(2,1)S(1)}, u32[]{:S(2)}, u32[]{:S(2)}) collective-permute-start(bf16[96,1664]{1,0:T(8,128)(2,1)S(1)} %join.15.refs_0_), channel_id=1, source_target_pairs={{0,32},{1,33},{2,34},{3,35},{4,36},{5,37},{6,38},{7,39},{8,40},{9,... | collective-permute-start | bytes 958472 | tf_op jit(solution)/shard_map/ppermute | solution.py:26
  97.6 7.1 %collective-permute-start.25 = (bf16[96,1664]{1,0:T(8,128)(2,1)S(1)}, bf16[96,1664]{1,0:T(8,128)(2,1)S(1)}, u32[]{:S(2)}, u32[]{:S(2)}) collective-permute-start(bf16[96,1664]{1,0:T(8,128)(2,1)S(1)} %join.18.refs_0_), channel_id=1, source_target_pairs={{0,32},{1,33},{2,34},{3,35},{4,36},{5,37},{6,38},{7,39},{8,40},{9,... | collective-permute-start | bytes 958472 | tf_op jit(solution)/shard_map/ppermute | solution.py:26
  98.1 6.8 %collective-permute-start.26 = (bf16[192,1664]{1,0:T(8,128)(2,1)S(1)}, bf16[192,1664]{1,0:T(8,128)(2,1)S(1)}, u32[]{:S(2)}, u32[]{:S(2)}) collective-permute-start(bf16[192,1664]{1,0:T(8,128)(2,1)S(1)} %join.16.refs_0_), channel_id=1, source_target_pairs={{0,16},{1,17},{2,18},{3,19},{4,20},{5,21},{6,22},{7,23},{8,24},{9,... | collective-permute-start | bytes 1916936 | tf_op jit(solution)/shard_map/ppermute | solution.py:26
  104.8 2.5 %copy-start.3 = (bf16[1664,1024]{1,0:T(8,128)(2,1)S(1)}, bf16[1664,1024]{1,0:T(8,128)(2,1)}, u32[]{:S(2)}) copy-start(bf16[1664,1024]{1,0:T(8,128)(2,1)} %param.7) | copy-start | bytes 10223620
  104.8 2.2 %collective-permute-start.27 = (bf16[192,1664]{1,0:T(8,128)(2,1)S(1)}, bf16[192,1664]{1,0:T(8,128)(2,1)S(1)}, u32[]{:S(2)}, u32[]{:S(2)}) collective-permute-start(bf16[192,1664]{1,0:T(8,128)(2,1)S(1)} %join.19.refs_1_), channel_id=1, source_target_pairs={{0,16},{1,17},{2,18},{3,19},{4,20},{5,21},{6,22},{7,23},{8,24},{9,... | collective-permute-start | bytes 1916936 | tf_op jit(solution)/shard_map/ppermute | solution.py:26
  108.8 9.1 %collective-permute-start.28 = (bf16[384,512]{1,0:T(8,128)(2,1)S(1)}, bf16[384,512]{1,0:T(8,128)(2,1)S(1)}, u32[]{:S(2)}, u32[]{:S(2)}) collective-permute-start(bf16[384,512]{1,0:T(8,128)(2,1)S(1)} %slice.193), channel_id=1, source_target_pairs={{0,12},{1,13},{2,14},{3,15},{4,8},{5,9},{6,10},{7,11},{8,4},{9,5},... | collective-permute-start | bytes 1179656 | tf_op jit(solution)/shard_map/ppermute | solution.py:26
  113.8 11.6 %collective-permute-start.30 = (bf16[384,512]{1,0:T(8,128)(2,1)S(1)}, bf16[384,512]{1,0:T(8,128)(2,1)S(1)}, u32[]{:S(2)}, u32[]{:S(2)}) collective-permute-start(bf16[384,512]{1,0:T(8,128)(2,1)S(1)} %slice.194), channel_id=1, source_target_pairs={{0,12},{1,13},{2,14},{3,15},{4,8},{5,9},{6,10},{7,11},{8,4},{9,5},... | collective-permute-start | bytes 1179656 | tf_op jit(solution)/shard_map/ppermute | solution.py:26
  118.0 7.6 %collective-permute-start.29 = (bf16[192,512]{1,0:T(8,128)(2,1)S(1)}, bf16[192,512]{1,0:T(8,128)(2,1)S(1)}, u32[]{:S(2)}, u32[]{:S(2)}) collective-permute-start(bf16[192,512]{1,0:T(8,128)(2,1)S(1)} %slice.196), channel_id=1, source_target_pairs={{0,4},{1,5},{2,6},{3,7},{4,0},{5,1},{6,2},{7,3},{8,12},{9,13},{10,... | collective-permute-start | bytes 589832 | tf_op jit(solution)/shard_map/ppermute | solution.py:26
  125.5 5.8 %collective-permute-start.31 = (bf16[192,512]{1,0:T(8,128)(2,1)S(1)}, bf16[192,512]{1,0:T(8,128)(2,1)S(1)}, u32[]{:S(2)}, u32[]{:S(2)}) collective-permute-start(bf16[192,512]{1,0:T(8,128)(2,1)S(1)} %slice.199), channel_id=1, source_target_pairs={{0,4},{1,5},{2,6},{3,7},{4,0},{5,1},{6,2},{7,3},{8,12},{9,13},{10,... | collective-permute-start | bytes 589832 | tf_op jit(solution)/shard_map/ppermute | solution.py:26
  125.7 5.6 %collective-permute-start.32 = (bf16[48,512]{1,0:T(8,128)(2,1)S(1)}, bf16[48,512]{1,0:T(8,128)(2,1)S(1)}, u32[]{:S(2)}, u32[]{:S(2)}) collective-permute-start(bf16[48,512]{1,0:T(8,128)(2,1)S(1)} %get-tuple-element.57), channel_id=1, source_target_pairs={{0,1},{1,0},{2,3},{3,2},{4,5},{5,4},{6,7},{7,6},{8,9},{9,8},{10,11... | collective-permute-start | bytes 147464 | tf_op jit(solution)/shard_map/ppermute | solution.py:26
  125.8 9.1 %collective-permute-start.33 = (bf16[48,512]{1,0:T(8,128)(2,1)S(1)}, bf16[48,512]{1,0:T(8,128)(2,1)S(1)}, u32[]{:S(2)}, u32[]{:S(2)}) collective-permute-start(bf16[48,512]{1,0:T(8,128)(2,1)S(1)} %get-tuple-element.55), channel_id=1, source_target_pairs={{0,2},{1,3},{2,0},{3,1},{4,6},{5,7},{6,4},{7,5},{8,10},{9,11},{10,... | collective-permute-start | bytes 147464 | tf_op jit(solution)/shard_map/ppermute | solution.py:26
  128.4 6.5 %collective-permute-start.34 = (bf16[48,512]{1,0:T(8,128)(2,1)S(1)}, bf16[48,512]{1,0:T(8,128)(2,1)S(1)}, u32[]{:S(2)}, u32[]{:S(2)}) collective-permute-start(bf16[48,512]{1,0:T(8,128)(2,1)S(1)} %get-tuple-element.56), channel_id=1, source_target_pairs={{0,3},{1,2},{2,1},{3,0},{4,7},{5,6},{6,5},{7,4},{8,11},{9,10},{10,... | collective-permute-start | bytes 147464 | tf_op jit(solution)/shard_map/ppermute | solution.py:26
  131.3 4.7 %collective-permute-start.35 = (bf16[48,512]{1,0:T(8,128)(2,1)S(1)}, bf16[48,512]{1,0:T(8,128)(2,1)S(1)}, u32[]{:S(2)}, u32[]{:S(2)}) collective-permute-start(bf16[48,512]{1,0:T(8,128)(2,1)S(1)} %get-tuple-element.58), channel_id=1, source_target_pairs={{0,1},{1,0},{2,3},{3,2},{4,5},{5,4},{6,7},{7,6},{8,9},{9,8},{10,11... | collective-permute-start | bytes 147464 | tf_op jit(solution)/shard_map/ppermute | solution.py:26
  131.4 6.1 %collective-permute-start.37 = (bf16[48,512]{1,0:T(8,128)(2,1)S(1)}, bf16[48,512]{1,0:T(8,128)(2,1)S(1)}, u32[]{:S(2)}, u32[]{:S(2)}) collective-permute-start(bf16[48,512]{1,0:T(8,128)(2,1)S(1)} %get-tuple-element.59), channel_id=1, source_target_pairs={{0,3},{1,2},{2,1},{3,0},{4,7},{5,6},{6,5},{7,4},{8,11},{9,10},{10,... | collective-permute-start | bytes 147464 | tf_op jit(solution)/shard_map/ppermute | solution.py:26
  133.6 5.0 %collective-permute-start.36 = (bf16[48,512]{1,0:T(8,128)(2,1)S(1)}, bf16[48,512]{1,0:T(8,128)(2,1)S(1)}, u32[]{:S(2)}, u32[]{:S(2)}) collective-permute-start(bf16[48,512]{1,0:T(8,128)(2,1)S(1)} %get-tuple-element.60), channel_id=1, source_target_pairs={{0,2},{1,3},{2,0},{3,1},{4,6},{5,7},{6,4},{7,5},{8,10},{9,11},{10,... | collective-permute-start | bytes 147464 | tf_op jit(solution)/shard_map/ppermute | solution.py:26

commit v7 on v5

--- a/solution.py
+++ b/solution.py
@@ -63,12 +63,15 @@
 
 
 def place_kernel(rows, *refs):
-    *pieces, out_ref = refs
+    *pieces, keep_ref, send_ref, out_ref = refs
     me = lax.axis_index("gx")
     for piece, (gx, z) in zip(pieces, [(me, 0), (me, 1), (me ^ 1, 0), (me ^ 1, 1)]):
         for part, blocks in enumerate(kept(gx)):
             target = pl.multiple_of(scattered_slot(me, blocks[z]) * rows, 16)
             out_ref[pl.ds(target, rows), :] = piece[pl.ds(part * rows, rows), :]
+    half = N // 2 * rows
+    send_ref[...] = out_ref[half:, :]
+    keep_ref[...] = out_ref[:half, :]
 
 
 def pack_kernel(gate_ref, up_ref, out_ref, sems):
@@ -128,8 +131,15 @@
 
 
 def place(pieces, rows):
-    shape = (N * rows, pieces[0].shape[1])
-    return in_vmem(functools.partial(place_kernel, rows), [shape], "place", *pieces)
+    width = pieces[0].shape[1]
+    return in_vmem(
+        functools.partial(place_kernel, rows),
+        [(N // 2 * rows, width)] * 2,
+        "place",
+        *pieces,
+        scratch=[pltpu.VMEM((N * rows, width), BF)],
+        limit=16,
+    )
 
 
 def silu_kernel(a_ref, b_ref, out_ref):
@@ -197,6 +207,10 @@
             if k == 4:
                 stays[c] = sent = silu(stays[c], got[c])
                 how = dict(zhi=1)
+                if c == 0:
+                    return sent
+                if c == 1:
+                    stays[0] = sent = join(stays[0], sent)
             else:
                 size, how = [(4, dict(masks_y=FIRST)), (2, dict(masks_y=SECOND)), (1, dict(zhi=1))][k - 1]
                 stays[c], sent = halve(stays[c], got[c], size * rows)
@@ -206,7 +220,7 @@
     turn = None
     for c, k in TURNS:
         turn = step(c, k, turn)
-    return stays, got
+    return [stays[0], stays[2]], [got[1], got[2]]
 
 
 def gather_hidden(own, other):
@@ -219,11 +233,15 @@
 
 
 def scatter_out(hidden, weight, rows):
-    parts, stays, got = (slice(0, 640), slice(640, None)), [None, None], [None, None]
+    parts, stays, got = (slice(0, 512), slice(512, None)), [None, None], [None, None]
+    turn = weight
     for c, part in enumerate(parts):
-        s = dot(hidden, weight[:, part])
-        stays[c], turn = s[: 8 * rows], s[8 * rows :]
+        first_rows, _ = tie(hidden[1], turn)
+        turn = dot(first_rows, weight[:, part])
         got[c] = exchange(turn, masks_x=SECOND)
+    for c, part in enumerate(parts):
+        kept_rows, _ = tie(hidden[0], turn)
+        (stays[c],) = tie(dot(kept_rows, weight[:, part]))
     for c in range(2):
         got[c], _ = tie(got[c], turn)
         stays[c], turn = halve(stays[c], got[c], 4 * rows)

time: 138 us -> 137 us (level)
  starting transfers between devices: 58 us -> 54.7 us
  waiting for transfers between devices: 58.4 us -> 60.4 us
    ppermute x38 -> x37, starting transfers between devices: 58 us -> 54.7 us  [exchange(): return lax.ppermute(value, ('gx', 'gy'), pairs)]
    ppermute x38 -> x37, waiting for transfers between devices: 58.4 us -> 60.4 us  [exchange(): return lax.ppermute(value, ('gx', 'gy'), pairs)]
    dot_general x5 -> x7, matrix products: 9.62 us -> 9.33 us  [dot(): return jnp.dot(a, b, preferred_element_type=F32).astype(BF)]
  transfers between devices with their start and end apart: 38 -> 37, of which waited for: 22 -> 22; matrix products, arithmetic and copies ran while one was open for 5% -> 6% of each run, Pallas kernels for 1% -> 1%
where the time goes in v7:
time: 137 us; the launch traced here: 135 us
  waiting for transfers between devices  60.4 us (44%)
  starting transfers between devices  54.7 us (40%)
  matrix products  9.33 us (7%)
  local copies, waits for them, and re-layouts  5.26 us (4%)
  Pallas kernels  2.46 us (2%)
  other arithmetic  2.06 us (2%)
    ppermute x37, waiting for transfers between devices, exchange(): return lax.ppermute(value, ('gx', 'gy'), pairs)  60.4 us
    ppermute x37, starting transfers between devices, exchange(): return lax.ppermute(value, ('gx', 'gy'), pairs)  54.7 us
    dot_general x7, matrix products, dot(): return jnp.dot(a, b, preferred_element_type=F32).astype(BF)  9.33 us
    unnamed x8, local copies, waits for them, and re-layouts  4.86 us
  transfers between devices with their start and end apart: 37, of which 22 were waited for; matrix products, arithmetic and copies ran while one was open for 6% of the time, Pallas kernels for 1%

profile of v7, /device:TPU:24, one launch (start us, length us, event | category | flops | bytes accessed | tf_op | source)
XLA Modules:
  0.0 134.8 jit_solution(5217742733117355774)
XLA Ops:
  0.0 1.9 %collective-permute-start = (bf16[48,1024]{1,0:T(8,128)(2,1)}, bf16[48,1024]{1,0:T(8,128)(2,1)S(1)}, u32[]{:S(2)}, u32[]{:S(2)}) collective-permute-start(bf16[48,1024]{1,0:T(8,128)(2,1)} %refs_0_.1), channel_id=1, source_target_pairs={{0,1},{1,0},{2,3},{3,2},{4,5},{5,4},{6,7},{7,6},{8,9},{9,8},{10,11... | collective-permute-start | bytes 294920 | tf_op jit(solution)/shard_map/ppermute | solution.py:26
  1.9 2.8 %collective-permute-start.4 = (bf16[48,1024]{1,0:T(8,128)(2,1)}, bf16[48,1024]{1,0:T(8,128)(2,1)S(1)}, u32[]{:S(2)}, u32[]{:S(2)}) collective-permute-start(bf16[48,1024]{1,0:T(8,128)(2,1)} %refs_0_.1), channel_id=1, source_target_pairs={{0,3},{1,2},{2,1},{3,0},{4,7},{5,6},{6,5},{7,4},{8,11},{9,10},{10,... | collective-permute-start | bytes 294920 | tf_op jit(solution)/shard_map/ppermute | solution.py:26
  5.2 0.9 copy-done.2
  6.1 1.6 %collective-permute-start.1 = (bf16[96,1024]{1,0:T(8,128)(2,1)S(1)}, bf16[96,1024]{1,0:T(8,128)(2,1)S(1)}, u32[]{:S(2)}, u32[]{:S(2)}) collective-permute-start(bf16[96,1024]{1,0:T(8,128)(2,1)S(1)} %join.11.refs_0_), channel_id=1, source_target_pairs={{0,4},{1,5},{2,6},{3,7},{4,0},{5,1},{6,2},{7,3},{8,12},{9,13},{10,... | collective-permute-start | bytes 589832 | tf_op jit(solution)/shard_map/ppermute | solution.py:26
  7.7 3.1 %collective-permute-done.4.refs_1_ = bf16[48,1024]{1,0:T(8,128)(2,1)S(1)} collective-permute-done((bf16[48,1024]{1,0:T(8,128)(2,1)}, bf16[48,1024]{1,0:T(8,128)(2,1)S(1)}, u32[]{:S(2)}, u32[]{:S(2)}) %collective-permute-start.4) | collective-permute-done | bytes 98336 | tf_op jit(solution)/shard_map/ppermute | solution.py:26
  10.8 3.5 %collective-permute-done.3.refs_0_ = bf16[48,1024]{1,0:T(8,128)(2,1)S(1)} collective-permute-done((bf16[48,1024]{1,0:T(8,128)(2,1)}, bf16[48,1024]{1,0:T(8,128)(2,1)S(1)}, u32[]{:S(2)}, u32[]{:S(2)}) %collective-permute-start.3) | collective-permute-done | bytes 98336 | tf_op jit(solution)/shard_map/ppermute | solution.py:26
  14.3 1.6 %collective-permute-start.5 = (bf16[96,1024]{1,0:T(8,128)(2,1)S(1)}, bf16[96,1024]{1,0:T(8,128)(2,1)S(1)}, u32[]{:S(2)}, u32[]{:S(2)}) collective-permute-start(bf16[96,1024]{1,0:T(8,128)(2,1)S(1)} %join.13.refs_0_.refs_3_), channel_id=1, source_target_pairs={{0,4},{1,5},{2,6},{3,7},{4,0},{5,1},{6,2},{7,3},{8,12},{9,13},{10,... | collective-permute-start | bytes 589832 | tf_op jit(solution)/shard_map/ppermute | solution.py:26
  15.9 2.2 %collective-permute-start.2 = (bf16[192,1024]{1,0:T(8,128)(2,1)S(1)}, bf16[192,1024]{1,0:T(8,128)(2,1)S(1)}, u32[]{:S(2)}, u32[]{:S(2)}) collective-permute-start(bf16[192,1024]{1,0:T(8,128)(2,1)S(1)} %join.12), channel_id=1, source_target_pairs={{0,12},{1,13},{2,14},{3,15},{4,8},{5,9},{6,10},{7,11},{8,4},{9,5},... | collective-permute-start | bytes 1179656 | tf_op jit(solution)/shard_map/ppermute | solution.py:26
  18.1 3.1 %collective-permute-done.5.refs_1_.refs_4_ = bf16[96,1024]{1,0:T(8,128)(2,1)S(1)} collective-permute-done((bf16[96,1024]{1,0:T(8,128)(2,1)S(1)}, bf16[96,1024]{1,0:T(8,128)(2,1)S(1)}, u32[]{:S(2)}, u32[]{:S(2)}) %collective-permute-start.5) | collective-permute-done | bytes 196640 | tf_op jit(solution)/shard_map/ppermute | solution.py:26
  21.2 3.9 %collective-permute-start.6 = (bf16[192,1024]{1,0:T(8,128)(2,1)S(1)}, bf16[192,1024]{1,0:T(8,128)(2,1)S(1)}, u32[]{:S(2)}, u32[]{:S(2)}) collective-permute-start(bf16[192,1024]{1,0:T(8,128)(2,1)S(1)} %join.14), channel_id=1, source_target_pairs={{0,12},{1,13},{2,14},{3,15},{4,8},{5,9},{6,10},{7,11},{8,4},{9,5},... | collective-permute-start | bytes 1179656 | tf_op jit(solution)/shard_map/ppermute | solution.py:26
  25.0 2.0 %copy-done = bf16[1024,1664]{1,0:T(8,128)(2,1)S(1)} copy-done((bf16[1024,1664]{1,0:T(8,128)(2,1)S(1)}, bf16[1024,1664]{1,0:T(8,128)(2,1)}, u32[]{:S(2)}) %copy-start) | copy-done | bytes 3407896
  27.0 2.0 %copy-done.1 = bf16[1024,1664]{1,0:T(8,128)(2,1)S(1)} copy-done((bf16[1024,1664]{1,0:T(8,128)(2,1)S(1)}, bf16[1024,1664]{1,0:T(8,128)(2,1)}, u32[]{:S(2)}) %copy-start.1) | copy-done | bytes 3407896
  29.0 1.5 %pack.1 = bf16[1024,3328]{1,0:T(8,128)(2,1)S(1)} custom-call(bf16[1024,1664]{1,0:T(8,128)(2,1)S(1)} %copy-done, bf16[1024,1664]{1,0:T(8,128)(2,1)S(1)} %copy-done.1), custom_call_target="tpu_custom_call" | custom-call | bytes 13631488 | tf_op jit(solution)/shard_map/pack/pallas_call | solution.py:94
  31.0 1.9 %convolution_convert_fusion.2 = bf16[256,3328]{1,0:T(8,128)(2,1)S(1)} fusion(bf16[256,1024]{1,0:T(8,128)(2,1)S(1)} %get-tuple-element.32, bf16[1024,3328]{1,0:T(8,128)(2,1)S(1)} %pack.1), kind=kOutput, calls=%fused_computation.2 | convolution fusion | flops 1745682432 | bytes 9043968 | tf_op jit(solution)/shard_map/dot_general | solution.py:174
  33.1 1.9 %convolution_convert_fusion.1 = bf16[256,3328]{1,0:T(8,128)(2,1)S(1)} fusion(bf16[256,1024]{1,0:T(8,128)(2,1)S(1)} %get-tuple-element.35, bf16[1024,3328]{1,0:T(8,128)(2,1)S(1)} %pack.1), kind=kOutput, calls=%fused_computation.1 | convolution fusion | flops 1745682432 | bytes 9043968 | tf_op jit(solution)/shard_map/dot_general | solution.py:174
  36.0 1.0 collective-permute-start.8
  37.0 1.9 %convolution_convert_fusion = bf16[256,3328]{1,0:T(8,128)(2,1)S(1)} fusion(bf16[256,1024]{1,0:T(8,128)(2,1)S(1)} %get-tuple-element.38, bf16[1024,3328]{1,0:T(8,128)(2,1)S(1)} %pack.1), kind=kOutput, calls=%fused_computation | convolution fusion | flops 1745682432 | bytes 9043968 | tf_op jit(solution)/shard_map/dot_general | solution.py:174
  39.3 1.4 %collective-permute-start.12 = (bf16[64,3328]{1,0:T(8,128)(2,1)S(1)}, bf16[64,3328]{1,0:T(8,128)(2,1)S(1)}, u32[]{:S(2)}, u32[]{:S(2)}) collective-permute-start(bf16[64,3328]{1,0:T(8,128)(2,1)S(1)} %slice.162), channel_id=1, source_target_pairs={{0,32},{1,33},{2,34},{3,35},{4,36},{5,37},{6,38},{7,39},{8,40},{9,... | collective-permute-start | bytes 1277960 | tf_op jit(solution)/shard_map/ppermute | solution.py:26
  41.7 1.4 %collective-permute-start.15 = (bf16[64,3328]{1,0:T(8,128)(2,1)S(1)}, bf16[64,3328]{1,0:T(8,128)(2,1)S(1)}, u32[]{:S(2)}, u32[]{:S(2)}) collective-permute-start(bf16[64,3328]{1,0:T(8,128)(2,1)S(1)} %slice.163), channel_id=1, source_target_pairs={{0,32},{1,33},{2,34},{3,35},{4,36},{5,37},{6,38},{7,39},{8,40},{9,... | collective-permute-start | bytes 1277960 | tf_op jit(solution)/shard_map/ppermute | solution.py:26
  43.1 1.3 collective-permute-done.8
  44.8 5.7 %collective-permute-done.12 = bf16[64,3328]{1,0:T(8,128)(2,1)S(1)} collective-permute-done((bf16[64,3328]{1,0:T(8,128)(2,1)S(1)}, bf16[64,3328]{1,0:T(8,128)(2,1)S(1)}, u32[]{:S(2)}, u32[]{:S(2)}) %collective-permute-start.12) | collective-permute-done | bytes 426016 | tf_op jit(solution)/shard_map/ppermute | solution.py:26
  50.7 1.3 collective-permute-start.14
  52.0 2.0 %collective-permute-done.11 = bf16[32,3328]{1,0:T(8,128)(2,1)S(1)} collective-permute-done((bf16[32,3328]{1,0:T(8,128)(2,1)S(1)}, bf16[32,3328]{1,0:T(8,128)(2,1)S(1)}, u32[]{:S(2)}, u32[]{:S(2)}) %collective-permute-start.11) | collective-permute-done | bytes 213024 | tf_op jit(solution)/shard_map/ppermute | solution.py:26
  54.1 5.6 %collective-permute-start.13 = (bf16[16,3328]{1,0:T(8,128)(2,1)S(1)}, bf16[16,3328]{1,0:T(8,128)(2,1)S(1)}, u32[]{:S(2)}, u32[]{:S(2)}) collective-permute-start(bf16[16,3328]{1,0:T(8,128)(2,1)S(1)} %get-tuple-element.63), channel_id=1, source_target_pairs={{0,128},{1,129},{2,130},{3,131},{4,132},{5,133},{6,134},{7,135},{8... | collective-permute-start | bytes 319496 | tf_op jit(solution)/shard_map/ppermute | solution.py:26
  60.2 4.6 %collective-permute-start.16 = (bf16[16,3328]{1,0:T(8,128)(2,1)S(1)}, bf16[16,3328]{1,0:T(8,128)(2,1)S(1)}, u32[]{:S(2)}, u32[]{:S(2)}) collective-permute-start(bf16[16,3328]{1,0:T(8,128)(2,1)S(1)} %get-tuple-element.62), channel_id=1, source_target_pairs={{0,128},{1,129},{2,130},{3,131},{4,132},{5,133},{6,134},{7,135},{8... | collective-permute-start | bytes 319496 | tf_op jit(solution)/shard_map/ppermute | solution.py:26
  64.9 2.1 %collective-permute-done.17 = bf16[32,3328]{1,0:T(8,128)(2,1)S(1)} collective-permute-done((bf16[32,3328]{1,0:T(8,128)(2,1)S(1)}, bf16[32,3328]{1,0:T(8,128)(2,1)S(1)}, u32[]{:S(2)}, u32[]{:S(2)}) %collective-permute-start.17) | collective-permute-done | bytes 213024 | tf_op jit(solution)/shard_map/ppermute | solution.py:26
  67.0 4.0 %collective-permute-start.18 = (bf16[16,3328]{1,0:T(8,128)(2,1)S(1)}, bf16[16,3328]{1,0:T(8,128)(2,1)S(1)}, u32[]{:S(2)}, u32[]{:S(2)}) collective-permute-start(bf16[16,3328]{1,0:T(8,128)(2,1)S(1)} %get-tuple-element.60), channel_id=1, source_target_pairs={{0,128},{1,129},{2,130},{3,131},{4,132},{5,133},{6,134},{7,135},{8... | collective-permute-start | bytes 319496 | tf_op jit(solution)/shard_map/ppermute | solution.py:26
  71.1 2.9 %collective-permute-start.21 = (bf16[32,1664]{1,0:T(8,128)(2,1)S(1)}, bf16[32,1664]{1,0:T(8,128)(2,1)S(1)}, u32[]{:S(2)}, u32[]{:S(2)}) collective-permute-start(bf16[32,1664]{1,0:T(8,128)(2,1)S(1)} %join.15.refs_0_), channel_id=1, source_target_pairs={{0,128},{1,129},{2,130},{3,131},{4,132},{5,133},{6,134},{7,135},{8... | collective-permute-start | bytes 319496 | tf_op jit(solution)/shard_map/ppermute | solution.py:26
  73.9 4.7 %collective-permute-done.18.b_ref = bf16[16,3328]{1,0:T(8,128)(2,1)S(1)} collective-permute-done((bf16[16,3328]{1,0:T(8,128)(2,1)S(1)}, bf16[16,3328]{1,0:T(8,128)(2,1)S(1)}, u32[]{:S(2)}, u32[]{:S(2)}) %collective-permute-start.18) | collective-permute-done | bytes 106528 | tf_op jit(solution)/shard_map/ppermute | solution.py:26
  78.7 2.6 %collective-permute-start.22 = (bf16[16,1664]{1,0:T(8,128)(2,1)S(1)}, bf16[16,1664]{1,0:T(8,128)(2,1)S(1)}, u32[]{:S(2)}, u32[]{:S(2)}) collective-permute-start(bf16[16,1664]{1,0:T(8,128)(2,1)S(1)} %silu.5.refs_1_), channel_id=1, source_target_pairs={{0,128},{1,129},{2,130},{3,131},{4,132},{5,133},{6,134},{7,135},{8... | collective-permute-start | bytes 159752 | tf_op jit(solution)/shard_map/ppermute | solution.py:26
  82.1 4.7 %collective-permute-done.22.refs_1_ = bf16[16,1664]{1,0:T(8,128)(2,1)S(1)} collective-permute-done((bf16[16,1664]{1,0:T(8,128)(2,1)S(1)}, bf16[16,1664]{1,0:T(8,128)(2,1)S(1)}, u32[]{:S(2)}, u32[]{:S(2)}) %collective-permute-start.22) | collective-permute-done | bytes 53280 | tf_op jit(solution)/shard_map/ppermute | solution.py:26
  86.9 1.2 collective-permute-start.23
  88.1 1.6 %collective-permute-done.19.refs_1_ = bf16[48,1664]{1,0:T(8,128)(2,1)S(1)} collective-permute-done((bf16[48,1664]{1,0:T(8,128)(2,1)S(1)}, bf16[48,1664]{1,0:T(8,128)(2,1)S(1)}, u32[]{:S(2)}, u32[]{:S(2)}) %collective-permute-start.19) | collective-permute-done | bytes 159776 | tf_op jit(solution)/shard_map/ppermute | solution.py:26
  89.8 5.4 %collective-permute-done.23.refs_1_ = bf16[48,1664]{1,0:T(8,128)(2,1)S(1)} collective-permute-done((bf16[48,1664]{1,0:T(8,128)(2,1)S(1)}, bf16[48,1664]{1,0:T(8,128)(2,1)S(1)}, u32[]{:S(2)}, u32[]{:S(2)}) %collective-permute-start.23) | collective-permute-done | bytes 159776 | tf_op jit(solution)/shard_map/ppermute | solution.py:26
  95.3 1.4 %collective-permute-done.20.refs_1_ = bf16[96,1664]{1,0:T(8,128)(2,1)S(1)} collective-permute-done((bf16[96,1664]{1,0:T(8,128)(2,1)S(1)}, bf16[96,1664]{1,0:T(8,128)(2,1)S(1)}, u32[]{:S(2)}, u32[]{:S(2)}) %collective-permute-start.20) | collective-permute-done | bytes 319520 | tf_op jit(solution)/shard_map/ppermute | solution.py:26
  96.9 5.4 %collective-permute-done.24.refs_1_ = bf16[96,1664]{1,0:T(8,128)(2,1)S(1)} collective-permute-done((bf16[96,1664]{1,0:T(8,128)(2,1)S(1)}, bf16[96,1664]{1,0:T(8,128)(2,1)S(1)}, u32[]{:S(2)}, u32[]{:S(2)}) %collective-permute-start.24) | collective-permute-done | bytes 319520 | tf_op jit(solution)/shard_map/ppermute | solution.py:26
  102.7 2.1 %collective-permute-done.26.refs_3_ = bf16[192,1664]{1,0:T(8,128)(2,1)S(1)} collective-permute-done((bf16[192,1664]{1,0:T(8,128)(2,1)S(1)}, bf16[192,1664]{1,0:T(8,128)(2,1)S(1)}, u32[]{:S(2)}, u32[]{:S(2)}) %collective-permute-start.26) | collective-permute-done | bytes 639008 | tf_op jit(solution)/shard_map/ppermute | solution.py:26
  106.0 3.3 %collective-permute-start.27 = (bf16[384,512]{1,0:T(8,128)(2,1)S(1)}, bf16[384,512]{1,0:T(8,128)(2,1)S(1)}, u32[]{:S(2)}, u32[]{:S(2)}) collective-permute-start(bf16[384,512]{1,0:T(8,128)(2,1)S(1)} %fusion.8), channel_id=1, source_target_pairs={{0,12},{1,13},{2,14},{3,15},{4,8},{5,9},{6,10},{7,11},{8,4},{9,5},... | collective-permute-start | bytes 1179656 | tf_op jit(solution)/shard_map/ppermute | solution.py:26
  111.2 0.9 fusion.11
  112.1 3.0 %collective-permute-done.27 = bf16[384,512]{1,0:T(8,128)(2,1)S(1)} collective-permute-done((bf16[384,512]{1,0:T(8,128)(2,1)S(1)}, bf16[384,512]{1,0:T(8,128)(2,1)S(1)}, u32[]{:S(2)}, u32[]{:S(2)}) %collective-permute-start.27) | collective-permute-done | bytes 393248 | tf_op jit(solution)/shard_map/ppermute | solution.py:26
  115.3 5.8 %collective-permute-done.29 = bf16[384,512]{1,0:T(8,128)(2,1)S(1)} collective-permute-done((bf16[384,512]{1,0:T(8,128)(2,1)S(1)}, bf16[384,512]{1,0:T(8,128)(2,1)S(1)}, u32[]{:S(2)}, u32[]{:S(2)}) %collective-permute-start.29) | collective-permute-done | bytes 393248 | tf_op jit(solution)/shard_map/ppermute | solution.py:26
  121.5 2.4 %collective-permute-start.32 = (bf16[48,512]{1,0:T(8,128)(2,1)S(1)}, bf16[48,512]{1,0:T(8,128)(2,1)S(1)}, u32[]{:S(2)}, u32[]{:S(2)}) collective-permute-start(bf16[48,512]{1,0:T(8,128)(2,1)S(1)} %get-tuple-element.65), channel_id=1, source_target_pairs={{0,2},{1,3},{2,0},{3,1},{4,6},{5,7},{6,4},{7,5},{8,10},{9,11},{10,... | collective-permute-start | bytes 147464 | tf_op jit(solution)/shard_map/ppermute | solution.py:26
  123.9 2.0 %collective-permute-start.33 = (bf16[48,512]{1,0:T(8,128)(2,1)S(1)}, bf16[48,512]{1,0:T(8,128)(2,1)S(1)}, u32[]{:S(2)}, u32[]{:S(2)}) collective-permute-start(bf16[48,512]{1,0:T(8,128)(2,1)S(1)} %get-tuple-element.66), channel_id=1, source_target_pairs={{0,3},{1,2},{2,1},{3,0},{4,7},{5,6},{6,5},{7,4},{8,11},{9,10},{10,... | collective-permute-start | bytes 147464 | tf_op jit(solution)/shard_map/ppermute | solution.py:26
  125.9 1.1 collective-permute-done.30
  127.2 1.9 %collective-permute-start.36 = (bf16[48,512]{1,0:T(8,128)(2,1)S(1)}, bf16[48,512]{1,0:T(8,128)(2,1)S(1)}, u32[]{:S(2)}, u32[]{:S(2)}) collective-permute-start(bf16[48,512]{1,0:T(8,128)(2,1)S(1)} %get-tuple-element.69), channel_id=1, source_target_pairs={{0,3},{1,2},{2,1},{3,0},{4,7},{5,6},{6,5},{7,4},{8,11},{9,10},{10,... | collective-permute-start | bytes 147464 | tf_op jit(solution)/shard_map/ppermute | solution.py:26
  129.1 1.6 %collective-permute-start.35 = (bf16[48,512]{1,0:T(8,128)(2,1)S(1)}, bf16[48,512]{1,0:T(8,128)(2,1)S(1)}, u32[]{:S(2)}, u32[]{:S(2)}) collective-permute-start(bf16[48,512]{1,0:T(8,128)(2,1)S(1)} %get-tuple-element.70), channel_id=1, source_target_pairs={{0,2},{1,3},{2,0},{3,1},{4,6},{5,7},{6,4},{7,5},{8,10},{9,11},{10,... | collective-permute-start | bytes 147464 | tf_op jit(solution)/shard_map/ppermute | solution.py:26
  130.7 1.0 collective-permute-done.34
  131.7 1.5 %collective-permute-done.36 = bf16[48,512]{1,0:T(8,128)(2,1)S(1)} collective-permute-done((bf16[48,512]{1,0:T(8,128)(2,1)S(1)}, bf16[48,512]{1,0:T(8,128)(2,1)S(1)}, u32[]{:S(2)}, u32[]{:S(2)}) %collective-permute-start.36) | collective-permute-done | bytes 49184 | tf_op jit(solution)/shard_map/ppermute | solution.py:26
  (90 shorter events, 11.8 us)
Async XLA Ops:
  0.0 5.2 %collective-permute-start = (bf16[48,1024]{1,0:T(8,128)(2,1)}, bf16[48,1024]{1,0:T(8,128)(2,1)S(1)}, u32[]{:S(2)}, u32[]{:S(2)}) collective-permute-start(bf16[48,1024]{1,0:T(8,128)(2,1)} %refs_0_.1), channel_id=1, source_target_pairs={{0,1},{1,0},{2,3},{3,2},{4,5},{5,4},{6,7},{7,6},{8,9},{9,8},{10,11... | collective-permute-start | bytes 294920 | tf_op jit(solution)/shard_map/ppermute | solution.py:26
  1.9 8.9 %collective-permute-start.4 = (bf16[48,1024]{1,0:T(8,128)(2,1)}, bf16[48,1024]{1,0:T(8,128)(2,1)S(1)}, u32[]{:S(2)}, u32[]{:S(2)}) collective-permute-start(bf16[48,1024]{1,0:T(8,128)(2,1)} %refs_0_.1), channel_id=1, source_target_pairs={{0,3},{1,2},{2,1},{3,0},{4,7},{5,6},{6,5},{7,4},{8,11},{9,10},{10,... | collective-permute-start | bytes 294920 | tf_op jit(solution)/shard_map/ppermute | solution.py:26
  4.7 9.5 %collective-permute-start.3 = (bf16[48,1024]{1,0:T(8,128)(2,1)}, bf16[48,1024]{1,0:T(8,128)(2,1)S(1)}, u32[]{:S(2)}, u32[]{:S(2)}) collective-permute-start(bf16[48,1024]{1,0:T(8,128)(2,1)} %refs_0_.1), channel_id=1, source_target_pairs={{0,2},{1,3},{2,0},{3,1},{4,6},{5,7},{6,4},{7,5},{8,10},{9,11},{10,... | collective-permute-start | bytes 294920 | tf_op jit(solution)/shard_map/ppermute | solution.py:26
  5.2 0.9 copy-start.2
  6.1 9.7 %collective-permute-start.1 = (bf16[96,1024]{1,0:T(8,128)(2,1)S(1)}, bf16[96,1024]{1,0:T(8,128)(2,1)S(1)}, u32[]{:S(2)}, u32[]{:S(2)}) collective-permute-start(bf16[96,1024]{1,0:T(8,128)(2,1)S(1)} %join.11.refs_0_), channel_id=1, source_target_pairs={{0,4},{1,5},{2,6},{3,7},{4,0},{5,1},{6,2},{7,3},{8,12},{9,13},{10,... | collective-permute-start | bytes 589832 | tf_op jit(solution)/shard_map/ppermute | solution.py:26
  14.3 6.9 %collective-permute-start.5 = (bf16[96,1024]{1,0:T(8,128)(2,1)S(1)}, bf16[96,1024]{1,0:T(8,128)(2,1)S(1)}, u32[]{:S(2)}, u32[]{:S(2)}) collective-permute-start(bf16[96,1024]{1,0:T(8,128)(2,1)S(1)} %join.13.refs_0_.refs_3_), channel_id=1, source_target_pairs={{0,4},{1,5},{2,6},{3,7},{4,0},{5,1},{6,2},{7,3},{8,12},{9,13},{10,... | collective-permute-start | bytes 589832 | tf_op jit(solution)/shard_map/ppermute | solution.py:26
  15.9 14.5 %collective-permute-start.2 = (bf16[192,1024]{1,0:T(8,128)(2,1)S(1)}, bf16[192,1024]{1,0:T(8,128)(2,1)S(1)}, u32[]{:S(2)}, u32[]{:S(2)}) collective-permute-start(bf16[192,1024]{1,0:T(8,128)(2,1)S(1)} %join.12), channel_id=1, source_target_pairs={{0,12},{1,13},{2,14},{3,15},{4,8},{5,9},{6,10},{7,11},{8,4},{9,5},... | collective-permute-start | bytes 1179656 | tf_op jit(solution)/shard_map/ppermute | solution.py:26
  21.2 9.6 %collective-permute-start.6 = (bf16[192,1024]{1,0:T(8,128)(2,1)S(1)}, bf16[192,1024]{1,0:T(8,128)(2,1)S(1)}, u32[]{:S(2)}, u32[]{:S(2)}) collective-permute-start(bf16[192,1024]{1,0:T(8,128)(2,1)S(1)} %join.14), channel_id=1, source_target_pairs={{0,12},{1,13},{2,14},{3,15},{4,8},{5,9},{6,10},{7,11},{8,4},{9,5},... | collective-permute-start | bytes 1179656 | tf_op jit(solution)/shard_map/ppermute | solution.py:26
  25.0 2.0 %copy-start = (bf16[1024,1664]{1,0:T(8,128)(2,1)S(1)}, bf16[1024,1664]{1,0:T(8,128)(2,1)}, u32[]{:S(2)}) copy-start(bf16[1024,1664]{1,0:T(8,128)(2,1)} %gate_ref) | copy-start | bytes 10223620
  27.0 2.0 %copy-start.1 = (bf16[1024,1664]{1,0:T(8,128)(2,1)S(1)}, bf16[1024,1664]{1,0:T(8,128)(2,1)}, u32[]{:S(2)}) copy-start(bf16[1024,1664]{1,0:T(8,128)(2,1)} %up_ref.1) | copy-start | bytes 10223620
  33.0 2.7 %collective-permute-start.7 = (bf16[128,3328]{1,0:T(8,128)(2,1)S(1)}, bf16[128,3328]{1,0:T(8,128)(2,1)S(1)}, u32[]{:S(2)}, u32[]{:S(2)}) collective-permute-start(bf16[128,3328]{1,0:T(8,128)(2,1)S(1)} %slice.155), channel_id=1, source_target_pairs={{0,16},{1,17},{2,18},{3,19},{4,20},{5,21},{6,22},{7,23},{8,24},{9,... | collective-permute-start | bytes 2555912 | tf_op jit(solution)/shard_map/ppermute | solution.py:26
  35.1 3.9 %collective-permute-start.10 = (bf16[128,3328]{1,0:T(8,128)(2,1)S(1)}, bf16[128,3328]{1,0:T(8,128)(2,1)S(1)}, u32[]{:S(2)}, u32[]{:S(2)}) collective-permute-start(bf16[128,3328]{1,0:T(8,128)(2,1)S(1)} %slice.156), channel_id=1, source_target_pairs={{0,16},{1,17},{2,18},{3,19},{4,20},{5,21},{6,22},{7,23},{8,24},{9,... | collective-permute-start | bytes 2555912 | tf_op jit(solution)/shard_map/ppermute | solution.py:26
  36.0 8.4 %collective-permute-start.8 = (bf16[64,3328]{1,0:T(8,128)(2,1)S(1)}, bf16[64,3328]{1,0:T(8,128)(2,1)S(1)}, u32[]{:S(2)}, u32[]{:S(2)}) collective-permute-start(bf16[64,3328]{1,0:T(8,128)(2,1)S(1)} %slice.158), channel_id=1, source_target_pairs={{0,32},{1,33},{2,34},{3,35},{4,36},{5,37},{6,38},{7,39},{8,40},{9,... | collective-permute-start | bytes 1277960 | tf_op jit(solution)/shard_map/ppermute | solution.py:26
  39.0 2.5 %collective-permute-start.9 = (bf16[128,3328]{1,0:T(8,128)(2,1)S(1)}, bf16[128,3328]{1,0:T(8,128)(2,1)S(1)}, u32[]{:S(2)}, u32[]{:S(2)}) collective-permute-start(bf16[128,3328]{1,0:T(8,128)(2,1)S(1)} %slice.160), channel_id=1, source_target_pairs={{0,16},{1,17},{2,18},{3,19},{4,20},{5,21},{6,22},{7,23},{8,24},{9,... | collective-permute-start | bytes 2555912 | tf_op jit(solution)/shard_map/ppermute | solution.py:26
  39.3 11.2 %collective-permute-start.12 = (bf16[64,3328]{1,0:T(8,128)(2,1)S(1)}, bf16[64,3328]{1,0:T(8,128)(2,1)S(1)}, u32[]{:S(2)}, u32[]{:S(2)}) collective-permute-start(bf16[64,3328]{1,0:T(8,128)(2,1)S(1)} %slice.162), channel_id=1, source_target_pairs={{0,32},{1,33},{2,34},{3,35},{4,36},{5,37},{6,38},{7,39},{8,40},{9,... | collective-permute-start | bytes 1277960 | tf_op jit(solution)/shard_map/ppermute | solution.py:26
  41.7 17.9 %collective-permute-start.15 = (bf16[64,3328]{1,0:T(8,128)(2,1)S(1)}, bf16[64,3328]{1,0:T(8,128)(2,1)S(1)}, u32[]{:S(2)}, u32[]{:S(2)}) collective-permute-start(bf16[64,3328]{1,0:T(8,128)(2,1)S(1)} %slice.163), channel_id=1, source_target_pairs={{0,32},{1,33},{2,34},{3,35},{4,36},{5,37},{6,38},{7,39},{8,40},{9,... | collective-permute-start | bytes 1277960 | tf_op jit(solution)/shard_map/ppermute | solution.py:26
  44.5 9.5 %collective-permute-start.11 = (bf16[32,3328]{1,0:T(8,128)(2,1)S(1)}, bf16[32,3328]{1,0:T(8,128)(2,1)S(1)}, u32[]{:S(2)}, u32[]{:S(2)}) collective-permute-start(bf16[32,3328]{1,0:T(8,128)(2,1)S(1)} %slice.165), channel_id=1, source_target_pairs={{0,96},{1,97},{2,98},{3,99},{4,100},{5,101},{6,102},{7,103},{8,104... | collective-permute-start | bytes 638984 | tf_op jit(solution)/shard_map/ppermute | solution.py:26
  50.7 9.4 %collective-permute-start.14 = (bf16[32,3328]{1,0:T(8,128)(2,1)S(1)}, bf16[32,3328]{1,0:T(8,128)(2,1)S(1)}, u32[]{:S(2)}, u32[]{:S(2)}) collective-permute-start(bf16[32,3328]{1,0:T(8,128)(2,1)S(1)} %slice.167), channel_id=1, source_target_pairs={{0,96},{1,97},{2,98},{3,99},{4,100},{5,101},{6,102},{7,103},{8,104... | collective-permute-start | bytes 638984 | tf_op jit(solution)/shard_map/ppermute | solution.py:26
  54.1 10.7 %collective-permute-start.13 = (bf16[16,3328]{1,0:T(8,128)(2,1)S(1)}, bf16[16,3328]{1,0:T(8,128)(2,1)S(1)}, u32[]{:S(2)}, u32[]{:S(2)}) collective-permute-start(bf16[16,3328]{1,0:T(8,128)(2,1)S(1)} %get-tuple-element.63), channel_id=1, source_target_pairs={{0,128},{1,129},{2,130},{3,131},{4,132},{5,133},{6,134},{7,135},{8... | collective-permute-start | bytes 319496 | tf_op jit(solution)/shard_map/ppermute | solution.py:26
  59.8 7.1 %collective-permute-start.17 = (bf16[32,3328]{1,0:T(8,128)(2,1)S(1)}, bf16[32,3328]{1,0:T(8,128)(2,1)S(1)}, u32[]{:S(2)}, u32[]{:S(2)}) collective-permute-start(bf16[32,3328]{1,0:T(8,128)(2,1)S(1)} %slice.172), channel_id=1, source_target_pairs={{0,96},{1,97},{2,98},{3,99},{4,100},{5,101},{6,102},{7,103},{8,104... | collective-permute-start | bytes 638984 | tf_op jit(solution)/shard_map/ppermute | solution.py:26
  60.2 10.8 %collective-permute-start.16 = (bf16[16,3328]{1,0:T(8,128)(2,1)S(1)}, bf16[16,3328]{1,0:T(8,128)(2,1)S(1)}, u32[]{:S(2)}, u32[]{:S(2)}) collective-permute-start(bf16[16,3328]{1,0:T(8,128)(2,1)S(1)} %get-tuple-element.62), channel_id=1, source_target_pairs={{0,128},{1,129},{2,130},{3,131},{4,132},{5,133},{6,134},{7,135},{8... | collective-permute-start | bytes 319496 | tf_op jit(solution)/shard_map/ppermute | solution.py:26
  67.0 11.7 %collective-permute-start.18 = (bf16[16,3328]{1,0:T(8,128)(2,1)S(1)}, bf16[16,3328]{1,0:T(8,128)(2,1)S(1)}, u32[]{:S(2)}, u32[]{:S(2)}) collective-permute-start(bf16[16,3328]{1,0:T(8,128)(2,1)S(1)} %get-tuple-element.60), channel_id=1, source_target_pairs={{0,128},{1,129},{2,130},{3,131},{4,132},{5,133},{6,134},{7,135},{8... | collective-permute-start | bytes 319496 | tf_op jit(solution)/shard_map/ppermute | solution.py:26
  71.1 11.0 %collective-permute-start.21 = (bf16[32,1664]{1,0:T(8,128)(2,1)S(1)}, bf16[32,1664]{1,0:T(8,128)(2,1)S(1)}, u32[]{:S(2)}, u32[]{:S(2)}) collective-permute-start(bf16[32,1664]{1,0:T(8,128)(2,1)S(1)} %join.15.refs_0_), channel_id=1, source_target_pairs={{0,128},{1,129},{2,130},{3,131},{4,132},{5,133},{6,134},{7,135},{8... | collective-permute-start | bytes 319496 | tf_op jit(solution)/shard_map/ppermute | solution.py:26
  78.7 8.1 %collective-permute-start.22 = (bf16[16,1664]{1,0:T(8,128)(2,1)S(1)}, bf16[16,1664]{1,0:T(8,128)(2,1)S(1)}, u32[]{:S(2)}, u32[]{:S(2)}) collective-permute-start(bf16[16,1664]{1,0:T(8,128)(2,1)S(1)} %silu.5.refs_1_), channel_id=1, source_target_pairs={{0,128},{1,129},{2,130},{3,131},{4,132},{5,133},{6,134},{7,135},{8... | collective-permute-start | bytes 159752 | tf_op jit(solution)/shard_map/ppermute | solution.py:26
  81.4 8.3 %collective-permute-start.19 = (bf16[48,1664]{1,0:T(8,128)(2,1)S(1)}, bf16[48,1664]{1,0:T(8,128)(2,1)S(1)}, u32[]{:S(2)}, u32[]{:S(2)}) collective-permute-start(bf16[48,1664]{1,0:T(8,128)(2,1)S(1)} %join.16.refs_0_), channel_id=1, source_target_pairs={{0,96},{1,97},{2,98},{3,99},{4,100},{5,101},{6,102},{7,103},{8,104... | collective-permute-start | bytes 479240 | tf_op jit(solution)/shard_map/ppermute | solution.py:26
  86.9 8.3 %collective-permute-start.23 = (bf16[48,1664]{1,0:T(8,128)(2,1)S(1)}, bf16[48,1664]{1,0:T(8,128)(2,1)S(1)}, u32[]{:S(2)}, u32[]{:S(2)}) collective-permute-start(bf16[48,1664]{1,0:T(8,128)(2,1)S(1)} %join.19.refs_0_), channel_id=1, source_target_pairs={{0,96},{1,97},{2,98},{3,99},{4,100},{5,101},{6,102},{7,103},{8,104... | collective-permute-start | bytes 479240 | tf_op jit(solution)/shard_map/ppermute | solution.py:26
  89.7 7.1 %collective-permute-start.20 = (bf16[96,1664]{1,0:T(8,128)(2,1)S(1)}, bf16[96,1664]{1,0:T(8,128)(2,1)S(1)}, u32[]{:S(2)}, u32[]{:S(2)}) collective-permute-start(bf16[96,1664]{1,0:T(8,128)(2,1)S(1)} %join.17.refs_0_), channel_id=1, source_target_pairs={{0,32},{1,33},{2,34},{3,35},{4,36},{5,37},{6,38},{7,39},{8,40},{9,... | collective-permute-start | bytes 958472 | tf_op jit(solution)/shard_map/ppermute | solution.py:26
  95.2 7.1 %collective-permute-start.24 = (bf16[96,1664]{1,0:T(8,128)(2,1)S(1)}, bf16[96,1664]{1,0:T(8,128)(2,1)S(1)}, u32[]{:S(2)}, u32[]{:S(2)}) collective-permute-start(bf16[96,1664]{1,0:T(8,128)(2,1)S(1)} %join.20.refs_0_), channel_id=1, source_target_pairs={{0,32},{1,33},{2,34},{3,35},{4,36},{5,37},{6,38},{7,39},{8,40},{9,... | collective-permute-start | bytes 958472 | tf_op jit(solution)/shard_map/ppermute | solution.py:26
  96.8 8.3 %copy-start.3 = (bf16[1664,1024]{1,0:T(8,128)(2,1)S(1)}, bf16[1664,1024]{1,0:T(8,128)(2,1)}, u32[]{:S(2)}) copy-start(bf16[1664,1024]{1,0:T(8,128)(2,1)} %param.7) | copy-start | bytes 10223620
  96.8 5.9 %collective-permute-start.25 = (bf16[192,1664]{1,0:T(8,128)(2,1)S(1)}, bf16[192,1664]{1,0:T(8,128)(2,1)S(1)}, u32[]{:S(2)}, u32[]{:S(2)}) collective-permute-start(bf16[192,1664]{1,0:T(8,128)(2,1)S(1)} %join.18.refs_0_), channel_id=1, source_target_pairs={{0,16},{1,17},{2,18},{3,19},{4,20},{5,21},{6,22},{7,23},{8,24},{9,... | collective-permute-start | bytes 1916936 | tf_op jit(solution)/shard_map/ppermute | solution.py:26
  102.4 2.4 %collective-permute-start.26 = (bf16[192,1664]{1,0:T(8,128)(2,1)S(1)}, bf16[192,1664]{1,0:T(8,128)(2,1)S(1)}, u32[]{:S(2)}, u32[]{:S(2)}) collective-permute-start(bf16[192,1664]{1,0:T(8,128)(2,1)S(1)} %join.21.refs_1_), channel_id=1, source_target_pairs={{0,16},{1,17},{2,18},{3,19},{4,20},{5,21},{6,22},{7,23},{8,24},{9,... | collective-permute-start | bytes 1916936 | tf_op jit(solution)/shard_map/ppermute | solution.py:26
  106.0 9.1 %collective-permute-start.27 = (bf16[384,512]{1,0:T(8,128)(2,1)S(1)}, bf16[384,512]{1,0:T(8,128)(2,1)S(1)}, u32[]{:S(2)}, u32[]{:S(2)}) collective-permute-start(bf16[384,512]{1,0:T(8,128)(2,1)S(1)} %fusion.8), channel_id=1, source_target_pairs={{0,12},{1,13},{2,14},{3,15},{4,8},{5,9},{6,10},{7,11},{8,4},{9,5},... | collective-permute-start | bytes 1179656 | tf_op jit(solution)/shard_map/ppermute | solution.py:26
  110.2 10.9 %collective-permute-start.29 = (bf16[384,512]{1,0:T(8,128)(2,1)S(1)}, bf16[384,512]{1,0:T(8,128)(2,1)S(1)}, u32[]{:S(2)}, u32[]{:S(2)}) collective-permute-start(bf16[384,512]{1,0:T(8,128)(2,1)S(1)} %fusion.14), channel_id=1, source_target_pairs={{0,12},{1,13},{2,14},{3,15},{4,8},{5,9},{6,10},{7,11},{8,4},{9,5},... | collective-permute-start | bytes 1179656 | tf_op jit(solution)/shard_map/ppermute | solution.py:26
  115.2 6.1 %collective-permute-start.28 = (bf16[192,512]{1,0:T(8,128)(2,1)S(1)}, bf16[192,512]{1,0:T(8,128)(2,1)S(1)}, u32[]{:S(2)}, u32[]{:S(2)}) collective-permute-start(bf16[192,512]{1,0:T(8,128)(2,1)S(1)} %slice.179), channel_id=1, source_target_pairs={{0,4},{1,5},{2,6},{3,7},{4,0},{5,1},{6,2},{7,3},{8,12},{9,13},{10,... | collective-permute-start | bytes 589832 | tf_op jit(solution)/shard_map/ppermute | solution.py:26
  121.2 5.8 %collective-permute-start.30 = (bf16[192,512]{1,0:T(8,128)(2,1)S(1)}, bf16[192,512]{1,0:T(8,128)(2,1)S(1)}, u32[]{:S(2)}, u32[]{:S(2)}) collective-permute-start(bf16[192,512]{1,0:T(8,128)(2,1)S(1)} %slice.181), channel_id=1, source_target_pairs={{0,4},{1,5},{2,6},{3,7},{4,0},{5,1},{6,2},{7,3},{8,12},{9,13},{10,... | collective-permute-start | bytes 589832 | tf_op jit(solution)/shard_map/ppermute | solution.py:26
  121.4 5.6 %collective-permute-start.31 = (bf16[48,512]{1,0:T(8,128)(2,1)S(1)}, bf16[48,512]{1,0:T(8,128)(2,1)S(1)}, u32[]{:S(2)}, u32[]{:S(2)}) collective-permute-start(bf16[48,512]{1,0:T(8,128)(2,1)S(1)} %get-tuple-element.67), channel_id=1, source_target_pairs={{0,1},{1,0},{2,3},{3,2},{4,5},{5,4},{6,7},{7,6},{8,9},{9,8},{10,11... | collective-permute-start | bytes 147464 | tf_op jit(solution)/shard_map/ppermute | solution.py:26
  121.5 9.1 %collective-permute-start.32 = (bf16[48,512]{1,0:T(8,128)(2,1)S(1)}, bf16[48,512]{1,0:T(8,128)(2,1)S(1)}, u32[]{:S(2)}, u32[]{:S(2)}) collective-permute-start(bf16[48,512]{1,0:T(8,128)(2,1)S(1)} %get-tuple-element.65), channel_id=1, source_target_pairs={{0,2},{1,3},{2,0},{3,1},{4,6},{5,7},{6,4},{7,5},{8,10},{9,11},{10,... | collective-permute-start | bytes 147464 | tf_op jit(solution)/shard_map/ppermute | solution.py:26
  123.9 6.7 %collective-permute-start.33 = (bf16[48,512]{1,0:T(8,128)(2,1)S(1)}, bf16[48,512]{1,0:T(8,128)(2,1)S(1)}, u32[]{:S(2)}, u32[]{:S(2)}) collective-permute-start(bf16[48,512]{1,0:T(8,128)(2,1)S(1)} %get-tuple-element.66), channel_id=1, source_target_pairs={{0,3},{1,2},{2,1},{3,0},{4,7},{5,6},{6,5},{7,4},{8,11},{9,10},{10,... | collective-permute-start | bytes 147464 | tf_op jit(solution)/shard_map/ppermute | solution.py:26
  127.1 4.6 %collective-permute-start.34 = (bf16[48,512]{1,0:T(8,128)(2,1)S(1)}, bf16[48,512]{1,0:T(8,128)(2,1)S(1)}, u32[]{:S(2)}, u32[]{:S(2)}) collective-permute-start(bf16[48,512]{1,0:T(8,128)(2,1)S(1)} %get-tuple-element.68), channel_id=1, source_target_pairs={{0,1},{1,0},{2,3},{3,2},{4,5},{5,4},{6,7},{7,6},{8,9},{9,8},{10,11... | collective-permute-start | bytes 147464 | tf_op jit(solution)/shard_map/ppermute | solution.py:26
  127.2 6.1 %collective-permute-start.36 = (bf16[48,512]{1,0:T(8,128)(2,1)S(1)}, bf16[48,512]{1,0:T(8,128)(2,1)S(1)}, u32[]{:S(2)}, u32[]{:S(2)}) collective-permute-start(bf16[48,512]{1,0:T(8,128)(2,1)S(1)} %get-tuple-element.69), channel_id=1, source_target_pairs={{0,3},{1,2},{2,1},{3,0},{4,7},{5,6},{6,5},{7,4},{8,11},{9,10},{10,... | collective-permute-start | bytes 147464 | tf_op jit(solution)/shard_map/ppermute | solution.py:26
  129.1 5.0 %collective-permute-start.35 = (bf16[48,512]{1,0:T(8,128)(2,1)S(1)}, bf16[48,512]{1,0:T(8,128)(2,1)S(1)}, u32[]{:S(2)}, u32[]{:S(2)}) collective-permute-start(bf16[48,512]{1,0:T(8,128)(2,1)S(1)} %get-tuple-element.70), channel_id=1, source_target_pairs={{0,2},{1,3},{2,0},{3,1},{4,6},{5,7},{6,4},{7,5},{8,10},{9,11},{10,... | collective-permute-start | bytes 147464 | tf_op jit(solution)/shard_map/ppermute | solution.py:26

commit v8 on v7

--- a/solution.py
+++ b/solution.py
@@ -17,11 +17,11 @@
 SECOND = (3, 1)
 
 
-def exchange(value, masks_x=(0, 0), z=0, masks_y=(0, 0), zhi=0, core=0):
+def exchange(value, masks_x=(0, 0), z=(0, 0), masks_y=(0, 0), zhi=0, core=0):
     pairs = []
     for gx in range(N):
         for gy in range(N):
-            other = (gx ^ (2 * masks_y[gx & 1]) ^ (8 * zhi) ^ core) * N + (gy ^ (4 * masks_x[gx & 1]) ^ z)
+            other = (gx ^ (2 * masks_y[gx & 1]) ^ (8 * zhi) ^ core) * N + (gy ^ (4 * masks_x[gx & 1]) ^ z[gx >> 3])
             pairs.append((gx * N + gy, other))
     return lax.ppermute(value, ("gx", "gy"), pairs)
 
@@ -37,15 +37,16 @@
 
 
 def x_place(gx, block):
-    return gray(lax.select((gx & 1) == 0, block >> 2, (3 * (block >> 2)) & 3))
+    x = (block >> 1) & 3
+    return gray(lax.select((gx & 1) == 0, x, (3 * x) & 3))
 
 
 def gathered_slot(gx, block):
-    return 8 * ((block >> 1) & 1) + 2 * x_place(gx, block) + (block & 1)
+    return 8 * (block & 1) + 2 * x_place(gx, block) + (block >> 3)
 
 
 def scattered_slot(gx, block):
-    return 4 * x_place(gx, block) + (block & 3)
+    return 2 * x_place(gx, block) + (block & 1)
 
 
 def pick_kernel(rows, n, *refs):
@@ -62,16 +63,15 @@
             out[pl.ds(k * rows, rows), :] = whole[pl.ds(source, rows), :]
 
 
-def place_kernel(rows, *refs):
-    *pieces, keep_ref, send_ref, out_ref = refs
+def place_kernel(rows, half, *refs):
+    *pieces, keep_ref, send_ref, whole = refs
     me = lax.axis_index("gx")
-    for piece, (gx, z) in zip(pieces, [(me, 0), (me, 1), (me ^ 1, 0), (me ^ 1, 1)]):
+    for piece, gx in zip(pieces, (me, me ^ 1)):
         for part, blocks in enumerate(kept(gx)):
-            target = pl.multiple_of(scattered_slot(me, blocks[z]) * rows, 16)
-            out_ref[pl.ds(target, rows), :] = piece[pl.ds(part * rows, rows), :]
-    half = N // 2 * rows
-    send_ref[...] = out_ref[half:, :]
-    keep_ref[...] = out_ref[:half, :]
+            target = pl.multiple_of(scattered_slot(me, blocks[half]) * rows, 16)
+            whole[pl.ds(target, rows), :] = piece[pl.ds(part * rows, rows), :]
+    send_ref[...] = whole[N // 4 * rows :, :]
+    keep_ref[...] = whole[: N // 4 * rows, :]
 
 
 def pack_kernel(gate_ref, up_ref, out_ref, sems):
@@ -130,15 +130,14 @@
     )
 
 
-def place(pieces, rows):
+def place(pieces, rows, half):
     width = pieces[0].shape[1]
     return in_vmem(
-        functools.partial(place_kernel, rows),
-        [(N // 2 * rows, width)] * 2,
+        functools.partial(place_kernel, rows, half),
+        [(N // 4 * rows, width)] * 2,
         "place",
         *pieces,
-        scratch=[pltpu.VMEM((N * rows, width), BF)],
-        limit=16,
+        scratch=[pltpu.VMEM((N // 2 * rows, width), BF)],
     )
 
 
@@ -179,7 +178,7 @@
 
 
 def gather_tokens(t, gate_weight, up_weight):
-    t1, t2, t3 = (exchange(t, z=m) for m in (1, 2, 3))
+    t1, t2, t3 = (exchange(t, z=(m, m)) for m in (1, 2, 3))
     pieces = []
     for h in join(t, t1), join(t2, t3):
         p = exchange(h, masks_x=FIRST)
@@ -223,45 +222,40 @@
     return [stays[0], stays[2]], [got[1], got[2]]
 
 
-def gather_hidden(own, other):
-    halves = []
-    for hidden in own, other:
-        h = join(*hidden)
-        h = join(h, exchange(h, masks_y=SECOND))
-        halves.append(join(h, exchange(h, masks_y=FIRST)))
-    return halves + [exchange(h, core=1) for h in halves]
-
-
-def scatter_out(hidden, weight, rows):
-    parts, stays, got = (slice(0, 512), slice(512, None)), [None, None], [None, None]
-    turn = weight
-    for c, part in enumerate(parts):
-        first_rows, _ = tie(hidden[1], turn)
-        turn = dot(first_rows, weight[:, part])
-        got[c] = exchange(turn, masks_x=SECOND)
-    for c, part in enumerate(parts):
-        kept_rows, _ = tie(hidden[0], turn)
-        (stays[c],) = tie(dot(kept_rows, weight[:, part]))
-    for c in range(2):
-        got[c], _ = tie(got[c], turn)
-        stays[c], turn = halve(stays[c], got[c], 4 * rows)
-        got[c] = exchange(turn, masks_x=FIRST)
-    columns = []
-    for c in range(2):
-        if c == 1:
-            got[1], z[1] = tie(got[1], z[1])
-        v = add(stays[c], got[c])
-        z = [v[:rows]] + [exchange(v[m * rows : (m + 1) * rows], z=m) for m in (1, 2, 3)]
-        columns.append(z)
-    columns = [functools.reduce(jnp.add, [p.astype(F32) for p in z]).astype(BF) for z in columns]
-    return jnp.concatenate(columns, axis=1)
+def hidden_to_output(own, other, weight, rows):
+    stays = [None, None]
+    hidden = [join(*own), join(*other)]
+    got = [exchange(h, masks_y=SECOND) for h in hidden]
+    hidden = [join(h, g) for h, g in zip(hidden, got)]
+    got = tie(*[exchange(h, masks_y=FIRST) for h in hidden])
+    got = list(got)
+    turn = hidden[1]
+    for k in range(2):
+        got[k], _ = tie(got[k], turn)
+        h = join(hidden[k], got[k])
+        keep, send = place([h, exchange(h, core=1)], rows, k)
+        turn = dot(send, weight)
+        keep, _ = tie(keep, turn)
+        (stays[k],) = tie(dot(keep, weight))
+        got[k] = exchange(turn, masks_x=SECOND)
+    for k in range(2):
+        got[k], _ = tie(got[k], turn)
+        stays[k], turn = halve(stays[k], got[k], 2 * rows)
+        got[k] = exchange(turn, masks_x=FIRST)
+    total = 0.0
+    for k in range(2):
+        got[k], _ = tie(got[k], turn)
+        v = turn = add(stays[k], got[k])
+        first, second = ((0, 1), (2, 3)) if k == 0 else ((1, 0), (3, 2))
+        total += exchange(v[rows:], z=second).astype(F32) + exchange(v[:rows], z=first).astype(F32)
+    return total.astype(BF)
 
 
 def shards(tokens, gate_weight, up_weight, down_weight):
     rows = tokens.shape[0]
     pieces, weight = gather_tokens(tokens, gate_weight, up_weight)
-    hidden = scatter_hidden(pick(pieces, rows // CHUNKS), weight, rows // CHUNKS)
-    return scatter_out(place(gather_hidden(*hidden), rows), down_weight, rows)
+    own, other = scatter_hidden(pick(pieces, rows // CHUNKS), weight, rows // CHUNKS)
+    return hidden_to_output(own, other, down_weight, rows)
 
 
 def solution(mesh):

time: 137 us -> 138 us (level); the launches traced: 135 us -> 138 us
  waiting for transfers between devices: 60.4 us -> 65.1 us
  starting transfers between devices: 54.7 us -> 53.3 us
    ppermute x37 -> x35, waiting for transfers between devices: 60.4 us -> 65.1 us  [exchange(): return lax.ppermute(value, ('gx', 'gy'), pairs)]
    ppermute x37 -> x35, starting transfers between devices: 54.7 us -> 53.3 us  [exchange(): return lax.ppermute(value, ('gx', 'gy'), pairs)]
  transfers between devices with their start and end apart: 37 -> 35, of which waited for: 22 -> 21; matrix products, arithmetic and copies ran while one was open for 6% -> 6% of each run, Pallas kernels for 1% -> 1%
where the time goes in v8:
time: 138 us
  waiting for transfers between devices  65.1 us (47%)
  starting transfers between devices  53.3 us (39%)
  matrix products  9.36 us (7%)
  local copies, waits for them, and re-layouts  5.27 us (4%)
  Pallas kernels  2.49 us (2%)
  other arithmetic  2.12 us (2%)
    ppermute x35, waiting for transfers between devices, exchange(): return lax.ppermute(value, ('gx', 'gy'), pairs)  65.1 us
    ppermute x35, starting transfers between devices, exchange(): return lax.ppermute(value, ('gx', 'gy'), pairs)  53.3 us
    dot_general x7, matrix products, dot(): return jnp.dot(a, b, preferred_element_type=F32).astype(BF)  9.36 us
    unnamed x8, local copies, waits for them, and re-layouts  4.85 us
  transfers between devices with their start and end apart: 35, of which 21 were waited for; matrix products, arithmetic and copies ran while one was open for 6% of the time, Pallas kernels for 1%

profile of v8, /device:TPU:24, one launch (start us, length us, event | category | flops | bytes accessed | tf_op | source)
XLA Modules:
  0.0 138.2 jit_solution(16639052416639819968)
XLA Ops:
  0.0 1.9 %collective-permute-start = (bf16[48,1024]{1,0:T(8,128)(2,1)}, bf16[48,1024]{1,0:T(8,128)(2,1)S(1)}, u32[]{:S(2)}, u32[]{:S(2)}) collective-permute-start(bf16[48,1024]{1,0:T(8,128)(2,1)} %refs_0_.1), channel_id=1, source_target_pairs={{0,1},{1,0},{2,3},{3,2},{4,5},{5,4},{6,7},{7,6},{8,9},{9,8},{10,11... | collective-permute-start | bytes 294920 | tf_op jit(solution)/shard_map/ppermute | solution.py:26
  1.9 2.8 %collective-permute-start.4 = (bf16[48,1024]{1,0:T(8,128)(2,1)}, bf16[48,1024]{1,0:T(8,128)(2,1)S(1)}, u32[]{:S(2)}, u32[]{:S(2)}) collective-permute-start(bf16[48,1024]{1,0:T(8,128)(2,1)} %refs_0_.1), channel_id=1, source_target_pairs={{0,3},{1,2},{2,1},{3,0},{4,7},{5,6},{6,5},{7,4},{8,11},{9,10},{10,... | collective-permute-start | bytes 294920 | tf_op jit(solution)/shard_map/ppermute | solution.py:26
  5.2 0.9 copy-done.3
  6.1 1.6 %collective-permute-start.1 = (bf16[96,1024]{1,0:T(8,128)(2,1)S(1)}, bf16[96,1024]{1,0:T(8,128)(2,1)S(1)}, u32[]{:S(2)}, u32[]{:S(2)}) collective-permute-start(bf16[96,1024]{1,0:T(8,128)(2,1)S(1)} %join.11.refs_0_), channel_id=1, source_target_pairs={{0,4},{1,5},{2,6},{3,7},{4,0},{5,1},{6,2},{7,3},{8,12},{9,13},{10,... | collective-permute-start | bytes 589832 | tf_op jit(solution)/shard_map/ppermute | solution.py:26
  7.7 3.1 %collective-permute-done.4.refs_1_ = bf16[48,1024]{1,0:T(8,128)(2,1)S(1)} collective-permute-done((bf16[48,1024]{1,0:T(8,128)(2,1)}, bf16[48,1024]{1,0:T(8,128)(2,1)S(1)}, u32[]{:S(2)}, u32[]{:S(2)}) %collective-permute-start.4) | collective-permute-done | bytes 98336 | tf_op jit(solution)/shard_map/ppermute | solution.py:26
  10.8 3.5 %collective-permute-done.3.refs_0_ = bf16[48,1024]{1,0:T(8,128)(2,1)S(1)} collective-permute-done((bf16[48,1024]{1,0:T(8,128)(2,1)}, bf16[48,1024]{1,0:T(8,128)(2,1)S(1)}, u32[]{:S(2)}, u32[]{:S(2)}) %collective-permute-start.3) | collective-permute-done | bytes 98336 | tf_op jit(solution)/shard_map/ppermute | solution.py:26
  14.3 1.6 %collective-permute-start.5 = (bf16[96,1024]{1,0:T(8,128)(2,1)S(1)}, bf16[96,1024]{1,0:T(8,128)(2,1)S(1)}, u32[]{:S(2)}, u32[]{:S(2)}) collective-permute-start(bf16[96,1024]{1,0:T(8,128)(2,1)S(1)} %join.13.refs_0_.refs_3_), channel_id=1, source_target_pairs={{0,4},{1,5},{2,6},{3,7},{4,0},{5,1},{6,2},{7,3},{8,12},{9,13},{10,... | collective-permute-start | bytes 589832 | tf_op jit(solution)/shard_map/ppermute | solution.py:26
  15.9 2.2 %collective-permute-start.2 = (bf16[192,1024]{1,0:T(8,128)(2,1)S(1)}, bf16[192,1024]{1,0:T(8,128)(2,1)S(1)}, u32[]{:S(2)}, u32[]{:S(2)}) collective-permute-start(bf16[192,1024]{1,0:T(8,128)(2,1)S(1)} %join.12), channel_id=1, source_target_pairs={{0,12},{1,13},{2,14},{3,15},{4,8},{5,9},{6,10},{7,11},{8,4},{9,5},... | collective-permute-start | bytes 1179656 | tf_op jit(solution)/shard_map/ppermute | solution.py:26
  18.1 3.1 %collective-permute-done.5.refs_1_.refs_4_ = bf16[96,1024]{1,0:T(8,128)(2,1)S(1)} collective-permute-done((bf16[96,1024]{1,0:T(8,128)(2,1)S(1)}, bf16[96,1024]{1,0:T(8,128)(2,1)S(1)}, u32[]{:S(2)}, u32[]{:S(2)}) %collective-permute-start.5) | collective-permute-done | bytes 196640 | tf_op jit(solution)/shard_map/ppermute | solution.py:26
  21.2 3.9 %collective-permute-start.6 = (bf16[192,1024]{1,0:T(8,128)(2,1)S(1)}, bf16[192,1024]{1,0:T(8,128)(2,1)S(1)}, u32[]{:S(2)}, u32[]{:S(2)}) collective-permute-start(bf16[192,1024]{1,0:T(8,128)(2,1)S(1)} %join.14), channel_id=1, source_target_pairs={{0,12},{1,13},{2,14},{3,15},{4,8},{5,9},{6,10},{7,11},{8,4},{9,5},... | collective-permute-start | bytes 1179656 | tf_op jit(solution)/shard_map/ppermute | solution.py:26
  25.0 2.0 %copy-done.1 = bf16[1024,1664]{1,0:T(8,128)(2,1)S(1)} copy-done((bf16[1024,1664]{1,0:T(8,128)(2,1)S(1)}, bf16[1024,1664]{1,0:T(8,128)(2,1)}, u32[]{:S(2)}) %copy-start.1) | copy-done | bytes 3407896
  27.0 2.0 %copy-done.2 = bf16[1024,1664]{1,0:T(8,128)(2,1)S(1)} copy-done((bf16[1024,1664]{1,0:T(8,128)(2,1)S(1)}, bf16[1024,1664]{1,0:T(8,128)(2,1)}, u32[]{:S(2)}) %copy-start.2) | copy-done | bytes 3407896
  29.0 1.5 %pack.1 = bf16[1024,3328]{1,0:T(8,128)(2,1)S(1)} custom-call(bf16[1024,1664]{1,0:T(8,128)(2,1)S(1)} %copy-done.1, bf16[1024,1664]{1,0:T(8,128)(2,1)S(1)} %copy-done.2), custom_call_target="tpu_custom_call" | custom-call | bytes 13631488 | tf_op jit(solution)/shard_map/pack/pallas_call | solution.py:94
  31.0 1.9 %convolution_convert_fusion.2 = bf16[256,3328]{1,0:T(8,128)(2,1)S(1)} fusion(bf16[256,1024]{1,0:T(8,128)(2,1)S(1)} %get-tuple-element.37, bf16[1024,3328]{1,0:T(8,128)(2,1)S(1)} %pack.1), kind=kOutput, calls=%fused_computation.2 | convolution fusion | flops 1745682432 | bytes 9043968 | tf_op jit(solution)/shard_map/dot_general | solution.py:173
  33.1 1.9 %convolution_convert_fusion.1 = bf16[256,3328]{1,0:T(8,128)(2,1)S(1)} fusion(bf16[256,1024]{1,0:T(8,128)(2,1)S(1)} %get-tuple-element.40, bf16[1024,3328]{1,0:T(8,128)(2,1)S(1)} %pack.1), kind=kOutput, calls=%fused_computation.1 | convolution fusion | flops 1745682432 | bytes 9043968 | tf_op jit(solution)/shard_map/dot_general | solution.py:173
  36.0 1.0 collective-permute-start.8
  37.0 1.9 %convolution_convert_fusion = bf16[256,3328]{1,0:T(8,128)(2,1)S(1)} fusion(bf16[256,1024]{1,0:T(8,128)(2,1)S(1)} %get-tuple-element.43, bf16[1024,3328]{1,0:T(8,128)(2,1)S(1)} %pack.1), kind=kOutput, calls=%fused_computation | convolution fusion | flops 1745682432 | bytes 9043968 | tf_op jit(solution)/shard_map/dot_general | solution.py:173
  39.3 1.4 collective-permute-start.12
  41.7 1.4 collective-permute-start.15
  43.1 1.3 collective-permute-done.8
  44.8 5.7 %collective-permute-done.12 = bf16[64,3328]{1,0:T(8,128)(2,1)S(1)} collective-permute-done((bf16[64,3328]{1,0:T(8,128)(2,1)S(1)}, bf16[64,3328]{1,0:T(8,128)(2,1)S(1)}, u32[]{:S(2)}, u32[]{:S(2)}) %collective-permute-start.12) | collective-permute-done | bytes 426016 | tf_op jit(solution)/shard_map/ppermute | solution.py:26
  50.7 1.3 collective-permute-start.14
  52.0 2.0 %collective-permute-done.11 = bf16[32,3328]{1,0:T(8,128)(2,1)S(1)} collective-permute-done((bf16[32,3328]{1,0:T(8,128)(2,1)S(1)}, bf16[32,3328]{1,0:T(8,128)(2,1)S(1)}, u32[]{:S(2)}, u32[]{:S(2)}) %collective-permute-start.11) | collective-permute-done | bytes 213024 | tf_op jit(solution)/shard_map/ppermute | solution.py:26
  54.1 5.6 %collective-permute-start.13 = (bf16[16,3328]{1,0:T(8,128)(2,1)S(1)}, bf16[16,3328]{1,0:T(8,128)(2,1)S(1)}, u32[]{:S(2)}, u32[]{:S(2)}) collective-permute-start(bf16[16,3328]{1,0:T(8,128)(2,1)S(1)} %get-tuple-element.73), channel_id=1, source_target_pairs={{0,128},{1,129},{2,130},{3,131},{4,132},{5,133},{6,134},{7,135},{8... | collective-permute-start | bytes 319496 | tf_op jit(solution)/shard_map/ppermute | solution.py:26
  60.2 4.6 %collective-permute-start.16 = (bf16[16,3328]{1,0:T(8,128)(2,1)S(1)}, bf16[16,3328]{1,0:T(8,128)(2,1)S(1)}, u32[]{:S(2)}, u32[]{:S(2)}) collective-permute-start(bf16[16,3328]{1,0:T(8,128)(2,1)S(1)} %get-tuple-element.72), channel_id=1, source_target_pairs={{0,128},{1,129},{2,130},{3,131},{4,132},{5,133},{6,134},{7,135},{8... | collective-permute-start | bytes 319496 | tf_op jit(solution)/shard_map/ppermute | solution.py:26
  64.9 2.1 %collective-permute-done.17 = bf16[32,3328]{1,0:T(8,128)(2,1)S(1)} collective-permute-done((bf16[32,3328]{1,0:T(8,128)(2,1)S(1)}, bf16[32,3328]{1,0:T(8,128)(2,1)S(1)}, u32[]{:S(2)}, u32[]{:S(2)}) %collective-permute-start.17) | collective-permute-done | bytes 213024 | tf_op jit(solution)/shard_map/ppermute | solution.py:26
  67.0 4.0 %collective-permute-start.18 = (bf16[16,3328]{1,0:T(8,128)(2,1)S(1)}, bf16[16,3328]{1,0:T(8,128)(2,1)S(1)}, u32[]{:S(2)}, u32[]{:S(2)}) collective-permute-start(bf16[16,3328]{1,0:T(8,128)(2,1)S(1)} %get-tuple-element.70), channel_id=1, source_target_pairs={{0,128},{1,129},{2,130},{3,131},{4,132},{5,133},{6,134},{7,135},{8... | collective-permute-start | bytes 319496 | tf_op jit(solution)/shard_map/ppermute | solution.py:26
  71.1 2.9 %collective-permute-start.21 = (bf16[32,1664]{1,0:T(8,128)(2,1)S(1)}, bf16[32,1664]{1,0:T(8,128)(2,1)S(1)}, u32[]{:S(2)}, u32[]{:S(2)}) collective-permute-start(bf16[32,1664]{1,0:T(8,128)(2,1)S(1)} %join.15.refs_0_), channel_id=1, source_target_pairs={{0,128},{1,129},{2,130},{3,131},{4,132},{5,133},{6,134},{7,135},{8... | collective-permute-start | bytes 319496 | tf_op jit(solution)/shard_map/ppermute | solution.py:26
  74.0 4.7 %collective-permute-done.18.b_ref = bf16[16,3328]{1,0:T(8,128)(2,1)S(1)} collective-permute-done((bf16[16,3328]{1,0:T(8,128)(2,1)S(1)}, bf16[16,3328]{1,0:T(8,128)(2,1)S(1)}, u32[]{:S(2)}, u32[]{:S(2)}) %collective-permute-start.18) | collective-permute-done | bytes 106528 | tf_op jit(solution)/shard_map/ppermute | solution.py:26
  78.8 4.3 %collective-permute-start.22 = (bf16[16,1664]{1,0:T(8,128)(2,1)S(1)}, bf16[16,1664]{1,0:T(8,128)(2,1)S(1)}, u32[]{:S(2)}, u32[]{:S(2)}) collective-permute-start(bf16[16,1664]{1,0:T(8,128)(2,1)S(1)} %silu.5.refs_1_), channel_id=1, source_target_pairs={{0,128},{1,129},{2,130},{3,131},{4,132},{5,133},{6,134},{7,135},{8... | collective-permute-start | bytes 159752 | tf_op jit(solution)/shard_map/ppermute | solution.py:26
  83.2 3.7 %collective-permute-done.22.refs_1_ = bf16[16,1664]{1,0:T(8,128)(2,1)S(1)} collective-permute-done((bf16[16,1664]{1,0:T(8,128)(2,1)S(1)}, bf16[16,1664]{1,0:T(8,128)(2,1)S(1)}, u32[]{:S(2)}, u32[]{:S(2)}) %collective-permute-start.22) | collective-permute-done | bytes 53280 | tf_op jit(solution)/shard_map/ppermute | solution.py:26
  86.9 1.1 collective-permute-start.23
  88.1 2.8 %collective-permute-done.19.refs_1_ = bf16[48,1664]{1,0:T(8,128)(2,1)S(1)} collective-permute-done((bf16[48,1664]{1,0:T(8,128)(2,1)S(1)}, bf16[48,1664]{1,0:T(8,128)(2,1)S(1)}, u32[]{:S(2)}, u32[]{:S(2)}) %collective-permute-start.19) | collective-permute-done | bytes 159776 | tf_op jit(solution)/shard_map/ppermute | solution.py:26
  91.0 4.3 %collective-permute-done.23.refs_1_ = bf16[48,1664]{1,0:T(8,128)(2,1)S(1)} collective-permute-done((bf16[48,1664]{1,0:T(8,128)(2,1)S(1)}, bf16[48,1664]{1,0:T(8,128)(2,1)S(1)}, u32[]{:S(2)}, u32[]{:S(2)}) %collective-permute-start.23) | collective-permute-done | bytes 159776 | tf_op jit(solution)/shard_map/ppermute | solution.py:26
  95.4 2.6 %collective-permute-done.20.refs_1_ = bf16[96,1664]{1,0:T(8,128)(2,1)S(1)} collective-permute-done((bf16[96,1664]{1,0:T(8,128)(2,1)S(1)}, bf16[96,1664]{1,0:T(8,128)(2,1)S(1)}, u32[]{:S(2)}, u32[]{:S(2)}) %collective-permute-start.20) | collective-permute-done | bytes 319520 | tf_op jit(solution)/shard_map/ppermute | solution.py:26
  98.0 4.4 %collective-permute-done.24.refs_1_ = bf16[96,1664]{1,0:T(8,128)(2,1)S(1)} collective-permute-done((bf16[96,1664]{1,0:T(8,128)(2,1)S(1)}, bf16[96,1664]{1,0:T(8,128)(2,1)S(1)}, u32[]{:S(2)}, u32[]{:S(2)}) %collective-permute-start.24) | collective-permute-done | bytes 319520 | tf_op jit(solution)/shard_map/ppermute | solution.py:26
  102.7 2.1 %collective-permute-done.25.refs_1_ = bf16[192,1664]{1,0:T(8,128)(2,1)S(1)} collective-permute-done((bf16[192,1664]{1,0:T(8,128)(2,1)S(1)}, bf16[192,1664]{1,0:T(8,128)(2,1)S(1)}, u32[]{:S(2)}, u32[]{:S(2)}) %collective-permute-start.25) | collective-permute-done | bytes 639008 | tf_op jit(solution)/shard_map/ppermute | solution.py:26
  106.2 3.2 %collective-permute-start.26 = (bf16[192,1024]{1,0:T(8,128)(2,1)S(1)}, bf16[192,1024]{1,0:T(8,128)(2,1)S(1)}, u32[]{:S(2)}, u32[]{:S(2)}) collective-permute-start(bf16[192,1024]{1,0:T(8,128)(2,1)S(1)} %convolution_convert_fusion.6), channel_id=1, source_target_pairs={{0,12},{1,13},{2,14},{3,15},{4,8},{5,9},{6,10},{7,11},{8,4},{9,5},... | collective-permute-start | bytes 1179656 | tf_op jit(solution)/shard_map/ppermute | solution.py:26
  109.4 0.9 convolution_convert_fusion.5
  110.5 0.9 convolution_convert_fusion.4
  111.4 1.1 collective-permute-start.29
  113.4 1.8 %collective-permute-done.26 = bf16[192,1024]{1,0:T(8,128)(2,1)S(1)} collective-permute-done((bf16[192,1024]{1,0:T(8,128)(2,1)S(1)}, bf16[192,1024]{1,0:T(8,128)(2,1)S(1)}, u32[]{:S(2)}, u32[]{:S(2)}) %collective-permute-start.26) | collective-permute-done | bytes 393248 | tf_op jit(solution)/shard_map/ppermute | solution.py:26
  115.4 7.6 %collective-permute-done.29 = bf16[192,1024]{1,0:T(8,128)(2,1)S(1)} collective-permute-done((bf16[192,1024]{1,0:T(8,128)(2,1)S(1)}, bf16[192,1024]{1,0:T(8,128)(2,1)S(1)}, u32[]{:S(2)}, u32[]{:S(2)}) %collective-permute-start.29) | collective-permute-done | bytes 393248 | tf_op jit(solution)/shard_map/ppermute | solution.py:26
  124.2 4.8 %collective-permute-done.32 = bf16[96,1024]{1,0:T(8,128)(2,1)S(1)} collective-permute-done((bf16[96,1024]{1,0:T(8,128)(2,1)S(1)}, bf16[96,1024]{1,0:T(8,128)(2,1)S(1)}, u32[]{:S(2)}, u32[]{:S(2)}) %collective-permute-start.32) | collective-permute-done | bytes 196640 | tf_op jit(solution)/shard_map/ppermute | solution.py:26
  129.1 1.9 %collective-permute-start.33 = (bf16[48,1024]{1,0:T(8,128)(2,1)S(1)}, bf16[48,1024]{1,0:T(8,128)(2,1)S(1)}, u32[]{:S(2)}, u32[]{:S(2)}) collective-permute-start(bf16[48,1024]{1,0:T(8,128)(2,1)S(1)} %get-tuple-element.77), channel_id=1, source_target_pairs={{0,3},{1,2},{2,1},{3,0},{4,7},{5,6},{6,5},{7,4},{8,11},{9,10},{10,... | collective-permute-start | bytes 294920 | tf_op jit(solution)/shard_map/ppermute | solution.py:26
  131.0 1.9 %collective-permute-start.34 = (bf16[48,1024]{1,0:T(8,128)(2,1)S(1)}, bf16[48,1024]{1,0:T(8,128)(2,1)S(1)}, u32[]{:S(2)}, u32[]{:S(2)}) collective-permute-start(bf16[48,1024]{1,0:T(8,128)(2,1)S(1)} %get-tuple-element.78), channel_id=1, source_target_pairs={{0,1},{1,0},{2,3},{3,2},{4,5},{5,4},{6,7},{7,6},{8,9},{9,8},{10,11... | collective-permute-start | bytes 294920 | tf_op jit(solution)/shard_map/ppermute | solution.py:26
  132.9 2.7 %collective-permute-done.33 = bf16[48,1024]{1,0:T(8,128)(2,1)S(1)} collective-permute-done((bf16[48,1024]{1,0:T(8,128)(2,1)S(1)}, bf16[48,1024]{1,0:T(8,128)(2,1)S(1)}, u32[]{:S(2)}, u32[]{:S(2)}) %collective-permute-start.33) | collective-permute-done | bytes 98336 | tf_op jit(solution)/shard_map/ppermute | solution.py:26
  135.6 1.9 %collective-permute-done.34 = bf16[48,1024]{1,0:T(8,128)(2,1)S(1)} collective-permute-done((bf16[48,1024]{1,0:T(8,128)(2,1)S(1)}, bf16[48,1024]{1,0:T(8,128)(2,1)S(1)}, u32[]{:S(2)}, u32[]{:S(2)}) %collective-permute-start.34) | collective-permute-done | bytes 98336 | tf_op jit(solution)/shard_map/ppermute | solution.py:26
  (85 shorter events, 10.1 us)
Async XLA Ops:
  0.0 105.0 %copy-start = (bf16[1664,1024]{1,0:T(8,128)(2,1)S(1)}, bf16[1664,1024]{1,0:T(8,128)(2,1)}, u32[]{:S(2)}) copy-start(bf16[1664,1024]{1,0:T(8,128)(2,1)} %param.7) | copy-start | bytes 10223620
  0.0 5.2 %collective-permute-start = (bf16[48,1024]{1,0:T(8,128)(2,1)}, bf16[48,1024]{1,0:T(8,128)(2,1)S(1)}, u32[]{:S(2)}, u32[]{:S(2)}) collective-permute-start(bf16[48,1024]{1,0:T(8,128)(2,1)} %refs_0_.1), channel_id=1, source_target_pairs={{0,1},{1,0},{2,3},{3,2},{4,5},{5,4},{6,7},{7,6},{8,9},{9,8},{10,11... | collective-permute-start | bytes 294920 | tf_op jit(solution)/shard_map/ppermute | solution.py:26
  1.9 8.9 %collective-permute-start.4 = (bf16[48,1024]{1,0:T(8,128)(2,1)}, bf16[48,1024]{1,0:T(8,128)(2,1)S(1)}, u32[]{:S(2)}, u32[]{:S(2)}) collective-permute-start(bf16[48,1024]{1,0:T(8,128)(2,1)} %refs_0_.1), channel_id=1, source_target_pairs={{0,3},{1,2},{2,1},{3,0},{4,7},{5,6},{6,5},{7,4},{8,11},{9,10},{10,... | collective-permute-start | bytes 294920 | tf_op jit(solution)/shard_map/ppermute | solution.py:26
  4.7 9.5 %collective-permute-start.3 = (bf16[48,1024]{1,0:T(8,128)(2,1)}, bf16[48,1024]{1,0:T(8,128)(2,1)S(1)}, u32[]{:S(2)}, u32[]{:S(2)}) collective-permute-start(bf16[48,1024]{1,0:T(8,128)(2,1)} %refs_0_.1), channel_id=1, source_target_pairs={{0,2},{1,3},{2,0},{3,1},{4,6},{5,7},{6,4},{7,5},{8,10},{9,11},{10,... | collective-permute-start | bytes 294920 | tf_op jit(solution)/shard_map/ppermute | solution.py:26
  5.2 0.9 copy-start.3
  6.1 9.7 %collective-permute-start.1 = (bf16[96,1024]{1,0:T(8,128)(2,1)S(1)}, bf16[96,1024]{1,0:T(8,128)(2,1)S(1)}, u32[]{:S(2)}, u32[]{:S(2)}) collective-permute-start(bf16[96,1024]{1,0:T(8,128)(2,1)S(1)} %join.11.refs_0_), channel_id=1, source_target_pairs={{0,4},{1,5},{2,6},{3,7},{4,0},{5,1},{6,2},{7,3},{8,12},{9,13},{10,... | collective-permute-start | bytes 589832 | tf_op jit(solution)/shard_map/ppermute | solution.py:26
  14.3 6.9 %collective-permute-start.5 = (bf16[96,1024]{1,0:T(8,128)(2,1)S(1)}, bf16[96,1024]{1,0:T(8,128)(2,1)S(1)}, u32[]{:S(2)}, u32[]{:S(2)}) collective-permute-start(bf16[96,1024]{1,0:T(8,128)(2,1)S(1)} %join.13.refs_0_.refs_3_), channel_id=1, source_target_pairs={{0,4},{1,5},{2,6},{3,7},{4,0},{5,1},{6,2},{7,3},{8,12},{9,13},{10,... | collective-permute-start | bytes 589832 | tf_op jit(solution)/shard_map/ppermute | solution.py:26
  15.9 14.5 %collective-permute-start.2 = (bf16[192,1024]{1,0:T(8,128)(2,1)S(1)}, bf16[192,1024]{1,0:T(8,128)(2,1)S(1)}, u32[]{:S(2)}, u32[]{:S(2)}) collective-permute-start(bf16[192,1024]{1,0:T(8,128)(2,1)S(1)} %join.12), channel_id=1, source_target_pairs={{0,12},{1,13},{2,14},{3,15},{4,8},{5,9},{6,10},{7,11},{8,4},{9,5},... | collective-permute-start | bytes 1179656 | tf_op jit(solution)/shard_map/ppermute | solution.py:26
  21.2 9.6 %collective-permute-start.6 = (bf16[192,1024]{1,0:T(8,128)(2,1)S(1)}, bf16[192,1024]{1,0:T(8,128)(2,1)S(1)}, u32[]{:S(2)}, u32[]{:S(2)}) collective-permute-start(bf16[192,1024]{1,0:T(8,128)(2,1)S(1)} %join.14), channel_id=1, source_target_pairs={{0,12},{1,13},{2,14},{3,15},{4,8},{5,9},{6,10},{7,11},{8,4},{9,5},... | collective-permute-start | bytes 1179656 | tf_op jit(solution)/shard_map/ppermute | solution.py:26
  25.0 2.0 %copy-start.1 = (bf16[1024,1664]{1,0:T(8,128)(2,1)S(1)}, bf16[1024,1664]{1,0:T(8,128)(2,1)}, u32[]{:S(2)}) copy-start(bf16[1024,1664]{1,0:T(8,128)(2,1)} %gate_ref) | copy-start | bytes 10223620
  27.0 2.0 %copy-start.2 = (bf16[1024,1664]{1,0:T(8,128)(2,1)S(1)}, bf16[1024,1664]{1,0:T(8,128)(2,1)}, u32[]{:S(2)}) copy-start(bf16[1024,1664]{1,0:T(8,128)(2,1)} %up_ref.1) | copy-start | bytes 10223620
  33.0 2.7 %collective-permute-start.7 = (bf16[128,3328]{1,0:T(8,128)(2,1)S(1)}, bf16[128,3328]{1,0:T(8,128)(2,1)S(1)}, u32[]{:S(2)}, u32[]{:S(2)}) collective-permute-start(bf16[128,3328]{1,0:T(8,128)(2,1)S(1)} %slice.129), channel_id=1, source_target_pairs={{0,16},{1,17},{2,18},{3,19},{4,20},{5,21},{6,22},{7,23},{8,24},{9,... | collective-permute-start | bytes 2555912 | tf_op jit(solution)/shard_map/ppermute | solution.py:26
  35.1 3.9 %collective-permute-start.10 = (bf16[128,3328]{1,0:T(8,128)(2,1)S(1)}, bf16[128,3328]{1,0:T(8,128)(2,1)S(1)}, u32[]{:S(2)}, u32[]{:S(2)}) collective-permute-start(bf16[128,3328]{1,0:T(8,128)(2,1)S(1)} %slice.130), channel_id=1, source_target_pairs={{0,16},{1,17},{2,18},{3,19},{4,20},{5,21},{6,22},{7,23},{8,24},{9,... | collective-permute-start | bytes 2555912 | tf_op jit(solution)/shard_map/ppermute | solution.py:26
  36.0 8.4 %collective-permute-start.8 = (bf16[64,3328]{1,0:T(8,128)(2,1)S(1)}, bf16[64,3328]{1,0:T(8,128)(2,1)S(1)}, u32[]{:S(2)}, u32[]{:S(2)}) collective-permute-start(bf16[64,3328]{1,0:T(8,128)(2,1)S(1)} %slice.132), channel_id=1, source_target_pairs={{0,32},{1,33},{2,34},{3,35},{4,36},{5,37},{6,38},{7,39},{8,40},{9,... | collective-permute-start | bytes 1277960 | tf_op jit(solution)/shard_map/ppermute | solution.py:26
  39.0 2.5 %collective-permute-start.9 = (bf16[128,3328]{1,0:T(8,128)(2,1)S(1)}, bf16[128,3328]{1,0:T(8,128)(2,1)S(1)}, u32[]{:S(2)}, u32[]{:S(2)}) collective-permute-start(bf16[128,3328]{1,0:T(8,128)(2,1)S(1)} %slice.134), channel_id=1, source_target_pairs={{0,16},{1,17},{2,18},{3,19},{4,20},{5,21},{6,22},{7,23},{8,24},{9,... | collective-permute-start | bytes 2555912 | tf_op jit(solution)/shard_map/ppermute | solution.py:26
  39.3 11.2 %collective-permute-start.12 = (bf16[64,3328]{1,0:T(8,128)(2,1)S(1)}, bf16[64,3328]{1,0:T(8,128)(2,1)S(1)}, u32[]{:S(2)}, u32[]{:S(2)}) collective-permute-start(bf16[64,3328]{1,0:T(8,128)(2,1)S(1)} %slice.136), channel_id=1, source_target_pairs={{0,32},{1,33},{2,34},{3,35},{4,36},{5,37},{6,38},{7,39},{8,40},{9,... | collective-permute-start | bytes 1277960 | tf_op jit(solution)/shard_map/ppermute | solution.py:26
  41.7 17.9 %collective-permute-start.15 = (bf16[64,3328]{1,0:T(8,128)(2,1)S(1)}, bf16[64,3328]{1,0:T(8,128)(2,1)S(1)}, u32[]{:S(2)}, u32[]{:S(2)}) collective-permute-start(bf16[64,3328]{1,0:T(8,128)(2,1)S(1)} %slice.137), channel_id=1, source_target_pairs={{0,32},{1,33},{2,34},{3,35},{4,36},{5,37},{6,38},{7,39},{8,40},{9,... | collective-permute-start | bytes 1277960 | tf_op jit(solution)/shard_map/ppermute | solution.py:26
  44.5 9.5 %collective-permute-start.11 = (bf16[32,3328]{1,0:T(8,128)(2,1)S(1)}, bf16[32,3328]{1,0:T(8,128)(2,1)S(1)}, u32[]{:S(2)}, u32[]{:S(2)}) collective-permute-start(bf16[32,3328]{1,0:T(8,128)(2,1)S(1)} %slice.139), channel_id=1, source_target_pairs={{0,96},{1,97},{2,98},{3,99},{4,100},{5,101},{6,102},{7,103},{8,104... | collective-permute-start | bytes 638984 | tf_op jit(solution)/shard_map/ppermute | solution.py:26
  50.7 9.4 %collective-permute-start.14 = (bf16[32,3328]{1,0:T(8,128)(2,1)S(1)}, bf16[32,3328]{1,0:T(8,128)(2,1)S(1)}, u32[]{:S(2)}, u32[]{:S(2)}) collective-permute-start(bf16[32,3328]{1,0:T(8,128)(2,1)S(1)} %slice.141), channel_id=1, source_target_pairs={{0,96},{1,97},{2,98},{3,99},{4,100},{5,101},{6,102},{7,103},{8,104... | collective-permute-start | bytes 638984 | tf_op jit(solution)/shard_map/ppermute | solution.py:26
  54.1 10.7 %collective-permute-start.13 = (bf16[16,3328]{1,0:T(8,128)(2,1)S(1)}, bf16[16,3328]{1,0:T(8,128)(2,1)S(1)}, u32[]{:S(2)}, u32[]{:S(2)}) collective-permute-start(bf16[16,3328]{1,0:T(8,128)(2,1)S(1)} %get-tuple-element.73), channel_id=1, source_target_pairs={{0,128},{1,129},{2,130},{3,131},{4,132},{5,133},{6,134},{7,135},{8... | collective-permute-start | bytes 319496 | tf_op jit(solution)/shard_map/ppermute | solution.py:26
  59.8 7.1 %collective-permute-start.17 = (bf16[32,3328]{1,0:T(8,128)(2,1)S(1)}, bf16[32,3328]{1,0:T(8,128)(2,1)S(1)}, u32[]{:S(2)}, u32[]{:S(2)}) collective-permute-start(bf16[32,3328]{1,0:T(8,128)(2,1)S(1)} %slice.146), channel_id=1, source_target_pairs={{0,96},{1,97},{2,98},{3,99},{4,100},{5,101},{6,102},{7,103},{8,104... | collective-permute-start | bytes 638984 | tf_op jit(solution)/shard_map/ppermute | solution.py:26
  60.2 10.8 %collective-permute-start.16 = (bf16[16,3328]{1,0:T(8,128)(2,1)S(1)}, bf16[16,3328]{1,0:T(8,128)(2,1)S(1)}, u32[]{:S(2)}, u32[]{:S(2)}) collective-permute-start(bf16[16,3328]{1,0:T(8,128)(2,1)S(1)} %get-tuple-element.72), channel_id=1, source_target_pairs={{0,128},{1,129},{2,130},{3,131},{4,132},{5,133},{6,134},{7,135},{8... | collective-permute-start | bytes 319496 | tf_op jit(solution)/shard_map/ppermute | solution.py:26
  67.0 11.7 %collective-permute-start.18 = (bf16[16,3328]{1,0:T(8,128)(2,1)S(1)}, bf16[16,3328]{1,0:T(8,128)(2,1)S(1)}, u32[]{:S(2)}, u32[]{:S(2)}) collective-permute-start(bf16[16,3328]{1,0:T(8,128)(2,1)S(1)} %get-tuple-element.70), channel_id=1, source_target_pairs={{0,128},{1,129},{2,130},{3,131},{4,132},{5,133},{6,134},{7,135},{8... | collective-permute-start | bytes 319496 | tf_op jit(solution)/shard_map/ppermute | solution.py:26
  71.1 12.2 %collective-permute-start.21 = (bf16[32,1664]{1,0:T(8,128)(2,1)S(1)}, bf16[32,1664]{1,0:T(8,128)(2,1)S(1)}, u32[]{:S(2)}, u32[]{:S(2)}) collective-permute-start(bf16[32,1664]{1,0:T(8,128)(2,1)S(1)} %join.15.refs_0_), channel_id=1, source_target_pairs={{0,128},{1,129},{2,130},{3,131},{4,132},{5,133},{6,134},{7,135},{8... | collective-permute-start | bytes 319496 | tf_op jit(solution)/shard_map/ppermute | solution.py:26
  78.8 8.1 %collective-permute-start.22 = (bf16[16,1664]{1,0:T(8,128)(2,1)S(1)}, bf16[16,1664]{1,0:T(8,128)(2,1)S(1)}, u32[]{:S(2)}, u32[]{:S(2)}) collective-permute-start(bf16[16,1664]{1,0:T(8,128)(2,1)S(1)} %silu.5.refs_1_), channel_id=1, source_target_pairs={{0,128},{1,129},{2,130},{3,131},{4,132},{5,133},{6,134},{7,135},{8... | collective-permute-start | bytes 159752 | tf_op jit(solution)/shard_map/ppermute | solution.py:26
  83.1 7.7 %collective-permute-start.19 = (bf16[48,1664]{1,0:T(8,128)(2,1)S(1)}, bf16[48,1664]{1,0:T(8,128)(2,1)S(1)}, u32[]{:S(2)}, u32[]{:S(2)}) collective-permute-start(bf16[48,1664]{1,0:T(8,128)(2,1)S(1)} %join.16.refs_0_), channel_id=1, source_target_pairs={{0,96},{1,97},{2,98},{3,99},{4,100},{5,101},{6,102},{7,103},{8,104... | collective-permute-start | bytes 479240 | tf_op jit(solution)/shard_map/ppermute | solution.py:26
  86.9 8.3 %collective-permute-start.23 = (bf16[48,1664]{1,0:T(8,128)(2,1)S(1)}, bf16[48,1664]{1,0:T(8,128)(2,1)S(1)}, u32[]{:S(2)}, u32[]{:S(2)}) collective-permute-start(bf16[48,1664]{1,0:T(8,128)(2,1)S(1)} %join.18.refs_0_), channel_id=1, source_target_pairs={{0,96},{1,97},{2,98},{3,99},{4,100},{5,101},{6,102},{7,103},{8,104... | collective-permute-start | bytes 479240 | tf_op jit(solution)/shard_map/ppermute | solution.py:26
  90.9 7.1 %collective-permute-start.20 = (bf16[96,1664]{1,0:T(8,128)(2,1)S(1)}, bf16[96,1664]{1,0:T(8,128)(2,1)S(1)}, u32[]{:S(2)}, u32[]{:S(2)}) collective-permute-start(bf16[96,1664]{1,0:T(8,128)(2,1)S(1)} %join.17.refs_0_), channel_id=1, source_target_pairs={{0,32},{1,33},{2,34},{3,35},{4,36},{5,37},{6,38},{7,39},{8,40},{9,... | collective-permute-start | bytes 958472 | tf_op jit(solution)/shard_map/ppermute | solution.py:26
  95.3 7.1 %collective-permute-start.24 = (bf16[96,1664]{1,0:T(8,128)(2,1)S(1)}, bf16[96,1664]{1,0:T(8,128)(2,1)S(1)}, u32[]{:S(2)}, u32[]{:S(2)}) collective-permute-start(bf16[96,1664]{1,0:T(8,128)(2,1)S(1)} %join.19.refs_0_), channel_id=1, source_target_pairs={{0,32},{1,33},{2,34},{3,35},{4,36},{5,37},{6,38},{7,39},{8,40},{9,... | collective-permute-start | bytes 958472 | tf_op jit(solution)/shard_map/ppermute | solution.py:26
  102.4 2.4 %collective-permute-start.25 = (bf16[192,1664]{1,0:T(8,128)(2,1)S(1)}, bf16[192,1664]{1,0:T(8,128)(2,1)S(1)}, u32[]{:S(2)}, u32[]{:S(2)}) collective-permute-start(bf16[192,1664]{1,0:T(8,128)(2,1)S(1)} %join.20.refs_0_), channel_id=1, source_target_pairs={{0,16},{1,17},{2,18},{3,19},{4,20},{5,21},{6,22},{7,23},{8,24},{9,... | collective-permute-start | bytes 1916936 | tf_op jit(solution)/shard_map/ppermute | solution.py:26
  106.0 4.3 %collective-permute-start.27 = (bf16[192,1664]{1,0:T(8,128)(2,1)S(1)}, bf16[192,1664]{1,0:T(8,128)(2,1)S(1)}, u32[]{:S(2)}, u32[]{:S(2)}) collective-permute-start(bf16[192,1664]{1,0:T(8,128)(2,1)S(1)} %join.21.refs_0_), channel_id=1, source_target_pairs={{0,16},{1,17},{2,18},{3,19},{4,20},{5,21},{6,22},{7,23},{8,24},{9,... | collective-permute-start | bytes 1916936 | tf_op jit(solution)/shard_map/ppermute | solution.py:26
  106.2 9.0 %collective-permute-start.26 = (bf16[192,1024]{1,0:T(8,128)(2,1)S(1)}, bf16[192,1024]{1,0:T(8,128)(2,1)S(1)}, u32[]{:S(2)}, u32[]{:S(2)}) collective-permute-start(bf16[192,1024]{1,0:T(8,128)(2,1)S(1)} %convolution_convert_fusion.6), channel_id=1, source_target_pairs={{0,12},{1,13},{2,14},{3,15},{4,8},{5,9},{6,10},{7,11},{8,4},{9,5},... | collective-permute-start | bytes 1179656 | tf_op jit(solution)/shard_map/ppermute | solution.py:26
  111.4 11.7 %collective-permute-start.29 = (bf16[192,1024]{1,0:T(8,128)(2,1)S(1)}, bf16[192,1024]{1,0:T(8,128)(2,1)S(1)}, u32[]{:S(2)}, u32[]{:S(2)}) collective-permute-start(bf16[192,1024]{1,0:T(8,128)(2,1)S(1)} %convolution_convert_fusion.4), channel_id=1, source_target_pairs={{0,12},{1,13},{2,14},{3,15},{4,8},{5,9},{6,10},{7,11},{8,4},{9,5},... | collective-permute-start | bytes 1179656 | tf_op jit(solution)/shard_map/ppermute | solution.py:26
  115.3 8.0 %collective-permute-start.28 = (bf16[96,1024]{1,0:T(8,128)(2,1)S(1)}, bf16[96,1024]{1,0:T(8,128)(2,1)S(1)}, u32[]{:S(2)}, u32[]{:S(2)}) collective-permute-start(bf16[96,1024]{1,0:T(8,128)(2,1)S(1)} %slice.153), channel_id=1, source_target_pairs={{0,4},{1,5},{2,6},{3,7},{4,0},{5,1},{6,2},{7,3},{8,12},{9,13},{10,... | collective-permute-start | bytes 589832 | tf_op jit(solution)/shard_map/ppermute | solution.py:26
  123.2 5.8 %collective-permute-start.32 = (bf16[96,1024]{1,0:T(8,128)(2,1)S(1)}, bf16[96,1024]{1,0:T(8,128)(2,1)S(1)}, u32[]{:S(2)}, u32[]{:S(2)}) collective-permute-start(bf16[96,1024]{1,0:T(8,128)(2,1)S(1)} %slice.154), channel_id=1, source_target_pairs={{0,4},{1,5},{2,6},{3,7},{4,0},{5,1},{6,2},{7,3},{8,12},{9,13},{10,... | collective-permute-start | bytes 589832 | tf_op jit(solution)/shard_map/ppermute | solution.py:26
  123.4 9.5 %collective-permute-start.30 = (bf16[48,1024]{1,0:T(8,128)(2,1)S(1)}, bf16[48,1024]{1,0:T(8,128)(2,1)S(1)}, u32[]{:S(2)}, u32[]{:S(2)}) collective-permute-start(bf16[48,1024]{1,0:T(8,128)(2,1)S(1)} %get-tuple-element.75), channel_id=1, source_target_pairs={{0,2},{1,3},{2,0},{3,1},{4,6},{5,7},{6,4},{7,5},{8,10},{9,11},{10,... | collective-permute-start | bytes 294920 | tf_op jit(solution)/shard_map/ppermute | solution.py:26
  123.5 9.4 %collective-permute-start.31 = (bf16[48,1024]{1,0:T(8,128)(2,1)S(1)}, bf16[48,1024]{1,0:T(8,128)(2,1)S(1)}, u32[]{:S(2)}, u32[]{:S(2)}) collective-permute-start(bf16[48,1024]{1,0:T(8,128)(2,1)S(1)} %get-tuple-element.76), channel_id=1, source_target_pairs={{0,0},{1,1},{2,2},{3,3},{4,4},{5,5},{6,6},{7,7},{8,8},{9,9},{10,10... | collective-permute-start | bytes 294920 | tf_op jit(solution)/shard_map/ppermute | solution.py:26
  129.1 6.5 %collective-permute-start.33 = (bf16[48,1024]{1,0:T(8,128)(2,1)S(1)}, bf16[48,1024]{1,0:T(8,128)(2,1)S(1)}, u32[]{:S(2)}, u32[]{:S(2)}) collective-permute-start(bf16[48,1024]{1,0:T(8,128)(2,1)S(1)} %get-tuple-element.77), channel_id=1, source_target_pairs={{0,3},{1,2},{2,1},{3,0},{4,7},{5,6},{6,5},{7,4},{8,11},{9,10},{10,... | collective-permute-start | bytes 294920 | tf_op jit(solution)/shard_map/ppermute | solution.py:26
  131.0 6.5 %collective-permute-start.34 = (bf16[48,1024]{1,0:T(8,128)(2,1)S(1)}, bf16[48,1024]{1,0:T(8,128)(2,1)S(1)}, u32[]{:S(2)}, u32[]{:S(2)}) collective-permute-start(bf16[48,1024]{1,0:T(8,128)(2,1)S(1)} %get-tuple-element.78), channel_id=1, source_target_pairs={{0,1},{1,0},{2,3},{3,2},{4,5},{5,4},{6,7},{7,6},{8,9},{9,8},{10,11... | collective-permute-start | bytes 294920 | tf_op jit(solution)/shard_map/ppermute | solution.py:26

commit v9 on v8

--- a/solution.py
+++ b/solution.py
@@ -227,19 +227,21 @@
     hidden = [join(*own), join(*other)]
     got = [exchange(h, masks_y=SECOND) for h in hidden]
     hidden = [join(h, g) for h, g in zip(hidden, got)]
-    got = tie(*[exchange(h, masks_y=FIRST) for h in hidden])
-    got = list(got)
-    turn = hidden[1]
+    got = [exchange(h, masks_y=FIRST) for h in hidden]
+    hidden = [join(h, g) for h, g in zip(hidden, got)]
+    got = list(tie(*[exchange(h, core=1) for h in hidden]))
     for k in range(2):
-        got[k], _ = tie(got[k], turn)
-        h = join(hidden[k], got[k])
-        keep, send = place([h, exchange(h, core=1)], rows, k)
+        if k == 1:
+            got[1], _ = tie(got[1], turn)
+        keep, send = place([hidden[k], got[k]], rows, k)
         turn = dot(send, weight)
         keep, _ = tie(keep, turn)
         (stays[k],) = tie(dot(keep, weight))
         got[k] = exchange(turn, masks_x=SECOND)
     for k in range(2):
         got[k], _ = tie(got[k], turn)
+        if k == 1:
+            got[1], got[0] = tie(got[1], got[0])
         stays[k], turn = halve(stays[k], got[k], 2 * rows)
         got[k] = exchange(turn, masks_x=FIRST)
     total = 0.0

time: 138 us -> 139 us (level); the launches traced: 138 us -> 137 us
  transfers between devices with their start and end apart: 35 -> 35, of which waited for: 21 -> 21; matrix products, arithmetic and copies ran while one was open for 6% -> 6% of each run, Pallas kernels for 1% -> 2%
where the time goes in v9:
time: 139 us; the launch traced here: 137 us
  waiting for transfers between devices  64.9 us (47%)
  starting transfers between devices  52.3 us (38%)
  matrix products  9.36 us (7%)
  local copies, waits for them, and re-layouts  5.27 us (4%)
  Pallas kernels  2.49 us (2%)
  other arithmetic  2.12 us (2%)
    ppermute x35, waiting for transfers between devices, exchange(): return lax.ppermute(value, ('gx', 'gy'), pairs)  64.9 us
    ppermute x35, starting transfers between devices, exchange(): return lax.ppermute(value, ('gx', 'gy'), pairs)  52.3 us
    dot_general x7, matrix products, dot(): return jnp.dot(a, b, preferred_element_type=F32).astype(BF)  9.36 us
    unnamed x8, local copies, waits for them, and re-layouts  4.85 us
  transfers between devices with their start and end apart: 35, of which 21 were waited for; matrix products, arithmetic and copies ran while one was open for 6% of the time, Pallas kernels for 2%

profile of v9, /device:TPU:24, one launch (start us, length us, event | category | flops | bytes accessed | tf_op | source)
XLA Modules:
  0.0 137.0 jit_solution(129203486973617307)
XLA Ops:
  0.0 1.9 %collective-permute-start = (bf16[48,1024]{1,0:T(8,128)(2,1)}, bf16[48,1024]{1,0:T(8,128)(2,1)S(1)}, u32[]{:S(2)}, u32[]{:S(2)}) collective-permute-start(bf16[48,1024]{1,0:T(8,128)(2,1)} %refs_0_.1), channel_id=1, source_target_pairs={{0,1},{1,0},{2,3},{3,2},{4,5},{5,4},{6,7},{7,6},{8,9},{9,8},{10,11... | collective-permute-start | bytes 294920 | tf_op jit(solution)/shard_map/ppermute | solution.py:26
  1.9 2.8 %collective-permute-start.4 = (bf16[48,1024]{1,0:T(8,128)(2,1)}, bf16[48,1024]{1,0:T(8,128)(2,1)S(1)}, u32[]{:S(2)}, u32[]{:S(2)}) collective-permute-start(bf16[48,1024]{1,0:T(8,128)(2,1)} %refs_0_.1), channel_id=1, source_target_pairs={{0,3},{1,2},{2,1},{3,0},{4,7},{5,6},{6,5},{7,4},{8,11},{9,10},{10,... | collective-permute-start | bytes 294920 | tf_op jit(solution)/shard_map/ppermute | solution.py:26
  5.2 0.9 copy-done.3
  6.1 1.6 %collective-permute-start.1 = (bf16[96,1024]{1,0:T(8,128)(2,1)S(1)}, bf16[96,1024]{1,0:T(8,128)(2,1)S(1)}, u32[]{:S(2)}, u32[]{:S(2)}) collective-permute-start(bf16[96,1024]{1,0:T(8,128)(2,1)S(1)} %join.11.refs_0_), channel_id=1, source_target_pairs={{0,4},{1,5},{2,6},{3,7},{4,0},{5,1},{6,2},{7,3},{8,12},{9,13},{10,... | collective-permute-start | bytes 589832 | tf_op jit(solution)/shard_map/ppermute | solution.py:26
  7.7 3.1 %collective-permute-done.4.refs_1_ = bf16[48,1024]{1,0:T(8,128)(2,1)S(1)} collective-permute-done((bf16[48,1024]{1,0:T(8,128)(2,1)}, bf16[48,1024]{1,0:T(8,128)(2,1)S(1)}, u32[]{:S(2)}, u32[]{:S(2)}) %collective-permute-start.4) | collective-permute-done | bytes 98336 | tf_op jit(solution)/shard_map/ppermute | solution.py:26
  10.8 3.5 %collective-permute-done.3.refs_0_ = bf16[48,1024]{1,0:T(8,128)(2,1)S(1)} collective-permute-done((bf16[48,1024]{1,0:T(8,128)(2,1)}, bf16[48,1024]{1,0:T(8,128)(2,1)S(1)}, u32[]{:S(2)}, u32[]{:S(2)}) %collective-permute-start.3) | collective-permute-done | bytes 98336 | tf_op jit(solution)/shard_map/ppermute | solution.py:26
  14.3 1.6 %collective-permute-start.5 = (bf16[96,1024]{1,0:T(8,128)(2,1)S(1)}, bf16[96,1024]{1,0:T(8,128)(2,1)S(1)}, u32[]{:S(2)}, u32[]{:S(2)}) collective-permute-start(bf16[96,1024]{1,0:T(8,128)(2,1)S(1)} %join.13.refs_0_.refs_3_), channel_id=1, source_target_pairs={{0,4},{1,5},{2,6},{3,7},{4,0},{5,1},{6,2},{7,3},{8,12},{9,13},{10,... | collective-permute-start | bytes 589832 | tf_op jit(solution)/shard_map/ppermute | solution.py:26
  15.9 2.2 %collective-permute-start.2 = (bf16[192,1024]{1,0:T(8,128)(2,1)S(1)}, bf16[192,1024]{1,0:T(8,128)(2,1)S(1)}, u32[]{:S(2)}, u32[]{:S(2)}) collective-permute-start(bf16[192,1024]{1,0:T(8,128)(2,1)S(1)} %join.12), channel_id=1, source_target_pairs={{0,12},{1,13},{2,14},{3,15},{4,8},{5,9},{6,10},{7,11},{8,4},{9,5},... | collective-permute-start | bytes 1179656 | tf_op jit(solution)/shard_map/ppermute | solution.py:26
  18.1 3.1 %collective-permute-done.5.refs_1_.refs_4_ = bf16[96,1024]{1,0:T(8,128)(2,1)S(1)} collective-permute-done((bf16[96,1024]{1,0:T(8,128)(2,1)S(1)}, bf16[96,1024]{1,0:T(8,128)(2,1)S(1)}, u32[]{:S(2)}, u32[]{:S(2)}) %collective-permute-start.5) | collective-permute-done | bytes 196640 | tf_op jit(solution)/shard_map/ppermute | solution.py:26
  21.2 3.9 %collective-permute-start.6 = (bf16[192,1024]{1,0:T(8,128)(2,1)S(1)}, bf16[192,1024]{1,0:T(8,128)(2,1)S(1)}, u32[]{:S(2)}, u32[]{:S(2)}) collective-permute-start(bf16[192,1024]{1,0:T(8,128)(2,1)S(1)} %join.14), channel_id=1, source_target_pairs={{0,12},{1,13},{2,14},{3,15},{4,8},{5,9},{6,10},{7,11},{8,4},{9,5},... | collective-permute-start | bytes 1179656 | tf_op jit(solution)/shard_map/ppermute | solution.py:26
  25.0 2.0 %copy-done.1 = bf16[1024,1664]{1,0:T(8,128)(2,1)S(1)} copy-done((bf16[1024,1664]{1,0:T(8,128)(2,1)S(1)}, bf16[1024,1664]{1,0:T(8,128)(2,1)}, u32[]{:S(2)}) %copy-start.1) | copy-done | bytes 3407896
  27.0 2.0 %copy-done.2 = bf16[1024,1664]{1,0:T(8,128)(2,1)S(1)} copy-done((bf16[1024,1664]{1,0:T(8,128)(2,1)S(1)}, bf16[1024,1664]{1,0:T(8,128)(2,1)}, u32[]{:S(2)}) %copy-start.2) | copy-done | bytes 3407896
  29.0 1.5 %pack.1 = bf16[1024,3328]{1,0:T(8,128)(2,1)S(1)} custom-call(bf16[1024,1664]{1,0:T(8,128)(2,1)S(1)} %copy-done.1, bf16[1024,1664]{1,0:T(8,128)(2,1)S(1)} %copy-done.2), custom_call_target="tpu_custom_call" | custom-call | bytes 13631488 | tf_op jit(solution)/shard_map/pack/pallas_call | solution.py:94
  31.0 1.9 %convolution_convert_fusion.2 = bf16[256,3328]{1,0:T(8,128)(2,1)S(1)} fusion(bf16[256,1024]{1,0:T(8,128)(2,1)S(1)} %get-tuple-element.38, bf16[1024,3328]{1,0:T(8,128)(2,1)S(1)} %pack.1), kind=kOutput, calls=%fused_computation.2 | convolution fusion | flops 1745682432 | bytes 9043968 | tf_op jit(solution)/shard_map/dot_general | solution.py:173
  33.1 1.9 %convolution_convert_fusion.1 = bf16[256,3328]{1,0:T(8,128)(2,1)S(1)} fusion(bf16[256,1024]{1,0:T(8,128)(2,1)S(1)} %get-tuple-element.41, bf16[1024,3328]{1,0:T(8,128)(2,1)S(1)} %pack.1), kind=kOutput, calls=%fused_computation.1 | convolution fusion | flops 1745682432 | bytes 9043968 | tf_op jit(solution)/shard_map/dot_general | solution.py:173
  36.0 1.0 collective-permute-start.8
  37.0 1.9 %convolution_convert_fusion = bf16[256,3328]{1,0:T(8,128)(2,1)S(1)} fusion(bf16[256,1024]{1,0:T(8,128)(2,1)S(1)} %get-tuple-element.44, bf16[1024,3328]{1,0:T(8,128)(2,1)S(1)} %pack.1), kind=kOutput, calls=%fused_computation | convolution fusion | flops 1745682432 | bytes 9043968 | tf_op jit(solution)/shard_map/dot_general | solution.py:173
  39.3 1.4 collective-permute-start.12
  41.7 1.4 collective-permute-start.15
  43.1 1.3 collective-permute-done.8
  44.8 5.7 %collective-permute-done.12 = bf16[64,3328]{1,0:T(8,128)(2,1)S(1)} collective-permute-done((bf16[64,3328]{1,0:T(8,128)(2,1)S(1)}, bf16[64,3328]{1,0:T(8,128)(2,1)S(1)}, u32[]{:S(2)}, u32[]{:S(2)}) %collective-permute-start.12) | collective-permute-done | bytes 426016 | tf_op jit(solution)/shard_map/ppermute | solution.py:26
  50.7 1.3 collective-permute-start.14
  52.0 2.0 %collective-permute-done.11 = bf16[32,3328]{1,0:T(8,128)(2,1)S(1)} collective-permute-done((bf16[32,3328]{1,0:T(8,128)(2,1)S(1)}, bf16[32,3328]{1,0:T(8,128)(2,1)S(1)}, u32[]{:S(2)}, u32[]{:S(2)}) %collective-permute-start.11) | collective-permute-done | bytes 213024 | tf_op jit(solution)/shard_map/ppermute | solution.py:26
  54.1 5.6 %collective-permute-start.13 = (bf16[16,3328]{1,0:T(8,128)(2,1)S(1)}, bf16[16,3328]{1,0:T(8,128)(2,1)S(1)}, u32[]{:S(2)}, u32[]{:S(2)}) collective-permute-start(bf16[16,3328]{1,0:T(8,128)(2,1)S(1)} %get-tuple-element.75), channel_id=1, source_target_pairs={{0,128},{1,129},{2,130},{3,131},{4,132},{5,133},{6,134},{7,135},{8... | collective-permute-start | bytes 319496 | tf_op jit(solution)/shard_map/ppermute | solution.py:26
  60.2 4.6 %collective-permute-start.16 = (bf16[16,3328]{1,0:T(8,128)(2,1)S(1)}, bf16[16,3328]{1,0:T(8,128)(2,1)S(1)}, u32[]{:S(2)}, u32[]{:S(2)}) collective-permute-start(bf16[16,3328]{1,0:T(8,128)(2,1)S(1)} %get-tuple-element.74), channel_id=1, source_target_pairs={{0,128},{1,129},{2,130},{3,131},{4,132},{5,133},{6,134},{7,135},{8... | collective-permute-start | bytes 319496 | tf_op jit(solution)/shard_map/ppermute | solution.py:26
  64.9 2.1 %collective-permute-done.17 = bf16[32,3328]{1,0:T(8,128)(2,1)S(1)} collective-permute-done((bf16[32,3328]{1,0:T(8,128)(2,1)S(1)}, bf16[32,3328]{1,0:T(8,128)(2,1)S(1)}, u32[]{:S(2)}, u32[]{:S(2)}) %collective-permute-start.17) | collective-permute-done | bytes 213024 | tf_op jit(solution)/shard_map/ppermute | solution.py:26
  67.0 4.0 %collective-permute-start.18 = (bf16[16,3328]{1,0:T(8,128)(2,1)S(1)}, bf16[16,3328]{1,0:T(8,128)(2,1)S(1)}, u32[]{:S(2)}, u32[]{:S(2)}) collective-permute-start(bf16[16,3328]{1,0:T(8,128)(2,1)S(1)} %get-tuple-element.72), channel_id=1, source_target_pairs={{0,128},{1,129},{2,130},{3,131},{4,132},{5,133},{6,134},{7,135},{8... | collective-permute-start | bytes 319496 | tf_op jit(solution)/shard_map/ppermute | solution.py:26
  71.1 2.9 %collective-permute-start.22 = (bf16[32,1664]{1,0:T(8,128)(2,1)S(1)}, bf16[32,1664]{1,0:T(8,128)(2,1)S(1)}, u32[]{:S(2)}, u32[]{:S(2)}) collective-permute-start(bf16[32,1664]{1,0:T(8,128)(2,1)S(1)} %join.15.refs_0_), channel_id=1, source_target_pairs={{0,128},{1,129},{2,130},{3,131},{4,132},{5,133},{6,134},{7,135},{8... | collective-permute-start | bytes 319496 | tf_op jit(solution)/shard_map/ppermute | solution.py:26
  74.0 4.7 %collective-permute-done.18.b_ref = bf16[16,3328]{1,0:T(8,128)(2,1)S(1)} collective-permute-done((bf16[16,3328]{1,0:T(8,128)(2,1)S(1)}, bf16[16,3328]{1,0:T(8,128)(2,1)S(1)}, u32[]{:S(2)}, u32[]{:S(2)}) %collective-permute-start.18) | collective-permute-done | bytes 106528 | tf_op jit(solution)/shard_map/ppermute | solution.py:26
  78.8 4.3 %collective-permute-start.23 = (bf16[16,1664]{1,0:T(8,128)(2,1)S(1)}, bf16[16,1664]{1,0:T(8,128)(2,1)S(1)}, u32[]{:S(2)}, u32[]{:S(2)}) collective-permute-start(bf16[16,1664]{1,0:T(8,128)(2,1)S(1)} %silu.5.refs_1_), channel_id=1, source_target_pairs={{0,128},{1,129},{2,130},{3,131},{4,132},{5,133},{6,134},{7,135},{8... | collective-permute-start | bytes 159752 | tf_op jit(solution)/shard_map/ppermute | solution.py:26
  83.2 3.7 %collective-permute-done.23.refs_1_ = bf16[16,1664]{1,0:T(8,128)(2,1)S(1)} collective-permute-done((bf16[16,1664]{1,0:T(8,128)(2,1)S(1)}, bf16[16,1664]{1,0:T(8,128)(2,1)S(1)}, u32[]{:S(2)}, u32[]{:S(2)}) %collective-permute-start.23) | collective-permute-done | bytes 53280 | tf_op jit(solution)/shard_map/ppermute | solution.py:26
  86.9 1.1 collective-permute-start.24
  88.1 2.8 %collective-permute-done.19.refs_1_ = bf16[48,1664]{1,0:T(8,128)(2,1)S(1)} collective-permute-done((bf16[48,1664]{1,0:T(8,128)(2,1)S(1)}, bf16[48,1664]{1,0:T(8,128)(2,1)S(1)}, u32[]{:S(2)}, u32[]{:S(2)}) %collective-permute-start.19) | collective-permute-done | bytes 159776 | tf_op jit(solution)/shard_map/ppermute | solution.py:26
  91.0 4.3 %collective-permute-done.24.refs_1_ = bf16[48,1664]{1,0:T(8,128)(2,1)S(1)} collective-permute-done((bf16[48,1664]{1,0:T(8,128)(2,1)S(1)}, bf16[48,1664]{1,0:T(8,128)(2,1)S(1)}, u32[]{:S(2)}, u32[]{:S(2)}) %collective-permute-start.24) | collective-permute-done | bytes 159776 | tf_op jit(solution)/shard_map/ppermute | solution.py:26
  95.4 2.6 %collective-permute-done.20.refs_1_ = bf16[96,1664]{1,0:T(8,128)(2,1)S(1)} collective-permute-done((bf16[96,1664]{1,0:T(8,128)(2,1)S(1)}, bf16[96,1664]{1,0:T(8,128)(2,1)S(1)}, u32[]{:S(2)}, u32[]{:S(2)}) %collective-permute-start.20) | collective-permute-done | bytes 319520 | tf_op jit(solution)/shard_map/ppermute | solution.py:26
  98.1 4.2 %collective-permute-done.25.refs_1_ = bf16[96,1664]{1,0:T(8,128)(2,1)S(1)} collective-permute-done((bf16[96,1664]{1,0:T(8,128)(2,1)S(1)}, bf16[96,1664]{1,0:T(8,128)(2,1)S(1)}, u32[]{:S(2)}, u32[]{:S(2)}) %collective-permute-start.25) | collective-permute-done | bytes 319520 | tf_op jit(solution)/shard_map/ppermute | solution.py:26
  102.8 2.1 %collective-permute-done.26.refs_1_ = bf16[192,1664]{1,0:T(8,128)(2,1)S(1)} collective-permute-done((bf16[192,1664]{1,0:T(8,128)(2,1)S(1)}, bf16[192,1664]{1,0:T(8,128)(2,1)S(1)}, u32[]{:S(2)}, u32[]{:S(2)}) %collective-permute-start.26) | collective-permute-done | bytes 639008 | tf_op jit(solution)/shard_map/ppermute | solution.py:26
  105.0 0.9 convolution_convert_fusion.6
  105.9 3.3 %collective-permute-start.27 = (bf16[192,1024]{1,0:T(8,128)(2,1)S(1)}, bf16[192,1024]{1,0:T(8,128)(2,1)S(1)}, u32[]{:S(2)}, u32[]{:S(2)}) collective-permute-start(bf16[192,1024]{1,0:T(8,128)(2,1)S(1)} %convolution_convert_fusion.6), channel_id=1, source_target_pairs={{0,12},{1,13},{2,14},{3,15},{4,8},{5,9},{6,10},{7,11},{8,4},{9,5},... | collective-permute-start | bytes 1179656 | tf_op jit(solution)/shard_map/ppermute | solution.py:26
  110.4 0.9 convolution_convert_fusion.5
  111.3 3.7 %collective-permute-done.27 = bf16[192,1024]{1,0:T(8,128)(2,1)S(1)} collective-permute-done((bf16[192,1024]{1,0:T(8,128)(2,1)S(1)}, bf16[192,1024]{1,0:T(8,128)(2,1)S(1)}, u32[]{:S(2)}, u32[]{:S(2)}) %collective-permute-start.27) | collective-permute-done | bytes 393248 | tf_op jit(solution)/shard_map/ppermute | solution.py:26
  115.2 0.9 convolution_convert_fusion.3
  116.1 5.1 %collective-permute-done.28 = bf16[192,1024]{1,0:T(8,128)(2,1)S(1)} collective-permute-done((bf16[192,1024]{1,0:T(8,128)(2,1)S(1)}, bf16[192,1024]{1,0:T(8,128)(2,1)S(1)}, u32[]{:S(2)}, u32[]{:S(2)}) %collective-permute-start.28) | collective-permute-done | bytes 393248 | tf_op jit(solution)/shard_map/ppermute | solution.py:26
  122.4 4.8 %collective-permute-done.32 = bf16[96,1024]{1,0:T(8,128)(2,1)S(1)} collective-permute-done((bf16[96,1024]{1,0:T(8,128)(2,1)S(1)}, bf16[96,1024]{1,0:T(8,128)(2,1)S(1)}, u32[]{:S(2)}, u32[]{:S(2)}) %collective-permute-start.32) | collective-permute-done | bytes 196640 | tf_op jit(solution)/shard_map/ppermute | solution.py:26
  127.3 1.9 %collective-permute-start.33 = (bf16[48,1024]{1,0:T(8,128)(2,1)S(1)}, bf16[48,1024]{1,0:T(8,128)(2,1)S(1)}, u32[]{:S(2)}, u32[]{:S(2)}) collective-permute-start(bf16[48,1024]{1,0:T(8,128)(2,1)S(1)} %get-tuple-element.79), channel_id=1, source_target_pairs={{0,3},{1,2},{2,1},{3,0},{4,7},{5,6},{6,5},{7,4},{8,11},{9,10},{10,... | collective-permute-start | bytes 294920 | tf_op jit(solution)/shard_map/ppermute | solution.py:26
  129.2 1.9 %collective-permute-start.34 = (bf16[48,1024]{1,0:T(8,128)(2,1)S(1)}, bf16[48,1024]{1,0:T(8,128)(2,1)S(1)}, u32[]{:S(2)}, u32[]{:S(2)}) collective-permute-start(bf16[48,1024]{1,0:T(8,128)(2,1)S(1)} %get-tuple-element.80), channel_id=1, source_target_pairs={{0,1},{1,0},{2,3},{3,2},{4,5},{5,4},{6,7},{7,6},{8,9},{9,8},{10,11... | collective-permute-start | bytes 294920 | tf_op jit(solution)/shard_map/ppermute | solution.py:26
  131.2 3.2 %collective-permute-done.33 = bf16[48,1024]{1,0:T(8,128)(2,1)S(1)} collective-permute-done((bf16[48,1024]{1,0:T(8,128)(2,1)S(1)}, bf16[48,1024]{1,0:T(8,128)(2,1)S(1)}, u32[]{:S(2)}, u32[]{:S(2)}) %collective-permute-start.33) | collective-permute-done | bytes 98336 | tf_op jit(solution)/shard_map/ppermute | solution.py:26
  134.4 1.9 %collective-permute-done.34 = bf16[48,1024]{1,0:T(8,128)(2,1)S(1)} collective-permute-done((bf16[48,1024]{1,0:T(8,128)(2,1)S(1)}, bf16[48,1024]{1,0:T(8,128)(2,1)S(1)}, u32[]{:S(2)}, u32[]{:S(2)}) %collective-permute-start.34) | collective-permute-done | bytes 98336 | tf_op jit(solution)/shard_map/ppermute | solution.py:26
  (85 shorter events, 9.2 us)
Async XLA Ops:
  0.0 105.0 %copy-start = (bf16[1664,1024]{1,0:T(8,128)(2,1)S(1)}, bf16[1664,1024]{1,0:T(8,128)(2,1)}, u32[]{:S(2)}) copy-start(bf16[1664,1024]{1,0:T(8,128)(2,1)} %param.7) | copy-start | bytes 10223620
  0.0 5.2 %collective-permute-start = (bf16[48,1024]{1,0:T(8,128)(2,1)}, bf16[48,1024]{1,0:T(8,128)(2,1)S(1)}, u32[]{:S(2)}, u32[]{:S(2)}) collective-permute-start(bf16[48,1024]{1,0:T(8,128)(2,1)} %refs_0_.1), channel_id=1, source_target_pairs={{0,1},{1,0},{2,3},{3,2},{4,5},{5,4},{6,7},{7,6},{8,9},{9,8},{10,11... | collective-permute-start | bytes 294920 | tf_op jit(solution)/shard_map/ppermute | solution.py:26
  1.9 8.9 %collective-permute-start.4 = (bf16[48,1024]{1,0:T(8,128)(2,1)}, bf16[48,1024]{1,0:T(8,128)(2,1)S(1)}, u32[]{:S(2)}, u32[]{:S(2)}) collective-permute-start(bf16[48,1024]{1,0:T(8,128)(2,1)} %refs_0_.1), channel_id=1, source_target_pairs={{0,3},{1,2},{2,1},{3,0},{4,7},{5,6},{6,5},{7,4},{8,11},{9,10},{10,... | collective-permute-start | bytes 294920 | tf_op jit(solution)/shard_map/ppermute | solution.py:26
  4.7 9.5 %collective-permute-start.3 = (bf16[48,1024]{1,0:T(8,128)(2,1)}, bf16[48,1024]{1,0:T(8,128)(2,1)S(1)}, u32[]{:S(2)}, u32[]{:S(2)}) collective-permute-start(bf16[48,1024]{1,0:T(8,128)(2,1)} %refs_0_.1), channel_id=1, source_target_pairs={{0,2},{1,3},{2,0},{3,1},{4,6},{5,7},{6,4},{7,5},{8,10},{9,11},{10,... | collective-permute-start | bytes 294920 | tf_op jit(solution)/shard_map/ppermute | solution.py:26
  5.2 0.9 copy-start.3
  6.1 9.7 %collective-permute-start.1 = (bf16[96,1024]{1,0:T(8,128)(2,1)S(1)}, bf16[96,1024]{1,0:T(8,128)(2,1)S(1)}, u32[]{:S(2)}, u32[]{:S(2)}) collective-permute-start(bf16[96,1024]{1,0:T(8,128)(2,1)S(1)} %join.11.refs_0_), channel_id=1, source_target_pairs={{0,4},{1,5},{2,6},{3,7},{4,0},{5,1},{6,2},{7,3},{8,12},{9,13},{10,... | collective-permute-start | bytes 589832 | tf_op jit(solution)/shard_map/ppermute | solution.py:26
  14.3 6.9 %collective-permute-start.5 = (bf16[96,1024]{1,0:T(8,128)(2,1)S(1)}, bf16[96,1024]{1,0:T(8,128)(2,1)S(1)}, u32[]{:S(2)}, u32[]{:S(2)}) collective-permute-start(bf16[96,1024]{1,0:T(8,128)(2,1)S(1)} %join.13.refs_0_.refs_3_), channel_id=1, source_target_pairs={{0,4},{1,5},{2,6},{3,7},{4,0},{5,1},{6,2},{7,3},{8,12},{9,13},{10,... | collective-permute-start | bytes 589832 | tf_op jit(solution)/shard_map/ppermute | solution.py:26
  15.9 14.5 %collective-permute-start.2 = (bf16[192,1024]{1,0:T(8,128)(2,1)S(1)}, bf16[192,1024]{1,0:T(8,128)(2,1)S(1)}, u32[]{:S(2)}, u32[]{:S(2)}) collective-permute-start(bf16[192,1024]{1,0:T(8,128)(2,1)S(1)} %join.12), channel_id=1, source_target_pairs={{0,12},{1,13},{2,14},{3,15},{4,8},{5,9},{6,10},{7,11},{8,4},{9,5},... | collective-permute-start | bytes 1179656 | tf_op jit(solution)/shard_map/ppermute | solution.py:26
  21.2 9.6 %collective-permute-start.6 = (bf16[192,1024]{1,0:T(8,128)(2,1)S(1)}, bf16[192,1024]{1,0:T(8,128)(2,1)S(1)}, u32[]{:S(2)}, u32[]{:S(2)}) collective-permute-start(bf16[192,1024]{1,0:T(8,128)(2,1)S(1)} %join.14), channel_id=1, source_target_pairs={{0,12},{1,13},{2,14},{3,15},{4,8},{5,9},{6,10},{7,11},{8,4},{9,5},... | collective-permute-start | bytes 1179656 | tf_op jit(solution)/shard_map/ppermute | solution.py:26
  25.0 2.0 %copy-start.1 = (bf16[1024,1664]{1,0:T(8,128)(2,1)S(1)}, bf16[1024,1664]{1,0:T(8,128)(2,1)}, u32[]{:S(2)}) copy-start(bf16[1024,1664]{1,0:T(8,128)(2,1)} %gate_ref) | copy-start | bytes 10223620
  27.0 2.0 %copy-start.2 = (bf16[1024,1664]{1,0:T(8,128)(2,1)S(1)}, bf16[1024,1664]{1,0:T(8,128)(2,1)}, u32[]{:S(2)}) copy-start(bf16[1024,1664]{1,0:T(8,128)(2,1)} %up_ref.1) | copy-start | bytes 10223620
  33.0 2.7 %collective-permute-start.7 = (bf16[128,3328]{1,0:T(8,128)(2,1)S(1)}, bf16[128,3328]{1,0:T(8,128)(2,1)S(1)}, u32[]{:S(2)}, u32[]{:S(2)}) collective-permute-start(bf16[128,3328]{1,0:T(8,128)(2,1)S(1)} %slice.129), channel_id=1, source_target_pairs={{0,16},{1,17},{2,18},{3,19},{4,20},{5,21},{6,22},{7,23},{8,24},{9,... | collective-permute-start | bytes 2555912 | tf_op jit(solution)/shard_map/ppermute | solution.py:26
  35.1 3.9 %collective-permute-start.10 = (bf16[128,3328]{1,0:T(8,128)(2,1)S(1)}, bf16[128,3328]{1,0:T(8,128)(2,1)S(1)}, u32[]{:S(2)}, u32[]{:S(2)}) collective-permute-start(bf16[128,3328]{1,0:T(8,128)(2,1)S(1)} %slice.130), channel_id=1, source_target_pairs={{0,16},{1,17},{2,18},{3,19},{4,20},{5,21},{6,22},{7,23},{8,24},{9,... | collective-permute-start | bytes 2555912 | tf_op jit(solution)/shard_map/ppermute | solution.py:26
  36.0 8.4 %collective-permute-start.8 = (bf16[64,3328]{1,0:T(8,128)(2,1)S(1)}, bf16[64,3328]{1,0:T(8,128)(2,1)S(1)}, u32[]{:S(2)}, u32[]{:S(2)}) collective-permute-start(bf16[64,3328]{1,0:T(8,128)(2,1)S(1)} %slice.132), channel_id=1, source_target_pairs={{0,32},{1,33},{2,34},{3,35},{4,36},{5,37},{6,38},{7,39},{8,40},{9,... | collective-permute-start | bytes 1277960 | tf_op jit(solution)/shard_map/ppermute | solution.py:26
  39.0 2.5 %collective-permute-start.9 = (bf16[128,3328]{1,0:T(8,128)(2,1)S(1)}, bf16[128,3328]{1,0:T(8,128)(2,1)S(1)}, u32[]{:S(2)}, u32[]{:S(2)}) collective-permute-start(bf16[128,3328]{1,0:T(8,128)(2,1)S(1)} %slice.134), channel_id=1, source_target_pairs={{0,16},{1,17},{2,18},{3,19},{4,20},{5,21},{6,22},{7,23},{8,24},{9,... | collective-permute-start | bytes 2555912 | tf_op jit(solution)/shard_map/ppermute | solution.py:26
  39.3 11.2 %collective-permute-start.12 = (bf16[64,3328]{1,0:T(8,128)(2,1)S(1)}, bf16[64,3328]{1,0:T(8,128)(2,1)S(1)}, u32[]{:S(2)}, u32[]{:S(2)}) collective-permute-start(bf16[64,3328]{1,0:T(8,128)(2,1)S(1)} %slice.136), channel_id=1, source_target_pairs={{0,32},{1,33},{2,34},{3,35},{4,36},{5,37},{6,38},{7,39},{8,40},{9,... | collective-permute-start | bytes 1277960 | tf_op jit(solution)/shard_map/ppermute | solution.py:26
  41.7 17.9 %collective-permute-start.15 = (bf16[64,3328]{1,0:T(8,128)(2,1)S(1)}, bf16[64,3328]{1,0:T(8,128)(2,1)S(1)}, u32[]{:S(2)}, u32[]{:S(2)}) collective-permute-start(bf16[64,3328]{1,0:T(8,128)(2,1)S(1)} %slice.137), channel_id=1, source_target_pairs={{0,32},{1,33},{2,34},{3,35},{4,36},{5,37},{6,38},{7,39},{8,40},{9,... | collective-permute-start | bytes 1277960 | tf_op jit(solution)/shard_map/ppermute | solution.py:26
  44.5 9.5 %collective-permute-start.11 = (bf16[32,3328]{1,0:T(8,128)(2,1)S(1)}, bf16[32,3328]{1,0:T(8,128)(2,1)S(1)}, u32[]{:S(2)}, u32[]{:S(2)}) collective-permute-start(bf16[32,3328]{1,0:T(8,128)(2,1)S(1)} %slice.139), channel_id=1, source_target_pairs={{0,96},{1,97},{2,98},{3,99},{4,100},{5,101},{6,102},{7,103},{8,104... | collective-permute-start | bytes 638984 | tf_op jit(solution)/shard_map/ppermute | solution.py:26
  50.7 9.4 %collective-permute-start.14 = (bf16[32,3328]{1,0:T(8,128)(2,1)S(1)}, bf16[32,3328]{1,0:T(8,128)(2,1)S(1)}, u32[]{:S(2)}, u32[]{:S(2)}) collective-permute-start(bf16[32,3328]{1,0:T(8,128)(2,1)S(1)} %slice.141), channel_id=1, source_target_pairs={{0,96},{1,97},{2,98},{3,99},{4,100},{5,101},{6,102},{7,103},{8,104... | collective-permute-start | bytes 638984 | tf_op jit(solution)/shard_map/ppermute | solution.py:26
  54.1 10.7 %collective-permute-start.13 = (bf16[16,3328]{1,0:T(8,128)(2,1)S(1)}, bf16[16,3328]{1,0:T(8,128)(2,1)S(1)}, u32[]{:S(2)}, u32[]{:S(2)}) collective-permute-start(bf16[16,3328]{1,0:T(8,128)(2,1)S(1)} %get-tuple-element.75), channel_id=1, source_target_pairs={{0,128},{1,129},{2,130},{3,131},{4,132},{5,133},{6,134},{7,135},{8... | collective-permute-start | bytes 319496 | tf_op jit(solution)/shard_map/ppermute | solution.py:26
  59.8 7.1 %collective-permute-start.17 = (bf16[32,3328]{1,0:T(8,128)(2,1)S(1)}, bf16[32,3328]{1,0:T(8,128)(2,1)S(1)}, u32[]{:S(2)}, u32[]{:S(2)}) collective-permute-start(bf16[32,3328]{1,0:T(8,128)(2,1)S(1)} %slice.146), channel_id=1, source_target_pairs={{0,96},{1,97},{2,98},{3,99},{4,100},{5,101},{6,102},{7,103},{8,104... | collective-permute-start | bytes 638984 | tf_op jit(solution)/shard_map/ppermute | solution.py:26
  60.2 10.8 %collective-permute-start.16 = (bf16[16,3328]{1,0:T(8,128)(2,1)S(1)}, bf16[16,3328]{1,0:T(8,128)(2,1)S(1)}, u32[]{:S(2)}, u32[]{:S(2)}) collective-permute-start(bf16[16,3328]{1,0:T(8,128)(2,1)S(1)} %get-tuple-element.74), channel_id=1, source_target_pairs={{0,128},{1,129},{2,130},{3,131},{4,132},{5,133},{6,134},{7,135},{8... | collective-permute-start | bytes 319496 | tf_op jit(solution)/shard_map/ppermute | solution.py:26
  67.0 11.7 %collective-permute-start.18 = (bf16[16,3328]{1,0:T(8,128)(2,1)S(1)}, bf16[16,3328]{1,0:T(8,128)(2,1)S(1)}, u32[]{:S(2)}, u32[]{:S(2)}) collective-permute-start(bf16[16,3328]{1,0:T(8,128)(2,1)S(1)} %get-tuple-element.72), channel_id=1, source_target_pairs={{0,128},{1,129},{2,130},{3,131},{4,132},{5,133},{6,134},{7,135},{8... | collective-permute-start | bytes 319496 | tf_op jit(solution)/shard_map/ppermute | solution.py:26
  71.1 12.2 %collective-permute-start.22 = (bf16[32,1664]{1,0:T(8,128)(2,1)S(1)}, bf16[32,1664]{1,0:T(8,128)(2,1)S(1)}, u32[]{:S(2)}, u32[]{:S(2)}) collective-permute-start(bf16[32,1664]{1,0:T(8,128)(2,1)S(1)} %join.15.refs_0_), channel_id=1, source_target_pairs={{0,128},{1,129},{2,130},{3,131},{4,132},{5,133},{6,134},{7,135},{8... | collective-permute-start | bytes 319496 | tf_op jit(solution)/shard_map/ppermute | solution.py:26
  78.8 8.1 %collective-permute-start.23 = (bf16[16,1664]{1,0:T(8,128)(2,1)S(1)}, bf16[16,1664]{1,0:T(8,128)(2,1)S(1)}, u32[]{:S(2)}, u32[]{:S(2)}) collective-permute-start(bf16[16,1664]{1,0:T(8,128)(2,1)S(1)} %silu.5.refs_1_), channel_id=1, source_target_pairs={{0,128},{1,129},{2,130},{3,131},{4,132},{5,133},{6,134},{7,135},{8... | collective-permute-start | bytes 159752 | tf_op jit(solution)/shard_map/ppermute | solution.py:26
  83.1 7.7 %collective-permute-start.19 = (bf16[48,1664]{1,0:T(8,128)(2,1)S(1)}, bf16[48,1664]{1,0:T(8,128)(2,1)S(1)}, u32[]{:S(2)}, u32[]{:S(2)}) collective-permute-start(bf16[48,1664]{1,0:T(8,128)(2,1)S(1)} %join.16.refs_0_), channel_id=1, source_target_pairs={{0,96},{1,97},{2,98},{3,99},{4,100},{5,101},{6,102},{7,103},{8,104... | collective-permute-start | bytes 479240 | tf_op jit(solution)/shard_map/ppermute | solution.py:26
  86.9 8.3 %collective-permute-start.24 = (bf16[48,1664]{1,0:T(8,128)(2,1)S(1)}, bf16[48,1664]{1,0:T(8,128)(2,1)S(1)}, u32[]{:S(2)}, u32[]{:S(2)}) collective-permute-start(bf16[48,1664]{1,0:T(8,128)(2,1)S(1)} %join.19.refs_0_), channel_id=1, source_target_pairs={{0,96},{1,97},{2,98},{3,99},{4,100},{5,101},{6,102},{7,103},{8,104... | collective-permute-start | bytes 479240 | tf_op jit(solution)/shard_map/ppermute | solution.py:26
  90.9 7.1 %collective-permute-start.20 = (bf16[96,1664]{1,0:T(8,128)(2,1)S(1)}, bf16[96,1664]{1,0:T(8,128)(2,1)S(1)}, u32[]{:S(2)}, u32[]{:S(2)}) collective-permute-start(bf16[96,1664]{1,0:T(8,128)(2,1)S(1)} %join.17.refs_0_), channel_id=1, source_target_pairs={{0,32},{1,33},{2,34},{3,35},{4,36},{5,37},{6,38},{7,39},{8,40},{9,... | collective-permute-start | bytes 958472 | tf_op jit(solution)/shard_map/ppermute | solution.py:26
  95.3 7.1 %collective-permute-start.25 = (bf16[96,1664]{1,0:T(8,128)(2,1)S(1)}, bf16[96,1664]{1,0:T(8,128)(2,1)S(1)}, u32[]{:S(2)}, u32[]{:S(2)}) collective-permute-start(bf16[96,1664]{1,0:T(8,128)(2,1)S(1)} %join.20.refs_0_), channel_id=1, source_target_pairs={{0,32},{1,33},{2,34},{3,35},{4,36},{5,37},{6,38},{7,39},{8,40},{9,... | collective-permute-start | bytes 958472 | tf_op jit(solution)/shard_map/ppermute | solution.py:26
  98.0 4.7 %collective-permute-start.21 = (bf16[192,1664]{1,0:T(8,128)(2,1)S(1)}, bf16[192,1664]{1,0:T(8,128)(2,1)S(1)}, u32[]{:S(2)}, u32[]{:S(2)}) collective-permute-start(bf16[192,1664]{1,0:T(8,128)(2,1)S(1)} %join.18.refs_0_), channel_id=1, source_target_pairs={{0,16},{1,17},{2,18},{3,19},{4,20},{5,21},{6,22},{7,23},{8,24},{9,... | collective-permute-start | bytes 1916936 | tf_op jit(solution)/shard_map/ppermute | solution.py:26
  102.4 2.4 %collective-permute-start.26 = (bf16[192,1664]{1,0:T(8,128)(2,1)S(1)}, bf16[192,1664]{1,0:T(8,128)(2,1)S(1)}, u32[]{:S(2)}, u32[]{:S(2)}) collective-permute-start(bf16[192,1664]{1,0:T(8,128)(2,1)S(1)} %join.21.refs_0_), channel_id=1, source_target_pairs={{0,16},{1,17},{2,18},{3,19},{4,20},{5,21},{6,22},{7,23},{8,24},{9,... | collective-permute-start | bytes 1916936 | tf_op jit(solution)/shard_map/ppermute | solution.py:26
  105.9 9.1 %collective-permute-start.27 = (bf16[192,1024]{1,0:T(8,128)(2,1)S(1)}, bf16[192,1024]{1,0:T(8,128)(2,1)S(1)}, u32[]{:S(2)}, u32[]{:S(2)}) collective-permute-start(bf16[192,1024]{1,0:T(8,128)(2,1)S(1)} %convolution_convert_fusion.6), channel_id=1, source_target_pairs={{0,12},{1,13},{2,14},{3,15},{4,8},{5,9},{6,10},{7,11},{8,4},{9,5},... | collective-permute-start | bytes 1179656 | tf_op jit(solution)/shard_map/ppermute | solution.py:26
  110.3 11.0 %collective-permute-start.28 = (bf16[192,1024]{1,0:T(8,128)(2,1)S(1)}, bf16[192,1024]{1,0:T(8,128)(2,1)S(1)}, u32[]{:S(2)}, u32[]{:S(2)}) collective-permute-start(bf16[192,1024]{1,0:T(8,128)(2,1)S(1)} %convolution_convert_fusion.4), channel_id=1, source_target_pairs={{0,12},{1,13},{2,14},{3,15},{4,8},{5,9},{6,10},{7,11},{8,4},{9,5},... | collective-permute-start | bytes 1179656 | tf_op jit(solution)/shard_map/ppermute | solution.py:26
  115.1 6.1 %collective-permute-start.29 = (bf16[96,1024]{1,0:T(8,128)(2,1)S(1)}, bf16[96,1024]{1,0:T(8,128)(2,1)S(1)}, u32[]{:S(2)}, u32[]{:S(2)}) collective-permute-start(bf16[96,1024]{1,0:T(8,128)(2,1)S(1)} %slice.153), channel_id=1, source_target_pairs={{0,4},{1,5},{2,6},{3,7},{4,0},{5,1},{6,2},{7,3},{8,12},{9,13},{10,... | collective-permute-start | bytes 589832 | tf_op jit(solution)/shard_map/ppermute | solution.py:26
  121.5 5.8 %collective-permute-start.32 = (bf16[96,1024]{1,0:T(8,128)(2,1)S(1)}, bf16[96,1024]{1,0:T(8,128)(2,1)S(1)}, u32[]{:S(2)}, u32[]{:S(2)}) collective-permute-start(bf16[96,1024]{1,0:T(8,128)(2,1)S(1)} %slice.154), channel_id=1, source_target_pairs={{0,4},{1,5},{2,6},{3,7},{4,0},{5,1},{6,2},{7,3},{8,12},{9,13},{10,... | collective-permute-start | bytes 589832 | tf_op jit(solution)/shard_map/ppermute | solution.py:26
  121.6 9.5 %collective-permute-start.30 = (bf16[48,1024]{1,0:T(8,128)(2,1)S(1)}, bf16[48,1024]{1,0:T(8,128)(2,1)S(1)}, u32[]{:S(2)}, u32[]{:S(2)}) collective-permute-start(bf16[48,1024]{1,0:T(8,128)(2,1)S(1)} %get-tuple-element.77), channel_id=1, source_target_pairs={{0,2},{1,3},{2,0},{3,1},{4,6},{5,7},{6,4},{7,5},{8,10},{9,11},{10,... | collective-permute-start | bytes 294920 | tf_op jit(solution)/shard_map/ppermute | solution.py:26
  121.7 9.4 %collective-permute-start.31 = (bf16[48,1024]{1,0:T(8,128)(2,1)S(1)}, bf16[48,1024]{1,0:T(8,128)(2,1)S(1)}, u32[]{:S(2)}, u32[]{:S(2)}) collective-permute-start(bf16[48,1024]{1,0:T(8,128)(2,1)S(1)} %get-tuple-element.78), channel_id=1, source_target_pairs={{0,0},{1,1},{2,2},{3,3},{4,4},{5,5},{6,6},{7,7},{8,8},{9,9},{10,10... | collective-permute-start | bytes 294920 | tf_op jit(solution)/shard_map/ppermute | solution.py:26
  127.3 7.1 %collective-permute-start.33 = (bf16[48,1024]{1,0:T(8,128)(2,1)S(1)}, bf16[48,1024]{1,0:T(8,128)(2,1)S(1)}, u32[]{:S(2)}, u32[]{:S(2)}) collective-permute-start(bf16[48,1024]{1,0:T(8,128)(2,1)S(1)} %get-tuple-element.79), channel_id=1, source_target_pairs={{0,3},{1,2},{2,1},{3,0},{4,7},{5,6},{6,5},{7,4},{8,11},{9,10},{10,... | collective-permute-start | bytes 294920 | tf_op jit(solution)/shard_map/ppermute | solution.py:26
  129.2 7.1 %collective-permute-start.34 = (bf16[48,1024]{1,0:T(8,128)(2,1)S(1)}, bf16[48,1024]{1,0:T(8,128)(2,1)S(1)}, u32[]{:S(2)}, u32[]{:S(2)}) collective-permute-start(bf16[48,1024]{1,0:T(8,128)(2,1)S(1)} %get-tuple-element.80), channel_id=1, source_target_pairs={{0,1},{1,0},{2,3},{3,2},{4,5},{5,4},{6,7},{7,6},{8,9},{9,8},{10,11... | collective-permute-start | bytes 294920 | tf_op jit(solution)/shard_map/ppermute | solution.py:26

commit v10 on v7

--- a/solution.py
+++ b/solution.py
@@ -233,7 +233,7 @@
 
 
 def scatter_out(hidden, weight, rows):
-    parts, stays, got = (slice(0, 512), slice(512, None)), [None, None], [None, None]
+    parts, stays, got = (slice(0, 640), slice(640, None)), [None, None], [None, None]
     turn = weight
     for c, part in enumerate(parts):
         first_rows, _ = tie(hidden[1], turn)

time: 137 us -> 137 us (level)
  transfers between devices with their start and end apart: 37 -> 37, of which waited for: 22 -> 23; matrix products, arithmetic and copies ran while one was open for 6% -> 6% of each run, Pallas kernels for 1% -> 1%
where the time goes in v10:
time: 137 us; the launch traced here: 135 us
  waiting for transfers between devices  60.2 us (44%)
  starting transfers between devices  54.7 us (40%)
  matrix products  9.93 us (7%)
  local copies, waits for them, and re-layouts  5.28 us (4%)
  Pallas kernels  2.46 us (2%)
  other arithmetic  2.07 us (2%)
    ppermute x37, waiting for transfers between devices, exchange(): return lax.ppermute(value, ('gx', 'gy'), pairs)  60.2 us
    ppermute x37, starting transfers between devices, exchange(): return lax.ppermute(value, ('gx', 'gy'), pairs)  54.7 us
    dot_general x7, matrix products, dot(): return jnp.dot(a, b, preferred_element_type=F32).astype(BF)  9.93 us
    unnamed x8, local copies, waits for them, and re-layouts  4.86 us
  transfers between devices with their start and end apart: 37, of which 23 were waited for; matrix products, arithmetic and copies ran while one was open for 6% of the time, Pallas kernels for 1%

profile of v10, /device:TPU:24, one launch (start us, length us, event | category | flops | bytes accessed | tf_op | source)
XLA Modules:
  0.0 135.1 jit_solution(15553983028391676389)
XLA Ops:
  0.0 1.9 %collective-permute-start = (bf16[48,1024]{1,0:T(8,128)(2,1)}, bf16[48,1024]{1,0:T(8,128)(2,1)S(1)}, u32[]{:S(2)}, u32[]{:S(2)}) collective-permute-start(bf16[48,1024]{1,0:T(8,128)(2,1)} %refs_0_.1), channel_id=1, source_target_pairs={{0,1},{1,0},{2,3},{3,2},{4,5},{5,4},{6,7},{7,6},{8,9},{9,8},{10,11... | collective-permute-start | bytes 294920 | tf_op jit(solution)/shard_map/ppermute | solution.py:26
  1.9 2.8 %collective-permute-start.4 = (bf16[48,1024]{1,0:T(8,128)(2,1)}, bf16[48,1024]{1,0:T(8,128)(2,1)S(1)}, u32[]{:S(2)}, u32[]{:S(2)}) collective-permute-start(bf16[48,1024]{1,0:T(8,128)(2,1)} %refs_0_.1), channel_id=1, source_target_pairs={{0,3},{1,2},{2,1},{3,0},{4,7},{5,6},{6,5},{7,4},{8,11},{9,10},{10,... | collective-permute-start | bytes 294920 | tf_op jit(solution)/shard_map/ppermute | solution.py:26
  5.2 0.9 copy-done.2
  6.1 1.6 %collective-permute-start.1 = (bf16[96,1024]{1,0:T(8,128)(2,1)S(1)}, bf16[96,1024]{1,0:T(8,128)(2,1)S(1)}, u32[]{:S(2)}, u32[]{:S(2)}) collective-permute-start(bf16[96,1024]{1,0:T(8,128)(2,1)S(1)} %join.11.refs_0_), channel_id=1, source_target_pairs={{0,4},{1,5},{2,6},{3,7},{4,0},{5,1},{6,2},{7,3},{8,12},{9,13},{10,... | collective-permute-start | bytes 589832 | tf_op jit(solution)/shard_map/ppermute | solution.py:26
  7.7 3.1 %collective-permute-done.4.refs_1_ = bf16[48,1024]{1,0:T(8,128)(2,1)S(1)} collective-permute-done((bf16[48,1024]{1,0:T(8,128)(2,1)}, bf16[48,1024]{1,0:T(8,128)(2,1)S(1)}, u32[]{:S(2)}, u32[]{:S(2)}) %collective-permute-start.4) | collective-permute-done | bytes 98336 | tf_op jit(solution)/shard_map/ppermute | solution.py:26
  10.8 3.5 %collective-permute-done.3.refs_0_ = bf16[48,1024]{1,0:T(8,128)(2,1)S(1)} collective-permute-done((bf16[48,1024]{1,0:T(8,128)(2,1)}, bf16[48,1024]{1,0:T(8,128)(2,1)S(1)}, u32[]{:S(2)}, u32[]{:S(2)}) %collective-permute-start.3) | collective-permute-done | bytes 98336 | tf_op jit(solution)/shard_map/ppermute | solution.py:26
  14.3 1.6 %collective-permute-start.5 = (bf16[96,1024]{1,0:T(8,128)(2,1)S(1)}, bf16[96,1024]{1,0:T(8,128)(2,1)S(1)}, u32[]{:S(2)}, u32[]{:S(2)}) collective-permute-start(bf16[96,1024]{1,0:T(8,128)(2,1)S(1)} %join.13.refs_0_.refs_3_), channel_id=1, source_target_pairs={{0,4},{1,5},{2,6},{3,7},{4,0},{5,1},{6,2},{7,3},{8,12},{9,13},{10,... | collective-permute-start | bytes 589832 | tf_op jit(solution)/shard_map/ppermute | solution.py:26
  15.9 2.2 %collective-permute-start.2 = (bf16[192,1024]{1,0:T(8,128)(2,1)S(1)}, bf16[192,1024]{1,0:T(8,128)(2,1)S(1)}, u32[]{:S(2)}, u32[]{:S(2)}) collective-permute-start(bf16[192,1024]{1,0:T(8,128)(2,1)S(1)} %join.12), channel_id=1, source_target_pairs={{0,12},{1,13},{2,14},{3,15},{4,8},{5,9},{6,10},{7,11},{8,4},{9,5},... | collective-permute-start | bytes 1179656 | tf_op jit(solution)/shard_map/ppermute | solution.py:26
  18.1 3.1 %collective-permute-done.5.refs_1_.refs_4_ = bf16[96,1024]{1,0:T(8,128)(2,1)S(1)} collective-permute-done((bf16[96,1024]{1,0:T(8,128)(2,1)S(1)}, bf16[96,1024]{1,0:T(8,128)(2,1)S(1)}, u32[]{:S(2)}, u32[]{:S(2)}) %collective-permute-start.5) | collective-permute-done | bytes 196640 | tf_op jit(solution)/shard_map/ppermute | solution.py:26
  21.2 3.9 %collective-permute-start.6 = (bf16[192,1024]{1,0:T(8,128)(2,1)S(1)}, bf16[192,1024]{1,0:T(8,128)(2,1)S(1)}, u32[]{:S(2)}, u32[]{:S(2)}) collective-permute-start(bf16[192,1024]{1,0:T(8,128)(2,1)S(1)} %join.14), channel_id=1, source_target_pairs={{0,12},{1,13},{2,14},{3,15},{4,8},{5,9},{6,10},{7,11},{8,4},{9,5},... | collective-permute-start | bytes 1179656 | tf_op jit(solution)/shard_map/ppermute | solution.py:26
  25.0 2.0 %copy-done = bf16[1024,1664]{1,0:T(8,128)(2,1)S(1)} copy-done((bf16[1024,1664]{1,0:T(8,128)(2,1)S(1)}, bf16[1024,1664]{1,0:T(8,128)(2,1)}, u32[]{:S(2)}) %copy-start) | copy-done | bytes 3407896
  27.0 2.0 %copy-done.1 = bf16[1024,1664]{1,0:T(8,128)(2,1)S(1)} copy-done((bf16[1024,1664]{1,0:T(8,128)(2,1)S(1)}, bf16[1024,1664]{1,0:T(8,128)(2,1)}, u32[]{:S(2)}) %copy-start.1) | copy-done | bytes 3407896
  29.0 1.5 %pack.1 = bf16[1024,3328]{1,0:T(8,128)(2,1)S(1)} custom-call(bf16[1024,1664]{1,0:T(8,128)(2,1)S(1)} %copy-done, bf16[1024,1664]{1,0:T(8,128)(2,1)S(1)} %copy-done.1), custom_call_target="tpu_custom_call" | custom-call | bytes 13631488 | tf_op jit(solution)/shard_map/pack/pallas_call | solution.py:94
  31.0 1.9 %convolution_convert_fusion.2 = bf16[256,3328]{1,0:T(8,128)(2,1)S(1)} fusion(bf16[256,1024]{1,0:T(8,128)(2,1)S(1)} %get-tuple-element.32, bf16[1024,3328]{1,0:T(8,128)(2,1)S(1)} %pack.1), kind=kOutput, calls=%fused_computation.2 | convolution fusion | flops 1745682432 | bytes 9043968 | tf_op jit(solution)/shard_map/dot_general | solution.py:174
  33.1 1.9 %convolution_convert_fusion.1 = bf16[256,3328]{1,0:T(8,128)(2,1)S(1)} fusion(bf16[256,1024]{1,0:T(8,128)(2,1)S(1)} %get-tuple-element.35, bf16[1024,3328]{1,0:T(8,128)(2,1)S(1)} %pack.1), kind=kOutput, calls=%fused_computation.1 | convolution fusion | flops 1745682432 | bytes 9043968 | tf_op jit(solution)/shard_map/dot_general | solution.py:174
  36.0 1.0 collective-permute-start.8
  37.0 1.9 %convolution_convert_fusion = bf16[256,3328]{1,0:T(8,128)(2,1)S(1)} fusion(bf16[256,1024]{1,0:T(8,128)(2,1)S(1)} %get-tuple-element.38, bf16[1024,3328]{1,0:T(8,128)(2,1)S(1)} %pack.1), kind=kOutput, calls=%fused_computation | convolution fusion | flops 1745682432 | bytes 9043968 | tf_op jit(solution)/shard_map/dot_general | solution.py:174
  39.3 1.4 %collective-permute-start.12 = (bf16[64,3328]{1,0:T(8,128)(2,1)S(1)}, bf16[64,3328]{1,0:T(8,128)(2,1)S(1)}, u32[]{:S(2)}, u32[]{:S(2)}) collective-permute-start(bf16[64,3328]{1,0:T(8,128)(2,1)S(1)} %slice.162), channel_id=1, source_target_pairs={{0,32},{1,33},{2,34},{3,35},{4,36},{5,37},{6,38},{7,39},{8,40},{9,... | collective-permute-start | bytes 1277960 | tf_op jit(solution)/shard_map/ppermute | solution.py:26
  41.7 1.4 %collective-permute-start.15 = (bf16[64,3328]{1,0:T(8,128)(2,1)S(1)}, bf16[64,3328]{1,0:T(8,128)(2,1)S(1)}, u32[]{:S(2)}, u32[]{:S(2)}) collective-permute-start(bf16[64,3328]{1,0:T(8,128)(2,1)S(1)} %slice.163), channel_id=1, source_target_pairs={{0,32},{1,33},{2,34},{3,35},{4,36},{5,37},{6,38},{7,39},{8,40},{9,... | collective-permute-start | bytes 1277960 | tf_op jit(solution)/shard_map/ppermute | solution.py:26
  43.1 1.3 collective-permute-done.8
  44.8 5.7 %collective-permute-done.12 = bf16[64,3328]{1,0:T(8,128)(2,1)S(1)} collective-permute-done((bf16[64,3328]{1,0:T(8,128)(2,1)S(1)}, bf16[64,3328]{1,0:T(8,128)(2,1)S(1)}, u32[]{:S(2)}, u32[]{:S(2)}) %collective-permute-start.12) | collective-permute-done | bytes 426016 | tf_op jit(solution)/shard_map/ppermute | solution.py:26
  50.7 1.3 collective-permute-start.14
  52.0 2.0 %collective-permute-done.11 = bf16[32,3328]{1,0:T(8,128)(2,1)S(1)} collective-permute-done((bf16[32,3328]{1,0:T(8,128)(2,1)S(1)}, bf16[32,3328]{1,0:T(8,128)(2,1)S(1)}, u32[]{:S(2)}, u32[]{:S(2)}) %collective-permute-start.11) | collective-permute-done | bytes 213024 | tf_op jit(solution)/shard_map/ppermute | solution.py:26
  54.1 5.6 %collective-permute-start.13 = (bf16[16,3328]{1,0:T(8,128)(2,1)S(1)}, bf16[16,3328]{1,0:T(8,128)(2,1)S(1)}, u32[]{:S(2)}, u32[]{:S(2)}) collective-permute-start(bf16[16,3328]{1,0:T(8,128)(2,1)S(1)} %get-tuple-element.66), channel_id=1, source_target_pairs={{0,128},{1,129},{2,130},{3,131},{4,132},{5,133},{6,134},{7,135},{8... | collective-permute-start | bytes 319496 | tf_op jit(solution)/shard_map/ppermute | solution.py:26
  60.2 4.6 %collective-permute-start.16 = (bf16[16,3328]{1,0:T(8,128)(2,1)S(1)}, bf16[16,3328]{1,0:T(8,128)(2,1)S(1)}, u32[]{:S(2)}, u32[]{:S(2)}) collective-permute-start(bf16[16,3328]{1,0:T(8,128)(2,1)S(1)} %get-tuple-element.65), channel_id=1, source_target_pairs={{0,128},{1,129},{2,130},{3,131},{4,132},{5,133},{6,134},{7,135},{8... | collective-permute-start | bytes 319496 | tf_op jit(solution)/shard_map/ppermute | solution.py:26
  64.9 2.1 %collective-permute-done.17 = bf16[32,3328]{1,0:T(8,128)(2,1)S(1)} collective-permute-done((bf16[32,3328]{1,0:T(8,128)(2,1)S(1)}, bf16[32,3328]{1,0:T(8,128)(2,1)S(1)}, u32[]{:S(2)}, u32[]{:S(2)}) %collective-permute-start.17) | collective-permute-done | bytes 213024 | tf_op jit(solution)/shard_map/ppermute | solution.py:26
  67.0 4.0 %collective-permute-start.18 = (bf16[16,3328]{1,0:T(8,128)(2,1)S(1)}, bf16[16,3328]{1,0:T(8,128)(2,1)S(1)}, u32[]{:S(2)}, u32[]{:S(2)}) collective-permute-start(bf16[16,3328]{1,0:T(8,128)(2,1)S(1)} %get-tuple-element.63), channel_id=1, source_target_pairs={{0,128},{1,129},{2,130},{3,131},{4,132},{5,133},{6,134},{7,135},{8... | collective-permute-start | bytes 319496 | tf_op jit(solution)/shard_map/ppermute | solution.py:26
  71.1 2.9 %collective-permute-start.21 = (bf16[32,1664]{1,0:T(8,128)(2,1)S(1)}, bf16[32,1664]{1,0:T(8,128)(2,1)S(1)}, u32[]{:S(2)}, u32[]{:S(2)}) collective-permute-start(bf16[32,1664]{1,0:T(8,128)(2,1)S(1)} %join.15.refs_0_), channel_id=1, source_target_pairs={{0,128},{1,129},{2,130},{3,131},{4,132},{5,133},{6,134},{7,135},{8... | collective-permute-start | bytes 319496 | tf_op jit(solution)/shard_map/ppermute | solution.py:26
  73.9 4.7 %collective-permute-done.18.b_ref = bf16[16,3328]{1,0:T(8,128)(2,1)S(1)} collective-permute-done((bf16[16,3328]{1,0:T(8,128)(2,1)S(1)}, bf16[16,3328]{1,0:T(8,128)(2,1)S(1)}, u32[]{:S(2)}, u32[]{:S(2)}) %collective-permute-start.18) | collective-permute-done | bytes 106528 | tf_op jit(solution)/shard_map/ppermute | solution.py:26
  78.7 2.6 %collective-permute-start.22 = (bf16[16,1664]{1,0:T(8,128)(2,1)S(1)}, bf16[16,1664]{1,0:T(8,128)(2,1)S(1)}, u32[]{:S(2)}, u32[]{:S(2)}) collective-permute-start(bf16[16,1664]{1,0:T(8,128)(2,1)S(1)} %silu.5.refs_1_), channel_id=1, source_target_pairs={{0,128},{1,129},{2,130},{3,131},{4,132},{5,133},{6,134},{7,135},{8... | collective-permute-start | bytes 159752 | tf_op jit(solution)/shard_map/ppermute | solution.py:26
  82.1 4.7 %collective-permute-done.22.refs_1_ = bf16[16,1664]{1,0:T(8,128)(2,1)S(1)} collective-permute-done((bf16[16,1664]{1,0:T(8,128)(2,1)S(1)}, bf16[16,1664]{1,0:T(8,128)(2,1)S(1)}, u32[]{:S(2)}, u32[]{:S(2)}) %collective-permute-start.22) | collective-permute-done | bytes 53280 | tf_op jit(solution)/shard_map/ppermute | solution.py:26
  86.9 1.2 collective-permute-start.23
  88.1 1.6 %collective-permute-done.19.refs_1_ = bf16[48,1664]{1,0:T(8,128)(2,1)S(1)} collective-permute-done((bf16[48,1664]{1,0:T(8,128)(2,1)S(1)}, bf16[48,1664]{1,0:T(8,128)(2,1)S(1)}, u32[]{:S(2)}, u32[]{:S(2)}) %collective-permute-start.19) | collective-permute-done | bytes 159776 | tf_op jit(solution)/shard_map/ppermute | solution.py:26
  89.8 5.4 %collective-permute-done.23.refs_1_ = bf16[48,1664]{1,0:T(8,128)(2,1)S(1)} collective-permute-done((bf16[48,1664]{1,0:T(8,128)(2,1)S(1)}, bf16[48,1664]{1,0:T(8,128)(2,1)S(1)}, u32[]{:S(2)}, u32[]{:S(2)}) %collective-permute-start.23) | collective-permute-done | bytes 159776 | tf_op jit(solution)/shard_map/ppermute | solution.py:26
  95.3 1.4 %collective-permute-done.20.refs_1_ = bf16[96,1664]{1,0:T(8,128)(2,1)S(1)} collective-permute-done((bf16[96,1664]{1,0:T(8,128)(2,1)S(1)}, bf16[96,1664]{1,0:T(8,128)(2,1)S(1)}, u32[]{:S(2)}, u32[]{:S(2)}) %collective-permute-start.20) | collective-permute-done | bytes 319520 | tf_op jit(solution)/shard_map/ppermute | solution.py:26
  96.9 5.4 %collective-permute-done.24.refs_1_ = bf16[96,1664]{1,0:T(8,128)(2,1)S(1)} collective-permute-done((bf16[96,1664]{1,0:T(8,128)(2,1)S(1)}, bf16[96,1664]{1,0:T(8,128)(2,1)S(1)}, u32[]{:S(2)}, u32[]{:S(2)}) %collective-permute-start.24) | collective-permute-done | bytes 319520 | tf_op jit(solution)/shard_map/ppermute | solution.py:26
  102.7 2.1 %collective-permute-done.26.refs_3_ = bf16[192,1664]{1,0:T(8,128)(2,1)S(1)} collective-permute-done((bf16[192,1664]{1,0:T(8,128)(2,1)S(1)}, bf16[192,1664]{1,0:T(8,128)(2,1)S(1)}, u32[]{:S(2)}, u32[]{:S(2)}) %collective-permute-start.26) | collective-permute-done | bytes 639008 | tf_op jit(solution)/shard_map/ppermute | solution.py:26
  105.1 1.2 fusion.4
  106.4 3.3 %collective-permute-start.27 = (bf16[384,640]{1,0:T(8,128)(2,1)S(1)}, bf16[384,640]{1,0:T(8,128)(2,1)S(1)}, u32[]{:S(2)}, u32[]{:S(2)}) collective-permute-start(bf16[384,640]{1,0:T(8,128)(2,1)S(1)} %fusion.4), channel_id=1, source_target_pairs={{0,12},{1,13},{2,14},{3,15},{4,8},{5,9},{6,10},{7,11},{8,4},{9,5},... | collective-permute-start | bytes 1474568 | tf_op jit(solution)/shard_map/ppermute | solution.py:26
  110.6 1.2 fusion.7
  112.7 3.8 %collective-permute-done.27 = bf16[384,640]{1,0:T(8,128)(2,1)S(1)} collective-permute-done((bf16[384,640]{1,0:T(8,128)(2,1)S(1)}, bf16[384,640]{1,0:T(8,128)(2,1)S(1)}, u32[]{:S(2)}, u32[]{:S(2)}) %collective-permute-start.27) | collective-permute-done | bytes 491552 | tf_op jit(solution)/shard_map/ppermute | solution.py:26
  116.7 3.6 %collective-permute-done.29 = bf16[384,384]{1,0:T(8,128)(2,1)S(1)} collective-permute-done((bf16[384,384]{1,0:T(8,128)(2,1)S(1)}, bf16[384,384]{1,0:T(8,128)(2,1)S(1)}, u32[]{:S(2)}, u32[]{:S(2)}) %collective-permute-start.29) | collective-permute-done | bytes 294944 | tf_op jit(solution)/shard_map/ppermute | solution.py:26
  120.5 2.4 %collective-permute-done.28 = bf16[192,640]{1,0:T(8,128)(2,1)S(1)} collective-permute-done((bf16[192,640]{1,0:T(8,128)(2,1)S(1)}, bf16[192,640]{1,0:T(8,128)(2,1)S(1)}, u32[]{:S(2)}, u32[]{:S(2)}) %collective-permute-start.28) | collective-permute-done | bytes 245792 | tf_op jit(solution)/shard_map/ppermute | solution.py:26
  123.1 2.4 %collective-permute-start.32 = (bf16[48,640]{1,0:T(8,128)(2,1)S(1)}, bf16[48,640]{1,0:T(8,128)(2,1)S(1)}, u32[]{:S(2)}, u32[]{:S(2)}) collective-permute-start(bf16[48,640]{1,0:T(8,128)(2,1)S(1)} %get-tuple-element.59), channel_id=1, source_target_pairs={{0,2},{1,3},{2,0},{3,1},{4,6},{5,7},{6,4},{7,5},{8,10},{9,11},{10,... | collective-permute-start | bytes 184328 | tf_op jit(solution)/shard_map/ppermute | solution.py:26
  125.5 2.0 %collective-permute-start.33 = (bf16[48,640]{1,0:T(8,128)(2,1)S(1)}, bf16[48,640]{1,0:T(8,128)(2,1)S(1)}, u32[]{:S(2)}, u32[]{:S(2)}) collective-permute-start(bf16[48,640]{1,0:T(8,128)(2,1)S(1)} %get-tuple-element.60), channel_id=1, source_target_pairs={{0,3},{1,2},{2,1},{3,0},{4,7},{5,6},{6,5},{7,4},{8,11},{9,10},{10,... | collective-permute-start | bytes 184328 | tf_op jit(solution)/shard_map/ppermute | solution.py:26
  127.8 1.7 %collective-permute-start.36 = (bf16[48,384]{1,0:T(8,128)(2,1)S(1)}, bf16[48,384]{1,0:T(8,128)(2,1)S(1)}, u32[]{:S(2)}, u32[]{:S(2)}) collective-permute-start(bf16[48,384]{1,0:T(8,128)(2,1)S(1)} %get-tuple-element.69), channel_id=1, source_target_pairs={{0,3},{1,2},{2,1},{3,0},{4,7},{5,6},{6,5},{7,4},{8,11},{9,10},{10,... | collective-permute-start | bytes 110600 | tf_op jit(solution)/shard_map/ppermute | solution.py:26
  129.6 1.6 %collective-permute-start.35 = (bf16[48,384]{1,0:T(8,128)(2,1)S(1)}, bf16[48,384]{1,0:T(8,128)(2,1)S(1)}, u32[]{:S(2)}, u32[]{:S(2)}) collective-permute-start(bf16[48,384]{1,0:T(8,128)(2,1)S(1)} %get-tuple-element.70), channel_id=1, source_target_pairs={{0,2},{1,3},{2,0},{3,1},{4,6},{5,7},{6,4},{7,5},{8,10},{9,11},{10,... | collective-permute-start | bytes 110600 | tf_op jit(solution)/shard_map/ppermute | solution.py:26
  132.0 1.6 %collective-permute-done.36 = bf16[48,384]{1,0:T(8,128)(2,1)S(1)} collective-permute-done((bf16[48,384]{1,0:T(8,128)(2,1)S(1)}, bf16[48,384]{1,0:T(8,128)(2,1)S(1)}, u32[]{:S(2)}, u32[]{:S(2)}) %collective-permute-start.36) | collective-permute-done | bytes 36896 | tf_op jit(solution)/shard_map/ppermute | solution.py:26
  (90 shorter events, 11.8 us)
Async XLA Ops:
  0.0 5.2 %collective-permute-start = (bf16[48,1024]{1,0:T(8,128)(2,1)}, bf16[48,1024]{1,0:T(8,128)(2,1)S(1)}, u32[]{:S(2)}, u32[]{:S(2)}) collective-permute-start(bf16[48,1024]{1,0:T(8,128)(2,1)} %refs_0_.1), channel_id=1, source_target_pairs={{0,1},{1,0},{2,3},{3,2},{4,5},{5,4},{6,7},{7,6},{8,9},{9,8},{10,11... | collective-permute-start | bytes 294920 | tf_op jit(solution)/shard_map/ppermute | solution.py:26
  1.9 8.9 %collective-permute-start.4 = (bf16[48,1024]{1,0:T(8,128)(2,1)}, bf16[48,1024]{1,0:T(8,128)(2,1)S(1)}, u32[]{:S(2)}, u32[]{:S(2)}) collective-permute-start(bf16[48,1024]{1,0:T(8,128)(2,1)} %refs_0_.1), channel_id=1, source_target_pairs={{0,3},{1,2},{2,1},{3,0},{4,7},{5,6},{6,5},{7,4},{8,11},{9,10},{10,... | collective-permute-start | bytes 294920 | tf_op jit(solution)/shard_map/ppermute | solution.py:26
  4.7 9.5 %collective-permute-start.3 = (bf16[48,1024]{1,0:T(8,128)(2,1)}, bf16[48,1024]{1,0:T(8,128)(2,1)S(1)}, u32[]{:S(2)}, u32[]{:S(2)}) collective-permute-start(bf16[48,1024]{1,0:T(8,128)(2,1)} %refs_0_.1), channel_id=1, source_target_pairs={{0,2},{1,3},{2,0},{3,1},{4,6},{5,7},{6,4},{7,5},{8,10},{9,11},{10,... | collective-permute-start | bytes 294920 | tf_op jit(solution)/shard_map/ppermute | solution.py:26
  5.2 0.9 copy-start.2
  6.1 9.7 %collective-permute-start.1 = (bf16[96,1024]{1,0:T(8,128)(2,1)S(1)}, bf16[96,1024]{1,0:T(8,128)(2,1)S(1)}, u32[]{:S(2)}, u32[]{:S(2)}) collective-permute-start(bf16[96,1024]{1,0:T(8,128)(2,1)S(1)} %join.11.refs_0_), channel_id=1, source_target_pairs={{0,4},{1,5},{2,6},{3,7},{4,0},{5,1},{6,2},{7,3},{8,12},{9,13},{10,... | collective-permute-start | bytes 589832 | tf_op jit(solution)/shard_map/ppermute | solution.py:26
  14.3 6.9 %collective-permute-start.5 = (bf16[96,1024]{1,0:T(8,128)(2,1)S(1)}, bf16[96,1024]{1,0:T(8,128)(2,1)S(1)}, u32[]{:S(2)}, u32[]{:S(2)}) collective-permute-start(bf16[96,1024]{1,0:T(8,128)(2,1)S(1)} %join.13.refs_0_.refs_3_), channel_id=1, source_target_pairs={{0,4},{1,5},{2,6},{3,7},{4,0},{5,1},{6,2},{7,3},{8,12},{9,13},{10,... | collective-permute-start | bytes 589832 | tf_op jit(solution)/shard_map/ppermute | solution.py:26
  15.9 14.5 %collective-permute-start.2 = (bf16[192,1024]{1,0:T(8,128)(2,1)S(1)}, bf16[192,1024]{1,0:T(8,128)(2,1)S(1)}, u32[]{:S(2)}, u32[]{:S(2)}) collective-permute-start(bf16[192,1024]{1,0:T(8,128)(2,1)S(1)} %join.12), channel_id=1, source_target_pairs={{0,12},{1,13},{2,14},{3,15},{4,8},{5,9},{6,10},{7,11},{8,4},{9,5},... | collective-permute-start | bytes 1179656 | tf_op jit(solution)/shard_map/ppermute | solution.py:26
  21.2 9.6 %collective-permute-start.6 = (bf16[192,1024]{1,0:T(8,128)(2,1)S(1)}, bf16[192,1024]{1,0:T(8,128)(2,1)S(1)}, u32[]{:S(2)}, u32[]{:S(2)}) collective-permute-start(bf16[192,1024]{1,0:T(8,128)(2,1)S(1)} %join.14), channel_id=1, source_target_pairs={{0,12},{1,13},{2,14},{3,15},{4,8},{5,9},{6,10},{7,11},{8,4},{9,5},... | collective-permute-start | bytes 1179656 | tf_op jit(solution)/shard_map/ppermute | solution.py:26
  25.0 2.0 %copy-start = (bf16[1024,1664]{1,0:T(8,128)(2,1)S(1)}, bf16[1024,1664]{1,0:T(8,128)(2,1)}, u32[]{:S(2)}) copy-start(bf16[1024,1664]{1,0:T(8,128)(2,1)} %gate_ref) | copy-start | bytes 10223620
  27.0 2.0 %copy-start.1 = (bf16[1024,1664]{1,0:T(8,128)(2,1)S(1)}, bf16[1024,1664]{1,0:T(8,128)(2,1)}, u32[]{:S(2)}) copy-start(bf16[1024,1664]{1,0:T(8,128)(2,1)} %up_ref.1) | copy-start | bytes 10223620
  33.0 2.7 %collective-permute-start.7 = (bf16[128,3328]{1,0:T(8,128)(2,1)S(1)}, bf16[128,3328]{1,0:T(8,128)(2,1)S(1)}, u32[]{:S(2)}, u32[]{:S(2)}) collective-permute-start(bf16[128,3328]{1,0:T(8,128)(2,1)S(1)} %slice.155), channel_id=1, source_target_pairs={{0,16},{1,17},{2,18},{3,19},{4,20},{5,21},{6,22},{7,23},{8,24},{9,... | collective-permute-start | bytes 2555912 | tf_op jit(solution)/shard_map/ppermute | solution.py:26
  35.1 3.9 %collective-permute-start.10 = (bf16[128,3328]{1,0:T(8,128)(2,1)S(1)}, bf16[128,3328]{1,0:T(8,128)(2,1)S(1)}, u32[]{:S(2)}, u32[]{:S(2)}) collective-permute-start(bf16[128,3328]{1,0:T(8,128)(2,1)S(1)} %slice.156), channel_id=1, source_target_pairs={{0,16},{1,17},{2,18},{3,19},{4,20},{5,21},{6,22},{7,23},{8,24},{9,... | collective-permute-start | bytes 2555912 | tf_op jit(solution)/shard_map/ppermute | solution.py:26
  36.0 8.4 %collective-permute-start.8 = (bf16[64,3328]{1,0:T(8,128)(2,1)S(1)}, bf16[64,3328]{1,0:T(8,128)(2,1)S(1)}, u32[]{:S(2)}, u32[]{:S(2)}) collective-permute-start(bf16[64,3328]{1,0:T(8,128)(2,1)S(1)} %slice.158), channel_id=1, source_target_pairs={{0,32},{1,33},{2,34},{3,35},{4,36},{5,37},{6,38},{7,39},{8,40},{9,... | collective-permute-start | bytes 1277960 | tf_op jit(solution)/shard_map/ppermute | solution.py:26
  39.0 2.5 %collective-permute-start.9 = (bf16[128,3328]{1,0:T(8,128)(2,1)S(1)}, bf16[128,3328]{1,0:T(8,128)(2,1)S(1)}, u32[]{:S(2)}, u32[]{:S(2)}) collective-permute-start(bf16[128,3328]{1,0:T(8,128)(2,1)S(1)} %slice.160), channel_id=1, source_target_pairs={{0,16},{1,17},{2,18},{3,19},{4,20},{5,21},{6,22},{7,23},{8,24},{9,... | collective-permute-start | bytes 2555912 | tf_op jit(solution)/shard_map/ppermute | solution.py:26
  39.3 11.2 %collective-permute-start.12 = (bf16[64,3328]{1,0:T(8,128)(2,1)S(1)}, bf16[64,3328]{1,0:T(8,128)(2,1)S(1)}, u32[]{:S(2)}, u32[]{:S(2)}) collective-permute-start(bf16[64,3328]{1,0:T(8,128)(2,1)S(1)} %slice.162), channel_id=1, source_target_pairs={{0,32},{1,33},{2,34},{3,35},{4,36},{5,37},{6,38},{7,39},{8,40},{9,... | collective-permute-start | bytes 1277960 | tf_op jit(solution)/shard_map/ppermute | solution.py:26
  41.7 17.9 %collective-permute-start.15 = (bf16[64,3328]{1,0:T(8,128)(2,1)S(1)}, bf16[64,3328]{1,0:T(8,128)(2,1)S(1)}, u32[]{:S(2)}, u32[]{:S(2)}) collective-permute-start(bf16[64,3328]{1,0:T(8,128)(2,1)S(1)} %slice.163), channel_id=1, source_target_pairs={{0,32},{1,33},{2,34},{3,35},{4,36},{5,37},{6,38},{7,39},{8,40},{9,... | collective-permute-start | bytes 1277960 | tf_op jit(solution)/shard_map/ppermute | solution.py:26
  44.5 9.5 %collective-permute-start.11 = (bf16[32,3328]{1,0:T(8,128)(2,1)S(1)}, bf16[32,3328]{1,0:T(8,128)(2,1)S(1)}, u32[]{:S(2)}, u32[]{:S(2)}) collective-permute-start(bf16[32,3328]{1,0:T(8,128)(2,1)S(1)} %slice.165), channel_id=1, source_target_pairs={{0,96},{1,97},{2,98},{3,99},{4,100},{5,101},{6,102},{7,103},{8,104... | collective-permute-start | bytes 638984 | tf_op jit(solution)/shard_map/ppermute | solution.py:26
  50.7 9.4 %collective-permute-start.14 = (bf16[32,3328]{1,0:T(8,128)(2,1)S(1)}, bf16[32,3328]{1,0:T(8,128)(2,1)S(1)}, u32[]{:S(2)}, u32[]{:S(2)}) collective-permute-start(bf16[32,3328]{1,0:T(8,128)(2,1)S(1)} %slice.167), channel_id=1, source_target_pairs={{0,96},{1,97},{2,98},{3,99},{4,100},{5,101},{6,102},{7,103},{8,104... | collective-permute-start | bytes 638984 | tf_op jit(solution)/shard_map/ppermute | solution.py:26
  54.1 10.7 %collective-permute-start.13 = (bf16[16,3328]{1,0:T(8,128)(2,1)S(1)}, bf16[16,3328]{1,0:T(8,128)(2,1)S(1)}, u32[]{:S(2)}, u32[]{:S(2)}) collective-permute-start(bf16[16,3328]{1,0:T(8,128)(2,1)S(1)} %get-tuple-element.66), channel_id=1, source_target_pairs={{0,128},{1,129},{2,130},{3,131},{4,132},{5,133},{6,134},{7,135},{8... | collective-permute-start | bytes 319496 | tf_op jit(solution)/shard_map/ppermute | solution.py:26
  59.8 7.1 %collective-permute-start.17 = (bf16[32,3328]{1,0:T(8,128)(2,1)S(1)}, bf16[32,3328]{1,0:T(8,128)(2,1)S(1)}, u32[]{:S(2)}, u32[]{:S(2)}) collective-permute-start(bf16[32,3328]{1,0:T(8,128)(2,1)S(1)} %slice.172), channel_id=1, source_target_pairs={{0,96},{1,97},{2,98},{3,99},{4,100},{5,101},{6,102},{7,103},{8,104... | collective-permute-start | bytes 638984 | tf_op jit(solution)/shard_map/ppermute | solution.py:26
  60.2 10.8 %collective-permute-start.16 = (bf16[16,3328]{1,0:T(8,128)(2,1)S(1)}, bf16[16,3328]{1,0:T(8,128)(2,1)S(1)}, u32[]{:S(2)}, u32[]{:S(2)}) collective-permute-start(bf16[16,3328]{1,0:T(8,128)(2,1)S(1)} %get-tuple-element.65), channel_id=1, source_target_pairs={{0,128},{1,129},{2,130},{3,131},{4,132},{5,133},{6,134},{7,135},{8... | collective-permute-start | bytes 319496 | tf_op jit(solution)/shard_map/ppermute | solution.py:26
  67.0 11.7 %collective-permute-start.18 = (bf16[16,3328]{1,0:T(8,128)(2,1)S(1)}, bf16[16,3328]{1,0:T(8,128)(2,1)S(1)}, u32[]{:S(2)}, u32[]{:S(2)}) collective-permute-start(bf16[16,3328]{1,0:T(8,128)(2,1)S(1)} %get-tuple-element.63), channel_id=1, source_target_pairs={{0,128},{1,129},{2,130},{3,131},{4,132},{5,133},{6,134},{7,135},{8... | collective-permute-start | bytes 319496 | tf_op jit(solution)/shard_map/ppermute | solution.py:26
  71.1 11.0 %collective-permute-start.21 = (bf16[32,1664]{1,0:T(8,128)(2,1)S(1)}, bf16[32,1664]{1,0:T(8,128)(2,1)S(1)}, u32[]{:S(2)}, u32[]{:S(2)}) collective-permute-start(bf16[32,1664]{1,0:T(8,128)(2,1)S(1)} %join.15.refs_0_), channel_id=1, source_target_pairs={{0,128},{1,129},{2,130},{3,131},{4,132},{5,133},{6,134},{7,135},{8... | collective-permute-start | bytes 319496 | tf_op jit(solution)/shard_map/ppermute | solution.py:26
  78.7 8.1 %collective-permute-start.22 = (bf16[16,1664]{1,0:T(8,128)(2,1)S(1)}, bf16[16,1664]{1,0:T(8,128)(2,1)S(1)}, u32[]{:S(2)}, u32[]{:S(2)}) collective-permute-start(bf16[16,1664]{1,0:T(8,128)(2,1)S(1)} %silu.5.refs_1_), channel_id=1, source_target_pairs={{0,128},{1,129},{2,130},{3,131},{4,132},{5,133},{6,134},{7,135},{8... | collective-permute-start | bytes 159752 | tf_op jit(solution)/shard_map/ppermute | solution.py:26
  81.4 8.3 %collective-permute-start.19 = (bf16[48,1664]{1,0:T(8,128)(2,1)S(1)}, bf16[48,1664]{1,0:T(8,128)(2,1)S(1)}, u32[]{:S(2)}, u32[]{:S(2)}) collective-permute-start(bf16[48,1664]{1,0:T(8,128)(2,1)S(1)} %join.16.refs_0_), channel_id=1, source_target_pairs={{0,96},{1,97},{2,98},{3,99},{4,100},{5,101},{6,102},{7,103},{8,104... | collective-permute-start | bytes 479240 | tf_op jit(solution)/shard_map/ppermute | solution.py:26
  86.9 8.3 %collective-permute-start.23 = (bf16[48,1664]{1,0:T(8,128)(2,1)S(1)}, bf16[48,1664]{1,0:T(8,128)(2,1)S(1)}, u32[]{:S(2)}, u32[]{:S(2)}) collective-permute-start(bf16[48,1664]{1,0:T(8,128)(2,1)S(1)} %join.19.refs_0_), channel_id=1, source_target_pairs={{0,96},{1,97},{2,98},{3,99},{4,100},{5,101},{6,102},{7,103},{8,104... | collective-permute-start | bytes 479240 | tf_op jit(solution)/shard_map/ppermute | solution.py:26
  89.7 7.1 %collective-permute-start.20 = (bf16[96,1664]{1,0:T(8,128)(2,1)S(1)}, bf16[96,1664]{1,0:T(8,128)(2,1)S(1)}, u32[]{:S(2)}, u32[]{:S(2)}) collective-permute-start(bf16[96,1664]{1,0:T(8,128)(2,1)S(1)} %join.17.refs_0_), channel_id=1, source_target_pairs={{0,32},{1,33},{2,34},{3,35},{4,36},{5,37},{6,38},{7,39},{8,40},{9,... | collective-permute-start | bytes 958472 | tf_op jit(solution)/shard_map/ppermute | solution.py:26
  95.2 7.1 %collective-permute-start.24 = (bf16[96,1664]{1,0:T(8,128)(2,1)S(1)}, bf16[96,1664]{1,0:T(8,128)(2,1)S(1)}, u32[]{:S(2)}, u32[]{:S(2)}) collective-permute-start(bf16[96,1664]{1,0:T(8,128)(2,1)S(1)} %join.20.refs_0_), channel_id=1, source_target_pairs={{0,32},{1,33},{2,34},{3,35},{4,36},{5,37},{6,38},{7,39},{8,40},{9,... | collective-permute-start | bytes 958472 | tf_op jit(solution)/shard_map/ppermute | solution.py:26
  96.8 8.3 %copy-start.3 = (bf16[1664,1024]{1,0:T(8,128)(2,1)S(1)}, bf16[1664,1024]{1,0:T(8,128)(2,1)}, u32[]{:S(2)}) copy-start(bf16[1664,1024]{1,0:T(8,128)(2,1)} %param.7) | copy-start | bytes 10223620
  96.8 5.9 %collective-permute-start.25 = (bf16[192,1664]{1,0:T(8,128)(2,1)S(1)}, bf16[192,1664]{1,0:T(8,128)(2,1)S(1)}, u32[]{:S(2)}, u32[]{:S(2)}) collective-permute-start(bf16[192,1664]{1,0:T(8,128)(2,1)S(1)} %join.18.refs_0_), channel_id=1, source_target_pairs={{0,16},{1,17},{2,18},{3,19},{4,20},{5,21},{6,22},{7,23},{8,24},{9,... | collective-permute-start | bytes 1916936 | tf_op jit(solution)/shard_map/ppermute | solution.py:26
  102.4 2.4 %collective-permute-start.26 = (bf16[192,1664]{1,0:T(8,128)(2,1)S(1)}, bf16[192,1664]{1,0:T(8,128)(2,1)S(1)}, u32[]{:S(2)}, u32[]{:S(2)}) collective-permute-start(bf16[192,1664]{1,0:T(8,128)(2,1)S(1)} %join.21.refs_1_), channel_id=1, source_target_pairs={{0,16},{1,17},{2,18},{3,19},{4,20},{5,21},{6,22},{7,23},{8,24},{9,... | collective-permute-start | bytes 1916936 | tf_op jit(solution)/shard_map/ppermute | solution.py:26
  106.4 10.1 %collective-permute-start.27 = (bf16[384,640]{1,0:T(8,128)(2,1)S(1)}, bf16[384,640]{1,0:T(8,128)(2,1)S(1)}, u32[]{:S(2)}, u32[]{:S(2)}) collective-permute-start(bf16[384,640]{1,0:T(8,128)(2,1)S(1)} %fusion.4), channel_id=1, source_target_pairs={{0,12},{1,13},{2,14},{3,15},{4,8},{5,9},{6,10},{7,11},{8,4},{9,5},... | collective-permute-start | bytes 1474568 | tf_op jit(solution)/shard_map/ppermute | solution.py:26
  110.5 9.8 %collective-permute-start.29 = (bf16[384,384]{1,0:T(8,128)(2,1)S(1)}, bf16[384,384]{1,0:T(8,128)(2,1)S(1)}, u32[]{:S(2)}, u32[]{:S(2)}) collective-permute-start(bf16[384,384]{1,0:T(8,128)(2,1)S(1)} %convolution_convert_fusion.4), channel_id=1, source_target_pairs={{0,12},{1,13},{2,14},{3,15},{4,8},{5,9},{6,10},{7,11},{8,4},{9,5},... | collective-permute-start | bytes 884744 | tf_op jit(solution)/shard_map/ppermute | solution.py:26
  116.6 6.3 %collective-permute-start.28 = (bf16[192,640]{1,0:T(8,128)(2,1)S(1)}, bf16[192,640]{1,0:T(8,128)(2,1)S(1)}, u32[]{:S(2)}, u32[]{:S(2)}) collective-permute-start(bf16[192,640]{1,0:T(8,128)(2,1)S(1)} %slice.179), channel_id=1, source_target_pairs={{0,4},{1,5},{2,6},{3,7},{4,0},{5,1},{6,2},{7,3},{8,12},{9,13},{10,... | collective-permute-start | bytes 737288 | tf_op jit(solution)/shard_map/ppermute | solution.py:26
  120.4 7.1 %collective-permute-start.30 = (bf16[192,384]{1,0:T(8,128)(2,1)S(1)}, bf16[192,384]{1,0:T(8,128)(2,1)S(1)}, u32[]{:S(2)}, u32[]{:S(2)}) collective-permute-start(bf16[192,384]{1,0:T(8,128)(2,1)S(1)} %slice.181), channel_id=1, source_target_pairs={{0,4},{1,5},{2,6},{3,7},{4,0},{5,1},{6,2},{7,3},{8,12},{9,13},{10,... | collective-permute-start | bytes 442376 | tf_op jit(solution)/shard_map/ppermute | solution.py:26
  123.0 4.5 %collective-permute-start.31 = (bf16[48,640]{1,0:T(8,128)(2,1)S(1)}, bf16[48,640]{1,0:T(8,128)(2,1)S(1)}, u32[]{:S(2)}, u32[]{:S(2)}) collective-permute-start(bf16[48,640]{1,0:T(8,128)(2,1)S(1)} %get-tuple-element.61), channel_id=1, source_target_pairs={{0,1},{1,0},{2,3},{3,2},{4,5},{5,4},{6,7},{7,6},{8,9},{9,8},{10,11... | collective-permute-start | bytes 184328 | tf_op jit(solution)/shard_map/ppermute | solution.py:26
  123.1 8.0 %collective-permute-start.32 = (bf16[48,640]{1,0:T(8,128)(2,1)S(1)}, bf16[48,640]{1,0:T(8,128)(2,1)S(1)}, u32[]{:S(2)}, u32[]{:S(2)}) collective-permute-start(bf16[48,640]{1,0:T(8,128)(2,1)S(1)} %get-tuple-element.59), channel_id=1, source_target_pairs={{0,2},{1,3},{2,0},{3,1},{4,6},{5,7},{6,4},{7,5},{8,10},{9,11},{10,... | collective-permute-start | bytes 184328 | tf_op jit(solution)/shard_map/ppermute | solution.py:26
  125.5 6.4 %collective-permute-start.33 = (bf16[48,640]{1,0:T(8,128)(2,1)S(1)}, bf16[48,640]{1,0:T(8,128)(2,1)S(1)}, u32[]{:S(2)}, u32[]{:S(2)}) collective-permute-start(bf16[48,640]{1,0:T(8,128)(2,1)S(1)} %get-tuple-element.60), channel_id=1, source_target_pairs={{0,3},{1,2},{2,1},{3,0},{4,7},{5,6},{6,5},{7,4},{8,11},{9,10},{10,... | collective-permute-start | bytes 184328 | tf_op jit(solution)/shard_map/ppermute | solution.py:26
  127.6 4.4 %collective-permute-start.34 = (bf16[48,384]{1,0:T(8,128)(2,1)S(1)}, bf16[48,384]{1,0:T(8,128)(2,1)S(1)}, u32[]{:S(2)}, u32[]{:S(2)}) collective-permute-start(bf16[48,384]{1,0:T(8,128)(2,1)S(1)} %get-tuple-element.68), channel_id=1, source_target_pairs={{0,1},{1,0},{2,3},{3,2},{4,5},{5,4},{6,7},{7,6},{8,9},{9,8},{10,11... | collective-permute-start | bytes 110600 | tf_op jit(solution)/shard_map/ppermute | solution.py:26
  127.8 5.8 %collective-permute-start.36 = (bf16[48,384]{1,0:T(8,128)(2,1)S(1)}, bf16[48,384]{1,0:T(8,128)(2,1)S(1)}, u32[]{:S(2)}, u32[]{:S(2)}) collective-permute-start(bf16[48,384]{1,0:T(8,128)(2,1)S(1)} %get-tuple-element.69), channel_id=1, source_target_pairs={{0,3},{1,2},{2,1},{3,0},{4,7},{5,6},{6,5},{7,4},{8,11},{9,10},{10,... | collective-permute-start | bytes 110600 | tf_op jit(solution)/shard_map/ppermute | solution.py:26
  129.6 4.9 %collective-permute-start.35 = (bf16[48,384]{1,0:T(8,128)(2,1)S(1)}, bf16[48,384]{1,0:T(8,128)(2,1)S(1)}, u32[]{:S(2)}, u32[]{:S(2)}) collective-permute-start(bf16[48,384]{1,0:T(8,128)(2,1)S(1)} %get-tuple-element.70), channel_id=1, source_target_pairs={{0,2},{1,3},{2,0},{3,1},{4,6},{5,7},{6,4},{7,5},{8,10},{9,11},{10,... | collective-permute-start | bytes 110600 | tf_op jit(solution)/shard_map/ppermute | solution.py:26
